TPU v7x, 32 devices: a whole 2x2x4 slice. The times are simulated.
32 devices in a mesh: dp: 16 (over z, x, core), fsdp: 2 (over y).
Axes of the slice: x: 2, y: 2, z: 4, core: 2. Of those that a mesh axis runs over, the one named last changes fastest.
Arguments:
- partials: bfloat16 [16, 3840, 1024], P('dp', None, 'fsdp'), may hold values from -16 to 16
- scales: float32 [16, 30, 1024], P('dp', None, 'fsdp'), may hold values from 0.25 to 4
Outputs:
- update: bfloat16 [3840, 1024], P('dp', 'fsdp')
All inputs are finite; a program needn't handle non-finite values.
Results may differ from a plain program's by a relative error of at most 0.0004.
Values may be sent and summed in bfloat16 or wider, within the bound.
No kernel may reach another device: no remote copies, remote signals or barrier semaphores. Data moves between devices by JAX's collectives and lax.ppermute only.
A program may use at most 64 MiB of HBM per device.

v0:
```python
import functools

import jax
import jax.numpy as jnp
import numpy as np
from jax import lax
from jax.experimental import pallas as pl
from jax.experimental.pallas import tpu as pltpu
from jax.sharding import PartitionSpec as P

BLOCK = 128
GRAIN = 16
CHUNKS = (3, 5, 4, 3)
LEAVE = (0, 1, 3)
STEPS = (
    ("sum", 0), ("halve", 0), ("sum", 1), ("halve", 1), ("finish", 0), ("sum", 2),
    ("sum", 3), ("halve", 2), ("finish", 1), ("finish", 2), ("finish", 3),
)
AFTER = {
    ("sum", 1): (("sent", 0), ("half", 0)),
    ("sum", 2): (("sent", 1), ("half", 1), ("grad", 0)),
    ("sum", 3): (("keep", 2),),
    ("halve", 2): (("keep", 3),),
    ("finish", 1): (("sent", 2), ("across", 0)),
    ("finish", 3): (("across", 1), ("grad", 2)),
}
ORDER = (0, 2, 1, 3)
PIECE = 256
HALF = PIECE // 2
NEAR = HALF + HALF // 2 + HALF
CROSS = 2 * HALF
PACKED = NEAR + CROSS
F32 = jnp.float32
BF16 = jnp.bfloat16
VMEM = 48 * 1024 * 1024
WHOLE = pl.BlockSpec(memory_space=pltpu.VMEM)
SCALARS = pl.BlockSpec(memory_space=pltpu.SMEM)
ANYWHERE = pl.BlockSpec(memory_space=pl.ANY)


def params():
    return pltpu.CompilerParams(vmem_limit_bytes=VMEM)


def split(value):
    high = value.astype(BF16)
    return high, (value - high.astype(F32)).astype(BF16)


def dot3(a, b, contract):
    dims = (contract, ((), ()))

    def one(u, v):
        return lax.dot_general(u, v, dims, preferred_element_type=F32)

    return one(a[0], b[0]) + (one(a[0], b[1]) + one(a[1], b[0]))


def slot_row(at, side, slot, own_rows):
    zed, ex, core = at[0], at[1], at[2]
    z = lax.bitwise_xor(zed, ORDER[slot])
    c = lax.bitwise_xor(core, side % 2)
    x = lax.bitwise_xor(ex, side // 2)
    return ((z * 2 + x) * 2 + c) * own_rows


SLOTS = len(ORDER)
GROUPS = {
    "halves": ((0, 1), (2,), (3,)),
    "pair": ((0, 1), (2, 3)),
    "direct": ((0,), (1,), (2,), (3,)),
}
ROUTES = ("halves", "halves", "halves", "direct")
SPAN = 4
TAIL = 3 * SLOTS * SPAN


def pack_kernel(own_rows, spans, at, values, scales, own, *refs):
    outs, gathered = refs[:-1], refs[-1]
    blocks = scales.shape[0]

    def copy(side, start, rows, out):
        for slot in range(SLOTS):
            base = pl.multiple_of(slot_row(at, side, slot, own_rows) + start, GRAIN)
            out[slot * rows : (slot + 1) * rows, :] = values[pl.ds(base, rows), :]

    def tail(side, out):
        for slot in range(SLOTS):
            first = slot_row(at, side, slot, own_rows) // BLOCK
            for n in range(SPAN):
                row = jnp.minimum(first + n, blocks - 1)
                gathered[slot * SPAN + n : slot * SPAN + n + 1, :] = scales[row]
        left = gathered[...]
        for n in range(3):
            part = left.astype(BF16)
            row = out.shape[0] - TAIL + n * SLOTS * SPAN
            out[row : row + SLOTS * SPAN, :] = part
            left = left - part.astype(F32)

    copy(0, 0, own_rows, own)
    copy(1, 0, own_rows, outs[0])
    tail(1, outs[0])
    for n, (start, rows) in enumerate(spans):
        for side in (2, 3):
            out = outs[2 * n + side - 1]
            copy(side, start, rows, out)
            if n == 0:
                tail(side, out)


def pack(values, scales, at, own_rows, spans):
    width = values.shape[1]
    lengths = [SLOTS * own_rows, SLOTS * own_rows + TAIL]
    for n, (_, rows) in enumerate(spans):
        lengths += [SLOTS * rows + (TAIL if n == 0 else 0)] * 2
    return pl.pallas_call(
        functools.partial(pack_kernel, own_rows, spans),
        in_specs=[SCALARS, WHOLE, WHOLE],
        out_specs=[WHOLE] * len(lengths),
        out_shape=[jax.ShapeDtypeStruct((rows, width), BF16) for rows in lengths],
        scratch_shapes=[pltpu.VMEM((SLOTS * SPAN, width), F32)],
        compiler_params=params(),
        name="pack_rows",
    )(at, values, scales)


def dequant_kernel(own_rows, start, rows, groups, at, scales, own, core_raw, *refs):
    heads, raws, refs = refs[:2], refs[2:4], refs[4:]
    outs, packed = refs[-1 - len(groups) : -1], refs[-1]
    size = SLOTS * SPAN
    for n, ref in enumerate((core_raw, *heads)):
        row = ref.shape[0] - TAIL
        parts = [
            ref[row + k * size : row + (k + 1) * size, :].astype(F32) for k in range(3)
        ]
        packed[n * size : (n + 1) * size, :] = parts[0] + parts[1] + parts[2]
    for slot in range(SLOTS):
        base = slot_row(at, 0, slot, own_rows)
        for g in range(rows // GRAIN):
            block = (base + (start + g * GRAIN)) // BLOCK
            span = slot * SPAN + block - base // BLOCK
            here = slice(g * GRAIN, (g + 1) * GRAIN)
            row = slot * own_rows + start + g * GRAIN
            there = slice(row, row + GRAIN)
            row = slot * rows + g * GRAIN
            total = own[there, :].astype(F32) * scales[block]
            total += core_raw[there, :].astype(F32) * packed[pl.ds(span, 1), :]
            for n, raw in enumerate(raws):
                part = raw[row : row + GRAIN, :].astype(F32)
                total += part * packed[pl.ds((n + 1) * size + span, 1), :]
            for out, group in zip(outs, groups):
                if slot in group and len(group) > 1:
                    out[group.index(slot), here, :] = total
                elif slot in group:
                    out[here, :] = total


def dequant(
    at, scales, own, core_raw, heads, raws, own_rows, start, rows, groups, after, carry
):
    width = own.shape[1]
    shapes = [
        jax.ShapeDtypeStruct((len(group), rows, width)[len(group) == 1 :], F32)
        for group in groups
    ]
    first, count, made = 8 + len(after), len(carry), len(groups)

    def kernel(*refs):
        kept = refs[:8] + refs[first + count : first + count + made] + refs[-1:]
        dequant_kernel(own_rows, start, rows, groups, *kept)

    outs = pl.pallas_call(
        kernel,
        in_specs=[SCALARS] + [WHOLE] * 7 + [ANYWHERE] * (len(after) + count),
        out_specs=[WHOLE] * made + [ANYWHERE] * count,
        out_shape=shapes + [jax.ShapeDtypeStruct(x.shape, x.dtype) for x in carry],
        scratch_shapes=[pltpu.VMEM((3 * SLOTS * SPAN, width), F32)],
        input_output_aliases={first + n: made + n for n in range(count)},
        compiler_params=params(),
        name="dequant_sum",
    )(at, scales, own, core_raw, *heads, *raws, *after, *carry)
    return outs[:made], outs[made:]


def add(terms, after, swap=False):
    def kernel(*refs):
        total = refs[0][...]
        for ref in refs[1 : len(terms) - swap]:
            total = total + ref[...]
        if swap:
            last = refs[len(terms) - 1]
            refs[-1][0] = total[0] + last[1]
            refs[-1][1] = total[1] + last[0]
        else:
            refs[-1][...] = total

    return pl.pallas_call(
        kernel,
        in_specs=[WHOLE] * len(terms) + [ANYWHERE] * len(after),
        out_specs=WHOLE,
        out_shape=jax.ShapeDtypeStruct(terms[0].shape, F32),
        compiler_params=params(),
        name="add_rows",
    )(*terms, *after)


def put_rows(slabs, high, low, column):
    row = 0
    for slab in slabs:
        here, share = slice(row, row + slab.shape[0]), slab.shape[1]
        high[here, column : column + share], low[here, column : column + share] = split(slab[...])
        row += slab.shape[0]


def put_slots(at, flat, out):
    part = out.shape[1]
    for slot in range(8):
        z = lax.bitwise_xor(at[0], ORDER[slot % 4])
        x = lax.bitwise_xor(at[1], slot // 4)
        out[slot] = flat[pl.ds(pl.multiple_of((z * 2 + x) * part, 8), part), :]


def near_kernel(count, at, *refs):
    slabs, outs, (high, low, flat) = refs[:count], refs[count : count + 2], refs[-3:]
    put_rows(slabs, high, low, 0)

    def take(start, width):
        lanes = pl.ds(pl.multiple_of(start, HALF), width)
        return high[:, lanes], low[:, lanes]

    contract = ((0,), (0,))
    for side, out in enumerate(outs):
        core = lax.bitwise_xor(at[2], side)
        own = take(core * PIECE, PIECE)
        block = dot3(own, own, contract)
        flat[0:HALF, :] = block[0:HALF, :]
        flat[HALF : HALF + HALF // 2, 0:HALF] = block[HALF : HALF + HALF // 2, HALF:]
        flat[HALF : HALF + HALF // 2, HALF:] = block[HALF + HALF // 2 :, HALF:]
        left = take(core * HALF, HALF)
        flat[NEAR - HALF :, :] = dot3(left, take(PIECE, PIECE), contract)
        put_slots(at, flat, out)


def cross_kernel(count, at, *refs):
    slabs, outs, (high, low, flat) = refs[: 2 * count], refs[-5:-3], refs[-3:]
    share = slabs[0].shape[1]
    put_rows(slabs[:count], high, low, 0)
    put_rows(slabs[count:], high, low, share)

    def take(start, width):
        lanes = pl.ds(pl.multiple_of(start, HALF), width)
        return high[:, lanes], low[:, lanes]

    contract = ((0,), (0,))
    half = at[3]
    for side, out in enumerate(outs):
        core = lax.bitwise_xor(at[2], side)
        for k in range(2):
            mine = core * PIECE
            other = share + lax.bitwise_xor(core, k) * PIECE
            left = jnp.where(half == 0, mine, other + HALF)
            right = jnp.where(half == 0, other, mine)
            flat[k * HALF : (k + 1) * HALF, :] = dot3(
                take(left, HALF), take(right, PIECE), contract
            )
        put_slots(at, flat, out)


def gram_part(kernel, at, slabs, count, packed, name, after):
    rows = sum(slab.shape[0] for slab in slabs[:count])
    width = slabs[0].shape[1] * (len(slabs) // count)
    return pl.pallas_call(
        functools.partial(kernel, count),
        in_specs=[SCALARS] + [WHOLE] * len(slabs) + [ANYWHERE] * len(after),
        out_specs=[WHOLE] * 2,
        out_shape=[jax.ShapeDtypeStruct((8, packed // 8, PIECE), F32)] * 2,
        scratch_shapes=[pltpu.VMEM((rows, width), BF16)] * 2 + [pltpu.VMEM((packed, PIECE), F32)],
        compiler_params=params(),
        name=name,
    )(at, *slabs, *after)


def update_kernel(scale, places, count, at, *refs):
    pieces, refs = refs[: len(places)], refs[len(places) :]
    owns, acrosses, refs = refs[:count], refs[count : 2 * count], refs[2 * count :]
    out, packed, gram, high, low = refs
    zed, ex, core, half = at[0], at[1], at[2], at[3]
    for ref, (first, slots) in zip(pieces, places):
        part = ref.shape[1]
        for n, (kz, kx, kc, kf) in enumerate(slots):
            quarter = 2 * lax.bitwise_xor(half, kf) + lax.bitwise_xor(core, kc)
            chip = 2 * lax.bitwise_xor(zed, kz) + lax.bitwise_xor(ex, kx)
            row = pl.multiple_of(quarter * PACKED + first + chip * part, 8)
            packed[pl.ds(row, part), :] = ref[n]
    trace = jnp.zeros((1, 1), F32)
    rows = lax.broadcasted_iota(jnp.int32, (HALF, HALF), 0)
    columns = lax.broadcasted_iota(jnp.int32, (HALF, HALF), 1)

    def put(block, row, column):
        h, l = split(block)
        here = (slice(row, row + block.shape[0]), slice(column, column + block.shape[1]))
        high[here] = h
        low[here] = l

    for q in range(4):
        base, edge = q * PACKED, q * PIECE
        top = packed[base : base + HALF, :]
        bottom = packed[base + HALF : base + HALF + HALF // 2, :]
        bottom = jnp.concatenate([bottom[:, :HALF], bottom[:, HALF:]], 0)
        for block in (top[:, :HALF], bottom):
            trace += jnp.sum(jnp.where(rows == columns, block, 0.0), keepdims=True)
        put(top, edge, edge)
        put(top[:, HALF:].T, edge + HALF, edge)
        put(bottom, edge + HALF, edge + HALF)
        for k in range(1, 4):
            other = q ^ k
            if q > other:
                continue
            row = PACKED + (k - 4) * HALF
            for first, owner in ((0, q), (HALF, other)):
                block = packed[owner * PACKED + row : owner * PACKED + row + HALF, :]
                put(block, edge + first, other * PIECE)
                put(block.T, other * PIECE, edge + first)
    inv = 1.0 / (jnp.sqrt(trace) + 1e-07)
    share = owns[0].shape[1]
    contract = ((1,), (0,))

    def mine(which):
        return pl.ds(pl.multiple_of(which * share, share), share)

    unit = jnp.concatenate([own[...] for own in owns], 0) * inv
    far = jnp.concatenate([across[...] for across in acrosses], 0) * inv
    first = dot3(split(unit), (high[mine(half), :], low[mine(half), :]), contract)
    first += dot3(split(far), (high[mine(1 - half), :], low[mine(1 - half), :]), contract)
    first = first * (inv * inv)
    gram[...] = first
    second = dot3(split(first), (high[:, mine(half)], low[:, mine(half)]), contract)
    second = second * (inv * inv)
    result = 3.4445 * unit + (-4.775 * gram[:, mine(half)] + 2.0315 * second)
    out[...] = (scale * result).astype(out.dtype)


def update(at, pieces, places, owns, acrosses, scale):
    rows = sum(own.shape[0] for own in owns)
    share = owns[0].shape[1]
    width = 2 * share
    return pl.pallas_call(
        functools.partial(update_kernel, scale, places, len(owns)),
        in_specs=[SCALARS] + [WHOLE] * (len(pieces) + 2 * len(owns)),
        out_specs=WHOLE,
        out_shape=jax.ShapeDtypeStruct((rows, share), BF16),
        scratch_shapes=[
            pltpu.VMEM((4 * PACKED, PIECE), F32),
            pltpu.VMEM((rows, width), F32),
            pltpu.VMEM((width, width), BF16),
            pltpu.VMEM((width, width), BF16),
        ],
        compiler_params=params(),
        name="update",
    )(at, *pieces, *owns, *acrosses)


AXIS_BITS = {"f": 1, "c": 2, "x": 4, "z1": 8, "z2": 16}


def flip(value, *names):
    mask = sum(AXIS_BITS[name] for name in names)
    count = lax.axis_size(("dp", "fsdp"))
    return lax.ppermute(value, ("dp", "fsdp"), [(i, i ^ mask) for i in range(count)])


ZEDS = (("z2",), ("z1",), ("z1", "z2"))
SIDES = (("x",), ("c", "x"))


def fast_body(partials, scales):
    values, scales = partials[0], scales.transpose(1, 0, 2)
    features, share = values.shape
    own_rows = features // lax.axis_size("dp")
    rank = lax.axis_index("dp")
    at = jnp.stack([rank // 4, rank // 2 % 2, rank % 2, lax.axis_index("fsdp")])
    unit = own_rows // sum(CHUNKS)
    spans, start = [], 0
    for size in CHUNKS:
        spans.append((start, size * unit))
        start += size * unit

    own, core_raw, *outs = pack(values, scales, at, own_rows, spans)
    core_raw = flip(core_raw, "c")

    def cross(pair):
        return [flip(out, *side) for out, side in zip(pair, SIDES)]

    outs = [outs[2 * n : 2 * n + 2] for n in range(len(spans))]
    raws = [cross(pair) for pair in outs[:2]]
    heads = raws[0]
    owns, acrosses, held = [], [], []
    made = {}

    def there(step, n):
        return [made[name] for name in AFTER.get((step, n), ())]

    def add_partials(n):
        start, rows = spans[n]
        carry = outs[n + 2] if n + 2 < len(spans) else []
        (keep, *go), carry = dequant(
            at, scales, own, core_raw, heads, raws[n], own_rows, start, rows,
            GROUPS[ROUTES[n]], there("sum", n), carry,
        )
        if carry:
            raws.append(cross(carry))
        made["keep", n] = keep
        if ROUTES[n] == "direct":
            made["got", n] = [flip(part, *names) for part, names in zip(go, ZEDS)]
        elif ROUTES[n] == "halves":
            made["got", n] = [flip(part, "z1") for part in go]
        else:
            made["got", n] = flip(go[0], "z1")

    def halve(n):
        keep, got = made["keep", n], made["got", n]
        made["sent", n] = add([keep[1], got[1]], there("halve", n))
        made["half", n] = keep[0] + got[0]

    def finish(n):
        if ROUTES[n] == "direct":
            terms = [made["keep", n], *made["got", n]]
        else:
            terms = [made["half", n], flip(made["sent", n], "z2")]
        made["grad", n] = add(terms, there("finish", n))
        held.append(made["grad", n])
        if n in LEAVE:
            group = jnp.concatenate(held) if len(held) > 1 else held[0]
            across = flip(group, "f")
            made["across", n] = across
            owns.append(group)
            acrosses.append(across)
            held.clear()

    for step, n in STEPS:
        {"sum": add_partials, "halve": halve, "finish": finish}[step](n)

    count = len(owns)
    own, far = gram_part(near_kernel, at, owns, count, NEAR, "gram_near", [])
    core = flip(far, "c")
    near_sent = add([own[4:], core[4:]], [])
    near_x = flip(near_sent, "x")
    cross_own, far = gram_part(
        cross_kernel, at, owns + acrosses, count, CROSS, "gram_cross", [near_sent]
    )
    cross_core = [flip(far[4:], "c"), flip(far[:4], "c")]
    cross_x = flip(add([cross_own[4:], cross_core[0]], [near_x]), "x")

    near = own[:4] + core[:4] + near_x
    near_z1 = flip(near[2:], "z1")
    near = near[:2] + near_z1
    near_z2 = flip(near, "z2")
    near = add([near, near_z2], [], swap=True)
    near_other = flip(near, "z1")

    cross = add([cross_own[:4], cross_core[1], cross_x], [near_z1])
    cross = add([cross[:2], flip(cross[2:], "z1")], [near_z2])
    cross = add([cross, flip(cross, "z2")], [near_other], swap=True)
    cross_other = flip(cross, "z1")

    near = jnp.concatenate([near, near_other])
    near = jnp.concatenate([near, flip(near, "x")])
    cross = jnp.concatenate([cross, cross_other])
    cross = jnp.concatenate([cross, flip(cross, "f")])
    parts = [near, flip(near, "f"), cross, flip(cross, "x")]
    parts += [flip(part, "c") for part in parts]
    near_slots = [(z, x, 0, 0) for x in range(2) for z in ORDER]
    cross_slots = [(z, 0, 0, f) for f in range(2) for z in ORDER]
    slots = [
        near_slots,
        [(z, x, c, 1) for z, x, c, _ in near_slots],
        cross_slots,
        [(z, 1, c, f) for z, _, c, f in cross_slots],
    ]
    slots += [[(z, x, 1, f) for z, x, _, f in group] for group in slots]
    firsts = [0, 0, NEAR, NEAR] * 2
    places = list(zip(firsts, slots))
    scale = float(0.25 * np.sqrt(np.float32(features * 2 * share)))
    return update(at, parts, places, owns, acrosses, scale)


def plain_body(partials, scales):
    values, scales = partials[0], scales[0]
    features, share = values.shape
    dp = lax.axis_size("dp")
    rows = values.reshape(scales.shape[0], -1, share).astype(F32) * scales[:, None, :]
    summed = lax.psum_scatter(
        rows.reshape(features, share), "dp", scatter_dimension=0, tiled=True
    )
    slab = lax.all_gather(summed, "fsdp", axis=1, tiled=True)
    width = slab.shape[1]
    highest = functools.partial(
        jnp.dot, precision=lax.Precision.HIGHEST, preferred_element_type=F32
    )
    half = lax.axis_index("fsdp")
    gram = lax.psum(highest(summed.T, slab), "dp")
    gram = lax.all_gather(gram, "fsdp", axis=0, tiled=True)
    inv = 1.0 / (jnp.sqrt(jnp.trace(gram)) + 1e-07)
    scaled = gram * (inv * inv)
    first = highest(slab * inv, scaled)
    mine = lambda value: lax.dynamic_slice_in_dim(value, half * share, share, 1)
    second = highest(first, mine(scaled))
    result = 3.4445 * (summed * inv) + (-4.775 * mine(first) + 2.0315 * second)
    return (0.25 * jnp.sqrt(F32(features * width)) * result).astype(BF16)


def solution(mesh):
    dp, fsdp = mesh.shape["dp"], mesh.shape["fsdp"]

    def run(partials, scales):
        features, width = partials.shape[1:]
        fast = (
            (dp, fsdp) == (16, 2)
            and features % (dp * GRAIN * sum(CHUNKS)) == 0
            and width == 4 * PIECE
        )
        return jax.shard_map(
            fast_body if fast else plain_body,
            mesh=mesh,
            in_specs=(P("dp", None, "fsdp"), P("dp", None, "fsdp")),
            out_specs=P("dp", "fsdp"),
            check_vma=False,
        )(partials, scales)

    return run
```

profile of v0, /device:TPU:1, one launch (start us, length us, event | category | flops | bytes accessed | tf_op | source)
XLA Modules:
  0.0 124.5 jit_solution(4890054020976774613)
XLA Ops:
  0.9 2.5 %pack_rows.1 = (bf16[960,512]{1,0:T(8,128)(2,1)S(1)}, bf16[1008,512]{1,0:T(8,128)(2,1)S(1)}, bf16[240,512]{1,0:T(8,128)(2,1)S(1)}, bf16[240,512]{1,0:T(8,128)(2,...) custom-call(s32[4]{0:T(128)S(1)} %pad_add_fusion.at.refs_0_, ...), custom_call_target="tpu_custom_call" | custom-call | tf_op jit(solution)/shard_map/pack_rows/pallas_call | solution.py:116
  3.5 2.7 %collective-permute-start.1 = (bf16[240,512]{1,0:T(8,128)(2,1)S(1)}, bf16[240,512]{1,0:T(8,128)(2,1)S(1)}, u32[]{:S(2)}, u32[]{:S(2)}) collective-permute-start(bf16[240,512]{1,0:T(8,128)(2,1)S(1)} %get-tuple-element.38), channel_id=1, source_target_pairs={{0,4},{1,5},{2,6},{3,7},{4,0},{5,1},{6,2},{7,3},{8,12},{9,13},{10,... | collective-permute-start | bytes 737288 | tf_op jit(solution)/shard_map/ppermute | solution.py:369
  8.2 4.2 %collective-permute-done.1.refs_4_.refs_6_ = bf16[240,512]{1,0:T(8,128)(2,1)S(1)} collective-permute-done((bf16[240,512]{1,0:T(8,128)(2,1)S(1)}, bf16[240,512]{1,0:T(8,128)(2,1)S(1)}, u32[]{:S(2)}, u32[]{:S(2)}) %collective-permute-start.1) | collective-permute-done | bytes 245792 | tf_op jit(solution)/shard_map/ppermute | solution.py:369
  12.4 5.5 %collective-permute-done.2.refs_5_.refs_7_ = bf16[240,512]{1,0:T(8,128)(2,1)S(1)} collective-permute-done((bf16[240,512]{1,0:T(8,128)(2,1)S(1)}, bf16[240,512]{1,0:T(8,128)(2,1)S(1)}, u32[]{:S(2)}, u32[]{:S(2)}) %collective-permute-start.2) | collective-permute-done | bytes 245792 | tf_op jit(solution)/shard_map/ppermute | solution.py:369
  18.6 1.8 %collective-permute-start.3 = (f32[48,512]{1,0:T(8,128)S(1)}, f32[48,512]{1,0:T(8,128)S(1)}, u32[]{:S(2)}, u32[]{:S(2)}) collective-permute-start(f32[48,512]{1,0:T(8,128)S(1)} %get-tuple-element.43), channel_id=1, source_target_pairs={{0,8},{1,9},{2,10},{3,11},{4,12},{5,13},{6,14},{7,15},{8,0},{9,1},... | collective-permute-start | bytes 294920 | tf_op jit(solution)/shard_map/ppermute | solution.py:369
  21.9 3.7 %collective-permute-done.4.refs_1_ = f32[48,512]{1,0:T(8,128)S(1)} collective-permute-done((f32[48,512]{1,0:T(8,128)S(1)}, f32[48,512]{1,0:T(8,128)S(1)}, u32[]{:S(2)}, u32[]{:S(2)}) %collective-permute-start.4) | collective-permute-done | bytes 98336 | tf_op jit(solution)/shard_map/ppermute | solution.py:369
  25.6 2.0 %collective-permute-start.12 = (bf16[256,512]{1,0:T(8,128)(2,1)S(1)}, bf16[256,512]{1,0:T(8,128)(2,1)S(1)}, u32[]{:S(2)}, u32[]{:S(2)}) collective-permute-start(bf16[256,512]{1,0:T(8,128)(2,1)S(1)} %get-tuple-element.53), channel_id=1, source_target_pairs={{0,6},{1,7},{2,4},{3,5},{4,2},{5,3},{6,0},{7,1},{8,14},{9,15},{10,... | collective-permute-start | bytes 786440 | tf_op jit(solution)/shard_map/ppermute | solution.py:369
  27.6 2.4 %collective-permute-start.5 = (f32[48,512]{1,0:T(8,128)S(1)}, f32[48,512]{1,0:T(8,128)S(1)}, u32[]{:S(2)}, u32[]{:S(2)}) collective-permute-start(f32[48,512]{1,0:T(8,128)S(1)} %add_rows.13.refs_8_), channel_id=1, source_target_pairs={{0,16},{1,17},{2,18},{3,19},{4,20},{5,21},{6,22},{7,23},{8,24},{9,... | collective-permute-start | bytes 294920 | tf_op jit(solution)/shard_map/ppermute | solution.py:369
  30.0 2.3 %collective-permute-done.7.refs_7_ = bf16[320,512]{1,0:T(8,128)(2,1)S(1)} collective-permute-done((bf16[320,512]{1,0:T(8,128)(2,1)S(1)}, bf16[320,512]{1,0:T(8,128)(2,1)S(1)}, u32[]{:S(2)}, u32[]{:S(2)}) %collective-permute-start.7) | collective-permute-done | bytes 327712 | tf_op jit(solution)/shard_map/ppermute | solution.py:369
  33.1 1.8 %collective-permute-start.8 = (f32[80,512]{1,0:T(8,128)S(1)}, f32[80,512]{1,0:T(8,128)S(1)}, u32[]{:S(2)}, u32[]{:S(2)}) collective-permute-start(f32[80,512]{1,0:T(8,128)S(1)} %get-tuple-element.50), channel_id=1, source_target_pairs={{0,8},{1,9},{2,10},{3,11},{4,12},{5,13},{6,14},{7,15},{8,0},{9,1},... | collective-permute-start | bytes 491528 | tf_op jit(solution)/shard_map/ppermute | solution.py:369
  36.4 6.7 %collective-permute-done.9.refs_1_ = f32[80,512]{1,0:T(8,128)S(1)} collective-permute-done((f32[80,512]{1,0:T(8,128)S(1)}, f32[80,512]{1,0:T(8,128)S(1)}, u32[]{:S(2)}, u32[]{:S(2)}) %collective-permute-start.9) | collective-permute-done | bytes 163872 | tf_op jit(solution)/shard_map/ppermute | solution.py:369
  46.1 2.3 %collective-permute-start.10 = (f32[80,512]{1,0:T(8,128)S(1)}, f32[80,512]{1,0:T(8,128)S(1)}, u32[]{:S(2)}, u32[]{:S(2)}) collective-permute-start(f32[80,512]{1,0:T(8,128)S(1)} %add_rows.15.refs_8_), channel_id=1, source_target_pairs={{0,16},{1,17},{2,18},{3,19},{4,20},{5,21},{6,22},{7,23},{8,24},{9,... | collective-permute-start | bytes 491528 | tf_op jit(solution)/shard_map/ppermute | solution.py:369
  52.4 2.6 %collective-permute-start.19 = (f32[48,512]{1,0:T(8,128)S(1)}, f32[48,512]{1,0:T(8,128)S(1)}, u32[]{:S(2)}, u32[]{:S(2)}) collective-permute-start(f32[48,512]{1,0:T(8,128)S(1)} %get-tuple-element.60), channel_id=1, source_target_pairs={{0,16},{1,17},{2,18},{3,19},{4,20},{5,21},{6,22},{7,23},{8,24},{9,... | collective-permute-start | bytes 294920 | tf_op jit(solution)/shard_map/ppermute | solution.py:369
  58.2 2.9 %collective-permute-done.17 = f32[64,512]{1,0:T(8,128)S(1)} collective-permute-done((f32[64,512]{1,0:T(8,128)S(1)}, f32[64,512]{1,0:T(8,128)S(1)}, u32[]{:S(2)}, u32[]{:S(2)}) %collective-permute-start.17) | collective-permute-done | bytes 131104 | tf_op jit(solution)/shard_map/ppermute | solution.py:369
  61.3 4.6 %collective-permute-done.18.refs_1_ = f32[64,512]{1,0:T(8,128)S(1)} collective-permute-done((f32[64,512]{1,0:T(8,128)S(1)}, f32[64,512]{1,0:T(8,128)S(1)}, u32[]{:S(2)}, u32[]{:S(2)}) %collective-permute-start.18) | collective-permute-done | bytes 131104 | tf_op jit(solution)/shard_map/ppermute | solution.py:369
  67.2 6.0 %collective-permute-start.23 = (f32[8,40,256]{2,1,0:T(8,128)S(1)}, f32[8,40,256]{2,1,0:T(8,128)S(1)}, u32[]{:S(2)}, u32[]{:S(2)}) collective-permute-start(f32[8,40,256]{2,1,0:T(8,128)S(1)} %get-tuple-element.64), channel_id=1, source_target_pairs={{0,2},{1,3},{2,0},{3,1},{4,6},{5,7},{6,4},{7,5},{8,10},{9,11},{10,... | collective-permute-start | bytes 983048 | tf_op jit(solution)/shard_map/ppermute | solution.py:369
  74.9 5.5 %collective-permute-done.30.refs_5_.refs_13_ = f32[112,512]{1,0:T(8,128)S(1)} collective-permute-done((f32[112,512]{1,0:T(8,128)S(1)}, f32[112,512]{1,0:T(8,128)S(1)}, u32[]{:S(2)}, u32[]{:S(2)}) %collective-permute-start.30) | collective-permute-done | bytes 229408 | tf_op jit(solution)/shard_map/ppermute | solution.py:369
  84.0 2.7 %collective-permute-done.25.refs_3_ = f32[2,40,256]{2,1,0:T(8,128)S(1)} collective-permute-done((f32[2,40,256]{2,1,0:T(8,128)S(1)}, f32[2,40,256]{2,1,0:T(8,128)S(1)}, u32[]{:S(2)}, u32[]{:S(2)}) %collective-permute-start.25) | collective-permute-done | bytes 81952 | tf_op jit(solution)/shard_map/ppermute | solution.py:369
  89.8 3.7 %collective-permute-done.26.refs_1_.refs_2_ = f32[2,40,256]{2,1,0:T(8,128)S(1)} collective-permute-done((f32[2,40,256]{2,1,0:T(8,128)S(1)}, f32[2,40,256]{2,1,0:T(8,128)S(1)}, u32[]{:S(2)}, u32[]{:S(2)}) %collective-permute-start.26) | collective-permute-done | bytes 81952 | tf_op jit(solution)/shard_map/ppermute | solution.py:369
  93.7 3.1 %collective-permute-start.35 = (f32[2,32,256]{2,1,0:T(8,128)S(1)}, f32[2,32,256]{2,1,0:T(8,128)S(1)}, u32[]{:S(2)}, u32[]{:S(2)}) collective-permute-start(f32[2,32,256]{2,1,0:T(8,128)S(1)} %add_rows.24.refs_0_), channel_id=1, source_target_pairs={{0,16},{1,17},{2,18},{3,19},{4,20},{5,21},{6,22},{7,23},{8,24},{9,... | collective-permute-start | bytes 196616 | tf_op jit(solution)/shard_map/ppermute | solution.py:369
  106.8 6.6 %collective-permute-start.39 = (f32[8,40,256]{2,1,0:T(8,128)S(1)}, f32[8,40,256]{2,1,0:T(8,128)S(1)}, u32[]{:S(2)}, u32[]{:S(2)}) collective-permute-start(f32[8,40,256]{2,1,0:T(8,128)S(1)} %pad_maximum_fusion.refs_0_), channel_id=1, source_target_pairs={{0,2},{1,3},{2,0},{3,1},{4,6},{5,7},{6,4},{7,5},{8,10},{9,11},{10,... | collective-permute-start | bytes 983048 | tf_op jit(solution)/shard_map/ppermute | solution.py:369
  113.4 2.5 %collective-permute-start.40 = (f32[8,40,256]{2,1,0:T(8,128)S(1)}, f32[8,40,256]{2,1,0:T(8,128)S(1)}, u32[]{:S(2)}, u32[]{:S(2)}) collective-permute-start(f32[8,40,256]{2,1,0:T(8,128)S(1)} %collective-permute-done.29.refs_1_), channel_id=1, source_target_pairs={{0,2},{1,3},{2,0},{3,1},{4,6},{5,7},{6,4},{7,5},{8,10},{9,11},{10,... | collective-permute-start | bytes 983048 | tf_op jit(solution)/shard_map/ppermute | solution.py:369
  115.9 2.8 %collective-permute-start.42 = (f32[8,32,256]{2,1,0:T(8,128)S(1)}, f32[8,32,256]{2,1,0:T(8,128)S(1)}, u32[]{:S(2)}, u32[]{:S(2)}) collective-permute-start(f32[8,32,256]{2,1,0:T(8,128)S(1)} %collective-permute-done.38.refs_3_), channel_id=1, source_target_pairs={{0,2},{1,3},{2,0},{3,1},{4,6},{5,7},{6,4},{7,5},{8,10},{9,11},{10,... | collective-permute-start | bytes 786440 | tf_op jit(solution)/shard_map/ppermute | solution.py:369
  119.9 4.7 %update.1 = bf16[240,512]{1,0:T(8,128)(2,1)} custom-call(s32[4]{0:T(128)S(1)} %pad_add_fusion.at.refs_0_, f32[8,40,256]{2,1,0:T(8,128)S(1)} %pad_maximum_fusion.refs_0_, f32[8,40,256]{2,1,0:T(8,128)S(1)} %collective-permute-done.29.refs_1_, f32[8,32,256]{2,1,0:T(8,128)S(1)} %pad_maximum_fusion.1.refs_2_, f32[8,32,256]{2,1,0:T(8,128)S(1)} %collective-permute-done.38.refs_3_, ...), custom_call_target="tpu_custom_call" | custom-call | tf_op jit(solution)/shard_map/update/pallas_call | solution.py:347
  (107 shorter events, 38.9 us)
Async XLA Ops:
  3.4 14.5 %collective-permute-start = (bf16[1008,512]{1,0:T(8,128)(2,1)S(1)}, bf16[1008,512]{1,0:T(8,128)(2,1)S(1)}, u32[]{:S(2)}, u32[]{:S(2)}) collective-permute-start(bf16[1008,512]{1,0:T(8,128)(2,1)S(1)} %get-tuple-element.37), channel_id=1, source_target_pairs={{0,2},{1,3},{2,0},{3,1},{4,6},{5,7},{6,4},{7,5},{8,10},{9,11},{10,... | collective-permute-start | bytes 3096584 | tf_op jit(solution)/shard_map/ppermute | solution.py:369
  3.5 8.9 %collective-permute-start.1 = (bf16[240,512]{1,0:T(8,128)(2,1)S(1)}, bf16[240,512]{1,0:T(8,128)(2,1)S(1)}, u32[]{:S(2)}, u32[]{:S(2)}) collective-permute-start(bf16[240,512]{1,0:T(8,128)(2,1)S(1)} %get-tuple-element.38), channel_id=1, source_target_pairs={{0,4},{1,5},{2,6},{3,7},{4,0},{5,1},{6,2},{7,3},{8,12},{9,13},{10,... | collective-permute-start | bytes 737288 | tf_op jit(solution)/shard_map/ppermute | solution.py:369
  6.2 11.7 %collective-permute-start.2 = (bf16[240,512]{1,0:T(8,128)(2,1)S(1)}, bf16[240,512]{1,0:T(8,128)(2,1)S(1)}, u32[]{:S(2)}, u32[]{:S(2)}) collective-permute-start(bf16[240,512]{1,0:T(8,128)(2,1)S(1)} %get-tuple-element.39), channel_id=1, source_target_pairs={{0,6},{1,7},{2,4},{3,5},{4,2},{5,3},{6,0},{7,1},{8,14},{9,15},{10,... | collective-permute-start | bytes 737288 | tf_op jit(solution)/shard_map/ppermute | solution.py:369
  6.2 23.8 %collective-permute-start.6 = (bf16[320,512]{1,0:T(8,128)(2,1)S(1)}, bf16[320,512]{1,0:T(8,128)(2,1)S(1)}, u32[]{:S(2)}, u32[]{:S(2)}) collective-permute-start(bf16[320,512]{1,0:T(8,128)(2,1)S(1)} %get-tuple-element.45), channel_id=1, source_target_pairs={{0,4},{1,5},{2,6},{3,7},{4,0},{5,1},{6,2},{7,3},{8,12},{9,13},{10,... | collective-permute-start | bytes 983048 | tf_op jit(solution)/shard_map/ppermute | solution.py:369
  7.9 24.4 %collective-permute-start.7 = (bf16[320,512]{1,0:T(8,128)(2,1)S(1)}, bf16[320,512]{1,0:T(8,128)(2,1)S(1)}, u32[]{:S(2)}, u32[]{:S(2)}) collective-permute-start(bf16[320,512]{1,0:T(8,128)(2,1)S(1)} %get-tuple-element.46), channel_id=1, source_target_pairs={{0,6},{1,7},{2,4},{3,5},{4,2},{5,3},{6,0},{7,1},{8,14},{9,15},{10,... | collective-permute-start | bytes 983048 | tf_op jit(solution)/shard_map/ppermute | solution.py:369
  18.6 9.0 %collective-permute-start.3 = (f32[48,512]{1,0:T(8,128)S(1)}, f32[48,512]{1,0:T(8,128)S(1)}, u32[]{:S(2)}, u32[]{:S(2)}) collective-permute-start(f32[48,512]{1,0:T(8,128)S(1)} %get-tuple-element.43), channel_id=1, source_target_pairs={{0,8},{1,9},{2,10},{3,11},{4,12},{5,13},{6,14},{7,15},{8,0},{9,1},... | collective-permute-start | bytes 294920 | tf_op jit(solution)/shard_map/ppermute | solution.py:369
  20.5 25.6 %collective-permute-start.11 = (bf16[256,512]{1,0:T(8,128)(2,1)S(1)}, bf16[256,512]{1,0:T(8,128)(2,1)S(1)}, u32[]{:S(2)}, u32[]{:S(2)}) collective-permute-start(bf16[256,512]{1,0:T(8,128)(2,1)S(1)} %get-tuple-element.52), channel_id=1, source_target_pairs={{0,4},{1,5},{2,6},{3,7},{4,0},{5,1},{6,2},{7,3},{8,12},{9,13},{10,... | collective-permute-start | bytes 786440 | tf_op jit(solution)/shard_map/ppermute | solution.py:369
  25.6 22.8 %collective-permute-start.12 = (bf16[256,512]{1,0:T(8,128)(2,1)S(1)}, bf16[256,512]{1,0:T(8,128)(2,1)S(1)}, u32[]{:S(2)}, u32[]{:S(2)}) collective-permute-start(bf16[256,512]{1,0:T(8,128)(2,1)S(1)} %get-tuple-element.53), channel_id=1, source_target_pairs={{0,6},{1,7},{2,4},{3,5},{4,2},{5,3},{6,0},{7,1},{8,14},{9,15},{10,... | collective-permute-start | bytes 786440 | tf_op jit(solution)/shard_map/ppermute | solution.py:369
  27.6 7.6 %collective-permute-start.5 = (f32[48,512]{1,0:T(8,128)S(1)}, f32[48,512]{1,0:T(8,128)S(1)}, u32[]{:S(2)}, u32[]{:S(2)}) collective-permute-start(f32[48,512]{1,0:T(8,128)S(1)} %add_rows.13.refs_8_), channel_id=1, source_target_pairs={{0,16},{1,17},{2,18},{3,19},{4,20},{5,21},{6,22},{7,23},{8,24},{9,... | collective-permute-start | bytes 294920 | tf_op jit(solution)/shard_map/ppermute | solution.py:369
  33.1 11.7 %collective-permute-start.8 = (f32[80,512]{1,0:T(8,128)S(1)}, f32[80,512]{1,0:T(8,128)S(1)}, u32[]{:S(2)}, u32[]{:S(2)}) collective-permute-start(f32[80,512]{1,0:T(8,128)S(1)} %get-tuple-element.50), channel_id=1, source_target_pairs={{0,8},{1,9},{2,10},{3,11},{4,12},{5,13},{6,14},{7,15},{8,0},{9,1},... | collective-permute-start | bytes 491528 | tf_op jit(solution)/shard_map/ppermute | solution.py:369
  34.9 8.2 %collective-permute-start.9 = (f32[80,512]{1,0:T(8,128)S(1)}, f32[80,512]{1,0:T(8,128)S(1)}, u32[]{:S(2)}, u32[]{:S(2)}) collective-permute-start(f32[80,512]{1,0:T(8,128)S(1)} %get-tuple-element.51), channel_id=1, source_target_pairs={{0,8},{1,9},{2,10},{3,11},{4,12},{5,13},{6,14},{7,15},{8,0},{9,1},... | collective-permute-start | bytes 491528 | tf_op jit(solution)/shard_map/ppermute | solution.py:369
  35.1 15.5 %collective-permute-start.14 = (bf16[192,512]{1,0:T(8,128)(2,1)S(1)}, bf16[192,512]{1,0:T(8,128)(2,1)S(1)}, u32[]{:S(2)}, u32[]{:S(2)}) collective-permute-start(bf16[192,512]{1,0:T(8,128)(2,1)S(1)} %get-tuple-element.56), channel_id=1, source_target_pairs={{0,4},{1,5},{2,6},{3,7},{4,0},{5,1},{6,2},{7,3},{8,12},{9,13},{10,... | collective-permute-start | bytes 589832 | tf_op jit(solution)/shard_map/ppermute | solution.py:369
  43.1 8.5 %collective-permute-start.15 = (bf16[192,512]{1,0:T(8,128)(2,1)S(1)}, bf16[192,512]{1,0:T(8,128)(2,1)S(1)}, u32[]{:S(2)}, u32[]{:S(2)}) collective-permute-start(bf16[192,512]{1,0:T(8,128)(2,1)S(1)} %get-tuple-element.57), channel_id=1, source_target_pairs={{0,6},{1,7},{2,4},{3,5},{4,2},{5,3},{6,0},{7,1},{8,14},{9,15},{10,... | collective-permute-start | bytes 589832 | tf_op jit(solution)/shard_map/ppermute | solution.py:369
  44.7 12.0 %collective-permute-start.16 = (f32[48,512]{1,0:T(8,128)S(1)}, f32[48,512]{1,0:T(8,128)S(1)}, u32[]{:S(2)}, u32[]{:S(2)}) collective-permute-start(f32[48,512]{1,0:T(8,128)S(1)} %add_rows.14.refs_10_.refs_0_.refs_8_), channel_id=1, source_target_pairs={{0,1},{1,0},{2,3},{3,2},{4,5},{5,4},{6,7},{7,6},{8,9},{9,8},{10,11... | collective-permute-start | bytes 294920 | tf_op jit(solution)/shard_map/ppermute | solution.py:369
  46.1 12.1 %collective-permute-start.10 = (f32[80,512]{1,0:T(8,128)S(1)}, f32[80,512]{1,0:T(8,128)S(1)}, u32[]{:S(2)}, u32[]{:S(2)}) collective-permute-start(f32[80,512]{1,0:T(8,128)S(1)} %add_rows.15.refs_8_), channel_id=1, source_target_pairs={{0,16},{1,17},{2,18},{3,19},{4,20},{5,21},{6,22},{7,23},{8,24},{9,... | collective-permute-start | bytes 491528 | tf_op jit(solution)/shard_map/ppermute | solution.py:369
  50.6 10.5 %collective-permute-start.17 = (f32[64,512]{1,0:T(8,128)S(1)}, f32[64,512]{1,0:T(8,128)S(1)}, u32[]{:S(2)}, u32[]{:S(2)}) collective-permute-start(f32[64,512]{1,0:T(8,128)S(1)} %get-tuple-element.59), channel_id=1, source_target_pairs={{0,8},{1,9},{2,10},{3,11},{4,12},{5,13},{6,14},{7,15},{8,0},{9,1},... | collective-permute-start | bytes 393224 | tf_op jit(solution)/shard_map/ppermute | solution.py:369
  52.4 13.6 %collective-permute-start.19 = (f32[48,512]{1,0:T(8,128)S(1)}, f32[48,512]{1,0:T(8,128)S(1)}, u32[]{:S(2)}, u32[]{:S(2)}) collective-permute-start(f32[48,512]{1,0:T(8,128)S(1)} %get-tuple-element.60), channel_id=1, source_target_pairs={{0,16},{1,17},{2,18},{3,19},{4,20},{5,21},{6,22},{7,23},{8,24},{9,... | collective-permute-start | bytes 294920 | tf_op jit(solution)/shard_map/ppermute | solution.py:369
  55.0 10.9 %collective-permute-start.20 = (f32[48,512]{1,0:T(8,128)S(1)}, f32[48,512]{1,0:T(8,128)S(1)}, u32[]{:S(2)}, u32[]{:S(2)}) collective-permute-start(f32[48,512]{1,0:T(8,128)S(1)} %get-tuple-element.61), channel_id=1, source_target_pairs={{0,8},{1,9},{2,10},{3,11},{4,12},{5,13},{6,14},{7,15},{8,0},{9,1},... | collective-permute-start | bytes 294920 | tf_op jit(solution)/shard_map/ppermute | solution.py:369
  56.8 9.2 %collective-permute-start.21 = (f32[48,512]{1,0:T(8,128)S(1)}, f32[48,512]{1,0:T(8,128)S(1)}, u32[]{:S(2)}, u32[]{:S(2)}) collective-permute-start(f32[48,512]{1,0:T(8,128)S(1)} %get-tuple-element.62), channel_id=1, source_target_pairs={{0,24},{1,25},{2,26},{3,27},{4,28},{5,29},{6,30},{7,31},{8,16},{9,... | collective-permute-start | bytes 294920 | tf_op jit(solution)/shard_map/ppermute | solution.py:369
  58.2 7.7 %collective-permute-start.18 = (f32[64,512]{1,0:T(8,128)S(1)}, f32[64,512]{1,0:T(8,128)S(1)}, u32[]{:S(2)}, u32[]{:S(2)}) collective-permute-start(f32[64,512]{1,0:T(8,128)S(1)} %add_rows.16.refs_2_), channel_id=1, source_target_pairs={{0,16},{1,17},{2,18},{3,19},{4,20},{5,21},{6,22},{7,23},{8,24},{9,... | collective-permute-start | bytes 393224 | tf_op jit(solution)/shard_map/ppermute | solution.py:369
  74.5 8.1 %collective-permute-start.24 = (f32[4,40,256]{2,1,0:T(8,128)S(1)}, f32[4,40,256]{2,1,0:T(8,128)S(1)}, u32[]{:S(2)}, u32[]{:S(2)}) collective-permute-start(f32[4,40,256]{2,1,0:T(8,128)S(1)} %add_rows.20.refs_6_), channel_id=1, source_target_pairs={{0,4},{1,5},{2,6},{3,7},{4,0},{5,1},{6,2},{7,3},{8,12},{9,13},{10,... | collective-permute-start | bytes 491528 | tf_op jit(solution)/shard_map/ppermute | solution.py:369
  104.3 9.1 %collective-permute-start.29 = (f32[8,40,256]{2,1,0:T(8,128)S(1)}, f32[8,40,256]{2,1,0:T(8,128)S(1)}, u32[]{:S(2)}, u32[]{:S(2)}) collective-permute-start(f32[8,40,256]{2,1,0:T(8,128)S(1)} %pad_maximum_fusion.refs_0_), channel_id=1, source_target_pairs={{0,1},{1,0},{2,3},{3,2},{4,5},{5,4},{6,7},{7,6},{8,9},{9,8},{10,11... | collective-permute-start | bytes 983048 | tf_op jit(solution)/shard_map/ppermute | solution.py:369
  105.9 10.0 %collective-permute-start.38 = (f32[8,32,256]{2,1,0:T(8,128)S(1)}, f32[8,32,256]{2,1,0:T(8,128)S(1)}, u32[]{:S(2)}, u32[]{:S(2)}) collective-permute-start(f32[8,32,256]{2,1,0:T(8,128)S(1)} %pad_maximum_fusion.1.refs_2_), channel_id=1, source_target_pairs={{0,4},{1,5},{2,6},{3,7},{4,0},{5,1},{6,2},{7,3},{8,12},{9,13},{10,... | collective-permute-start | bytes 786440 | tf_op jit(solution)/shard_map/ppermute | solution.py:369
  106.8 11.9 %collective-permute-start.39 = (f32[8,40,256]{2,1,0:T(8,128)S(1)}, f32[8,40,256]{2,1,0:T(8,128)S(1)}, u32[]{:S(2)}, u32[]{:S(2)}) collective-permute-start(f32[8,40,256]{2,1,0:T(8,128)S(1)} %pad_maximum_fusion.refs_0_), channel_id=1, source_target_pairs={{0,2},{1,3},{2,0},{3,1},{4,6},{5,7},{6,4},{7,5},{8,10},{9,11},{10,... | collective-permute-start | bytes 983048 | tf_op jit(solution)/shard_map/ppermute | solution.py:369
  (21 other events, 124.0 us)
where the time goes:
time: 125 us
  starting transfers between devices  60.4 us (48%)
  waiting for transfers between devices  49.9 us (40%)
  Pallas kernels  12.7 us (10%)
    ppermute x43, starting transfers between devices, flip(): lax.ppermute(value, ('dp', 'fsdp'), [(i, i ^ mask) for i in range(count)])  60.4 us
    ppermute x43, waiting for transfers between devices, flip(): lax.ppermute(value, ('dp', 'fsdp'), [(i, i ^ mask) for i in range(count)])  49.9 us
    pallas_call x1, Pallas kernels, update(): pl.pallas_call(functools.partial(update_kernel, scale, places, len(owns))...  4.66 us
    pallas_call x4, Pallas kernels, dequant(): pl.pallas_call(kernel, in_specs=[SCALARS] + [WHOLE] * 7 + [ANYWHERE] * (l...  2.98 us
  transfers between devices with their start and end apart: 43, of which 20 were waited for; matrix products, arithmetic and copies ran while one was open for 0% of the time, Pallas kernels for 4%

commit v1 on v0

--- a/solution.py
+++ b/solution.py
@@ -13,16 +13,19 @@
 CHUNKS = (3, 5, 4, 3)
 LEAVE = (0, 1, 3)
 STEPS = (
-    ("sum", 0), ("halve", 0), ("sum", 1), ("halve", 1), ("finish", 0), ("sum", 2),
-    ("sum", 3), ("halve", 2), ("finish", 1), ("finish", 2), ("finish", 3),
+    ("sum", 0), ("halve", 0), ("sum", 1), ("sum", 2), ("halve", 1), ("finish", 0), ("sum", 3),
+    ("halve", 2), ("finish", 1), ("halve", 3), ("finish", 2), ("finish", 3),
 )
 AFTER = {
     ("sum", 1): (("sent", 0), ("half", 0)),
-    ("sum", 2): (("sent", 1), ("half", 1), ("grad", 0)),
-    ("sum", 3): (("keep", 2),),
+    ("sum", 2): (("near", 1), ("last", 1)),
+    ("halve", 1): (("keep", 2),),
+    ("finish", 0): (("keep", 2),),
+    ("sum", 3): (("sent", 1), ("grad", 0)),
     ("halve", 2): (("keep", 3),),
-    ("finish", 1): (("sent", 2), ("across", 0)),
-    ("finish", 3): (("across", 1), ("grad", 2)),
+    ("finish", 1): (("sent", 2), ("last", 3), ("across", 0)),
+    ("finish", 2): (("sent", 3),),
+    ("finish", 3): (("across", 1),),
 }
 ORDER = (0, 2, 1, 3)
 PIECE = 256
@@ -70,7 +73,7 @@
     "pair": ((0, 1), (2, 3)),
     "direct": ((0,), (1,), (2,), (3,)),
 }
-ROUTES = ("halves", "halves", "halves", "direct")
+ROUTES = ("halves", "halves", "halves", "halves")
 SPAN = 4
 TAIL = 3 * SLOTS * SPAN
 
@@ -414,6 +417,7 @@
             made["got", n] = [flip(part, *names) for part, names in zip(go, ZEDS)]
         elif ROUTES[n] == "halves":
             made["got", n] = [flip(part, "z1") for part in go]
+            made["near", n], made["last", n] = made["got", n]
         else:
             made["got", n] = flip(go[0], "z1")
 

time: 125 us -> 125 us (level)
  waiting for transfers between devices: 49.9 us -> 57.7 us
  starting transfers between devices: 60.4 us -> 53.1 us
    ppermute x43, waiting for transfers between devices: 49.9 us -> 57.7 us  [flip(): lax.ppermute(value, ('dp', 'fsdp'), [(i, i ^ mask) for i in range(count)])]
    ppermute x43, starting transfers between devices: 60.4 us -> 53.1 us  [flip(): lax.ppermute(value, ('dp', 'fsdp'), [(i, i ^ mask) for i in range(count)])]
  transfers between devices with their start and end apart: 43 -> 43, of which waited for: 20 -> 24; matrix products, arithmetic and copies ran while one was open for 0% -> 0% of each run, Pallas kernels for 4% -> 4%
where the time goes in v1:
time: 125 us
  waiting for transfers between devices  57.7 us (46%)
  starting transfers between devices  53.1 us (42%)
  Pallas kernels  12.7 us (10%)
    ppermute x43, waiting for transfers between devices, flip(): lax.ppermute(value, ('dp', 'fsdp'), [(i, i ^ mask) for i in range(count)])  57.7 us
    ppermute x43, starting transfers between devices, flip(): lax.ppermute(value, ('dp', 'fsdp'), [(i, i ^ mask) for i in range(count)])  53.1 us
    pallas_call x1, Pallas kernels, update(): pl.pallas_call(functools.partial(update_kernel, scale, places, len(owns))...  4.67 us
    pallas_call x4, Pallas kernels, dequant(): pl.pallas_call(kernel, in_specs=[SCALARS] + [WHOLE] * 7 + [ANYWHERE] * (l...  2.97 us
  transfers between devices with their start and end apart: 43, of which 24 were waited for; matrix products, arithmetic and copies ran while one was open for 0% of the time, Pallas kernels for 4%

profile of v1, /device:TPU:1, one launch (start us, length us, event | category | flops | bytes accessed | tf_op | source)
XLA Modules:
  0.0 125.0 jit_solution(12388959153532134898)
XLA Ops:
  0.9 2.5 %pack_rows.1 = (bf16[960,512]{1,0:T(8,128)(2,1)S(1)}, bf16[1008,512]{1,0:T(8,128)(2,1)S(1)}, bf16[240,512]{1,0:T(8,128)(2,1)S(1)}, bf16[240,512]{1,0:T(8,128)(2,...) custom-call(s32[4]{0:T(128)S(1)} %pad_add_fusion.at.refs_0_, ...), custom_call_target="tpu_custom_call" | custom-call | tf_op jit(solution)/shard_map/pack_rows/pallas_call | solution.py:119
  3.5 2.7 %collective-permute-start.1 = (bf16[240,512]{1,0:T(8,128)(2,1)S(1)}, bf16[240,512]{1,0:T(8,128)(2,1)S(1)}, u32[]{:S(2)}, u32[]{:S(2)}) collective-permute-start(bf16[240,512]{1,0:T(8,128)(2,1)S(1)} %get-tuple-element.37), channel_id=1, source_target_pairs={{0,4},{1,5},{2,6},{3,7},{4,0},{5,1},{6,2},{7,3},{8,12},{9,13},{10,... | collective-permute-start | bytes 737288 | tf_op jit(solution)/shard_map/ppermute | solution.py:372
  8.2 4.2 %collective-permute-done.1.refs_4_.refs_6_ = bf16[240,512]{1,0:T(8,128)(2,1)S(1)} collective-permute-done((bf16[240,512]{1,0:T(8,128)(2,1)S(1)}, bf16[240,512]{1,0:T(8,128)(2,1)S(1)}, u32[]{:S(2)}, u32[]{:S(2)}) %collective-permute-start.1) | collective-permute-done | bytes 245792 | tf_op jit(solution)/shard_map/ppermute | solution.py:372
  12.4 5.5 %collective-permute-done.2.refs_5_.refs_7_ = bf16[240,512]{1,0:T(8,128)(2,1)S(1)} collective-permute-done((bf16[240,512]{1,0:T(8,128)(2,1)S(1)}, bf16[240,512]{1,0:T(8,128)(2,1)S(1)}, u32[]{:S(2)}, u32[]{:S(2)}) %collective-permute-start.2) | collective-permute-done | bytes 245792 | tf_op jit(solution)/shard_map/ppermute | solution.py:372
  21.9 3.7 %collective-permute-done.4.refs_1_ = f32[48,512]{1,0:T(8,128)S(1)} collective-permute-done((f32[48,512]{1,0:T(8,128)S(1)}, f32[48,512]{1,0:T(8,128)S(1)}, u32[]{:S(2)}, u32[]{:S(2)}) %collective-permute-start.4) | collective-permute-done | bytes 98336 | tf_op jit(solution)/shard_map/ppermute | solution.py:372
  25.6 2.0 %collective-permute-start.7 = (bf16[256,512]{1,0:T(8,128)(2,1)S(1)}, bf16[256,512]{1,0:T(8,128)(2,1)S(1)}, u32[]{:S(2)}, u32[]{:S(2)}) collective-permute-start(bf16[256,512]{1,0:T(8,128)(2,1)S(1)} %get-tuple-element.45), channel_id=1, source_target_pairs={{0,6},{1,7},{2,4},{3,5},{4,2},{5,3},{6,0},{7,1},{8,14},{9,15},{10,... | collective-permute-start | bytes 786440 | tf_op jit(solution)/shard_map/ppermute | solution.py:372
  27.6 2.4 %collective-permute-start.5 = (f32[48,512]{1,0:T(8,128)S(1)}, f32[48,512]{1,0:T(8,128)S(1)}, u32[]{:S(2)}, u32[]{:S(2)}) collective-permute-start(f32[48,512]{1,0:T(8,128)S(1)} %add_rows.14.refs_8_), channel_id=1, source_target_pairs={{0,16},{1,17},{2,18},{3,19},{4,20},{5,21},{6,22},{7,23},{8,24},{9,... | collective-permute-start | bytes 294920 | tf_op jit(solution)/shard_map/ppermute | solution.py:372
  30.0 2.3 %collective-permute-done.9.refs_7_ = bf16[320,512]{1,0:T(8,128)(2,1)S(1)} collective-permute-done((bf16[320,512]{1,0:T(8,128)(2,1)S(1)}, bf16[320,512]{1,0:T(8,128)(2,1)S(1)}, u32[]{:S(2)}, u32[]{:S(2)}) %collective-permute-start.9) | collective-permute-done | bytes 327712 | tf_op jit(solution)/shard_map/ppermute | solution.py:372
  35.0 4.6 %collective-permute-done.10.refs_8_ = f32[80,512]{1,0:T(8,128)S(1)} collective-permute-done((f32[80,512]{1,0:T(8,128)S(1)}, f32[80,512]{1,0:T(8,128)S(1)}, u32[]{:S(2)}, u32[]{:S(2)}) %collective-permute-start.10) | collective-permute-done | bytes 163872 | tf_op jit(solution)/shard_map/ppermute | solution.py:372
  41.0 2.1 %collective-permute-done.11.refs_9_.refs_1_ = f32[80,512]{1,0:T(8,128)S(1)} collective-permute-done((f32[80,512]{1,0:T(8,128)S(1)}, f32[80,512]{1,0:T(8,128)S(1)}, u32[]{:S(2)}, u32[]{:S(2)}) %collective-permute-start.11) | collective-permute-done | bytes 163872 | tf_op jit(solution)/shard_map/ppermute | solution.py:372
  48.4 2.3 %collective-permute-start.12 = (f32[80,512]{1,0:T(8,128)S(1)}, f32[80,512]{1,0:T(8,128)S(1)}, u32[]{:S(2)}, u32[]{:S(2)}) collective-permute-start(f32[80,512]{1,0:T(8,128)S(1)} %add_rows.16.refs_8_), channel_id=1, source_target_pairs={{0,16},{1,17},{2,18},{3,19},{4,20},{5,21},{6,22},{7,23},{8,24},{9,... | collective-permute-start | bytes 491528 | tf_op jit(solution)/shard_map/ppermute | solution.py:372
  54.1 3.8 %collective-permute-done.18 = f32[64,512]{1,0:T(8,128)S(1)} collective-permute-done((f32[64,512]{1,0:T(8,128)S(1)}, f32[64,512]{1,0:T(8,128)S(1)}, u32[]{:S(2)}, u32[]{:S(2)}) %collective-permute-start.18) | collective-permute-done | bytes 131104 | tf_op jit(solution)/shard_map/ppermute | solution.py:372
  60.0 2.4 %collective-permute-start.21 = (f32[48,512]{1,0:T(8,128)S(1)}, f32[48,512]{1,0:T(8,128)S(1)}, u32[]{:S(2)}, u32[]{:S(2)}) collective-permute-start(f32[48,512]{1,0:T(8,128)S(1)} %add_rows.19.refs_2_), channel_id=1, source_target_pairs={{0,16},{1,17},{2,18},{3,19},{4,20},{5,21},{6,22},{7,23},{8,24},{9,... | collective-permute-start | bytes 294920 | tf_op jit(solution)/shard_map/ppermute | solution.py:372
  64.1 6.4 %collective-permute-done.21.refs_1_ = f32[48,512]{1,0:T(8,128)S(1)} collective-permute-done((f32[48,512]{1,0:T(8,128)S(1)}, f32[48,512]{1,0:T(8,128)S(1)}, u32[]{:S(2)}, u32[]{:S(2)}) %collective-permute-start.21) | collective-permute-done | bytes 98336 | tf_op jit(solution)/shard_map/ppermute | solution.py:372
  71.7 2.1 %collective-permute-start.23 = (f32[8,40,256]{2,1,0:T(8,128)S(1)}, f32[8,40,256]{2,1,0:T(8,128)S(1)}, u32[]{:S(2)}, u32[]{:S(2)}) collective-permute-start(f32[8,40,256]{2,1,0:T(8,128)S(1)} %get-tuple-element.62), channel_id=1, source_target_pairs={{0,2},{1,3},{2,0},{3,1},{4,6},{5,7},{6,4},{7,5},{8,10},{9,11},{10,... | collective-permute-start | bytes 983048 | tf_op jit(solution)/shard_map/ppermute | solution.py:372
  75.4 5.6 %collective-permute-done.30.refs_5_.refs_13_ = f32[112,512]{1,0:T(8,128)S(1)} collective-permute-done((f32[112,512]{1,0:T(8,128)S(1)}, f32[112,512]{1,0:T(8,128)S(1)}, u32[]{:S(2)}, u32[]{:S(2)}) %collective-permute-start.30) | collective-permute-done | bytes 229408 | tf_op jit(solution)/shard_map/ppermute | solution.py:372
  84.5 2.9 %collective-permute-done.25.refs_3_ = f32[2,40,256]{2,1,0:T(8,128)S(1)} collective-permute-done((f32[2,40,256]{2,1,0:T(8,128)S(1)}, f32[2,40,256]{2,1,0:T(8,128)S(1)}, u32[]{:S(2)}, u32[]{:S(2)}) %collective-permute-start.25) | collective-permute-done | bytes 81952 | tf_op jit(solution)/shard_map/ppermute | solution.py:372
  90.2 3.9 %collective-permute-done.26.refs_1_.refs_2_ = f32[2,40,256]{2,1,0:T(8,128)S(1)} collective-permute-done((f32[2,40,256]{2,1,0:T(8,128)S(1)}, f32[2,40,256]{2,1,0:T(8,128)S(1)}, u32[]{:S(2)}, u32[]{:S(2)}) %collective-permute-start.26) | collective-permute-done | bytes 81952 | tf_op jit(solution)/shard_map/ppermute | solution.py:372
  94.2 2.7 %collective-permute-start.35 = (f32[2,32,256]{2,1,0:T(8,128)S(1)}, f32[2,32,256]{2,1,0:T(8,128)S(1)}, u32[]{:S(2)}, u32[]{:S(2)}) collective-permute-start(f32[2,32,256]{2,1,0:T(8,128)S(1)} %add_rows.26.refs_0_), channel_id=1, source_target_pairs={{0,16},{1,17},{2,18},{3,19},{4,20},{5,21},{6,22},{7,23},{8,24},{9,... | collective-permute-start | bytes 196616 | tf_op jit(solution)/shard_map/ppermute | solution.py:372
  102.4 2.3 %collective-permute-done.28 = f32[4,40,256]{2,1,0:T(8,128)S(1)} collective-permute-done((f32[4,40,256]{2,1,0:T(8,128)S(1)}, f32[4,40,256]{2,1,0:T(8,128)S(1)}, u32[]{:S(2)}, u32[]{:S(2)}) %collective-permute-start.28) | collective-permute-done | bytes 163872 | tf_op jit(solution)/shard_map/ppermute | solution.py:372
  106.8 6.6 %collective-permute-start.39 = (f32[8,40,256]{2,1,0:T(8,128)S(1)}, f32[8,40,256]{2,1,0:T(8,128)S(1)}, u32[]{:S(2)}, u32[]{:S(2)}) collective-permute-start(f32[8,40,256]{2,1,0:T(8,128)S(1)} %pad_maximum_fusion.refs_0_), channel_id=1, source_target_pairs={{0,2},{1,3},{2,0},{3,1},{4,6},{5,7},{6,4},{7,5},{8,10},{9,11},{10,... | collective-permute-start | bytes 983048 | tf_op jit(solution)/shard_map/ppermute | solution.py:372
  113.4 2.9 %collective-permute-start.40 = (f32[8,40,256]{2,1,0:T(8,128)S(1)}, f32[8,40,256]{2,1,0:T(8,128)S(1)}, u32[]{:S(2)}, u32[]{:S(2)}) collective-permute-start(f32[8,40,256]{2,1,0:T(8,128)S(1)} %collective-permute-done.29.refs_1_), channel_id=1, source_target_pairs={{0,2},{1,3},{2,0},{3,1},{4,6},{5,7},{6,4},{7,5},{8,10},{9,11},{10,... | collective-permute-start | bytes 983048 | tf_op jit(solution)/shard_map/ppermute | solution.py:372
  116.3 2.9 %collective-permute-start.42 = (f32[8,32,256]{2,1,0:T(8,128)S(1)}, f32[8,32,256]{2,1,0:T(8,128)S(1)}, u32[]{:S(2)}, u32[]{:S(2)}) collective-permute-start(f32[8,32,256]{2,1,0:T(8,128)S(1)} %collective-permute-done.38.refs_3_), channel_id=1, source_target_pairs={{0,2},{1,3},{2,0},{3,1},{4,6},{5,7},{6,4},{7,5},{8,10},{9,11},{10,... | collective-permute-start | bytes 786440 | tf_op jit(solution)/shard_map/ppermute | solution.py:372
  120.3 4.7 %update.1 = bf16[240,512]{1,0:T(8,128)(2,1)} custom-call(s32[4]{0:T(128)S(1)} %pad_add_fusion.at.refs_0_, f32[8,40,256]{2,1,0:T(8,128)S(1)} %pad_maximum_fusion.refs_0_, f32[8,40,256]{2,1,0:T(8,128)S(1)} %collective-permute-done.29.refs_1_, f32[8,32,256]{2,1,0:T(8,128)S(1)} %pad_maximum_fusion.1.refs_2_, f32[8,32,256]{2,1,0:T(8,128)S(1)} %collective-permute-done.38.refs_3_, ...), custom_call_target="tpu_custom_call" | custom-call | tf_op jit(solution)/shard_map/update/pallas_call | solution.py:350
  (110 shorter events, 41.7 us)
Async XLA Ops:
  3.4 14.5 %collective-permute-start = (bf16[1008,512]{1,0:T(8,128)(2,1)S(1)}, bf16[1008,512]{1,0:T(8,128)(2,1)S(1)}, u32[]{:S(2)}, u32[]{:S(2)}) collective-permute-start(bf16[1008,512]{1,0:T(8,128)(2,1)S(1)} %get-tuple-element.36), channel_id=1, source_target_pairs={{0,2},{1,3},{2,0},{3,1},{4,6},{5,7},{6,4},{7,5},{8,10},{9,11},{10,... | collective-permute-start | bytes 3096584 | tf_op jit(solution)/shard_map/ppermute | solution.py:372
  3.5 8.9 %collective-permute-start.1 = (bf16[240,512]{1,0:T(8,128)(2,1)S(1)}, bf16[240,512]{1,0:T(8,128)(2,1)S(1)}, u32[]{:S(2)}, u32[]{:S(2)}) collective-permute-start(bf16[240,512]{1,0:T(8,128)(2,1)S(1)} %get-tuple-element.37), channel_id=1, source_target_pairs={{0,4},{1,5},{2,6},{3,7},{4,0},{5,1},{6,2},{7,3},{8,12},{9,13},{10,... | collective-permute-start | bytes 737288 | tf_op jit(solution)/shard_map/ppermute | solution.py:372
  6.2 11.7 %collective-permute-start.2 = (bf16[240,512]{1,0:T(8,128)(2,1)S(1)}, bf16[240,512]{1,0:T(8,128)(2,1)S(1)}, u32[]{:S(2)}, u32[]{:S(2)}) collective-permute-start(bf16[240,512]{1,0:T(8,128)(2,1)S(1)} %get-tuple-element.38), channel_id=1, source_target_pairs={{0,6},{1,7},{2,4},{3,5},{4,2},{5,3},{6,0},{7,1},{8,14},{9,15},{10,... | collective-permute-start | bytes 737288 | tf_op jit(solution)/shard_map/ppermute | solution.py:372
  6.2 23.8 %collective-permute-start.8 = (bf16[320,512]{1,0:T(8,128)(2,1)S(1)}, bf16[320,512]{1,0:T(8,128)(2,1)S(1)}, u32[]{:S(2)}, u32[]{:S(2)}) collective-permute-start(bf16[320,512]{1,0:T(8,128)(2,1)S(1)} %get-tuple-element.46), channel_id=1, source_target_pairs={{0,4},{1,5},{2,6},{3,7},{4,0},{5,1},{6,2},{7,3},{8,12},{9,13},{10,... | collective-permute-start | bytes 983048 | tf_op jit(solution)/shard_map/ppermute | solution.py:372
  7.9 24.4 %collective-permute-start.9 = (bf16[320,512]{1,0:T(8,128)(2,1)S(1)}, bf16[320,512]{1,0:T(8,128)(2,1)S(1)}, u32[]{:S(2)}, u32[]{:S(2)}) collective-permute-start(bf16[320,512]{1,0:T(8,128)(2,1)S(1)} %get-tuple-element.47), channel_id=1, source_target_pairs={{0,6},{1,7},{2,4},{3,5},{4,2},{5,3},{6,0},{7,1},{8,14},{9,15},{10,... | collective-permute-start | bytes 983048 | tf_op jit(solution)/shard_map/ppermute | solution.py:372
  18.6 9.0 %collective-permute-start.3 = (f32[48,512]{1,0:T(8,128)S(1)}, f32[48,512]{1,0:T(8,128)S(1)}, u32[]{:S(2)}, u32[]{:S(2)}) collective-permute-start(f32[48,512]{1,0:T(8,128)S(1)} %get-tuple-element.42), channel_id=1, source_target_pairs={{0,8},{1,9},{2,10},{3,11},{4,12},{5,13},{6,14},{7,15},{8,0},{9,1},... | collective-permute-start | bytes 294920 | tf_op jit(solution)/shard_map/ppermute | solution.py:372
  20.5 24.2 %collective-permute-start.6 = (bf16[256,512]{1,0:T(8,128)(2,1)S(1)}, bf16[256,512]{1,0:T(8,128)(2,1)S(1)}, u32[]{:S(2)}, u32[]{:S(2)}) collective-permute-start(bf16[256,512]{1,0:T(8,128)(2,1)S(1)} %get-tuple-element.44), channel_id=1, source_target_pairs={{0,4},{1,5},{2,6},{3,7},{4,0},{5,1},{6,2},{7,3},{8,12},{9,13},{10,... | collective-permute-start | bytes 786440 | tf_op jit(solution)/shard_map/ppermute | solution.py:372
  25.6 19.1 %collective-permute-start.7 = (bf16[256,512]{1,0:T(8,128)(2,1)S(1)}, bf16[256,512]{1,0:T(8,128)(2,1)S(1)}, u32[]{:S(2)}, u32[]{:S(2)}) collective-permute-start(bf16[256,512]{1,0:T(8,128)(2,1)S(1)} %get-tuple-element.45), channel_id=1, source_target_pairs={{0,6},{1,7},{2,4},{3,5},{4,2},{5,3},{6,0},{7,1},{8,14},{9,15},{10,... | collective-permute-start | bytes 786440 | tf_op jit(solution)/shard_map/ppermute | solution.py:372
  27.6 17.9 %collective-permute-start.5 = (f32[48,512]{1,0:T(8,128)S(1)}, f32[48,512]{1,0:T(8,128)S(1)}, u32[]{:S(2)}, u32[]{:S(2)}) collective-permute-start(f32[48,512]{1,0:T(8,128)S(1)} %add_rows.14.refs_8_), channel_id=1, source_target_pairs={{0,16},{1,17},{2,18},{3,19},{4,20},{5,21},{6,22},{7,23},{8,24},{9,... | collective-permute-start | bytes 294920 | tf_op jit(solution)/shard_map/ppermute | solution.py:372
  34.9 8.2 %collective-permute-start.11 = (f32[80,512]{1,0:T(8,128)S(1)}, f32[80,512]{1,0:T(8,128)S(1)}, u32[]{:S(2)}, u32[]{:S(2)}) collective-permute-start(f32[80,512]{1,0:T(8,128)S(1)} %get-tuple-element.51), channel_id=1, source_target_pairs={{0,8},{1,9},{2,10},{3,11},{4,12},{5,13},{6,14},{7,15},{8,0},{9,1},... | collective-permute-start | bytes 491528 | tf_op jit(solution)/shard_map/ppermute | solution.py:372
  39.6 8.8 %collective-permute-start.14 = (bf16[192,512]{1,0:T(8,128)(2,1)S(1)}, bf16[192,512]{1,0:T(8,128)(2,1)S(1)}, u32[]{:S(2)}, u32[]{:S(2)}) collective-permute-start(bf16[192,512]{1,0:T(8,128)(2,1)S(1)} %get-tuple-element.55), channel_id=1, source_target_pairs={{0,4},{1,5},{2,6},{3,7},{4,0},{5,1},{6,2},{7,3},{8,12},{9,13},{10,... | collective-permute-start | bytes 589832 | tf_op jit(solution)/shard_map/ppermute | solution.py:372
  43.1 8.5 %collective-permute-start.15 = (bf16[192,512]{1,0:T(8,128)(2,1)S(1)}, bf16[192,512]{1,0:T(8,128)(2,1)S(1)}, u32[]{:S(2)}, u32[]{:S(2)}) collective-permute-start(bf16[192,512]{1,0:T(8,128)(2,1)S(1)} %get-tuple-element.56), channel_id=1, source_target_pairs={{0,6},{1,7},{2,4},{3,5},{4,2},{5,3},{6,0},{7,1},{8,14},{9,15},{10,... | collective-permute-start | bytes 589832 | tf_op jit(solution)/shard_map/ppermute | solution.py:372
  45.5 16.9 %collective-permute-start.17 = (f32[48,512]{1,0:T(8,128)S(1)}, f32[48,512]{1,0:T(8,128)S(1)}, u32[]{:S(2)}, u32[]{:S(2)}) collective-permute-start(f32[48,512]{1,0:T(8,128)S(1)} %add_rows.15.refs_9_.refs_0_.refs_8_), channel_id=1, source_target_pairs={{0,1},{1,0},{2,3},{3,2},{4,5},{5,4},{6,7},{7,6},{8,9},{9,8},{10,11... | collective-permute-start | bytes 294920 | tf_op jit(solution)/shard_map/ppermute | solution.py:372
  48.0 9.9 %collective-permute-start.18 = (f32[64,512]{1,0:T(8,128)S(1)}, f32[64,512]{1,0:T(8,128)S(1)}, u32[]{:S(2)}, u32[]{:S(2)}) collective-permute-start(f32[64,512]{1,0:T(8,128)S(1)} %get-tuple-element.59), channel_id=1, source_target_pairs={{0,8},{1,9},{2,10},{3,11},{4,12},{5,13},{6,14},{7,15},{8,0},{9,1},... | collective-permute-start | bytes 393224 | tf_op jit(solution)/shard_map/ppermute | solution.py:372
  48.4 14.0 %collective-permute-start.12 = (f32[80,512]{1,0:T(8,128)S(1)}, f32[80,512]{1,0:T(8,128)S(1)}, u32[]{:S(2)}, u32[]{:S(2)}) collective-permute-start(f32[80,512]{1,0:T(8,128)S(1)} %add_rows.16.refs_8_), channel_id=1, source_target_pairs={{0,16},{1,17},{2,18},{3,19},{4,20},{5,21},{6,22},{7,23},{8,24},{9,... | collective-permute-start | bytes 491528 | tf_op jit(solution)/shard_map/ppermute | solution.py:372
  52.4 7.6 %collective-permute-start.16 = (f32[48,512]{1,0:T(8,128)S(1)}, f32[48,512]{1,0:T(8,128)S(1)}, u32[]{:S(2)}, u32[]{:S(2)}) collective-permute-start(f32[48,512]{1,0:T(8,128)S(1)} %get-tuple-element.58), channel_id=1, source_target_pairs={{0,8},{1,9},{2,10},{3,11},{4,12},{5,13},{6,14},{7,15},{8,0},{9,1},... | collective-permute-start | bytes 294920 | tf_op jit(solution)/shard_map/ppermute | solution.py:372
  54.0 9.5 %collective-permute-start.20 = (f32[48,512]{1,0:T(8,128)S(1)}, f32[48,512]{1,0:T(8,128)S(1)}, u32[]{:S(2)}, u32[]{:S(2)}) collective-permute-start(f32[48,512]{1,0:T(8,128)S(1)} %get-tuple-element.60), channel_id=1, source_target_pairs={{0,8},{1,9},{2,10},{3,11},{4,12},{5,13},{6,14},{7,15},{8,0},{9,1},... | collective-permute-start | bytes 294920 | tf_op jit(solution)/shard_map/ppermute | solution.py:372
  60.0 10.4 %collective-permute-start.21 = (f32[48,512]{1,0:T(8,128)S(1)}, f32[48,512]{1,0:T(8,128)S(1)}, u32[]{:S(2)}, u32[]{:S(2)}) collective-permute-start(f32[48,512]{1,0:T(8,128)S(1)} %add_rows.19.refs_2_), channel_id=1, source_target_pairs={{0,16},{1,17},{2,18},{3,19},{4,20},{5,21},{6,22},{7,23},{8,24},{9,... | collective-permute-start | bytes 294920 | tf_op jit(solution)/shard_map/ppermute | solution.py:372
  62.4 8.0 %collective-permute-start.22 = (f32[80,512]{1,0:T(8,128)S(1)}, f32[80,512]{1,0:T(8,128)S(1)}, u32[]{:S(2)}, u32[]{:S(2)}) collective-permute-start(f32[80,512]{1,0:T(8,128)S(1)} %add_rows.18.refs_1_.refs_9_), channel_id=1, source_target_pairs={{0,1},{1,0},{2,3},{3,2},{4,5},{5,4},{6,7},{7,6},{8,9},{9,8},{10,11... | collective-permute-start | bytes 491528 | tf_op jit(solution)/shard_map/ppermute | solution.py:372
  73.8 7.2 %collective-permute-start.30 = (f32[112,512]{1,0:T(8,128)S(1)}, f32[112,512]{1,0:T(8,128)S(1)}, u32[]{:S(2)}, u32[]{:S(2)}) collective-permute-start(f32[112,512]{1,0:T(8,128)S(1)} %pad_maximum_fusion.2.refs_2_.refs_10_), channel_id=1, source_target_pairs={{0,1},{1,0},{2,3},{3,2},{4,5},{5,4},{6,7},{7,6},{8,9},{9,8},{10,11... | collective-permute-start | bytes 688136 | tf_op jit(solution)/shard_map/ppermute | solution.py:372
  75.1 8.1 %collective-permute-start.24 = (f32[4,40,256]{2,1,0:T(8,128)S(1)}, f32[4,40,256]{2,1,0:T(8,128)S(1)}, u32[]{:S(2)}, u32[]{:S(2)}) collective-permute-start(f32[4,40,256]{2,1,0:T(8,128)S(1)} %add_rows.22.refs_6_), channel_id=1, source_target_pairs={{0,4},{1,5},{2,6},{3,7},{4,0},{5,1},{6,2},{7,3},{8,12},{9,13},{10,... | collective-permute-start | bytes 491528 | tf_op jit(solution)/shard_map/ppermute | solution.py:372
  104.7 8.7 %collective-permute-start.29 = (f32[8,40,256]{2,1,0:T(8,128)S(1)}, f32[8,40,256]{2,1,0:T(8,128)S(1)}, u32[]{:S(2)}, u32[]{:S(2)}) collective-permute-start(f32[8,40,256]{2,1,0:T(8,128)S(1)} %pad_maximum_fusion.refs_0_), channel_id=1, source_target_pairs={{0,1},{1,0},{2,3},{3,2},{4,5},{5,4},{6,7},{7,6},{8,9},{9,8},{10,11... | collective-permute-start | bytes 983048 | tf_op jit(solution)/shard_map/ppermute | solution.py:372
  106.3 10.0 %collective-permute-start.38 = (f32[8,32,256]{2,1,0:T(8,128)S(1)}, f32[8,32,256]{2,1,0:T(8,128)S(1)}, u32[]{:S(2)}, u32[]{:S(2)}) collective-permute-start(f32[8,32,256]{2,1,0:T(8,128)S(1)} %pad_maximum_fusion.1.refs_2_), channel_id=1, source_target_pairs={{0,4},{1,5},{2,6},{3,7},{4,0},{5,1},{6,2},{7,3},{8,12},{9,13},{10,... | collective-permute-start | bytes 786440 | tf_op jit(solution)/shard_map/ppermute | solution.py:372
  106.8 12.4 %collective-permute-start.39 = (f32[8,40,256]{2,1,0:T(8,128)S(1)}, f32[8,40,256]{2,1,0:T(8,128)S(1)}, u32[]{:S(2)}, u32[]{:S(2)}) collective-permute-start(f32[8,40,256]{2,1,0:T(8,128)S(1)} %pad_maximum_fusion.refs_0_), channel_id=1, source_target_pairs={{0,2},{1,3},{2,0},{3,1},{4,6},{5,7},{6,4},{7,5},{8,10},{9,11},{10,... | collective-permute-start | bytes 983048 | tf_op jit(solution)/shard_map/ppermute | solution.py:372
  (21 other events, 121.8 us)

commit v2 on v1

--- a/solution.py
+++ b/solution.py
@@ -10,7 +10,7 @@
 
 BLOCK = 128
 GRAIN = 16
-CHUNKS = (3, 5, 4, 3)
+CHUNKS = (3, 4, 5, 3)
 LEAVE = (0, 1, 3)
 STEPS = (
     ("sum", 0), ("halve", 0), ("sum", 1), ("sum", 2), ("halve", 1), ("finish", 0), ("sum", 3),
@@ -23,6 +23,7 @@
     ("finish", 0): (("keep", 2),),
     ("sum", 3): (("sent", 1), ("grad", 0)),
     ("halve", 2): (("keep", 3),),
+    ("halve", 3): (("sent", 2),),
     ("finish", 1): (("sent", 2), ("last", 3), ("across", 0)),
     ("finish", 2): (("sent", 3),),
     ("finish", 3): (("across", 1),),
@@ -73,7 +74,7 @@
     "pair": ((0, 1), (2, 3)),
     "direct": ((0,), (1,), (2,), (3,)),
 }
-ROUTES = ("halves", "halves", "halves", "halves")
+ROUTES = ("halves", "halves", "pair", "halves")
 SPAN = 4
 TAIL = 3 * SLOTS * SPAN
 

time: 125 us -> 127 us (1.016)
  starting transfers between devices: 53.1 us -> 65.9 us
  waiting for transfers between devices: 57.7 us -> 46 us
    ppermute x43 -> x42, starting transfers between devices: 53.1 us -> 65.9 us  [flip(): lax.ppermute(value, ('dp', 'fsdp'), [(i, i ^ mask) for i in range(count)])]
    ppermute x43 -> x42, waiting for transfers between devices: 57.7 us -> 46 us  [flip(): lax.ppermute(value, ('dp', 'fsdp'), [(i, i ^ mask) for i in range(count)])]
  transfers between devices with their start and end apart: 43 -> 42, of which waited for: 24 -> 18; matrix products, arithmetic and copies ran while one was open for 0% -> 0% of each run, Pallas kernels for 4% -> 3%
where the time goes in v2:
time: 127 us; the launch traced here: 126 us
  starting transfers between devices  65.9 us (52%)
  waiting for transfers between devices  46 us (36%)
  Pallas kernels  12.7 us (10%)
    ppermute x42, starting transfers between devices, flip(): lax.ppermute(value, ('dp', 'fsdp'), [(i, i ^ mask) for i in range(count)])  65.9 us
    ppermute x42, waiting for transfers between devices, flip(): lax.ppermute(value, ('dp', 'fsdp'), [(i, i ^ mask) for i in range(count)])  46 us
    pallas_call x1, Pallas kernels, update(): pl.pallas_call(functools.partial(update_kernel, scale, places, len(owns))...  4.66 us
    pallas_call x4, Pallas kernels, dequant(): pl.pallas_call(kernel, in_specs=[SCALARS] + [WHOLE] * 7 + [ANYWHERE] * (l...  2.97 us
  transfers between devices with their start and end apart: 42, of which 18 were waited for; matrix products, arithmetic and copies ran while one was open for 0% of the time, Pallas kernels for 3%

profile of v2, /device:TPU:1, one launch (start us, length us, event | category | flops | bytes accessed | tf_op | source)
XLA Modules:
  0.0 126.2 jit_solution(13666417431183467888)
XLA Ops:
  0.9 2.5 %pack_rows.1 = (bf16[960,512]{1,0:T(8,128)(2,1)S(1)}, bf16[1008,512]{1,0:T(8,128)(2,1)S(1)}, bf16[240,512]{1,0:T(8,128)(2,1)S(1)}, bf16[240,512]{1,0:T(8,128)(2,...) custom-call(s32[4]{0:T(128)S(1)} %pad_add_fusion.at.refs_0_, ...), custom_call_target="tpu_custom_call" | custom-call | tf_op jit(solution)/shard_map/pack_rows/pallas_call | solution.py:120
  3.5 2.7 %collective-permute-start.1 = (bf16[240,512]{1,0:T(8,128)(2,1)S(1)}, bf16[240,512]{1,0:T(8,128)(2,1)S(1)}, u32[]{:S(2)}, u32[]{:S(2)}) collective-permute-start(bf16[240,512]{1,0:T(8,128)(2,1)S(1)} %get-tuple-element.36), channel_id=1, source_target_pairs={{0,4},{1,5},{2,6},{3,7},{4,0},{5,1},{6,2},{7,3},{8,12},{9,13},{10,... | collective-permute-start | bytes 737288 | tf_op jit(solution)/shard_map/ppermute | solution.py:373
  8.2 4.2 %collective-permute-done.1.refs_4_.refs_6_ = bf16[240,512]{1,0:T(8,128)(2,1)S(1)} collective-permute-done((bf16[240,512]{1,0:T(8,128)(2,1)S(1)}, bf16[240,512]{1,0:T(8,128)(2,1)S(1)}, u32[]{:S(2)}, u32[]{:S(2)}) %collective-permute-start.1) | collective-permute-done | bytes 245792 | tf_op jit(solution)/shard_map/ppermute | solution.py:373
  12.4 5.5 %collective-permute-done.2.refs_5_.refs_7_ = bf16[240,512]{1,0:T(8,128)(2,1)S(1)} collective-permute-done((bf16[240,512]{1,0:T(8,128)(2,1)S(1)}, bf16[240,512]{1,0:T(8,128)(2,1)S(1)}, u32[]{:S(2)}, u32[]{:S(2)}) %collective-permute-start.2) | collective-permute-done | bytes 245792 | tf_op jit(solution)/shard_map/ppermute | solution.py:373
  18.6 1.8 %collective-permute-start.3 = (f32[48,512]{1,0:T(8,128)S(1)}, f32[48,512]{1,0:T(8,128)S(1)}, u32[]{:S(2)}, u32[]{:S(2)}) collective-permute-start(f32[48,512]{1,0:T(8,128)S(1)} %get-tuple-element.41), channel_id=1, source_target_pairs={{0,8},{1,9},{2,10},{3,11},{4,12},{5,13},{6,14},{7,15},{8,0},{9,1},... | collective-permute-start | bytes 294920 | tf_op jit(solution)/shard_map/ppermute | solution.py:373
  21.9 3.7 %collective-permute-done.4.refs_1_ = f32[48,512]{1,0:T(8,128)S(1)} collective-permute-done((f32[48,512]{1,0:T(8,128)S(1)}, f32[48,512]{1,0:T(8,128)S(1)}, u32[]{:S(2)}, u32[]{:S(2)}) %collective-permute-start.4) | collective-permute-done | bytes 98336 | tf_op jit(solution)/shard_map/ppermute | solution.py:373
  25.6 2.0 %collective-permute-start.7 = (bf16[320,512]{1,0:T(8,128)(2,1)S(1)}, bf16[320,512]{1,0:T(8,128)(2,1)S(1)}, u32[]{:S(2)}, u32[]{:S(2)}) collective-permute-start(bf16[320,512]{1,0:T(8,128)(2,1)S(1)} %get-tuple-element.44), channel_id=1, source_target_pairs={{0,6},{1,7},{2,4},{3,5},{4,2},{5,3},{6,0},{7,1},{8,14},{9,15},{10,... | collective-permute-start | bytes 983048 | tf_op jit(solution)/shard_map/ppermute | solution.py:373
  27.6 2.4 %collective-permute-start.5 = (f32[48,512]{1,0:T(8,128)S(1)}, f32[48,512]{1,0:T(8,128)S(1)}, u32[]{:S(2)}, u32[]{:S(2)}) collective-permute-start(f32[48,512]{1,0:T(8,128)S(1)} %add_rows.14.refs_8_), channel_id=1, source_target_pairs={{0,16},{1,17},{2,18},{3,19},{4,20},{5,21},{6,22},{7,23},{8,24},{9,... | collective-permute-start | bytes 294920 | tf_op jit(solution)/shard_map/ppermute | solution.py:373
  32.3 4.5 %collective-permute-done.10.refs_8_ = f32[64,512]{1,0:T(8,128)S(1)} collective-permute-done((f32[64,512]{1,0:T(8,128)S(1)}, f32[64,512]{1,0:T(8,128)S(1)}, u32[]{:S(2)}, u32[]{:S(2)}) %collective-permute-start.10) | collective-permute-done | bytes 131104 | tf_op jit(solution)/shard_map/ppermute | solution.py:373
  41.2 2.0 %collective-permute-done.7.refs_7_ = bf16[320,512]{1,0:T(8,128)(2,1)S(1)} collective-permute-done((bf16[320,512]{1,0:T(8,128)(2,1)S(1)}, bf16[320,512]{1,0:T(8,128)(2,1)S(1)}, u32[]{:S(2)}, u32[]{:S(2)}) %collective-permute-start.7) | collective-permute-done | bytes 327712 | tf_op jit(solution)/shard_map/ppermute | solution.py:373
  44.0 1.8 %collective-permute-start.13 = (f32[2,80,512]{2,1,0:T(8,128)S(1)}, f32[2,80,512]{2,1,0:T(8,128)S(1)}, u32[]{:S(2)}, u32[]{:S(2)}) collective-permute-start(f32[2,80,512]{2,1,0:T(8,128)S(1)} %get-tuple-element.53), channel_id=1, source_target_pairs={{0,8},{1,9},{2,10},{3,11},{4,12},{5,13},{6,14},{7,15},{8,0},{9,1},... | collective-permute-start | bytes 983048 | tf_op jit(solution)/shard_map/ppermute | solution.py:373
  47.2 2.4 %collective-permute-start.12 = (f32[64,512]{1,0:T(8,128)S(1)}, f32[64,512]{1,0:T(8,128)S(1)}, u32[]{:S(2)}, u32[]{:S(2)}) collective-permute-start(f32[64,512]{1,0:T(8,128)S(1)} %add_rows.16.refs_8_), channel_id=1, source_target_pairs={{0,16},{1,17},{2,18},{3,19},{4,20},{5,21},{6,22},{7,23},{8,24},{9,... | collective-permute-start | bytes 393224 | tf_op jit(solution)/shard_map/ppermute | solution.py:373
  49.6 2.1 %collective-permute-done.15.refs_7_ = bf16[192,512]{1,0:T(8,128)(2,1)S(1)} collective-permute-done((bf16[192,512]{1,0:T(8,128)(2,1)S(1)}, bf16[192,512]{1,0:T(8,128)(2,1)S(1)}, u32[]{:S(2)}, u32[]{:S(2)}) %collective-permute-start.15) | collective-permute-done | bytes 196640 | tf_op jit(solution)/shard_map/ppermute | solution.py:373
  54.1 2.5 %collective-permute-done.13 = f32[2,80,512]{2,1,0:T(8,128)S(1)} collective-permute-done((f32[2,80,512]{2,1,0:T(8,128)S(1)}, f32[2,80,512]{2,1,0:T(8,128)S(1)}, u32[]{:S(2)}, u32[]{:S(2)}) %collective-permute-start.13) | collective-permute-done | bytes 327712 | tf_op jit(solution)/shard_map/ppermute | solution.py:373
  58.7 2.6 %collective-permute-start.20 = (f32[48,512]{1,0:T(8,128)S(1)}, f32[48,512]{1,0:T(8,128)S(1)}, u32[]{:S(2)}, u32[]{:S(2)}) collective-permute-start(f32[48,512]{1,0:T(8,128)S(1)} %add_rows.19.refs_2_), channel_id=1, source_target_pairs={{0,16},{1,17},{2,18},{3,19},{4,20},{5,21},{6,22},{7,23},{8,24},{9,... | collective-permute-start | bytes 294920 | tf_op jit(solution)/shard_map/ppermute | solution.py:373
  63.8 6.4 %collective-permute-done.20.refs_1_ = f32[48,512]{1,0:T(8,128)S(1)} collective-permute-done((f32[48,512]{1,0:T(8,128)S(1)}, f32[48,512]{1,0:T(8,128)S(1)}, u32[]{:S(2)}, u32[]{:S(2)}) %collective-permute-start.20) | collective-permute-done | bytes 98336 | tf_op jit(solution)/shard_map/ppermute | solution.py:373
  76.2 5.1 %collective-permute-done.29.refs_5_.refs_13_ = f32[128,512]{1,0:T(8,128)S(1)} collective-permute-done((f32[128,512]{1,0:T(8,128)S(1)}, f32[128,512]{1,0:T(8,128)S(1)}, u32[]{:S(2)}, u32[]{:S(2)}) %collective-permute-start.29) | collective-permute-done | bytes 262176 | tf_op jit(solution)/shard_map/ppermute | solution.py:373
  87.6 2.6 %collective-permute-start.25 = (f32[2,40,256]{2,1,0:T(8,128)S(1)}, f32[2,40,256]{2,1,0:T(8,128)S(1)}, u32[]{:S(2)}, u32[]{:S(2)}) collective-permute-start(f32[2,40,256]{2,1,0:T(8,128)S(1)} %slice_add_fusion.2.refs_0_), channel_id=1, source_target_pairs={{0,16},{1,17},{2,18},{3,19},{4,20},{5,21},{6,22},{7,23},{8,24},{9,... | collective-permute-start | bytes 245768 | tf_op jit(solution)/shard_map/ppermute | solution.py:373
  92.0 3.3 %collective-permute-start.26 = (f32[2,40,256]{2,1,0:T(8,128)S(1)}, f32[2,40,256]{2,1,0:T(8,128)S(1)}, u32[]{:S(2)}, u32[]{:S(2)}) collective-permute-start(f32[2,40,256]{2,1,0:T(8,128)S(1)} %add_rows.23), channel_id=1, source_target_pairs={{0,8},{1,9},{2,10},{3,11},{4,12},{5,13},{6,14},{7,15},{8,0},{9,1},... | collective-permute-start | bytes 245768 | tf_op jit(solution)/shard_map/ppermute | solution.py:373
  95.3 3.2 %collective-permute-start.34 = (f32[2,32,256]{2,1,0:T(8,128)S(1)}, f32[2,32,256]{2,1,0:T(8,128)S(1)}, u32[]{:S(2)}, u32[]{:S(2)}) collective-permute-start(f32[2,32,256]{2,1,0:T(8,128)S(1)} %add_rows.26.refs_0_), channel_id=1, source_target_pairs={{0,16},{1,17},{2,18},{3,19},{4,20},{5,21},{6,22},{7,23},{8,24},{9,... | collective-permute-start | bytes 196616 | tf_op jit(solution)/shard_map/ppermute | solution.py:373
  109.0 6.5 %collective-permute-start.38 = (f32[8,40,256]{2,1,0:T(8,128)S(1)}, f32[8,40,256]{2,1,0:T(8,128)S(1)}, u32[]{:S(2)}, u32[]{:S(2)}) collective-permute-start(f32[8,40,256]{2,1,0:T(8,128)S(1)} %pad_maximum_fusion.refs_0_), channel_id=1, source_target_pairs={{0,2},{1,3},{2,0},{3,1},{4,6},{5,7},{6,4},{7,5},{8,10},{9,11},{10,... | collective-permute-start | bytes 983048 | tf_op jit(solution)/shard_map/ppermute | solution.py:373
  115.5 2.4 %collective-permute-start.39 = (f32[8,40,256]{2,1,0:T(8,128)S(1)}, f32[8,40,256]{2,1,0:T(8,128)S(1)}, u32[]{:S(2)}, u32[]{:S(2)}) collective-permute-start(f32[8,40,256]{2,1,0:T(8,128)S(1)} %collective-permute-done.28.refs_1_), channel_id=1, source_target_pairs={{0,2},{1,3},{2,0},{3,1},{4,6},{5,7},{6,4},{7,5},{8,10},{9,11},{10,... | collective-permute-start | bytes 983048 | tf_op jit(solution)/shard_map/ppermute | solution.py:373
  118.0 2.4 %collective-permute-start.41 = (f32[8,32,256]{2,1,0:T(8,128)S(1)}, f32[8,32,256]{2,1,0:T(8,128)S(1)}, u32[]{:S(2)}, u32[]{:S(2)}) collective-permute-start(f32[8,32,256]{2,1,0:T(8,128)S(1)} %collective-permute-done.37.refs_3_), channel_id=1, source_target_pairs={{0,2},{1,3},{2,0},{3,1},{4,6},{5,7},{6,4},{7,5},{8,10},{9,11},{10,... | collective-permute-start | bytes 786440 | tf_op jit(solution)/shard_map/ppermute | solution.py:373
  121.6 4.7 %update.1 = bf16[240,512]{1,0:T(8,128)(2,1)} custom-call(s32[4]{0:T(128)S(1)} %pad_add_fusion.at.refs_0_, f32[8,40,256]{2,1,0:T(8,128)S(1)} %pad_maximum_fusion.refs_0_, f32[8,40,256]{2,1,0:T(8,128)S(1)} %collective-permute-done.28.refs_1_, f32[8,32,256]{2,1,0:T(8,128)S(1)} %pad_maximum_fusion.2.refs_2_, f32[8,32,256]{2,1,0:T(8,128)S(1)} %collective-permute-done.37.refs_3_, ...), custom_call_target="tpu_custom_call" | custom-call | tf_op jit(solution)/shard_map/update/pallas_call | solution.py:351
  (107 shorter events, 46.9 us)
Async XLA Ops:
  3.4 14.5 %collective-permute-start = (bf16[1008,512]{1,0:T(8,128)(2,1)S(1)}, bf16[1008,512]{1,0:T(8,128)(2,1)S(1)}, u32[]{:S(2)}, u32[]{:S(2)}) collective-permute-start(bf16[1008,512]{1,0:T(8,128)(2,1)S(1)} %get-tuple-element.35), channel_id=1, source_target_pairs={{0,2},{1,3},{2,0},{3,1},{4,6},{5,7},{6,4},{7,5},{8,10},{9,11},{10,... | collective-permute-start | bytes 3096584 | tf_op jit(solution)/shard_map/ppermute | solution.py:373
  3.5 8.9 %collective-permute-start.1 = (bf16[240,512]{1,0:T(8,128)(2,1)S(1)}, bf16[240,512]{1,0:T(8,128)(2,1)S(1)}, u32[]{:S(2)}, u32[]{:S(2)}) collective-permute-start(bf16[240,512]{1,0:T(8,128)(2,1)S(1)} %get-tuple-element.36), channel_id=1, source_target_pairs={{0,4},{1,5},{2,6},{3,7},{4,0},{5,1},{6,2},{7,3},{8,12},{9,13},{10,... | collective-permute-start | bytes 737288 | tf_op jit(solution)/shard_map/ppermute | solution.py:373
  6.2 11.7 %collective-permute-start.2 = (bf16[240,512]{1,0:T(8,128)(2,1)S(1)}, bf16[240,512]{1,0:T(8,128)(2,1)S(1)}, u32[]{:S(2)}, u32[]{:S(2)}) collective-permute-start(bf16[240,512]{1,0:T(8,128)(2,1)S(1)} %get-tuple-element.37), channel_id=1, source_target_pairs={{0,6},{1,7},{2,4},{3,5},{4,2},{5,3},{6,0},{7,1},{8,14},{9,15},{10,... | collective-permute-start | bytes 737288 | tf_op jit(solution)/shard_map/ppermute | solution.py:373
  6.2 23.8 %collective-permute-start.8 = (bf16[256,512]{1,0:T(8,128)(2,1)S(1)}, bf16[256,512]{1,0:T(8,128)(2,1)S(1)}, u32[]{:S(2)}, u32[]{:S(2)}) collective-permute-start(bf16[256,512]{1,0:T(8,128)(2,1)S(1)} %get-tuple-element.45), channel_id=1, source_target_pairs={{0,4},{1,5},{2,6},{3,7},{4,0},{5,1},{6,2},{7,3},{8,12},{9,13},{10,... | collective-permute-start | bytes 786440 | tf_op jit(solution)/shard_map/ppermute | solution.py:373
  7.9 22.1 %collective-permute-start.9 = (bf16[256,512]{1,0:T(8,128)(2,1)S(1)}, bf16[256,512]{1,0:T(8,128)(2,1)S(1)}, u32[]{:S(2)}, u32[]{:S(2)}) collective-permute-start(bf16[256,512]{1,0:T(8,128)(2,1)S(1)} %get-tuple-element.46), channel_id=1, source_target_pairs={{0,6},{1,7},{2,4},{3,5},{4,2},{5,3},{6,0},{7,1},{8,14},{9,15},{10,... | collective-permute-start | bytes 786440 | tf_op jit(solution)/shard_map/ppermute | solution.py:373
  18.6 9.0 %collective-permute-start.3 = (f32[48,512]{1,0:T(8,128)S(1)}, f32[48,512]{1,0:T(8,128)S(1)}, u32[]{:S(2)}, u32[]{:S(2)}) collective-permute-start(f32[48,512]{1,0:T(8,128)S(1)} %get-tuple-element.41), channel_id=1, source_target_pairs={{0,8},{1,9},{2,10},{3,11},{4,12},{5,13},{6,14},{7,15},{8,0},{9,1},... | collective-permute-start | bytes 294920 | tf_op jit(solution)/shard_map/ppermute | solution.py:373
  20.5 20.7 %collective-permute-start.6 = (bf16[320,512]{1,0:T(8,128)(2,1)S(1)}, bf16[320,512]{1,0:T(8,128)(2,1)S(1)}, u32[]{:S(2)}, u32[]{:S(2)}) collective-permute-start(bf16[320,512]{1,0:T(8,128)(2,1)S(1)} %get-tuple-element.43), channel_id=1, source_target_pairs={{0,4},{1,5},{2,6},{3,7},{4,0},{5,1},{6,2},{7,3},{8,12},{9,13},{10,... | collective-permute-start | bytes 983048 | tf_op jit(solution)/shard_map/ppermute | solution.py:373
  25.6 17.6 %collective-permute-start.7 = (bf16[320,512]{1,0:T(8,128)(2,1)S(1)}, bf16[320,512]{1,0:T(8,128)(2,1)S(1)}, u32[]{:S(2)}, u32[]{:S(2)}) collective-permute-start(bf16[320,512]{1,0:T(8,128)(2,1)S(1)} %get-tuple-element.44), channel_id=1, source_target_pairs={{0,6},{1,7},{2,4},{3,5},{4,2},{5,3},{6,0},{7,1},{8,14},{9,15},{10,... | collective-permute-start | bytes 983048 | tf_op jit(solution)/shard_map/ppermute | solution.py:373
  27.6 18.3 %collective-permute-start.5 = (f32[48,512]{1,0:T(8,128)S(1)}, f32[48,512]{1,0:T(8,128)S(1)}, u32[]{:S(2)}, u32[]{:S(2)}) collective-permute-start(f32[48,512]{1,0:T(8,128)S(1)} %add_rows.14.refs_8_), channel_id=1, source_target_pairs={{0,16},{1,17},{2,18},{3,19},{4,20},{5,21},{6,22},{7,23},{8,24},{9,... | collective-permute-start | bytes 294920 | tf_op jit(solution)/shard_map/ppermute | solution.py:373
  32.1 7.5 %collective-permute-start.11 = (f32[64,512]{1,0:T(8,128)S(1)}, f32[64,512]{1,0:T(8,128)S(1)}, u32[]{:S(2)}, u32[]{:S(2)}) collective-permute-start(f32[64,512]{1,0:T(8,128)S(1)} %get-tuple-element.50), channel_id=1, source_target_pairs={{0,8},{1,9},{2,10},{3,11},{4,12},{5,13},{6,14},{7,15},{8,0},{9,1},... | collective-permute-start | bytes 393224 | tf_op jit(solution)/shard_map/ppermute | solution.py:373
  36.8 12.8 %collective-permute-start.14 = (bf16[192,512]{1,0:T(8,128)(2,1)S(1)}, bf16[192,512]{1,0:T(8,128)(2,1)S(1)}, u32[]{:S(2)}, u32[]{:S(2)}) collective-permute-start(bf16[192,512]{1,0:T(8,128)(2,1)S(1)} %get-tuple-element.54), channel_id=1, source_target_pairs={{0,4},{1,5},{2,6},{3,7},{4,0},{5,1},{6,2},{7,3},{8,12},{9,13},{10,... | collective-permute-start | bytes 589832 | tf_op jit(solution)/shard_map/ppermute | solution.py:373
  39.6 12.1 %collective-permute-start.15 = (bf16[192,512]{1,0:T(8,128)(2,1)S(1)}, bf16[192,512]{1,0:T(8,128)(2,1)S(1)}, u32[]{:S(2)}, u32[]{:S(2)}) collective-permute-start(bf16[192,512]{1,0:T(8,128)(2,1)S(1)} %get-tuple-element.55), channel_id=1, source_target_pairs={{0,6},{1,7},{2,4},{3,5},{4,2},{5,3},{6,0},{7,1},{8,14},{9,15},{10,... | collective-permute-start | bytes 589832 | tf_op jit(solution)/shard_map/ppermute | solution.py:373
  44.0 12.6 %collective-permute-start.13 = (f32[2,80,512]{2,1,0:T(8,128)S(1)}, f32[2,80,512]{2,1,0:T(8,128)S(1)}, u32[]{:S(2)}, u32[]{:S(2)}) collective-permute-start(f32[2,80,512]{2,1,0:T(8,128)S(1)} %get-tuple-element.53), channel_id=1, source_target_pairs={{0,8},{1,9},{2,10},{3,11},{4,12},{5,13},{6,14},{7,15},{8,0},{9,1},... | collective-permute-start | bytes 983048 | tf_op jit(solution)/shard_map/ppermute | solution.py:373
  45.9 15.4 %collective-permute-start.17 = (f32[48,512]{1,0:T(8,128)S(1)}, f32[48,512]{1,0:T(8,128)S(1)}, u32[]{:S(2)}, u32[]{:S(2)}) collective-permute-start(f32[48,512]{1,0:T(8,128)S(1)} %add_rows.15.refs_9_.refs_0_.refs_8_), channel_id=1, source_target_pairs={{0,1},{1,0},{2,3},{3,2},{4,5},{5,4},{6,7},{7,6},{8,9},{9,8},{10,11... | collective-permute-start | bytes 294920 | tf_op jit(solution)/shard_map/ppermute | solution.py:373
  47.2 14.1 %collective-permute-start.12 = (f32[64,512]{1,0:T(8,128)S(1)}, f32[64,512]{1,0:T(8,128)S(1)}, u32[]{:S(2)}, u32[]{:S(2)}) collective-permute-start(f32[64,512]{1,0:T(8,128)S(1)} %add_rows.16.refs_8_), channel_id=1, source_target_pairs={{0,16},{1,17},{2,18},{3,19},{4,20},{5,21},{6,22},{7,23},{8,24},{9,... | collective-permute-start | bytes 393224 | tf_op jit(solution)/shard_map/ppermute | solution.py:373
  54.0 9.8 %collective-permute-start.19 = (f32[48,512]{1,0:T(8,128)S(1)}, f32[48,512]{1,0:T(8,128)S(1)}, u32[]{:S(2)}, u32[]{:S(2)}) collective-permute-start(f32[48,512]{1,0:T(8,128)S(1)} %get-tuple-element.58), channel_id=1, source_target_pairs={{0,8},{1,9},{2,10},{3,11},{4,12},{5,13},{6,14},{7,15},{8,0},{9,1},... | collective-permute-start | bytes 294920 | tf_op jit(solution)/shard_map/ppermute | solution.py:373
  56.6 13.6 %collective-permute-start.18 = (f32[80,512]{1,0:T(8,128)S(1)}, f32[80,512]{1,0:T(8,128)S(1)}, u32[]{:S(2)}, u32[]{:S(2)}) collective-permute-start(f32[80,512]{1,0:T(8,128)S(1)} %add_rows.17.refs_2_), channel_id=1, source_target_pairs={{0,16},{1,17},{2,18},{3,19},{4,20},{5,21},{6,22},{7,23},{8,24},{9,... | collective-permute-start | bytes 491528 | tf_op jit(solution)/shard_map/ppermute | solution.py:373
  58.7 11.6 %collective-permute-start.20 = (f32[48,512]{1,0:T(8,128)S(1)}, f32[48,512]{1,0:T(8,128)S(1)}, u32[]{:S(2)}, u32[]{:S(2)}) collective-permute-start(f32[48,512]{1,0:T(8,128)S(1)} %add_rows.19.refs_2_), channel_id=1, source_target_pairs={{0,16},{1,17},{2,18},{3,19},{4,20},{5,21},{6,22},{7,23},{8,24},{9,... | collective-permute-start | bytes 294920 | tf_op jit(solution)/shard_map/ppermute | solution.py:373
  61.3 8.9 %collective-permute-start.21 = (f32[64,512]{1,0:T(8,128)S(1)}, f32[64,512]{1,0:T(8,128)S(1)}, u32[]{:S(2)}, u32[]{:S(2)}) collective-permute-start(f32[64,512]{1,0:T(8,128)S(1)} %add_rows.18.refs_1_.refs_9_), channel_id=1, source_target_pairs={{0,1},{1,0},{2,3},{3,2},{4,5},{5,4},{6,7},{7,6},{8,9},{9,8},{10,11... | collective-permute-start | bytes 393224 | tf_op jit(solution)/shard_map/ppermute | solution.py:373
  73.3 7.9 %collective-permute-start.29 = (f32[128,512]{1,0:T(8,128)S(1)}, f32[128,512]{1,0:T(8,128)S(1)}, u32[]{:S(2)}, u32[]{:S(2)}) collective-permute-start(f32[128,512]{1,0:T(8,128)S(1)} %pad_maximum_fusion.1.refs_2_.refs_10_), channel_id=1, source_target_pairs={{0,1},{1,0},{2,3},{3,2},{4,5},{5,4},{6,7},{7,6},{8,9},{9,8},{10,11... | collective-permute-start | bytes 786440 | tf_op jit(solution)/shard_map/ppermute | solution.py:373
  74.9 8.5 %collective-permute-start.23 = (f32[4,40,256]{2,1,0:T(8,128)S(1)}, f32[4,40,256]{2,1,0:T(8,128)S(1)}, u32[]{:S(2)}, u32[]{:S(2)}) collective-permute-start(f32[4,40,256]{2,1,0:T(8,128)S(1)} %add_rows.22.refs_6_), channel_id=1, source_target_pairs={{0,4},{1,5},{2,6},{3,7},{4,0},{5,1},{6,2},{7,3},{8,12},{9,13},{10,... | collective-permute-start | bytes 491528 | tf_op jit(solution)/shard_map/ppermute | solution.py:373
  106.4 9.2 %collective-permute-start.28 = (f32[8,40,256]{2,1,0:T(8,128)S(1)}, f32[8,40,256]{2,1,0:T(8,128)S(1)}, u32[]{:S(2)}, u32[]{:S(2)}) collective-permute-start(f32[8,40,256]{2,1,0:T(8,128)S(1)} %pad_maximum_fusion.refs_0_), channel_id=1, source_target_pairs={{0,1},{1,0},{2,3},{3,2},{4,5},{5,4},{6,7},{7,6},{8,9},{9,8},{10,11... | collective-permute-start | bytes 983048 | tf_op jit(solution)/shard_map/ppermute | solution.py:373
  107.7 10.3 %collective-permute-start.37 = (f32[8,32,256]{2,1,0:T(8,128)S(1)}, f32[8,32,256]{2,1,0:T(8,128)S(1)}, u32[]{:S(2)}, u32[]{:S(2)}) collective-permute-start(f32[8,32,256]{2,1,0:T(8,128)S(1)} %pad_maximum_fusion.2.refs_2_), channel_id=1, source_target_pairs={{0,4},{1,5},{2,6},{3,7},{4,0},{5,1},{6,2},{7,3},{8,12},{9,13},{10,... | collective-permute-start | bytes 786440 | tf_op jit(solution)/shard_map/ppermute | solution.py:373
  109.0 11.4 %collective-permute-start.38 = (f32[8,40,256]{2,1,0:T(8,128)S(1)}, f32[8,40,256]{2,1,0:T(8,128)S(1)}, u32[]{:S(2)}, u32[]{:S(2)}) collective-permute-start(f32[8,40,256]{2,1,0:T(8,128)S(1)} %pad_maximum_fusion.refs_0_), channel_id=1, source_target_pairs={{0,2},{1,3},{2,0},{3,1},{4,6},{5,7},{6,4},{7,5},{8,10},{9,11},{10,... | collective-permute-start | bytes 983048 | tf_op jit(solution)/shard_map/ppermute | solution.py:373
  (20 other events, 113.3 us)

commit v3 on v0

--- a/solution.py
+++ b/solution.py
@@ -56,6 +56,14 @@
     return one(a[0], b[0]) + (one(a[0], b[1]) + one(a[1], b[0]))
 
 
+def dot_rows(a, high, low):
+    rows = a.shape[0]
+    upper, lower = split(a)
+    stacked = jnp.concatenate([upper, lower], 0)
+    both = jnp.dot(stacked, high, preferred_element_type=F32)
+    return both[:rows] + (both[rows:] + jnp.dot(upper, low, preferred_element_type=F32))
+
+
 def slot_row(at, side, slot, own_rows):
     zed, ex, core = at[0], at[1], at[2]
     z = lax.bitwise_xor(zed, ORDER[slot])
@@ -76,13 +84,21 @@
 
 
 def pack_kernel(own_rows, spans, at, values, scales, own, *refs):
-    outs, gathered = refs[:-1], refs[-1]
+    outs, (gathered, staged, sem) = refs[:-3], refs[-3:]
     blocks = scales.shape[0]
-
-    def copy(side, start, rows, out):
+    copies = []
+
+    def copy(side, out):
         for slot in range(SLOTS):
-            base = pl.multiple_of(slot_row(at, side, slot, own_rows) + start, GRAIN)
-            out[slot * rows : (slot + 1) * rows, :] = values[pl.ds(base, rows), :]
+            base = pl.multiple_of(slot_row(at, side, slot, own_rows), GRAIN)
+            copies.append(
+                pltpu.make_async_copy(
+                    values.at[pl.ds(base, own_rows), :],
+                    out.at[pl.ds((side // 3 * SLOTS + slot) * own_rows, own_rows), :],
+                    sem.at[len(copies)],
+                )
+            )
+            copies[-1].start()
 
     def tail(side, out):
         for slot in range(SLOTS):
@@ -97,15 +113,17 @@
             out[row : row + SLOTS * SPAN, :] = part
             left = left - part.astype(F32)
 
-    copy(0, 0, own_rows, own)
-    copy(1, 0, own_rows, outs[0])
-    tail(1, outs[0])
-    for n, (start, rows) in enumerate(spans):
-        for side in (2, 3):
-            out = outs[2 * n + side - 1]
-            copy(side, start, rows, out)
-            if n == 0:
-                tail(side, out)
+    for side, out in ((2, staged), (3, staged), (1, outs[0]), (0, own)):
+        copy(side, out)
+    for side in range(1, 4):
+        tail(side, outs[side - 1])
+    for n, each in enumerate(copies):
+        each.wait()
+        if n < 2 * SLOTS:
+            side, slot = n // SLOTS, n % SLOTS
+            for k, (start, rows) in enumerate(spans):
+                row = n * own_rows + start
+                outs[1 + 2 * k + side][slot * rows : (slot + 1) * rows, :] = staged[row : row + rows, :]
 
 
 def pack(values, scales, at, own_rows, spans):
@@ -115,10 +133,14 @@
         lengths += [SLOTS * rows + (TAIL if n == 0 else 0)] * 2
     return pl.pallas_call(
         functools.partial(pack_kernel, own_rows, spans),
-        in_specs=[SCALARS, WHOLE, WHOLE],
+        in_specs=[SCALARS, pl.BlockSpec(memory_space=pltpu.HBM), WHOLE],
         out_specs=[WHOLE] * len(lengths),
         out_shape=[jax.ShapeDtypeStruct((rows, width), BF16) for rows in lengths],
-        scratch_shapes=[pltpu.VMEM((SLOTS * SPAN, width), F32)],
+        scratch_shapes=[
+            pltpu.VMEM((SLOTS * SPAN, width), F32),
+            pltpu.VMEM((2 * SLOTS * own_rows, width), BF16),
+            pltpu.SemaphoreType.DMA((4 * SLOTS,)),
+        ],
         compiler_params=params(),
         name="pack_rows",
     )(at, values, scales)
@@ -323,18 +345,17 @@
                 put(block.T, other * PIECE, edge + first)
     inv = 1.0 / (jnp.sqrt(trace) + 1e-07)
     share = owns[0].shape[1]
-    contract = ((1,), (0,))
 
     def mine(which):
         return pl.ds(pl.multiple_of(which * share, share), share)
 
     unit = jnp.concatenate([own[...] for own in owns], 0) * inv
     far = jnp.concatenate([across[...] for across in acrosses], 0) * inv
-    first = dot3(split(unit), (high[mine(half), :], low[mine(half), :]), contract)
-    first += dot3(split(far), (high[mine(1 - half), :], low[mine(1 - half), :]), contract)
+    first = dot_rows(unit, high[mine(half), :], low[mine(half), :])
+    first += dot_rows(far, high[mine(1 - half), :], low[mine(1 - half), :])
     first = first * (inv * inv)
     gram[...] = first
-    second = dot3(split(first), (high[:, mine(half)], low[:, mine(half)]), contract)
+    second = dot_rows(first, high[:, mine(half)], low[:, mine(half)])
     second = second * (inv * inv)
     result = 3.4445 * unit + (-4.775 * gram[:, mine(half)] + 2.0315 * second)
     out[...] = (scale * result).astype(out.dtype)
@@ -442,8 +463,8 @@
 
     count = len(owns)
     own, far = gram_part(near_kernel, at, owns, count, NEAR, "gram_near", [])
-    core = flip(far, "c")
-    near_sent = add([own[4:], core[4:]], [])
+    core = [flip(far[4:], "c"), flip(far[:4], "c")]
+    near_sent = add([own[4:], core[0]], [])
     near_x = flip(near_sent, "x")
     cross_own, far = gram_part(
         cross_kernel, at, owns + acrosses, count, CROSS, "gram_cross", [near_sent]
@@ -451,7 +472,7 @@
     cross_core = [flip(far[4:], "c"), flip(far[:4], "c")]
     cross_x = flip(add([cross_own[4:], cross_core[0]], [near_x]), "x")
 
-    near = own[:4] + core[:4] + near_x
+    near = own[:4] + core[1] + near_x
     near_z1 = flip(near[2:], "z1")
     near = near[:2] + near_z1
     near_z2 = flip(near, "z2")

time: 125 us -> 123 us (0.984)
  waiting for transfers between devices: 49.9 us -> 42.3 us
  starting transfers between devices: 60.4 us -> 65.6 us
    ppermute x43 -> x44, waiting for transfers between devices: 49.9 us -> 42.3 us  [flip(): lax.ppermute(value, ('dp', 'fsdp'), [(i, i ^ mask) for i in range(count)])]
    ppermute x43 -> x44, starting transfers between devices: 60.4 us -> 65.6 us  [flip(): lax.ppermute(value, ('dp', 'fsdp'), [(i, i ^ mask) for i in range(count)])]
  transfers between devices with their start and end apart: 43 -> 44, of which waited for: 20 -> 20; matrix products, arithmetic and copies ran while one was open for 0% -> 0% of each run, Pallas kernels for 4% -> 5%
where the time goes in v3:
time: 123 us
  starting transfers between devices  65.6 us (53%)
  waiting for transfers between devices  42.3 us (34%)
  Pallas kernels  13.1 us (11%)
    ppermute x44, starting transfers between devices, flip(): lax.ppermute(value, ('dp', 'fsdp'), [(i, i ^ mask) for i in range(count)])  65.6 us
    ppermute x44, waiting for transfers between devices, flip(): lax.ppermute(value, ('dp', 'fsdp'), [(i, i ^ mask) for i in range(count)])  42.3 us
    pallas_call x1, Pallas kernels, update(): pl.pallas_call(functools.partial(update_kernel, scale, places, len(owns))...  4.67 us
    pallas_call x4, Pallas kernels, dequant(): pl.pallas_call(kernel, in_specs=[SCALARS] + [WHOLE] * 7 + [ANYWHERE] * (l...  2.98 us
    pallas_call x1, Pallas kernels, pack(): pl.pallas_call(functools.partial(pack_kernel, own_rows, spans), in_specs=...  2.89 us
  transfers between devices with their start and end apart: 44, of which 20 were waited for; matrix products, arithmetic and copies ran while one was open for 0% of the time, Pallas kernels for 5%

profile of v3, /device:TPU:1, one launch (start us, length us, event | category | flops | bytes accessed | tf_op | source)
XLA Modules:
  0.0 122.5 jit_solution(10458985295055476192)
XLA Ops:
  0.9 2.9 %pack_rows.1 = (bf16[960,512]{1,0:T(8,128)(2,1)S(1)}, bf16[1008,512]{1,0:T(8,128)(2,1)S(1)}, bf16[240,512]{1,0:T(8,128)(2,1)S(1)}, bf16[240,512]{1,0:T(8,128)(2,...) custom-call(s32[4]{0:T(128)S(1)} %pad_add_fusion.at.refs_0_, ...), custom_call_target="tpu_custom_call" | custom-call | tf_op jit(solution)/shard_map/pack_rows/pallas_call | solution.py:134
  3.9 2.7 %collective-permute-start.1 = (bf16[240,512]{1,0:T(8,128)(2,1)S(1)}, bf16[240,512]{1,0:T(8,128)(2,1)S(1)}, u32[]{:S(2)}, u32[]{:S(2)}) collective-permute-start(bf16[240,512]{1,0:T(8,128)(2,1)S(1)} %get-tuple-element.38), channel_id=1, source_target_pairs={{0,4},{1,5},{2,6},{3,7},{4,0},{5,1},{6,2},{7,3},{8,12},{9,13},{10,... | collective-permute-start | bytes 737288 | tf_op jit(solution)/shard_map/ppermute | solution.py:390
  8.7 4.2 %collective-permute-done.1.refs_4_.refs_6_ = bf16[240,512]{1,0:T(8,128)(2,1)S(1)} collective-permute-done((bf16[240,512]{1,0:T(8,128)(2,1)S(1)}, bf16[240,512]{1,0:T(8,128)(2,1)S(1)}, u32[]{:S(2)}, u32[]{:S(2)}) %collective-permute-start.1) | collective-permute-done | bytes 245792 | tf_op jit(solution)/shard_map/ppermute | solution.py:390
  12.8 5.5 %collective-permute-done.2.refs_5_.refs_7_ = bf16[240,512]{1,0:T(8,128)(2,1)S(1)} collective-permute-done((bf16[240,512]{1,0:T(8,128)(2,1)S(1)}, bf16[240,512]{1,0:T(8,128)(2,1)S(1)}, u32[]{:S(2)}, u32[]{:S(2)}) %collective-permute-start.2) | collective-permute-done | bytes 245792 | tf_op jit(solution)/shard_map/ppermute | solution.py:390
  19.0 1.8 %collective-permute-start.3 = (f32[48,512]{1,0:T(8,128)S(1)}, f32[48,512]{1,0:T(8,128)S(1)}, u32[]{:S(2)}, u32[]{:S(2)}) collective-permute-start(f32[48,512]{1,0:T(8,128)S(1)} %get-tuple-element.43), channel_id=1, source_target_pairs={{0,8},{1,9},{2,10},{3,11},{4,12},{5,13},{6,14},{7,15},{8,0},{9,1},... | collective-permute-start | bytes 294920 | tf_op jit(solution)/shard_map/ppermute | solution.py:390
  22.3 3.7 %collective-permute-done.4.refs_1_ = f32[48,512]{1,0:T(8,128)S(1)} collective-permute-done((f32[48,512]{1,0:T(8,128)S(1)}, f32[48,512]{1,0:T(8,128)S(1)}, u32[]{:S(2)}, u32[]{:S(2)}) %collective-permute-start.4) | collective-permute-done | bytes 98336 | tf_op jit(solution)/shard_map/ppermute | solution.py:390
  26.0 2.0 %collective-permute-start.12 = (bf16[256,512]{1,0:T(8,128)(2,1)S(1)}, bf16[256,512]{1,0:T(8,128)(2,1)S(1)}, u32[]{:S(2)}, u32[]{:S(2)}) collective-permute-start(bf16[256,512]{1,0:T(8,128)(2,1)S(1)} %get-tuple-element.53), channel_id=1, source_target_pairs={{0,6},{1,7},{2,4},{3,5},{4,2},{5,3},{6,0},{7,1},{8,14},{9,15},{10,... | collective-permute-start | bytes 786440 | tf_op jit(solution)/shard_map/ppermute | solution.py:390
  28.0 2.4 %collective-permute-start.5 = (f32[48,512]{1,0:T(8,128)S(1)}, f32[48,512]{1,0:T(8,128)S(1)}, u32[]{:S(2)}, u32[]{:S(2)}) collective-permute-start(f32[48,512]{1,0:T(8,128)S(1)} %add_rows.13.refs_8_), channel_id=1, source_target_pairs={{0,16},{1,17},{2,18},{3,19},{4,20},{5,21},{6,22},{7,23},{8,24},{9,... | collective-permute-start | bytes 294920 | tf_op jit(solution)/shard_map/ppermute | solution.py:390
  30.4 2.3 %collective-permute-done.7.refs_7_ = bf16[320,512]{1,0:T(8,128)(2,1)S(1)} collective-permute-done((bf16[320,512]{1,0:T(8,128)(2,1)S(1)}, bf16[320,512]{1,0:T(8,128)(2,1)S(1)}, u32[]{:S(2)}, u32[]{:S(2)}) %collective-permute-start.7) | collective-permute-done | bytes 327712 | tf_op jit(solution)/shard_map/ppermute | solution.py:390
  36.8 6.7 %collective-permute-done.9.refs_1_ = f32[80,512]{1,0:T(8,128)S(1)} collective-permute-done((f32[80,512]{1,0:T(8,128)S(1)}, f32[80,512]{1,0:T(8,128)S(1)}, u32[]{:S(2)}, u32[]{:S(2)}) %collective-permute-start.9) | collective-permute-done | bytes 163872 | tf_op jit(solution)/shard_map/ppermute | solution.py:390
  46.5 2.3 %collective-permute-start.10 = (f32[80,512]{1,0:T(8,128)S(1)}, f32[80,512]{1,0:T(8,128)S(1)}, u32[]{:S(2)}, u32[]{:S(2)}) collective-permute-start(f32[80,512]{1,0:T(8,128)S(1)} %add_rows.15.refs_8_), channel_id=1, source_target_pairs={{0,16},{1,17},{2,18},{3,19},{4,20},{5,21},{6,22},{7,23},{8,24},{9,... | collective-permute-start | bytes 491528 | tf_op jit(solution)/shard_map/ppermute | solution.py:390
  52.8 2.6 %collective-permute-start.19 = (f32[48,512]{1,0:T(8,128)S(1)}, f32[48,512]{1,0:T(8,128)S(1)}, u32[]{:S(2)}, u32[]{:S(2)}) collective-permute-start(f32[48,512]{1,0:T(8,128)S(1)} %get-tuple-element.60), channel_id=1, source_target_pairs={{0,16},{1,17},{2,18},{3,19},{4,20},{5,21},{6,22},{7,23},{8,24},{9,... | collective-permute-start | bytes 294920 | tf_op jit(solution)/shard_map/ppermute | solution.py:390
  58.6 2.9 %collective-permute-done.17 = f32[64,512]{1,0:T(8,128)S(1)} collective-permute-done((f32[64,512]{1,0:T(8,128)S(1)}, f32[64,512]{1,0:T(8,128)S(1)}, u32[]{:S(2)}, u32[]{:S(2)}) %collective-permute-start.17) | collective-permute-done | bytes 131104 | tf_op jit(solution)/shard_map/ppermute | solution.py:390
  61.8 4.6 %collective-permute-done.18.refs_1_ = f32[64,512]{1,0:T(8,128)S(1)} collective-permute-done((f32[64,512]{1,0:T(8,128)S(1)}, f32[64,512]{1,0:T(8,128)S(1)}, u32[]{:S(2)}, u32[]{:S(2)}) %collective-permute-start.18) | collective-permute-done | bytes 131104 | tf_op jit(solution)/shard_map/ppermute | solution.py:390
  66.5 3.4 %collective-permute-start.31 = (f32[112,512]{1,0:T(8,128)S(1)}, f32[112,512]{1,0:T(8,128)S(1)}, u32[]{:S(2)}, u32[]{:S(2)}) collective-permute-start(f32[112,512]{1,0:T(8,128)S(1)} %pad_maximum_fusion.2.refs_2_.refs_10_), channel_id=1, source_target_pairs={{0,1},{1,0},{2,3},{3,2},{4,5},{5,4},{6,7},{7,6},{8,9},{9,8},{10,11... | collective-permute-start | bytes 688136 | tf_op jit(solution)/shard_map/ppermute | solution.py:390
  71.1 3.4 %collective-permute-start.24 = (f32[4,40,256]{2,1,0:T(8,128)S(1)}, f32[4,40,256]{2,1,0:T(8,128)S(1)}, u32[]{:S(2)}, u32[]{:S(2)}) collective-permute-start(f32[4,40,256]{2,1,0:T(8,128)S(1)} %get-tuple-element.68), channel_id=1, source_target_pairs={{0,2},{1,3},{2,0},{3,1},{4,6},{5,7},{6,4},{7,5},{8,10},{9,11},{10,... | collective-permute-start | bytes 491528 | tf_op jit(solution)/shard_map/ppermute | solution.py:390
  77.8 2.0 %collective-permute-start.33 = (f32[4,32,256]{2,1,0:T(8,128)S(1)}, f32[4,32,256]{2,1,0:T(8,128)S(1)}, u32[]{:S(2)}, u32[]{:S(2)}) collective-permute-start(f32[4,32,256]{2,1,0:T(8,128)S(1)} %get-tuple-element.69), channel_id=1, source_target_pairs={{0,2},{1,3},{2,0},{3,1},{4,6},{5,7},{6,4},{7,5},{8,10},{9,11},{10,... | collective-permute-start | bytes 393224 | tf_op jit(solution)/shard_map/ppermute | solution.py:390
  84.5 2.9 %collective-permute-start.27 = (f32[2,40,256]{2,1,0:T(8,128)S(1)}, f32[2,40,256]{2,1,0:T(8,128)S(1)}, u32[]{:S(2)}, u32[]{:S(2)}) collective-permute-start(f32[2,40,256]{2,1,0:T(8,128)S(1)} %slice_add_fusion.refs_0_), channel_id=1, source_target_pairs={{0,16},{1,17},{2,18},{3,19},{4,20},{5,21},{6,22},{7,23},{8,24},{9,... | collective-permute-start | bytes 245768 | tf_op jit(solution)/shard_map/ppermute | solution.py:390
  90.1 1.9 %collective-permute-done.35.refs_1_ = f32[2,32,256]{2,1,0:T(8,128)S(1)} collective-permute-done((f32[2,32,256]{2,1,0:T(8,128)S(1)}, f32[2,32,256]{2,1,0:T(8,128)S(1)}, u32[]{:S(2)}, u32[]{:S(2)}) %collective-permute-start.35) | collective-permute-done | bytes 65568 | tf_op jit(solution)/shard_map/ppermute | solution.py:390
  92.0 2.4 %collective-permute-start.36 = (f32[2,32,256]{2,1,0:T(8,128)S(1)}, f32[2,32,256]{2,1,0:T(8,128)S(1)}, u32[]{:S(2)}, u32[]{:S(2)}) collective-permute-start(f32[2,32,256]{2,1,0:T(8,128)S(1)} %add_rows.24.refs_0_), channel_id=1, source_target_pairs={{0,16},{1,17},{2,18},{3,19},{4,20},{5,21},{6,22},{7,23},{8,24},{9,... | collective-permute-start | bytes 196616 | tf_op jit(solution)/shard_map/ppermute | solution.py:390
  104.6 6.9 %collective-permute-start.40 = (f32[8,40,256]{2,1,0:T(8,128)S(1)}, f32[8,40,256]{2,1,0:T(8,128)S(1)}, u32[]{:S(2)}, u32[]{:S(2)}) collective-permute-start(f32[8,40,256]{2,1,0:T(8,128)S(1)} %pad_maximum_fusion.refs_0_), channel_id=1, source_target_pairs={{0,2},{1,3},{2,0},{3,1},{4,6},{5,7},{6,4},{7,5},{8,10},{9,11},{10,... | collective-permute-start | bytes 983048 | tf_op jit(solution)/shard_map/ppermute | solution.py:390
  111.6 2.2 %collective-permute-start.41 = (f32[8,40,256]{2,1,0:T(8,128)S(1)}, f32[8,40,256]{2,1,0:T(8,128)S(1)}, u32[]{:S(2)}, u32[]{:S(2)}) collective-permute-start(f32[8,40,256]{2,1,0:T(8,128)S(1)} %collective-permute-done.30.refs_1_), channel_id=1, source_target_pairs={{0,2},{1,3},{2,0},{3,1},{4,6},{5,7},{6,4},{7,5},{8,10},{9,11},{10,... | collective-permute-start | bytes 983048 | tf_op jit(solution)/shard_map/ppermute | solution.py:390
  113.8 2.9 %collective-permute-start.43 = (f32[8,32,256]{2,1,0:T(8,128)S(1)}, f32[8,32,256]{2,1,0:T(8,128)S(1)}, u32[]{:S(2)}, u32[]{:S(2)}) collective-permute-start(f32[8,32,256]{2,1,0:T(8,128)S(1)} %collective-permute-done.39.refs_3_), channel_id=1, source_target_pairs={{0,2},{1,3},{2,0},{3,1},{4,6},{5,7},{6,4},{7,5},{8,10},{9,11},{10,... | collective-permute-start | bytes 786440 | tf_op jit(solution)/shard_map/ppermute | solution.py:390
  117.9 4.7 %update.1 = bf16[240,512]{1,0:T(8,128)(2,1)} custom-call(s32[4]{0:T(128)S(1)} %pad_add_fusion.at.refs_0_, f32[8,40,256]{2,1,0:T(8,128)S(1)} %pad_maximum_fusion.refs_0_, f32[8,40,256]{2,1,0:T(8,128)S(1)} %collective-permute-done.30.refs_1_, f32[8,32,256]{2,1,0:T(8,128)S(1)} %pad_maximum_fusion.1.refs_2_, f32[8,32,256]{2,1,0:T(8,128)S(1)} %collective-permute-done.39.refs_3_, ...), custom_call_target="tpu_custom_call" | custom-call | tf_op jit(solution)/shard_map/update/pallas_call | solution.py:368
  (109 shorter events, 43.0 us)
Async XLA Ops:
  3.8 14.5 %collective-permute-start = (bf16[1008,512]{1,0:T(8,128)(2,1)S(1)}, bf16[1008,512]{1,0:T(8,128)(2,1)S(1)}, u32[]{:S(2)}, u32[]{:S(2)}) collective-permute-start(bf16[1008,512]{1,0:T(8,128)(2,1)S(1)} %get-tuple-element.37), channel_id=1, source_target_pairs={{0,2},{1,3},{2,0},{3,1},{4,6},{5,7},{6,4},{7,5},{8,10},{9,11},{10,... | collective-permute-start | bytes 3096584 | tf_op jit(solution)/shard_map/ppermute | solution.py:390
  3.9 8.9 %collective-permute-start.1 = (bf16[240,512]{1,0:T(8,128)(2,1)S(1)}, bf16[240,512]{1,0:T(8,128)(2,1)S(1)}, u32[]{:S(2)}, u32[]{:S(2)}) collective-permute-start(bf16[240,512]{1,0:T(8,128)(2,1)S(1)} %get-tuple-element.38), channel_id=1, source_target_pairs={{0,4},{1,5},{2,6},{3,7},{4,0},{5,1},{6,2},{7,3},{8,12},{9,13},{10,... | collective-permute-start | bytes 737288 | tf_op jit(solution)/shard_map/ppermute | solution.py:390
  6.6 11.7 %collective-permute-start.2 = (bf16[240,512]{1,0:T(8,128)(2,1)S(1)}, bf16[240,512]{1,0:T(8,128)(2,1)S(1)}, u32[]{:S(2)}, u32[]{:S(2)}) collective-permute-start(bf16[240,512]{1,0:T(8,128)(2,1)S(1)} %get-tuple-element.39), channel_id=1, source_target_pairs={{0,6},{1,7},{2,4},{3,5},{4,2},{5,3},{6,0},{7,1},{8,14},{9,15},{10,... | collective-permute-start | bytes 737288 | tf_op jit(solution)/shard_map/ppermute | solution.py:390
  6.6 23.8 %collective-permute-start.6 = (bf16[320,512]{1,0:T(8,128)(2,1)S(1)}, bf16[320,512]{1,0:T(8,128)(2,1)S(1)}, u32[]{:S(2)}, u32[]{:S(2)}) collective-permute-start(bf16[320,512]{1,0:T(8,128)(2,1)S(1)} %get-tuple-element.45), channel_id=1, source_target_pairs={{0,4},{1,5},{2,6},{3,7},{4,0},{5,1},{6,2},{7,3},{8,12},{9,13},{10,... | collective-permute-start | bytes 983048 | tf_op jit(solution)/shard_map/ppermute | solution.py:390
  8.3 24.4 %collective-permute-start.7 = (bf16[320,512]{1,0:T(8,128)(2,1)S(1)}, bf16[320,512]{1,0:T(8,128)(2,1)S(1)}, u32[]{:S(2)}, u32[]{:S(2)}) collective-permute-start(bf16[320,512]{1,0:T(8,128)(2,1)S(1)} %get-tuple-element.46), channel_id=1, source_target_pairs={{0,6},{1,7},{2,4},{3,5},{4,2},{5,3},{6,0},{7,1},{8,14},{9,15},{10,... | collective-permute-start | bytes 983048 | tf_op jit(solution)/shard_map/ppermute | solution.py:390
  19.0 9.0 %collective-permute-start.3 = (f32[48,512]{1,0:T(8,128)S(1)}, f32[48,512]{1,0:T(8,128)S(1)}, u32[]{:S(2)}, u32[]{:S(2)}) collective-permute-start(f32[48,512]{1,0:T(8,128)S(1)} %get-tuple-element.43), channel_id=1, source_target_pairs={{0,8},{1,9},{2,10},{3,11},{4,12},{5,13},{6,14},{7,15},{8,0},{9,1},... | collective-permute-start | bytes 294920 | tf_op jit(solution)/shard_map/ppermute | solution.py:390
  21.0 25.6 %collective-permute-start.11 = (bf16[256,512]{1,0:T(8,128)(2,1)S(1)}, bf16[256,512]{1,0:T(8,128)(2,1)S(1)}, u32[]{:S(2)}, u32[]{:S(2)}) collective-permute-start(bf16[256,512]{1,0:T(8,128)(2,1)S(1)} %get-tuple-element.52), channel_id=1, source_target_pairs={{0,4},{1,5},{2,6},{3,7},{4,0},{5,1},{6,2},{7,3},{8,12},{9,13},{10,... | collective-permute-start | bytes 786440 | tf_op jit(solution)/shard_map/ppermute | solution.py:390
  26.0 22.8 %collective-permute-start.12 = (bf16[256,512]{1,0:T(8,128)(2,1)S(1)}, bf16[256,512]{1,0:T(8,128)(2,1)S(1)}, u32[]{:S(2)}, u32[]{:S(2)}) collective-permute-start(bf16[256,512]{1,0:T(8,128)(2,1)S(1)} %get-tuple-element.53), channel_id=1, source_target_pairs={{0,6},{1,7},{2,4},{3,5},{4,2},{5,3},{6,0},{7,1},{8,14},{9,15},{10,... | collective-permute-start | bytes 786440 | tf_op jit(solution)/shard_map/ppermute | solution.py:390
  28.0 7.6 %collective-permute-start.5 = (f32[48,512]{1,0:T(8,128)S(1)}, f32[48,512]{1,0:T(8,128)S(1)}, u32[]{:S(2)}, u32[]{:S(2)}) collective-permute-start(f32[48,512]{1,0:T(8,128)S(1)} %add_rows.13.refs_8_), channel_id=1, source_target_pairs={{0,16},{1,17},{2,18},{3,19},{4,20},{5,21},{6,22},{7,23},{8,24},{9,... | collective-permute-start | bytes 294920 | tf_op jit(solution)/shard_map/ppermute | solution.py:390
  33.5 11.7 %collective-permute-start.8 = (f32[80,512]{1,0:T(8,128)S(1)}, f32[80,512]{1,0:T(8,128)S(1)}, u32[]{:S(2)}, u32[]{:S(2)}) collective-permute-start(f32[80,512]{1,0:T(8,128)S(1)} %get-tuple-element.50), channel_id=1, source_target_pairs={{0,8},{1,9},{2,10},{3,11},{4,12},{5,13},{6,14},{7,15},{8,0},{9,1},... | collective-permute-start | bytes 491528 | tf_op jit(solution)/shard_map/ppermute | solution.py:390
  35.3 8.2 %collective-permute-start.9 = (f32[80,512]{1,0:T(8,128)S(1)}, f32[80,512]{1,0:T(8,128)S(1)}, u32[]{:S(2)}, u32[]{:S(2)}) collective-permute-start(f32[80,512]{1,0:T(8,128)S(1)} %get-tuple-element.51), channel_id=1, source_target_pairs={{0,8},{1,9},{2,10},{3,11},{4,12},{5,13},{6,14},{7,15},{8,0},{9,1},... | collective-permute-start | bytes 491528 | tf_op jit(solution)/shard_map/ppermute | solution.py:390
  35.6 15.5 %collective-permute-start.14 = (bf16[192,512]{1,0:T(8,128)(2,1)S(1)}, bf16[192,512]{1,0:T(8,128)(2,1)S(1)}, u32[]{:S(2)}, u32[]{:S(2)}) collective-permute-start(bf16[192,512]{1,0:T(8,128)(2,1)S(1)} %get-tuple-element.56), channel_id=1, source_target_pairs={{0,4},{1,5},{2,6},{3,7},{4,0},{5,1},{6,2},{7,3},{8,12},{9,13},{10,... | collective-permute-start | bytes 589832 | tf_op jit(solution)/shard_map/ppermute | solution.py:390
  43.5 8.5 %collective-permute-start.15 = (bf16[192,512]{1,0:T(8,128)(2,1)S(1)}, bf16[192,512]{1,0:T(8,128)(2,1)S(1)}, u32[]{:S(2)}, u32[]{:S(2)}) collective-permute-start(bf16[192,512]{1,0:T(8,128)(2,1)S(1)} %get-tuple-element.57), channel_id=1, source_target_pairs={{0,6},{1,7},{2,4},{3,5},{4,2},{5,3},{6,0},{7,1},{8,14},{9,15},{10,... | collective-permute-start | bytes 589832 | tf_op jit(solution)/shard_map/ppermute | solution.py:390
  45.2 12.0 %collective-permute-start.16 = (f32[48,512]{1,0:T(8,128)S(1)}, f32[48,512]{1,0:T(8,128)S(1)}, u32[]{:S(2)}, u32[]{:S(2)}) collective-permute-start(f32[48,512]{1,0:T(8,128)S(1)} %add_rows.14.refs_10_.refs_0_.refs_8_), channel_id=1, source_target_pairs={{0,1},{1,0},{2,3},{3,2},{4,5},{5,4},{6,7},{7,6},{8,9},{9,8},{10,11... | collective-permute-start | bytes 294920 | tf_op jit(solution)/shard_map/ppermute | solution.py:390
  46.5 12.1 %collective-permute-start.10 = (f32[80,512]{1,0:T(8,128)S(1)}, f32[80,512]{1,0:T(8,128)S(1)}, u32[]{:S(2)}, u32[]{:S(2)}) collective-permute-start(f32[80,512]{1,0:T(8,128)S(1)} %add_rows.15.refs_8_), channel_id=1, source_target_pairs={{0,16},{1,17},{2,18},{3,19},{4,20},{5,21},{6,22},{7,23},{8,24},{9,... | collective-permute-start | bytes 491528 | tf_op jit(solution)/shard_map/ppermute | solution.py:390
  51.0 10.5 %collective-permute-start.17 = (f32[64,512]{1,0:T(8,128)S(1)}, f32[64,512]{1,0:T(8,128)S(1)}, u32[]{:S(2)}, u32[]{:S(2)}) collective-permute-start(f32[64,512]{1,0:T(8,128)S(1)} %get-tuple-element.59), channel_id=1, source_target_pairs={{0,8},{1,9},{2,10},{3,11},{4,12},{5,13},{6,14},{7,15},{8,0},{9,1},... | collective-permute-start | bytes 393224 | tf_op jit(solution)/shard_map/ppermute | solution.py:390
  52.8 13.6 %collective-permute-start.19 = (f32[48,512]{1,0:T(8,128)S(1)}, f32[48,512]{1,0:T(8,128)S(1)}, u32[]{:S(2)}, u32[]{:S(2)}) collective-permute-start(f32[48,512]{1,0:T(8,128)S(1)} %get-tuple-element.60), channel_id=1, source_target_pairs={{0,16},{1,17},{2,18},{3,19},{4,20},{5,21},{6,22},{7,23},{8,24},{9,... | collective-permute-start | bytes 294920 | tf_op jit(solution)/shard_map/ppermute | solution.py:390
  55.4 10.9 %collective-permute-start.20 = (f32[48,512]{1,0:T(8,128)S(1)}, f32[48,512]{1,0:T(8,128)S(1)}, u32[]{:S(2)}, u32[]{:S(2)}) collective-permute-start(f32[48,512]{1,0:T(8,128)S(1)} %get-tuple-element.61), channel_id=1, source_target_pairs={{0,8},{1,9},{2,10},{3,11},{4,12},{5,13},{6,14},{7,15},{8,0},{9,1},... | collective-permute-start | bytes 294920 | tf_op jit(solution)/shard_map/ppermute | solution.py:390
  57.2 9.2 %collective-permute-start.21 = (f32[48,512]{1,0:T(8,128)S(1)}, f32[48,512]{1,0:T(8,128)S(1)}, u32[]{:S(2)}, u32[]{:S(2)}) collective-permute-start(f32[48,512]{1,0:T(8,128)S(1)} %get-tuple-element.62), channel_id=1, source_target_pairs={{0,24},{1,25},{2,26},{3,27},{4,28},{5,29},{6,30},{7,31},{8,16},{9,... | collective-permute-start | bytes 294920 | tf_op jit(solution)/shard_map/ppermute | solution.py:390
  58.6 7.7 %collective-permute-start.18 = (f32[64,512]{1,0:T(8,128)S(1)}, f32[64,512]{1,0:T(8,128)S(1)}, u32[]{:S(2)}, u32[]{:S(2)}) collective-permute-start(f32[64,512]{1,0:T(8,128)S(1)} %add_rows.16.refs_2_), channel_id=1, source_target_pairs={{0,16},{1,17},{2,18},{3,19},{4,20},{5,21},{6,22},{7,23},{8,24},{9,... | collective-permute-start | bytes 393224 | tf_op jit(solution)/shard_map/ppermute | solution.py:390
  66.5 10.1 %collective-permute-start.31 = (f32[112,512]{1,0:T(8,128)S(1)}, f32[112,512]{1,0:T(8,128)S(1)}, u32[]{:S(2)}, u32[]{:S(2)}) collective-permute-start(f32[112,512]{1,0:T(8,128)S(1)} %pad_maximum_fusion.2.refs_2_.refs_10_), channel_id=1, source_target_pairs={{0,1},{1,0},{2,3},{3,2},{4,5},{5,4},{6,7},{7,6},{8,9},{9,8},{10,11... | collective-permute-start | bytes 688136 | tf_op jit(solution)/shard_map/ppermute | solution.py:390
  102.2 9.4 %collective-permute-start.30 = (f32[8,40,256]{2,1,0:T(8,128)S(1)}, f32[8,40,256]{2,1,0:T(8,128)S(1)}, u32[]{:S(2)}, u32[]{:S(2)}) collective-permute-start(f32[8,40,256]{2,1,0:T(8,128)S(1)} %pad_maximum_fusion.refs_0_), channel_id=1, source_target_pairs={{0,1},{1,0},{2,3},{3,2},{4,5},{5,4},{6,7},{7,6},{8,9},{9,8},{10,11... | collective-permute-start | bytes 983048 | tf_op jit(solution)/shard_map/ppermute | solution.py:390
  103.5 10.3 %collective-permute-start.39 = (f32[8,32,256]{2,1,0:T(8,128)S(1)}, f32[8,32,256]{2,1,0:T(8,128)S(1)}, u32[]{:S(2)}, u32[]{:S(2)}) collective-permute-start(f32[8,32,256]{2,1,0:T(8,128)S(1)} %pad_maximum_fusion.1.refs_2_), channel_id=1, source_target_pairs={{0,4},{1,5},{2,6},{3,7},{4,0},{5,1},{6,2},{7,3},{8,12},{9,13},{10,... | collective-permute-start | bytes 786440 | tf_op jit(solution)/shard_map/ppermute | solution.py:390
  104.6 12.1 %collective-permute-start.40 = (f32[8,40,256]{2,1,0:T(8,128)S(1)}, f32[8,40,256]{2,1,0:T(8,128)S(1)}, u32[]{:S(2)}, u32[]{:S(2)}) collective-permute-start(f32[8,40,256]{2,1,0:T(8,128)S(1)} %pad_maximum_fusion.refs_0_), channel_id=1, source_target_pairs={{0,2},{1,3},{2,0},{3,1},{4,6},{5,7},{6,4},{7,5},{8,10},{9,11},{10,... | collective-permute-start | bytes 983048 | tf_op jit(solution)/shard_map/ppermute | solution.py:390
  (22 other events, 126.1 us)

commit v4 on v0

--- a/solution.py
+++ b/solution.py
@@ -54,6 +54,10 @@
         return lax.dot_general(u, v, dims, preferred_element_type=F32)
 
     return one(a[0], b[0]) + (one(a[0], b[1]) + one(a[1], b[0]))
+
+
+def dot_rows(a, high, low, flipped=False):
+    return dot3(split(a), (high, low), ((1,), (int(flipped),)))
 
 
 def slot_row(at, side, slot, own_rows):
@@ -280,84 +284,115 @@
     )(at, *slabs, *after)
 
 
-def update_kernel(scale, places, count, at, *refs):
-    pieces, refs = refs[: len(places)], refs[len(places) :]
-    owns, acrosses, refs = refs[:count], refs[count : 2 * count], refs[2 * count :]
-    out, packed, gram, high, low = refs
+def unpack(at, pieces, places, packed, length):
     zed, ex, core, half = at[0], at[1], at[2], at[3]
-    for ref, (first, slots) in zip(pieces, places):
+    for ref, slots in zip(pieces, places):
         part = ref.shape[1]
         for n, (kz, kx, kc, kf) in enumerate(slots):
             quarter = 2 * lax.bitwise_xor(half, kf) + lax.bitwise_xor(core, kc)
             chip = 2 * lax.bitwise_xor(zed, kz) + lax.bitwise_xor(ex, kx)
-            row = pl.multiple_of(quarter * PACKED + first + chip * part, 8)
+            row = pl.multiple_of(quarter * length + chip * part, 8)
             packed[pl.ds(row, part), :] = ref[n]
+
+
+def start_kernel(places, count, at, *refs):
+    pieces, refs = refs[: len(places)], refs[len(places) :]
+    owns, acrosses, refs = refs[:count], refs[count : 2 * count], refs[2 * count :]
+    high, low, inv_out, own_part, far_part, packed = refs
+    half = at[3]
+    unpack(at, pieces, places, packed, NEAR)
     trace = jnp.zeros((1, 1), F32)
     rows = lax.broadcasted_iota(jnp.int32, (HALF, HALF), 0)
     columns = lax.broadcasted_iota(jnp.int32, (HALF, HALF), 1)
 
-    def put(block, row, column):
-        h, l = split(block)
-        here = (slice(row, row + block.shape[0]), slice(column, column + block.shape[1]))
-        high[here] = h
-        low[here] = l
+    def put(f, block, row, column):
+        here = (f, slice(row, row + block.shape[0]), slice(column, column + block.shape[1]))
+        high[here], low[here] = split(block)
 
     for q in range(4):
-        base, edge = q * PACKED, q * PIECE
+        f, edge = q // 2, q % 2 * PIECE
+        base = q * NEAR
         top = packed[base : base + HALF, :]
         bottom = packed[base + HALF : base + HALF + HALF // 2, :]
         bottom = jnp.concatenate([bottom[:, :HALF], bottom[:, HALF:]], 0)
         for block in (top[:, :HALF], bottom):
             trace += jnp.sum(jnp.where(rows == columns, block, 0.0), keepdims=True)
-        put(top, edge, edge)
-        put(top[:, HALF:].T, edge + HALF, edge)
-        put(bottom, edge + HALF, edge + HALF)
-        for k in range(1, 4):
-            other = q ^ k
-            if q > other:
-                continue
-            row = PACKED + (k - 4) * HALF
-            for first, owner in ((0, q), (HALF, other)):
-                block = packed[owner * PACKED + row : owner * PACKED + row + HALF, :]
-                put(block, edge + first, other * PIECE)
-                put(block.T, other * PIECE, edge + first)
+        put(f, top, edge, edge)
+        put(f, top[:, HALF:].T, edge + HALF, edge)
+        put(f, bottom, edge + HALF, edge + HALF)
+        block = packed[base + NEAR - HALF : base + NEAR, :]
+        first = q % 2 * HALF
+        put(f, block, first, PIECE)
+        put(f, block.T, PIECE, first)
     inv = 1.0 / (jnp.sqrt(trace) + 1e-07)
-    share = owns[0].shape[1]
-    contract = ((1,), (0,))
-
-    def mine(which):
-        return pl.ds(pl.multiple_of(which * share, share), share)
-
+    inv_out[...] = jnp.broadcast_to(inv, inv_out.shape)
     unit = jnp.concatenate([own[...] for own in owns], 0) * inv
     far = jnp.concatenate([across[...] for across in acrosses], 0) * inv
-    first = dot3(split(unit), (high[mine(half), :], low[mine(half), :]), contract)
-    first += dot3(split(far), (high[mine(1 - half), :], low[mine(1 - half), :]), contract)
-    first = first * (inv * inv)
-    gram[...] = first
-    second = dot3(split(first), (high[:, mine(half)], low[:, mine(half)]), contract)
-    second = second * (inv * inv)
-    result = 3.4445 * unit + (-4.775 * gram[:, mine(half)] + 2.0315 * second)
-    out[...] = (scale * result).astype(out.dtype)
-
-
-def update(at, pieces, places, owns, acrosses, scale):
+    own_part[...] = dot_rows(unit, high[half], low[half])
+    far_part[...] = dot_rows(far, high[1 - half], low[1 - half])
+
+
+def finish_kernel(scale, places, count, at, *refs):
+    pieces, refs = refs[: len(places)], refs[len(places) :]
+    owns, acrosses, refs = refs[:count], refs[count : 2 * count], refs[2 * count :]
+    near_high, near_low, inv_in, own_part, far_part, out, packed, high, low = refs
+    half = at[3]
+    unpack(at, pieces, places, packed, CROSS)
+    for a in range(2):
+        for b in range(2, 4):
+            row = ((a ^ b) - 2) * HALF
+            for first, owner in ((0, a), (HALF, b)):
+                base = owner * CROSS + row
+                here = (
+                    slice(a * PIECE + first, a * PIECE + first + HALF),
+                    slice((b - 2) * PIECE, (b - 1) * PIECE),
+                )
+                high[here], low[here] = split(packed[base : base + HALF, :])
+    inv = inv_in[0:1, 0:1]
+    unit = jnp.concatenate([own[...] for own in owns], 0) * inv
+    far = jnp.concatenate([across[...] for across in acrosses], 0) * inv
+
+    def last(second_half):
+        block = (high[...], low[...])
+        first = own_part[...] + dot_rows(far, *block, flipped=not second_half)
+        other = far_part[...] + dot_rows(unit, *block, flipped=second_half)
+        first, other = first * (inv * inv), other * (inv * inv)
+        second = dot_rows(first, near_high[half], near_low[half])
+        second += dot_rows(other, *block, flipped=not second_half)
+        second = second * (inv * inv)
+        result = 3.4445 * unit + (-4.775 * first + 2.0315 * second)
+        out[...] = (scale * result).astype(out.dtype)
+
+    pl.when(half == 0)(lambda: last(False))
+    pl.when(half == 1)(lambda: last(True))
+
+
+def update(at, near, cross, owns, acrosses, scale):
     rows = sum(own.shape[0] for own in owns)
-    share = owns[0].shape[1]
-    width = 2 * share
+    share, count = owns[0].shape[1], len(owns)
+    pieces, places = zip(*near)
+    square = jax.ShapeDtypeStruct((2, share, share), BF16)
+    part = jax.ShapeDtypeStruct((rows, share), F32)
+    started = pl.pallas_call(
+        functools.partial(start_kernel, places, count),
+        in_specs=[SCALARS] + [WHOLE] * (len(pieces) + 2 * count),
+        out_specs=[WHOLE] * 5,
+        out_shape=[square, square, jax.ShapeDtypeStruct((8, 128), F32), part, part],
+        scratch_shapes=[pltpu.VMEM((4 * NEAR, PIECE), F32)],
+        compiler_params=params(),
+        name="update_start",
+    )(at, *pieces, *owns, *acrosses)
+    pieces, places = zip(*cross)
     return pl.pallas_call(
-        functools.partial(update_kernel, scale, places, len(owns)),
-        in_specs=[SCALARS] + [WHOLE] * (len(pieces) + 2 * len(owns)),
+        functools.partial(finish_kernel, scale, places, count),
+        in_specs=[SCALARS] + [WHOLE] * (len(pieces) + 2 * count + 5),
         out_specs=WHOLE,
         out_shape=jax.ShapeDtypeStruct((rows, share), BF16),
-        scratch_shapes=[
-            pltpu.VMEM((4 * PACKED, PIECE), F32),
-            pltpu.VMEM((rows, width), F32),
-            pltpu.VMEM((width, width), BF16),
-            pltpu.VMEM((width, width), BF16),
-        ],
+        scratch_shapes=[pltpu.VMEM((4 * CROSS, PIECE), F32)]
+        + [pltpu.VMEM((share, share), BF16)] * 2,
         compiler_params=params(),
-        name="update",
-    )(at, *pieces, *owns, *acrosses)
+        name="update_finish",
+    )(at, *pieces, *owns, *acrosses, *started)
 
 
 AXIS_BITS = {"f": 1, "c": 2, "x": 4, "z1": 8, "z2": 16}
@@ -442,8 +477,8 @@
 
     count = len(owns)
     own, far = gram_part(near_kernel, at, owns, count, NEAR, "gram_near", [])
-    core = flip(far, "c")
-    near_sent = add([own[4:], core[4:]], [])
+    core = [flip(far[4:], "c"), flip(far[:4], "c")]
+    near_sent = add([own[4:], core[0]], [])
     near_x = flip(near_sent, "x")
     cross_own, far = gram_part(
         cross_kernel, at, owns + acrosses, count, CROSS, "gram_cross", [near_sent]
@@ -451,7 +486,7 @@
     cross_core = [flip(far[4:], "c"), flip(far[:4], "c")]
     cross_x = flip(add([cross_own[4:], cross_core[0]], [near_x]), "x")
 
-    near = own[:4] + core[:4] + near_x
+    near = own[:4] + core[1] + near_x
     near_z1 = flip(near[2:], "z1")
     near = near[:2] + near_z1
     near_z2 = flip(near, "z2")
@@ -467,21 +502,16 @@
     near = jnp.concatenate([near, flip(near, "x")])
     cross = jnp.concatenate([cross, cross_other])
     cross = jnp.concatenate([cross, flip(cross, "f")])
-    parts = [near, flip(near, "f"), cross, flip(cross, "x")]
-    parts += [flip(part, "c") for part in parts]
     near_slots = [(z, x, 0, 0) for x in range(2) for z in ORDER]
     cross_slots = [(z, 0, 0, f) for f in range(2) for z in ORDER]
-    slots = [
-        near_slots,
-        [(z, x, c, 1) for z, x, c, _ in near_slots],
-        cross_slots,
-        [(z, 1, c, f) for z, _, c, f in cross_slots],
-    ]
-    slots += [[(z, x, 1, f) for z, x, _, f in group] for group in slots]
-    firsts = [0, 0, NEAR, NEAR] * 2
-    places = list(zip(firsts, slots))
+    near = [(near, near_slots), (flip(near, "f"), [(z, x, 0, 1) for z, x, _, _ in near_slots])]
+    cross = [(cross, cross_slots), (flip(cross, "x"), [(z, 1, 0, f) for z, _, _, f in cross_slots])]
+    for group in (near, cross):
+        group += [
+            (flip(part, "c"), [(z, x, 1, f) for z, x, _, f in slots]) for part, slots in group
+        ]
     scale = float(0.25 * np.sqrt(np.float32(features * 2 * share)))
-    return update(at, parts, places, owns, acrosses, scale)
+    return update(at, near, cross, owns, acrosses, scale)
 
 
 def plain_body(partials, scales):

time: 125 us -> 122 us (0.976)
  waiting for transfers between devices: 49.9 us -> 41.1 us
  starting transfers between devices: 60.4 us -> 66.1 us
    ppermute x43 -> x44, waiting for transfers between devices: 49.9 us -> 41.1 us  [flip(): lax.ppermute(value, ('dp', 'fsdp'), [(i, i ^ mask) for i in range(count)])]
    ppermute x43 -> x44, starting transfers between devices: 60.4 us -> 66.1 us  [flip(): lax.ppermute(value, ('dp', 'fsdp'), [(i, i ^ mask) for i in range(count)])]
    pallas_call x1 -> x2, Pallas kernels: 4.66 us -> 5.4 us  [the longest x1 3.42 us: update(): pl.pallas_call(functools.partial(finish_kernel, scale, places, count), in...]
  transfers between devices with their start and end apart: 43 -> 44, of which waited for: 20 -> 18; matrix products, arithmetic and copies ran while one was open for 0% -> 0% of each run, Pallas kernels for 4% -> 5%
where the time goes in v4:
time: 122 us
  starting transfers between devices  66.1 us (54%)
  waiting for transfers between devices  41.1 us (34%)
  Pallas kernels  13.5 us (11%)
    ppermute x44, starting transfers between devices, flip(): lax.ppermute(value, ('dp', 'fsdp'), [(i, i ^ mask) for i in range(count)])  66.1 us
    ppermute x44, waiting for transfers between devices, flip(): lax.ppermute(value, ('dp', 'fsdp'), [(i, i ^ mask) for i in range(count)])  41.1 us
    pallas_call x1, Pallas kernels, update(): pl.pallas_call(functools.partial(finish_kernel, scale, places, count), in...  3.42 us
    pallas_call x4, Pallas kernels, dequant(): pl.pallas_call(kernel, in_specs=[SCALARS] + [WHOLE] * 7 + [ANYWHERE] * (l...  2.97 us
    pallas_call x1, Pallas kernels, pack(): pl.pallas_call(functools.partial(pack_kernel, own_rows, spans), in_specs=...  2.47 us
  transfers between devices with their start and end apart: 44, of which 18 were waited for; matrix products, arithmetic and copies ran while one was open for 0% of the time, Pallas kernels for 5%

profile of v4, /device:TPU:1, one launch (start us, length us, event | category | flops | bytes accessed | tf_op | source)
XLA Modules:
  0.0 122.2 jit_solution(10826733656521987277)
XLA Ops:
  0.9 2.5 %pack_rows.1 = (bf16[960,512]{1,0:T(8,128)(2,1)S(1)}, bf16[1008,512]{1,0:T(8,128)(2,1)S(1)}, bf16[240,512]{1,0:T(8,128)(2,1)S(1)}, bf16[240,512]{1,0:T(8,128)(2,...) custom-call(s32[4]{0:T(128)S(1)} %pad_add_fusion.at.refs_0_, ...), custom_call_target="tpu_custom_call" | custom-call | tf_op jit(solution)/shard_map/pack_rows/pallas_call | solution.py:120
  3.5 2.7 %collective-permute-start.1 = (bf16[240,512]{1,0:T(8,128)(2,1)S(1)}, bf16[240,512]{1,0:T(8,128)(2,1)S(1)}, u32[]{:S(2)}, u32[]{:S(2)}) collective-permute-start(bf16[240,512]{1,0:T(8,128)(2,1)S(1)} %get-tuple-element.43), channel_id=1, source_target_pairs={{0,4},{1,5},{2,6},{3,7},{4,0},{5,1},{6,2},{7,3},{8,12},{9,13},{10,... | collective-permute-start | bytes 737288 | tf_op jit(solution)/shard_map/ppermute | solution.py:404
  8.2 4.2 %collective-permute-done.1.refs_4_.refs_6_ = bf16[240,512]{1,0:T(8,128)(2,1)S(1)} collective-permute-done((bf16[240,512]{1,0:T(8,128)(2,1)S(1)}, bf16[240,512]{1,0:T(8,128)(2,1)S(1)}, u32[]{:S(2)}, u32[]{:S(2)}) %collective-permute-start.1) | collective-permute-done | bytes 245792 | tf_op jit(solution)/shard_map/ppermute | solution.py:404
  12.4 5.5 %collective-permute-done.2.refs_5_.refs_7_ = bf16[240,512]{1,0:T(8,128)(2,1)S(1)} collective-permute-done((bf16[240,512]{1,0:T(8,128)(2,1)S(1)}, bf16[240,512]{1,0:T(8,128)(2,1)S(1)}, u32[]{:S(2)}, u32[]{:S(2)}) %collective-permute-start.2) | collective-permute-done | bytes 245792 | tf_op jit(solution)/shard_map/ppermute | solution.py:404
  23.5 2.2 %collective-permute-start.12 = (bf16[256,512]{1,0:T(8,128)(2,1)S(1)}, bf16[256,512]{1,0:T(8,128)(2,1)S(1)}, u32[]{:S(2)}, u32[]{:S(2)}) collective-permute-start(bf16[256,512]{1,0:T(8,128)(2,1)S(1)} %get-tuple-element.58), channel_id=1, source_target_pairs={{0,6},{1,7},{2,4},{3,5},{4,2},{5,3},{6,0},{7,1},{8,14},{9,15},{10,... | collective-permute-start | bytes 786440 | tf_op jit(solution)/shard_map/ppermute | solution.py:404
  25.7 2.4 %collective-permute-start.5 = (f32[48,512]{1,0:T(8,128)S(1)}, f32[48,512]{1,0:T(8,128)S(1)}, u32[]{:S(2)}, u32[]{:S(2)}) collective-permute-start(f32[48,512]{1,0:T(8,128)S(1)} %add_rows.13.refs_8_), channel_id=1, source_target_pairs={{0,16},{1,17},{2,18},{3,19},{4,20},{5,21},{6,22},{7,23},{8,24},{9,... | collective-permute-start | bytes 294920 | tf_op jit(solution)/shard_map/ppermute | solution.py:404
  28.2 4.1 %collective-permute-done.7.refs_7_ = bf16[320,512]{1,0:T(8,128)(2,1)S(1)} collective-permute-done((bf16[320,512]{1,0:T(8,128)(2,1)S(1)}, bf16[320,512]{1,0:T(8,128)(2,1)S(1)}, u32[]{:S(2)}, u32[]{:S(2)}) %collective-permute-start.7) | collective-permute-done | bytes 327712 | tf_op jit(solution)/shard_map/ppermute | solution.py:404
  36.4 2.6 %collective-permute-done.9.refs_1_ = f32[80,512]{1,0:T(8,128)S(1)} collective-permute-done((f32[80,512]{1,0:T(8,128)S(1)}, f32[80,512]{1,0:T(8,128)S(1)}, u32[]{:S(2)}, u32[]{:S(2)}) %collective-permute-start.9) | collective-permute-done | bytes 163872 | tf_op jit(solution)/shard_map/ppermute | solution.py:404
  39.0 2.2 %collective-permute-start.15 = (bf16[192,512]{1,0:T(8,128)(2,1)S(1)}, bf16[192,512]{1,0:T(8,128)(2,1)S(1)}, u32[]{:S(2)}, u32[]{:S(2)}) collective-permute-start(bf16[192,512]{1,0:T(8,128)(2,1)S(1)} %get-tuple-element.62), channel_id=1, source_target_pairs={{0,6},{1,7},{2,4},{3,5},{4,2},{5,3},{6,0},{7,1},{8,14},{9,15},{10,... | collective-permute-start | bytes 589832 | tf_op jit(solution)/shard_map/ppermute | solution.py:404
  44.5 2.2 %collective-permute-start.10 = (f32[80,512]{1,0:T(8,128)S(1)}, f32[80,512]{1,0:T(8,128)S(1)}, u32[]{:S(2)}, u32[]{:S(2)}) collective-permute-start(f32[80,512]{1,0:T(8,128)S(1)} %add_rows.15.refs_8_), channel_id=1, source_target_pairs={{0,16},{1,17},{2,18},{3,19},{4,20},{5,21},{6,22},{7,23},{8,24},{9,... | collective-permute-start | bytes 491528 | tf_op jit(solution)/shard_map/ppermute | solution.py:404
  49.1 2.3 %collective-permute-done.15.refs_7_ = bf16[192,512]{1,0:T(8,128)(2,1)S(1)} collective-permute-done((bf16[192,512]{1,0:T(8,128)(2,1)S(1)}, bf16[192,512]{1,0:T(8,128)(2,1)S(1)}, u32[]{:S(2)}, u32[]{:S(2)}) %collective-permute-start.15) | collective-permute-done | bytes 196640 | tf_op jit(solution)/shard_map/ppermute | solution.py:404
  52.1 2.9 %collective-permute-start.19 = (f32[48,512]{1,0:T(8,128)S(1)}, f32[48,512]{1,0:T(8,128)S(1)}, u32[]{:S(2)}, u32[]{:S(2)}) collective-permute-start(f32[48,512]{1,0:T(8,128)S(1)} %get-tuple-element.65), channel_id=1, source_target_pairs={{0,16},{1,17},{2,18},{3,19},{4,20},{5,21},{6,22},{7,23},{8,24},{9,... | collective-permute-start | bytes 294920 | tf_op jit(solution)/shard_map/ppermute | solution.py:404
  55.0 3.5 %collective-permute-done.13.refs_1_ = f32[64,512]{1,0:T(8,128)S(1)} collective-permute-done((f32[64,512]{1,0:T(8,128)S(1)}, f32[64,512]{1,0:T(8,128)S(1)}, u32[]{:S(2)}, u32[]{:S(2)}) %collective-permute-start.13) | collective-permute-done | bytes 131104 | tf_op jit(solution)/shard_map/ppermute | solution.py:404
  61.4 9.0 %collective-permute-done.18.refs_1_ = f32[64,512]{1,0:T(8,128)S(1)} collective-permute-done((f32[64,512]{1,0:T(8,128)S(1)}, f32[64,512]{1,0:T(8,128)S(1)}, u32[]{:S(2)}, u32[]{:S(2)}) %collective-permute-start.18) | collective-permute-done | bytes 131104 | tf_op jit(solution)/shard_map/ppermute | solution.py:404
  72.3 2.0 %collective-permute-start.24 = (f32[4,40,256]{2,1,0:T(8,128)S(1)}, f32[4,40,256]{2,1,0:T(8,128)S(1)}, u32[]{:S(2)}, u32[]{:S(2)}) collective-permute-start(f32[4,40,256]{2,1,0:T(8,128)S(1)} %get-tuple-element.78), channel_id=1, source_target_pairs={{0,2},{1,3},{2,0},{3,1},{4,6},{5,7},{6,4},{7,5},{8,10},{9,11},{10,... | collective-permute-start | bytes 491528 | tf_op jit(solution)/shard_map/ppermute | solution.py:404
  77.9 3.6 %collective-permute-start.26 = (f32[4,32,256]{2,1,0:T(8,128)S(1)}, f32[4,32,256]{2,1,0:T(8,128)S(1)}, u32[]{:S(2)}, u32[]{:S(2)}) collective-permute-start(f32[4,32,256]{2,1,0:T(8,128)S(1)} %get-tuple-element.79), channel_id=1, source_target_pairs={{0,2},{1,3},{2,0},{3,1},{4,6},{5,7},{6,4},{7,5},{8,10},{9,11},{10,... | collective-permute-start | bytes 393224 | tf_op jit(solution)/shard_map/ppermute | solution.py:404
  91.4 2.6 %collective-permute-start.33 = (f32[2,32,256]{2,1,0:T(8,128)S(1)}, f32[2,32,256]{2,1,0:T(8,128)S(1)}, u32[]{:S(2)}, u32[]{:S(2)}) collective-permute-start(f32[2,32,256]{2,1,0:T(8,128)S(1)} %add_rows.23.refs_0_), channel_id=1, source_target_pairs={{0,16},{1,17},{2,18},{3,19},{4,20},{5,21},{6,22},{7,23},{8,24},{9,... | collective-permute-start | bytes 196616 | tf_op jit(solution)/shard_map/ppermute | solution.py:404
  99.2 2.5 %collective-permute-start.36 = (f32[4,32,256]{2,1,0:T(8,128)S(1)}, f32[4,32,256]{2,1,0:T(8,128)S(1)}, u32[]{:S(2)}, u32[]{:S(2)}) collective-permute-start(f32[4,32,256]{2,1,0:T(8,128)S(1)} %pad_maximum_fusion.4), channel_id=1, source_target_pairs={{0,1},{1,0},{2,3},{3,2},{4,5},{5,4},{6,7},{7,6},{8,9},{9,8},{10,11... | collective-permute-start | bytes 393224 | tf_op jit(solution)/shard_map/ppermute | solution.py:404
  101.7 2.5 %collective-permute-start.41 = (f32[8,40,256]{2,1,0:T(8,128)S(1)}, f32[8,40,256]{2,1,0:T(8,128)S(1)}, u32[]{:S(2)}, u32[]{:S(2)}) collective-permute-start(f32[8,40,256]{2,1,0:T(8,128)S(1)} %pad_maximum_fusion.refs_0_), channel_id=1, source_target_pairs={{0,1},{1,0},{2,3},{3,2},{4,5},{5,4},{6,7},{7,6},{8,9},{9,8},{10,11... | collective-permute-start | bytes 983048 | tf_op jit(solution)/shard_map/ppermute | solution.py:404
  105.6 6.7 %collective-permute-start.42 = (f32[8,40,256]{2,1,0:T(8,128)S(1)}, f32[8,40,256]{2,1,0:T(8,128)S(1)}, u32[]{:S(2)}, u32[]{:S(2)}) collective-permute-start(f32[8,40,256]{2,1,0:T(8,128)S(1)} %pad_maximum_fusion.refs_0_), channel_id=1, source_target_pairs={{0,2},{1,3},{2,0},{3,1},{4,6},{5,7},{6,4},{7,5},{8,10},{9,11},{10,... | collective-permute-start | bytes 983048 | tf_op jit(solution)/shard_map/ppermute | solution.py:404
  112.3 2.0 %collective-permute-start.43 = (f32[8,40,256]{2,1,0:T(8,128)S(1)}, f32[8,40,256]{2,1,0:T(8,128)S(1)}, u32[]{:S(2)}, u32[]{:S(2)}) collective-permute-start(f32[8,40,256]{2,1,0:T(8,128)S(1)} %collective-permute-done.41.refs_1_), channel_id=1, source_target_pairs={{0,2},{1,3},{2,0},{3,1},{4,6},{5,7},{6,4},{7,5},{8,10},{9,11},{10,... | collective-permute-start | bytes 983048 | tf_op jit(solution)/shard_map/ppermute | solution.py:404
  114.3 2.5 %collective-permute-start.39 = (f32[8,32,256]{2,1,0:T(8,128)S(1)}, f32[8,32,256]{2,1,0:T(8,128)S(1)}, u32[]{:S(2)}, u32[]{:S(2)}) collective-permute-start(f32[8,32,256]{2,1,0:T(8,128)S(1)} %collective-permute-done.37.refs_1_), channel_id=1, source_target_pairs={{0,2},{1,3},{2,0},{3,1},{4,6},{5,7},{6,4},{7,5},{8,10},{9,11},{10,... | collective-permute-start | bytes 786440 | tf_op jit(solution)/shard_map/ppermute | solution.py:404
  116.8 2.0 %update_start.1 = (bf16[2,512,512]{2,1,0:T(8,128)(2,1)S(1)}, bf16[2,512,512]{2,1,0:T(8,128)(2,1)S(1)}, f32[8,128]{1,0:T(8,128)S(1)}, f32[240,512]{1,0:T(8,128)S(1)}, f32[240,512]{1,0:T(8,128)S(1)}) custom-call(s32[4]{0:T(128)S(1)} %pad_add_fusion.at.refs_0_, f32[8,40,256]{2,1,0:T(8,128)S(1)} %pad_maximum_fusion.refs_0_, ...), custom_call_target="tpu_custom_call" | custom-call | tf_op jit(solution)/shard_map/update_start/pallas_call | solution.py:376
  118.8 3.4 %update_finish.1 = bf16[240,512]{1,0:T(8,128)(2,1)} custom-call(s32[4]{0:T(128)S(1)} %pad_add_fusion.at.refs_0_, f32[8,32,256]{2,1,0:T(8,128)S(1)} %pad_maximum_fusion.1.refs_0_, f32[8,32,256]{2,1,0:T(8,128)S(1)} %collective-permute-done.37.refs_1_, f32[8,32,256]{2,1,0:T(8,128)S(1)} %collective-permute-done.38.refs_2_, ...), custom_call_target="tpu_custom_call" | custom-call | tf_op jit(solution)/shard_map/update_finish/pallas_call | solution.py:386
  (110 shorter events, 43.8 us)
Async XLA Ops:
  3.4 14.5 %collective-permute-start = (bf16[1008,512]{1,0:T(8,128)(2,1)S(1)}, bf16[1008,512]{1,0:T(8,128)(2,1)S(1)}, u32[]{:S(2)}, u32[]{:S(2)}) collective-permute-start(bf16[1008,512]{1,0:T(8,128)(2,1)S(1)} %get-tuple-element.42), channel_id=1, source_target_pairs={{0,2},{1,3},{2,0},{3,1},{4,6},{5,7},{6,4},{7,5},{8,10},{9,11},{10,... | collective-permute-start | bytes 3096584 | tf_op jit(solution)/shard_map/ppermute | solution.py:404
  3.5 8.9 %collective-permute-start.1 = (bf16[240,512]{1,0:T(8,128)(2,1)S(1)}, bf16[240,512]{1,0:T(8,128)(2,1)S(1)}, u32[]{:S(2)}, u32[]{:S(2)}) collective-permute-start(bf16[240,512]{1,0:T(8,128)(2,1)S(1)} %get-tuple-element.43), channel_id=1, source_target_pairs={{0,4},{1,5},{2,6},{3,7},{4,0},{5,1},{6,2},{7,3},{8,12},{9,13},{10,... | collective-permute-start | bytes 737288 | tf_op jit(solution)/shard_map/ppermute | solution.py:404
  6.2 11.7 %collective-permute-start.2 = (bf16[240,512]{1,0:T(8,128)(2,1)S(1)}, bf16[240,512]{1,0:T(8,128)(2,1)S(1)}, u32[]{:S(2)}, u32[]{:S(2)}) collective-permute-start(bf16[240,512]{1,0:T(8,128)(2,1)S(1)} %get-tuple-element.44), channel_id=1, source_target_pairs={{0,6},{1,7},{2,4},{3,5},{4,2},{5,3},{6,0},{7,1},{8,14},{9,15},{10,... | collective-permute-start | bytes 737288 | tf_op jit(solution)/shard_map/ppermute | solution.py:404
  6.2 21.9 %collective-permute-start.6 = (bf16[320,512]{1,0:T(8,128)(2,1)S(1)}, bf16[320,512]{1,0:T(8,128)(2,1)S(1)}, u32[]{:S(2)}, u32[]{:S(2)}) collective-permute-start(bf16[320,512]{1,0:T(8,128)(2,1)S(1)} %get-tuple-element.50), channel_id=1, source_target_pairs={{0,4},{1,5},{2,6},{3,7},{4,0},{5,1},{6,2},{7,3},{8,12},{9,13},{10,... | collective-permute-start | bytes 983048 | tf_op jit(solution)/shard_map/ppermute | solution.py:404
  7.9 24.4 %collective-permute-start.7 = (bf16[320,512]{1,0:T(8,128)(2,1)S(1)}, bf16[320,512]{1,0:T(8,128)(2,1)S(1)}, u32[]{:S(2)}, u32[]{:S(2)}) collective-permute-start(bf16[320,512]{1,0:T(8,128)(2,1)S(1)} %get-tuple-element.51), channel_id=1, source_target_pairs={{0,6},{1,7},{2,4},{3,5},{4,2},{5,3},{6,0},{7,1},{8,14},{9,15},{10,... | collective-permute-start | bytes 983048 | tf_op jit(solution)/shard_map/ppermute | solution.py:404
  20.5 23.9 %collective-permute-start.11 = (bf16[256,512]{1,0:T(8,128)(2,1)S(1)}, bf16[256,512]{1,0:T(8,128)(2,1)S(1)}, u32[]{:S(2)}, u32[]{:S(2)}) collective-permute-start(bf16[256,512]{1,0:T(8,128)(2,1)S(1)} %get-tuple-element.57), channel_id=1, source_target_pairs={{0,4},{1,5},{2,6},{3,7},{4,0},{5,1},{6,2},{7,3},{8,12},{9,13},{10,... | collective-permute-start | bytes 786440 | tf_op jit(solution)/shard_map/ppermute | solution.py:404
  23.5 23.2 %collective-permute-start.12 = (bf16[256,512]{1,0:T(8,128)(2,1)S(1)}, bf16[256,512]{1,0:T(8,128)(2,1)S(1)}, u32[]{:S(2)}, u32[]{:S(2)}) collective-permute-start(bf16[256,512]{1,0:T(8,128)(2,1)S(1)} %get-tuple-element.58), channel_id=1, source_target_pairs={{0,6},{1,7},{2,4},{3,5},{4,2},{5,3},{6,0},{7,1},{8,14},{9,15},{10,... | collective-permute-start | bytes 786440 | tf_op jit(solution)/shard_map/ppermute | solution.py:404
  25.7 9.0 %collective-permute-start.5 = (f32[48,512]{1,0:T(8,128)S(1)}, f32[48,512]{1,0:T(8,128)S(1)}, u32[]{:S(2)}, u32[]{:S(2)}) collective-permute-start(f32[48,512]{1,0:T(8,128)S(1)} %add_rows.13.refs_8_), channel_id=1, source_target_pairs={{0,16},{1,17},{2,18},{3,19},{4,20},{5,21},{6,22},{7,23},{8,24},{9,... | collective-permute-start | bytes 294920 | tf_op jit(solution)/shard_map/ppermute | solution.py:404
  34.6 7.9 %collective-permute-start.8 = (f32[80,512]{1,0:T(8,128)S(1)}, f32[80,512]{1,0:T(8,128)S(1)}, u32[]{:S(2)}, u32[]{:S(2)}) collective-permute-start(f32[80,512]{1,0:T(8,128)S(1)} %get-tuple-element.55), channel_id=1, source_target_pairs={{0,8},{1,9},{2,10},{3,11},{4,12},{5,13},{6,14},{7,15},{8,0},{9,1},... | collective-permute-start | bytes 491528 | tf_op jit(solution)/shard_map/ppermute | solution.py:404
  34.7 14.3 %collective-permute-start.14 = (bf16[192,512]{1,0:T(8,128)(2,1)S(1)}, bf16[192,512]{1,0:T(8,128)(2,1)S(1)}, u32[]{:S(2)}, u32[]{:S(2)}) collective-permute-start(bf16[192,512]{1,0:T(8,128)(2,1)S(1)} %get-tuple-element.61), channel_id=1, source_target_pairs={{0,4},{1,5},{2,6},{3,7},{4,0},{5,1},{6,2},{7,3},{8,12},{9,13},{10,... | collective-permute-start | bytes 589832 | tf_op jit(solution)/shard_map/ppermute | solution.py:404
  39.0 12.4 %collective-permute-start.15 = (bf16[192,512]{1,0:T(8,128)(2,1)S(1)}, bf16[192,512]{1,0:T(8,128)(2,1)S(1)}, u32[]{:S(2)}, u32[]{:S(2)}) collective-permute-start(bf16[192,512]{1,0:T(8,128)(2,1)S(1)} %get-tuple-element.62), channel_id=1, source_target_pairs={{0,6},{1,7},{2,4},{3,5},{4,2},{5,3},{6,0},{7,1},{8,14},{9,15},{10,... | collective-permute-start | bytes 589832 | tf_op jit(solution)/shard_map/ppermute | solution.py:404
  42.5 16.0 %collective-permute-start.16 = (f32[48,512]{1,0:T(8,128)S(1)}, f32[48,512]{1,0:T(8,128)S(1)}, u32[]{:S(2)}, u32[]{:S(2)}) collective-permute-start(f32[48,512]{1,0:T(8,128)S(1)} %add_rows.14.refs_10_.refs_0_.refs_4_), channel_id=1, source_target_pairs={{0,1},{1,0},{2,3},{3,2},{4,5},{5,4},{6,7},{7,6},{8,9},{9,8},{10,11... | collective-permute-start | bytes 294920 | tf_op jit(solution)/shard_map/ppermute | solution.py:404
  44.5 15.1 %collective-permute-start.10 = (f32[80,512]{1,0:T(8,128)S(1)}, f32[80,512]{1,0:T(8,128)S(1)}, u32[]{:S(2)}, u32[]{:S(2)}) collective-permute-start(f32[80,512]{1,0:T(8,128)S(1)} %add_rows.15.refs_8_), channel_id=1, source_target_pairs={{0,16},{1,17},{2,18},{3,19},{4,20},{5,21},{6,22},{7,23},{8,24},{9,... | collective-permute-start | bytes 491528 | tf_op jit(solution)/shard_map/ppermute | solution.py:404
  47.5 13.8 %collective-permute-start.17 = (f32[64,512]{1,0:T(8,128)S(1)}, f32[64,512]{1,0:T(8,128)S(1)}, u32[]{:S(2)}, u32[]{:S(2)}) collective-permute-start(f32[64,512]{1,0:T(8,128)S(1)} %get-tuple-element.64), channel_id=1, source_target_pairs={{0,8},{1,9},{2,10},{3,11},{4,12},{5,13},{6,14},{7,15},{8,0},{9,1},... | collective-permute-start | bytes 393224 | tf_op jit(solution)/shard_map/ppermute | solution.py:404
  49.0 9.5 %collective-permute-start.13 = (f32[64,512]{1,0:T(8,128)S(1)}, f32[64,512]{1,0:T(8,128)S(1)}, u32[]{:S(2)}, u32[]{:S(2)}) collective-permute-start(f32[64,512]{1,0:T(8,128)S(1)} %get-tuple-element.60), channel_id=1, source_target_pairs={{0,8},{1,9},{2,10},{3,11},{4,12},{5,13},{6,14},{7,15},{8,0},{9,1},... | collective-permute-start | bytes 393224 | tf_op jit(solution)/shard_map/ppermute | solution.py:404
  52.1 18.3 %collective-permute-start.19 = (f32[48,512]{1,0:T(8,128)S(1)}, f32[48,512]{1,0:T(8,128)S(1)}, u32[]{:S(2)}, u32[]{:S(2)}) collective-permute-start(f32[48,512]{1,0:T(8,128)S(1)} %get-tuple-element.65), channel_id=1, source_target_pairs={{0,16},{1,17},{2,18},{3,19},{4,20},{5,21},{6,22},{7,23},{8,24},{9,... | collective-permute-start | bytes 294920 | tf_op jit(solution)/shard_map/ppermute | solution.py:404
  58.5 11.9 %collective-permute-start.20 = (f32[48,512]{1,0:T(8,128)S(1)}, f32[48,512]{1,0:T(8,128)S(1)}, u32[]{:S(2)}, u32[]{:S(2)}) collective-permute-start(f32[48,512]{1,0:T(8,128)S(1)} %get-tuple-element.66), channel_id=1, source_target_pairs={{0,8},{1,9},{2,10},{3,11},{4,12},{5,13},{6,14},{7,15},{8,0},{9,1},... | collective-permute-start | bytes 294920 | tf_op jit(solution)/shard_map/ppermute | solution.py:404
  58.6 11.9 %collective-permute-start.21 = (f32[48,512]{1,0:T(8,128)S(1)}, f32[48,512]{1,0:T(8,128)S(1)}, u32[]{:S(2)}, u32[]{:S(2)}) collective-permute-start(f32[48,512]{1,0:T(8,128)S(1)} %get-tuple-element.67), channel_id=1, source_target_pairs={{0,24},{1,25},{2,26},{3,27},{4,28},{5,29},{6,30},{7,31},{8,16},{9,... | collective-permute-start | bytes 294920 | tf_op jit(solution)/shard_map/ppermute | solution.py:404
  59.6 10.8 %collective-permute-start.18 = (f32[64,512]{1,0:T(8,128)S(1)}, f32[64,512]{1,0:T(8,128)S(1)}, u32[]{:S(2)}, u32[]{:S(2)}) collective-permute-start(f32[64,512]{1,0:T(8,128)S(1)} %add_rows.16.refs_2_), channel_id=1, source_target_pairs={{0,16},{1,17},{2,18},{3,19},{4,20},{5,21},{6,22},{7,23},{8,24},{9,... | collective-permute-start | bytes 393224 | tf_op jit(solution)/shard_map/ppermute | solution.py:404
  61.3 9.1 %collective-permute-start.22 = (f32[80,512]{1,0:T(8,128)S(1)}, f32[80,512]{1,0:T(8,128)S(1)}, u32[]{:S(2)}, u32[]{:S(2)}) collective-permute-start(f32[80,512]{1,0:T(8,128)S(1)} %add_rows.17.refs_1_.refs_5_), channel_id=1, source_target_pairs={{0,1},{1,0},{2,3},{3,2},{4,5},{5,4},{6,7},{7,6},{8,9},{9,8},{10,11... | collective-permute-start | bytes 491528 | tf_op jit(solution)/shard_map/ppermute | solution.py:404
  74.3 7.2 %collective-permute-start.29 = (f32[4,40,256]{2,1,0:T(8,128)S(1)}, f32[4,40,256]{2,1,0:T(8,128)S(1)}, u32[]{:S(2)}, u32[]{:S(2)}) collective-permute-start(f32[4,40,256]{2,1,0:T(8,128)S(1)} %get-tuple-element.77), channel_id=1, source_target_pairs={{0,2},{1,3},{2,0},{3,1},{4,6},{5,7},{6,4},{7,5},{8,10},{9,11},{10,... | collective-permute-start | bytes 491528 | tf_op jit(solution)/shard_map/ppermute | solution.py:404
  101.7 10.6 %collective-permute-start.41 = (f32[8,40,256]{2,1,0:T(8,128)S(1)}, f32[8,40,256]{2,1,0:T(8,128)S(1)}, u32[]{:S(2)}, u32[]{:S(2)}) collective-permute-start(f32[8,40,256]{2,1,0:T(8,128)S(1)} %pad_maximum_fusion.refs_0_), channel_id=1, source_target_pairs={{0,1},{1,0},{2,3},{3,2},{4,5},{5,4},{6,7},{7,6},{8,9},{9,8},{10,11... | collective-permute-start | bytes 983048 | tf_op jit(solution)/shard_map/ppermute | solution.py:404
  104.4 9.9 %collective-permute-start.37 = (f32[8,32,256]{2,1,0:T(8,128)S(1)}, f32[8,32,256]{2,1,0:T(8,128)S(1)}, u32[]{:S(2)}, u32[]{:S(2)}) collective-permute-start(f32[8,32,256]{2,1,0:T(8,128)S(1)} %pad_maximum_fusion.1.refs_0_), channel_id=1, source_target_pairs={{0,4},{1,5},{2,6},{3,7},{4,0},{5,1},{6,2},{7,3},{8,12},{9,13},{10,... | collective-permute-start | bytes 786440 | tf_op jit(solution)/shard_map/ppermute | solution.py:404
  105.6 11.2 %collective-permute-start.42 = (f32[8,40,256]{2,1,0:T(8,128)S(1)}, f32[8,40,256]{2,1,0:T(8,128)S(1)}, u32[]{:S(2)}, u32[]{:S(2)}) collective-permute-start(f32[8,40,256]{2,1,0:T(8,128)S(1)} %pad_maximum_fusion.refs_0_), channel_id=1, source_target_pairs={{0,2},{1,3},{2,0},{3,1},{4,6},{5,7},{6,4},{7,5},{8,10},{9,11},{10,... | collective-permute-start | bytes 983048 | tf_op jit(solution)/shard_map/ppermute | solution.py:404
  (22 other events, 124.2 us)

commit v5 on v4

--- a/solution.py
+++ b/solution.py
@@ -11,18 +11,20 @@
 BLOCK = 128
 GRAIN = 16
 CHUNKS = (3, 5, 4, 3)
-LEAVE = (0, 1, 3)
+LEAVE = (1, 3)
 STEPS = (
-    ("sum", 0), ("halve", 0), ("sum", 1), ("halve", 1), ("finish", 0), ("sum", 2),
-    ("sum", 3), ("halve", 2), ("finish", 1), ("finish", 2), ("finish", 3),
+    ("sum", 0), ("halve", 0), ("sum", 1), ("sum", 2), ("halve", 1), ("finish", 0), ("sum", 3),
+    ("halve", 2), ("halve", 3), ("finish", 1), ("finish", 2), ("finish", 3),
 )
 AFTER = {
     ("sum", 1): (("sent", 0), ("half", 0)),
-    ("sum", 2): (("sent", 1), ("half", 1), ("grad", 0)),
-    ("sum", 3): (("keep", 2),),
+    ("sum", 2): (("near", 1), ("last", 1)),
+    ("halve", 1): (("keep", 2),),
+    ("finish", 0): (("keep", 2),),
+    ("sum", 3): (("sent", 1), ("grad", 0)),
     ("halve", 2): (("keep", 3),),
-    ("finish", 1): (("sent", 2), ("across", 0)),
-    ("finish", 3): (("across", 1), ("grad", 2)),
+    ("finish", 1): (("sent", 2), ("sent", 3)),
+    ("finish", 3): (("across", 1),),
 }
 ORDER = (0, 2, 1, 3)
 PIECE = 256
@@ -74,12 +76,12 @@
     "pair": ((0, 1), (2, 3)),
     "direct": ((0,), (1,), (2,), (3,)),
 }
-ROUTES = ("halves", "halves", "halves", "direct")
+ROUTES = ("halves", "halves", "halves", "halves")
 SPAN = 4
 TAIL = 3 * SLOTS * SPAN
 
 
-def pack_kernel(own_rows, spans, at, values, scales, own, *refs):
+def pack_kernel(own_rows, spans, at, values, scales, own, table, *refs):
     outs, gathered = refs[:-1], refs[-1]
     blocks = scales.shape[0]
 
@@ -88,12 +90,15 @@
             base = pl.multiple_of(slot_row(at, side, slot, own_rows) + start, GRAIN)
             out[slot * rows : (slot + 1) * rows, :] = values[pl.ds(base, rows), :]
 
-    def tail(side, out):
+    def gather(side, out):
         for slot in range(SLOTS):
             first = slot_row(at, side, slot, own_rows) // BLOCK
             for n in range(SPAN):
                 row = jnp.minimum(first + n, blocks - 1)
-                gathered[slot * SPAN + n : slot * SPAN + n + 1, :] = scales[row]
+                out[slot * SPAN + n : slot * SPAN + n + 1, :] = scales[row]
+
+    def tail(side, out):
+        gather(side, gathered)
         left = gathered[...]
         for n in range(3):
             part = left.astype(BF16)
@@ -101,6 +106,7 @@
             out[row : row + SLOTS * SPAN, :] = part
             left = left - part.astype(F32)
 
+    gather(0, table)
     copy(0, 0, own_rows, own)
     copy(1, 0, own_rows, outs[0])
     tail(1, outs[0])
@@ -120,8 +126,10 @@
     return pl.pallas_call(
         functools.partial(pack_kernel, own_rows, spans),
         in_specs=[SCALARS, WHOLE, WHOLE],
-        out_specs=[WHOLE] * len(lengths),
-        out_shape=[jax.ShapeDtypeStruct((rows, width), BF16) for rows in lengths],
+        out_specs=[WHOLE] * (1 + len(lengths)),
+        out_shape=[jax.ShapeDtypeStruct((lengths[0], width), BF16)]
+        + [jax.ShapeDtypeStruct((SLOTS * SPAN, width), F32)]
+        + [jax.ShapeDtypeStruct((rows, width), BF16) for rows in lengths[1:]],
         scratch_shapes=[pltpu.VMEM((SLOTS * SPAN, width), F32)],
         compiler_params=params(),
         name="pack_rows",
@@ -147,7 +155,7 @@
             row = slot * own_rows + start + g * GRAIN
             there = slice(row, row + GRAIN)
             row = slot * rows + g * GRAIN
-            total = own[there, :].astype(F32) * scales[block]
+            total = own[there, :].astype(F32) * scales[pl.ds(span, 1), :]
             total += core_raw[there, :].astype(F32) * packed[pl.ds(span, 1), :]
             for n, raw in enumerate(raws):
                 part = raw[row : row + GRAIN, :].astype(F32)
@@ -420,7 +428,7 @@
         spans.append((start, size * unit))
         start += size * unit
 
-    own, core_raw, *outs = pack(values, scales, at, own_rows, spans)
+    own, table, core_raw, *outs = pack(values, scales, at, own_rows, spans)
     core_raw = flip(core_raw, "c")
 
     def cross(pair):
@@ -439,7 +447,7 @@
         start, rows = spans[n]
         carry = outs[n + 2] if n + 2 < len(spans) else []
         (keep, *go), carry = dequant(
-            at, scales, own, core_raw, heads, raws[n], own_rows, start, rows,
+            at, table, own, core_raw, heads, raws[n], own_rows, start, rows,
             GROUPS[ROUTES[n]], there("sum", n), carry,
         )
         if carry:
@@ -449,6 +457,7 @@
             made["got", n] = [flip(part, *names) for part, names in zip(go, ZEDS)]
         elif ROUTES[n] == "halves":
             made["got", n] = [flip(part, "z1") for part in go]
+            made["near", n], made["last", n] = made["got", n]
         else:
             made["got", n] = flip(go[0], "z1")
 

time: 122 us -> 121 us (level)
  starting transfers between devices: 66.1 us -> 55.4 us
  waiting for transfers between devices: 41.1 us -> 50.6 us
    ppermute x44 -> x43, starting transfers between devices: 66.1 us -> 55.4 us  [flip(): lax.ppermute(value, ('dp', 'fsdp'), [(i, i ^ mask) for i in range(count)])]
    ppermute x44 -> x43, waiting for transfers between devices: 41.1 us -> 50.6 us  [flip(): lax.ppermute(value, ('dp', 'fsdp'), [(i, i ^ mask) for i in range(count)])]
  transfers between devices with their start and end apart: 44 -> 43, of which waited for: 18 -> 21; matrix products, arithmetic and copies ran while one was open for 0% -> 0% of each run, Pallas kernels for 5% -> 5%
where the time goes in v5:
time: 121 us
  starting transfers between devices  55.4 us (46%)
  waiting for transfers between devices  50.6 us (42%)
  Pallas kernels  13.6 us (11%)
    ppermute x43, starting transfers between devices, flip(): lax.ppermute(value, ('dp', 'fsdp'), [(i, i ^ mask) for i in range(count)])  55.4 us
    ppermute x43, waiting for transfers between devices, flip(): lax.ppermute(value, ('dp', 'fsdp'), [(i, i ^ mask) for i in range(count)])  50.6 us
    pallas_call x1, Pallas kernels, update(): pl.pallas_call(functools.partial(finish_kernel, scale, places, count), in...  3.43 us
    pallas_call x4, Pallas kernels, dequant(): pl.pallas_call(kernel, in_specs=[SCALARS] + [WHOLE] * 7 + [ANYWHERE] * (l...  2.98 us
    pallas_call x1, Pallas kernels, pack(): pl.pallas_call(functools.partial(pack_kernel, own_rows, spans), in_specs=...  2.51 us
    pallas_call x2, Pallas kernels, gram_part(): pl.pallas_call(functools.partial(kernel, count), in_specs=[SCALARS] + [WH...  2.44 us
  transfers between devices with their start and end apart: 43, of which 21 were waited for; matrix products, arithmetic and copies ran while one was open for 0% of the time, Pallas kernels for 5%

profile of v5, /device:TPU:1, one launch (start us, length us, event | category | flops | bytes accessed | tf_op | source)
XLA Modules:
  0.0 121.2 jit_solution(10691944297413510993)
XLA Ops:
  0.9 2.5 %pack_rows.1 = (bf16[960,512]{1,0:T(8,128)(2,1)S(1)}, f32[16,512]{1,0:T(8,128)S(1)}, bf16[1008,512]{1,0:T(8,128)(2,1)S(1)}, bf16[240,512]{1,0:T(8,128)(2,1)S(1)}...) custom-call(s32[4]{0:T(128)S(1)} %pad_add_fusion.at.refs_0_, ...), custom_call_target="tpu_custom_call" | custom-call | tf_op jit(solution)/shard_map/pack_rows/pallas_call | solution.py:126
  3.5 2.7 %collective-permute-start.1 = (bf16[240,512]{1,0:T(8,128)(2,1)S(1)}, bf16[240,512]{1,0:T(8,128)(2,1)S(1)}, u32[]{:S(2)}, u32[]{:S(2)}) collective-permute-start(bf16[240,512]{1,0:T(8,128)(2,1)S(1)} %get-tuple-element.44), channel_id=1, source_target_pairs={{0,4},{1,5},{2,6},{3,7},{4,0},{5,1},{6,2},{7,3},{8,12},{9,13},{10,... | collective-permute-start | bytes 737288 | tf_op jit(solution)/shard_map/ppermute | solution.py:412
  8.3 4.2 %collective-permute-done.1.refs_4_.refs_6_ = bf16[240,512]{1,0:T(8,128)(2,1)S(1)} collective-permute-done((bf16[240,512]{1,0:T(8,128)(2,1)S(1)}, bf16[240,512]{1,0:T(8,128)(2,1)S(1)}, u32[]{:S(2)}, u32[]{:S(2)}) %collective-permute-start.1) | collective-permute-done | bytes 245792 | tf_op jit(solution)/shard_map/ppermute | solution.py:412
  12.5 5.5 %collective-permute-done.2.refs_5_.refs_7_ = bf16[240,512]{1,0:T(8,128)(2,1)S(1)} collective-permute-done((bf16[240,512]{1,0:T(8,128)(2,1)S(1)}, bf16[240,512]{1,0:T(8,128)(2,1)S(1)}, u32[]{:S(2)}, u32[]{:S(2)}) %collective-permute-start.2) | collective-permute-done | bytes 245792 | tf_op jit(solution)/shard_map/ppermute | solution.py:412
  21.9 3.7 %collective-permute-done.4.refs_1_ = f32[48,512]{1,0:T(8,128)S(1)} collective-permute-done((f32[48,512]{1,0:T(8,128)S(1)}, f32[48,512]{1,0:T(8,128)S(1)}, u32[]{:S(2)}, u32[]{:S(2)}) %collective-permute-start.4) | collective-permute-done | bytes 98336 | tf_op jit(solution)/shard_map/ppermute | solution.py:412
  25.6 2.0 %collective-permute-start.7 = (bf16[256,512]{1,0:T(8,128)(2,1)S(1)}, bf16[256,512]{1,0:T(8,128)(2,1)S(1)}, u32[]{:S(2)}, u32[]{:S(2)}) collective-permute-start(bf16[256,512]{1,0:T(8,128)(2,1)S(1)} %get-tuple-element.52), channel_id=1, source_target_pairs={{0,6},{1,7},{2,4},{3,5},{4,2},{5,3},{6,0},{7,1},{8,14},{9,15},{10,... | collective-permute-start | bytes 786440 | tf_op jit(solution)/shard_map/ppermute | solution.py:412
  27.6 2.4 %collective-permute-start.5 = (f32[48,512]{1,0:T(8,128)S(1)}, f32[48,512]{1,0:T(8,128)S(1)}, u32[]{:S(2)}, u32[]{:S(2)}) collective-permute-start(f32[48,512]{1,0:T(8,128)S(1)} %add_rows.14.refs_8_), channel_id=1, source_target_pairs={{0,16},{1,17},{2,18},{3,19},{4,20},{5,21},{6,22},{7,23},{8,24},{9,... | collective-permute-start | bytes 294920 | tf_op jit(solution)/shard_map/ppermute | solution.py:412
  30.0 2.3 %collective-permute-done.9.refs_7_ = bf16[320,512]{1,0:T(8,128)(2,1)S(1)} collective-permute-done((bf16[320,512]{1,0:T(8,128)(2,1)S(1)}, bf16[320,512]{1,0:T(8,128)(2,1)S(1)}, u32[]{:S(2)}, u32[]{:S(2)}) %collective-permute-start.9) | collective-permute-done | bytes 327712 | tf_op jit(solution)/shard_map/ppermute | solution.py:412
  35.0 4.6 %collective-permute-done.10.refs_8_ = f32[80,512]{1,0:T(8,128)S(1)} collective-permute-done((f32[80,512]{1,0:T(8,128)S(1)}, f32[80,512]{1,0:T(8,128)S(1)}, u32[]{:S(2)}, u32[]{:S(2)}) %collective-permute-start.10) | collective-permute-done | bytes 163872 | tf_op jit(solution)/shard_map/ppermute | solution.py:412
  41.0 2.1 %collective-permute-done.11.refs_9_.refs_1_ = f32[80,512]{1,0:T(8,128)S(1)} collective-permute-done((f32[80,512]{1,0:T(8,128)S(1)}, f32[80,512]{1,0:T(8,128)S(1)}, u32[]{:S(2)}, u32[]{:S(2)}) %collective-permute-start.11) | collective-permute-done | bytes 163872 | tf_op jit(solution)/shard_map/ppermute | solution.py:412
  47.1 2.3 %collective-permute-start.12 = (f32[80,512]{1,0:T(8,128)S(1)}, f32[80,512]{1,0:T(8,128)S(1)}, u32[]{:S(2)}, u32[]{:S(2)}) collective-permute-start(f32[80,512]{1,0:T(8,128)S(1)} %add_rows.16.refs_8_), channel_id=1, source_target_pairs={{0,16},{1,17},{2,18},{3,19},{4,20},{5,21},{6,22},{7,23},{8,24},{9,... | collective-permute-start | bytes 491528 | tf_op jit(solution)/shard_map/ppermute | solution.py:412
  49.5 2.2 %collective-permute-done.15.refs_7_ = bf16[192,512]{1,0:T(8,128)(2,1)S(1)} collective-permute-done((bf16[192,512]{1,0:T(8,128)(2,1)S(1)}, bf16[192,512]{1,0:T(8,128)(2,1)S(1)}, u32[]{:S(2)}, u32[]{:S(2)}) %collective-permute-start.15) | collective-permute-done | bytes 196640 | tf_op jit(solution)/shard_map/ppermute | solution.py:412
  54.1 2.8 %collective-permute-done.13.refs_1_ = f32[64,512]{1,0:T(8,128)S(1)} collective-permute-done((f32[64,512]{1,0:T(8,128)S(1)}, f32[64,512]{1,0:T(8,128)S(1)}, u32[]{:S(2)}, u32[]{:S(2)}) %collective-permute-start.13) | collective-permute-done | bytes 131104 | tf_op jit(solution)/shard_map/ppermute | solution.py:412
  60.5 2.4 %collective-permute-start.20 = (f32[48,512]{1,0:T(8,128)S(1)}, f32[48,512]{1,0:T(8,128)S(1)}, u32[]{:S(2)}, u32[]{:S(2)}) collective-permute-start(f32[48,512]{1,0:T(8,128)S(1)} %add_rows.18.refs_3_), channel_id=1, source_target_pairs={{0,16},{1,17},{2,18},{3,19},{4,20},{5,21},{6,22},{7,23},{8,24},{9,... | collective-permute-start | bytes 294920 | tf_op jit(solution)/shard_map/ppermute | solution.py:412
  63.5 7.3 %collective-permute-done.20.refs_1_ = f32[48,512]{1,0:T(8,128)S(1)} collective-permute-done((f32[48,512]{1,0:T(8,128)S(1)}, f32[48,512]{1,0:T(8,128)S(1)}, u32[]{:S(2)}, u32[]{:S(2)}) %collective-permute-start.20) | collective-permute-done | bytes 98336 | tf_op jit(solution)/shard_map/ppermute | solution.py:412
  75.6 3.2 %collective-permute-done.22.refs_3_.refs_7_ = f32[112,512]{1,0:T(8,128)S(1)} collective-permute-done((f32[112,512]{1,0:T(8,128)S(1)}, f32[112,512]{1,0:T(8,128)S(1)}, u32[]{:S(2)}, u32[]{:S(2)}) %collective-permute-start.22) | collective-permute-done | bytes 229408 | tf_op jit(solution)/shard_map/ppermute | solution.py:412
  82.8 2.1 %collective-permute-done.29.refs_3_ = f32[2,40,256]{2,1,0:T(8,128)S(1)} collective-permute-done((f32[2,40,256]{2,1,0:T(8,128)S(1)}, f32[2,40,256]{2,1,0:T(8,128)S(1)}, u32[]{:S(2)}, u32[]{:S(2)}) %collective-permute-start.29) | collective-permute-done | bytes 81952 | tf_op jit(solution)/shard_map/ppermute | solution.py:412
  91.2 2.2 %collective-permute-start.32 = (f32[2,32,256]{2,1,0:T(8,128)S(1)}, f32[2,32,256]{2,1,0:T(8,128)S(1)}, u32[]{:S(2)}, u32[]{:S(2)}) collective-permute-start(f32[2,32,256]{2,1,0:T(8,128)S(1)} %add_rows.25.refs_0_), channel_id=1, source_target_pairs={{0,16},{1,17},{2,18},{3,19},{4,20},{5,21},{6,22},{7,23},{8,24},{9,... | collective-permute-start | bytes 196616 | tf_op jit(solution)/shard_map/ppermute | solution.py:412
  101.2 2.1 %collective-permute-start.40 = (f32[8,40,256]{2,1,0:T(8,128)S(1)}, f32[8,40,256]{2,1,0:T(8,128)S(1)}, u32[]{:S(2)}, u32[]{:S(2)}) collective-permute-start(f32[8,40,256]{2,1,0:T(8,128)S(1)} %pad_maximum_fusion.refs_0_), channel_id=1, source_target_pairs={{0,1},{1,0},{2,3},{3,2},{4,5},{5,4},{6,7},{7,6},{8,9},{9,8},{10,11... | collective-permute-start | bytes 983048 | tf_op jit(solution)/shard_map/ppermute | solution.py:412
  103.7 6.2 %collective-permute-start.41 = (f32[8,40,256]{2,1,0:T(8,128)S(1)}, f32[8,40,256]{2,1,0:T(8,128)S(1)}, u32[]{:S(2)}, u32[]{:S(2)}) collective-permute-start(f32[8,40,256]{2,1,0:T(8,128)S(1)} %pad_maximum_fusion.refs_0_), channel_id=1, source_target_pairs={{0,2},{1,3},{2,0},{3,1},{4,6},{5,7},{6,4},{7,5},{8,10},{9,11},{10,... | collective-permute-start | bytes 983048 | tf_op jit(solution)/shard_map/ppermute | solution.py:412
  109.9 3.4 %collective-permute-start.42 = (f32[8,40,256]{2,1,0:T(8,128)S(1)}, f32[8,40,256]{2,1,0:T(8,128)S(1)}, u32[]{:S(2)}, u32[]{:S(2)}) collective-permute-start(f32[8,40,256]{2,1,0:T(8,128)S(1)} %collective-permute-done.40.refs_1_), channel_id=1, source_target_pairs={{0,2},{1,3},{2,0},{3,1},{4,6},{5,7},{6,4},{7,5},{8,10},{9,11},{10,... | collective-permute-start | bytes 983048 | tf_op jit(solution)/shard_map/ppermute | solution.py:412
  113.4 2.3 %collective-permute-start.38 = (f32[8,32,256]{2,1,0:T(8,128)S(1)}, f32[8,32,256]{2,1,0:T(8,128)S(1)}, u32[]{:S(2)}, u32[]{:S(2)}) collective-permute-start(f32[8,32,256]{2,1,0:T(8,128)S(1)} %collective-permute-done.36.refs_1_), channel_id=1, source_target_pairs={{0,2},{1,3},{2,0},{3,1},{4,6},{5,7},{6,4},{7,5},{8,10},{9,11},{10,... | collective-permute-start | bytes 786440 | tf_op jit(solution)/shard_map/ppermute | solution.py:412
  115.7 2.0 %update_start.1 = (bf16[2,512,512]{2,1,0:T(8,128)(2,1)S(1)}, bf16[2,512,512]{2,1,0:T(8,128)(2,1)S(1)}, f32[8,128]{1,0:T(8,128)S(1)}, f32[240,512]{1,0:T(8,128)S(1)}, f32[240,512]{1,0:T(8,128)S(1)}) custom-call(s32[4]{0:T(128)S(1)} %pad_add_fusion.at.refs_0_, f32[8,40,256]{2,1,0:T(8,128)S(1)} %pad_maximum_fusion.refs_0_, ...), custom_call_target="tpu_custom_call" | custom-call | tf_op jit(solution)/shard_map/update_start/pallas_call | solution.py:384
  117.7 3.4 %update_finish.1 = bf16[240,512]{1,0:T(8,128)(2,1)} custom-call(s32[4]{0:T(128)S(1)} %pad_add_fusion.at.refs_0_, f32[8,32,256]{2,1,0:T(8,128)S(1)} %pad_maximum_fusion.2.refs_0_, f32[8,32,256]{2,1,0:T(8,128)S(1)} %collective-permute-done.36.refs_1_, f32[8,32,256]{2,1,0:T(8,128)S(1)} %collective-permute-done.37.refs_2_, ...), custom_call_target="tpu_custom_call" | custom-call | tf_op jit(solution)/shard_map/update_finish/pallas_call | solution.py:394
  (110 shorter events, 44.9 us)
Async XLA Ops:
  3.4 14.5 %collective-permute-start = (bf16[1008,512]{1,0:T(8,128)(2,1)S(1)}, bf16[1008,512]{1,0:T(8,128)(2,1)S(1)}, u32[]{:S(2)}, u32[]{:S(2)}) collective-permute-start(bf16[1008,512]{1,0:T(8,128)(2,1)S(1)} %get-tuple-element.43), channel_id=1, source_target_pairs={{0,2},{1,3},{2,0},{3,1},{4,6},{5,7},{6,4},{7,5},{8,10},{9,11},{10,... | collective-permute-start | bytes 3096584 | tf_op jit(solution)/shard_map/ppermute | solution.py:412
  3.5 8.9 %collective-permute-start.1 = (bf16[240,512]{1,0:T(8,128)(2,1)S(1)}, bf16[240,512]{1,0:T(8,128)(2,1)S(1)}, u32[]{:S(2)}, u32[]{:S(2)}) collective-permute-start(bf16[240,512]{1,0:T(8,128)(2,1)S(1)} %get-tuple-element.44), channel_id=1, source_target_pairs={{0,4},{1,5},{2,6},{3,7},{4,0},{5,1},{6,2},{7,3},{8,12},{9,13},{10,... | collective-permute-start | bytes 737288 | tf_op jit(solution)/shard_map/ppermute | solution.py:412
  6.2 11.7 %collective-permute-start.2 = (bf16[240,512]{1,0:T(8,128)(2,1)S(1)}, bf16[240,512]{1,0:T(8,128)(2,1)S(1)}, u32[]{:S(2)}, u32[]{:S(2)}) collective-permute-start(bf16[240,512]{1,0:T(8,128)(2,1)S(1)} %get-tuple-element.45), channel_id=1, source_target_pairs={{0,6},{1,7},{2,4},{3,5},{4,2},{5,3},{6,0},{7,1},{8,14},{9,15},{10,... | collective-permute-start | bytes 737288 | tf_op jit(solution)/shard_map/ppermute | solution.py:412
  6.3 23.8 %collective-permute-start.8 = (bf16[320,512]{1,0:T(8,128)(2,1)S(1)}, bf16[320,512]{1,0:T(8,128)(2,1)S(1)}, u32[]{:S(2)}, u32[]{:S(2)}) collective-permute-start(bf16[320,512]{1,0:T(8,128)(2,1)S(1)} %get-tuple-element.53), channel_id=1, source_target_pairs={{0,4},{1,5},{2,6},{3,7},{4,0},{5,1},{6,2},{7,3},{8,12},{9,13},{10,... | collective-permute-start | bytes 983048 | tf_op jit(solution)/shard_map/ppermute | solution.py:412
  7.9 24.4 %collective-permute-start.9 = (bf16[320,512]{1,0:T(8,128)(2,1)S(1)}, bf16[320,512]{1,0:T(8,128)(2,1)S(1)}, u32[]{:S(2)}, u32[]{:S(2)}) collective-permute-start(bf16[320,512]{1,0:T(8,128)(2,1)S(1)} %get-tuple-element.54), channel_id=1, source_target_pairs={{0,6},{1,7},{2,4},{3,5},{4,2},{5,3},{6,0},{7,1},{8,14},{9,15},{10,... | collective-permute-start | bytes 983048 | tf_op jit(solution)/shard_map/ppermute | solution.py:412
  18.7 9.0 %collective-permute-start.3 = (f32[48,512]{1,0:T(8,128)S(1)}, f32[48,512]{1,0:T(8,128)S(1)}, u32[]{:S(2)}, u32[]{:S(2)}) collective-permute-start(f32[48,512]{1,0:T(8,128)S(1)} %get-tuple-element.49), channel_id=1, source_target_pairs={{0,8},{1,9},{2,10},{3,11},{4,12},{5,13},{6,14},{7,15},{8,0},{9,1},... | collective-permute-start | bytes 294920 | tf_op jit(solution)/shard_map/ppermute | solution.py:412
  20.6 24.1 %collective-permute-start.6 = (bf16[256,512]{1,0:T(8,128)(2,1)S(1)}, bf16[256,512]{1,0:T(8,128)(2,1)S(1)}, u32[]{:S(2)}, u32[]{:S(2)}) collective-permute-start(bf16[256,512]{1,0:T(8,128)(2,1)S(1)} %get-tuple-element.51), channel_id=1, source_target_pairs={{0,4},{1,5},{2,6},{3,7},{4,0},{5,1},{6,2},{7,3},{8,12},{9,13},{10,... | collective-permute-start | bytes 786440 | tf_op jit(solution)/shard_map/ppermute | solution.py:412
  25.6 19.1 %collective-permute-start.7 = (bf16[256,512]{1,0:T(8,128)(2,1)S(1)}, bf16[256,512]{1,0:T(8,128)(2,1)S(1)}, u32[]{:S(2)}, u32[]{:S(2)}) collective-permute-start(bf16[256,512]{1,0:T(8,128)(2,1)S(1)} %get-tuple-element.52), channel_id=1, source_target_pairs={{0,6},{1,7},{2,4},{3,5},{4,2},{5,3},{6,0},{7,1},{8,14},{9,15},{10,... | collective-permute-start | bytes 786440 | tf_op jit(solution)/shard_map/ppermute | solution.py:412
  27.6 19.5 %collective-permute-start.5 = (f32[48,512]{1,0:T(8,128)S(1)}, f32[48,512]{1,0:T(8,128)S(1)}, u32[]{:S(2)}, u32[]{:S(2)}) collective-permute-start(f32[48,512]{1,0:T(8,128)S(1)} %add_rows.14.refs_8_), channel_id=1, source_target_pairs={{0,16},{1,17},{2,18},{3,19},{4,20},{5,21},{6,22},{7,23},{8,24},{9,... | collective-permute-start | bytes 294920 | tf_op jit(solution)/shard_map/ppermute | solution.py:412
  34.9 8.2 %collective-permute-start.11 = (f32[80,512]{1,0:T(8,128)S(1)}, f32[80,512]{1,0:T(8,128)S(1)}, u32[]{:S(2)}, u32[]{:S(2)}) collective-permute-start(f32[80,512]{1,0:T(8,128)S(1)} %get-tuple-element.58), channel_id=1, source_target_pairs={{0,8},{1,9},{2,10},{3,11},{4,12},{5,13},{6,14},{7,15},{8,0},{9,1},... | collective-permute-start | bytes 491528 | tf_op jit(solution)/shard_map/ppermute | solution.py:412
  39.6 9.8 %collective-permute-start.14 = (bf16[192,512]{1,0:T(8,128)(2,1)S(1)}, bf16[192,512]{1,0:T(8,128)(2,1)S(1)}, u32[]{:S(2)}, u32[]{:S(2)}) collective-permute-start(bf16[192,512]{1,0:T(8,128)(2,1)S(1)} %get-tuple-element.62), channel_id=1, source_target_pairs={{0,4},{1,5},{2,6},{3,7},{4,0},{5,1},{6,2},{7,3},{8,12},{9,13},{10,... | collective-permute-start | bytes 589832 | tf_op jit(solution)/shard_map/ppermute | solution.py:412
  43.1 8.5 %collective-permute-start.15 = (bf16[192,512]{1,0:T(8,128)(2,1)S(1)}, bf16[192,512]{1,0:T(8,128)(2,1)S(1)}, u32[]{:S(2)}, u32[]{:S(2)}) collective-permute-start(bf16[192,512]{1,0:T(8,128)(2,1)S(1)} %get-tuple-element.63), channel_id=1, source_target_pairs={{0,6},{1,7},{2,4},{3,5},{4,2},{5,3},{6,0},{7,1},{8,14},{9,15},{10,... | collective-permute-start | bytes 589832 | tf_op jit(solution)/shard_map/ppermute | solution.py:412
  45.5 15.0 %collective-permute-start.17 = (f32[64,512]{1,0:T(8,128)S(1)}, f32[64,512]{1,0:T(8,128)S(1)}, u32[]{:S(2)}, u32[]{:S(2)}) collective-permute-start(f32[64,512]{1,0:T(8,128)S(1)} %get-tuple-element.66), channel_id=1, source_target_pairs={{0,8},{1,9},{2,10},{3,11},{4,12},{5,13},{6,14},{7,15},{8,0},{9,1},... | collective-permute-start | bytes 393224 | tf_op jit(solution)/shard_map/ppermute | solution.py:412
  46.7 10.2 %collective-permute-start.13 = (f32[64,512]{1,0:T(8,128)S(1)}, f32[64,512]{1,0:T(8,128)S(1)}, u32[]{:S(2)}, u32[]{:S(2)}) collective-permute-start(f32[64,512]{1,0:T(8,128)S(1)} %get-tuple-element.61), channel_id=1, source_target_pairs={{0,8},{1,9},{2,10},{3,11},{4,12},{5,13},{6,14},{7,15},{8,0},{9,1},... | collective-permute-start | bytes 393224 | tf_op jit(solution)/shard_map/ppermute | solution.py:412
  47.1 12.0 %collective-permute-start.12 = (f32[80,512]{1,0:T(8,128)S(1)}, f32[80,512]{1,0:T(8,128)S(1)}, u32[]{:S(2)}, u32[]{:S(2)}) collective-permute-start(f32[80,512]{1,0:T(8,128)S(1)} %add_rows.16.refs_8_), channel_id=1, source_target_pairs={{0,16},{1,17},{2,18},{3,19},{4,20},{5,21},{6,22},{7,23},{8,24},{9,... | collective-permute-start | bytes 491528 | tf_op jit(solution)/shard_map/ppermute | solution.py:412
  52.4 6.7 %collective-permute-start.16 = (f32[48,512]{1,0:T(8,128)S(1)}, f32[48,512]{1,0:T(8,128)S(1)}, u32[]{:S(2)}, u32[]{:S(2)}) collective-permute-start(f32[48,512]{1,0:T(8,128)S(1)} %get-tuple-element.65), channel_id=1, source_target_pairs={{0,8},{1,9},{2,10},{3,11},{4,12},{5,13},{6,14},{7,15},{8,0},{9,1},... | collective-permute-start | bytes 294920 | tf_op jit(solution)/shard_map/ppermute | solution.py:412
  54.0 9.4 %collective-permute-start.19 = (f32[48,512]{1,0:T(8,128)S(1)}, f32[48,512]{1,0:T(8,128)S(1)}, u32[]{:S(2)}, u32[]{:S(2)}) collective-permute-start(f32[48,512]{1,0:T(8,128)S(1)} %get-tuple-element.67), channel_id=1, source_target_pairs={{0,8},{1,9},{2,10},{3,11},{4,12},{5,13},{6,14},{7,15},{8,0},{9,1},... | collective-permute-start | bytes 294920 | tf_op jit(solution)/shard_map/ppermute | solution.py:412
  59.1 11.6 %collective-permute-start.21 = (f32[128,512]{1,0:T(8,128)S(1)}, f32[128,512]{1,0:T(8,128)S(1)}, u32[]{:S(2)}, u32[]{:S(2)}) collective-permute-start(f32[128,512]{1,0:T(8,128)S(1)} %pad_maximum_fusion.1.refs_0_.refs_4_), channel_id=1, source_target_pairs={{0,1},{1,0},{2,3},{3,2},{4,5},{5,4},{6,7},{7,6},{8,9},{9,8},{10,11... | collective-permute-start | bytes 786440 | tf_op jit(solution)/shard_map/ppermute | solution.py:412
  60.5 10.3 %collective-permute-start.20 = (f32[48,512]{1,0:T(8,128)S(1)}, f32[48,512]{1,0:T(8,128)S(1)}, u32[]{:S(2)}, u32[]{:S(2)}) collective-permute-start(f32[48,512]{1,0:T(8,128)S(1)} %add_rows.18.refs_3_), channel_id=1, source_target_pairs={{0,16},{1,17},{2,18},{3,19},{4,20},{5,21},{6,22},{7,23},{8,24},{9,... | collective-permute-start | bytes 294920 | tf_op jit(solution)/shard_map/ppermute | solution.py:412
  72.0 6.7 %collective-permute-start.22 = (f32[112,512]{1,0:T(8,128)S(1)}, f32[112,512]{1,0:T(8,128)S(1)}, u32[]{:S(2)}, u32[]{:S(2)}) collective-permute-start(f32[112,512]{1,0:T(8,128)S(1)} %pad_maximum_fusion.3.refs_1_.refs_5_), channel_id=1, source_target_pairs={{0,1},{1,0},{2,3},{3,2},{4,5},{5,4},{6,7},{7,6},{8,9},{9,8},{10,11... | collective-permute-start | bytes 688136 | tf_op jit(solution)/shard_map/ppermute | solution.py:412
  74.2 7.2 %collective-permute-start.28 = (f32[4,40,256]{2,1,0:T(8,128)S(1)}, f32[4,40,256]{2,1,0:T(8,128)S(1)}, u32[]{:S(2)}, u32[]{:S(2)}) collective-permute-start(f32[4,40,256]{2,1,0:T(8,128)S(1)} %get-tuple-element.77), channel_id=1, source_target_pairs={{0,2},{1,3},{2,0},{3,1},{4,6},{5,7},{6,4},{7,5},{8,10},{9,11},{10,... | collective-permute-start | bytes 491528 | tf_op jit(solution)/shard_map/ppermute | solution.py:412
  101.2 8.8 %collective-permute-start.40 = (f32[8,40,256]{2,1,0:T(8,128)S(1)}, f32[8,40,256]{2,1,0:T(8,128)S(1)}, u32[]{:S(2)}, u32[]{:S(2)}) collective-permute-start(f32[8,40,256]{2,1,0:T(8,128)S(1)} %pad_maximum_fusion.refs_0_), channel_id=1, source_target_pairs={{0,1},{1,0},{2,3},{3,2},{4,5},{5,4},{6,7},{7,6},{8,9},{9,8},{10,11... | collective-permute-start | bytes 983048 | tf_op jit(solution)/shard_map/ppermute | solution.py:412
  103.3 10.1 %collective-permute-start.36 = (f32[8,32,256]{2,1,0:T(8,128)S(1)}, f32[8,32,256]{2,1,0:T(8,128)S(1)}, u32[]{:S(2)}, u32[]{:S(2)}) collective-permute-start(f32[8,32,256]{2,1,0:T(8,128)S(1)} %pad_maximum_fusion.2.refs_0_), channel_id=1, source_target_pairs={{0,4},{1,5},{2,6},{3,7},{4,0},{5,1},{6,2},{7,3},{8,12},{9,13},{10,... | collective-permute-start | bytes 786440 | tf_op jit(solution)/shard_map/ppermute | solution.py:412
  103.7 12.0 %collective-permute-start.41 = (f32[8,40,256]{2,1,0:T(8,128)S(1)}, f32[8,40,256]{2,1,0:T(8,128)S(1)}, u32[]{:S(2)}, u32[]{:S(2)}) collective-permute-start(f32[8,40,256]{2,1,0:T(8,128)S(1)} %pad_maximum_fusion.refs_0_), channel_id=1, source_target_pairs={{0,2},{1,3},{2,0},{3,1},{4,6},{5,7},{6,4},{7,5},{8,10},{9,11},{10,... | collective-permute-start | bytes 983048 | tf_op jit(solution)/shard_map/ppermute | solution.py:412
  (20 other events, 85.4 us)

commit v6 on v5

--- a/solution.py
+++ b/solution.py
@@ -232,8 +232,18 @@
         out[slot] = flat[pl.ds(pl.multiple_of((z * 2 + x) * part, 8), part), :]
 
 
-def near_kernel(count, at, *refs):
-    slabs, outs, (high, low, flat) = refs[:count], refs[count : count + 2], refs[-3:]
+def put_out(at, side, bases, flat, outs, early):
+    if bases:
+        flat[...] += bases[0][side]
+    if early:
+        outs[0][side] = flat[...]
+    else:
+        put_slots(at, flat, outs[side])
+
+
+def near_kernel(count, based, early, at, *refs):
+    slabs, bases, (high, low, flat) = refs[:count], refs[count : count + based], refs[-3:]
+    outs = refs[-4:-3] if early else refs[-5:-3]
     put_rows(slabs, high, low, 0)
 
     def take(start, width):
@@ -241,7 +251,7 @@
         return high[:, lanes], low[:, lanes]
 
     contract = ((0,), (0,))
-    for side, out in enumerate(outs):
+    for side in range(2):
         core = lax.bitwise_xor(at[2], side)
         own = take(core * PIECE, PIECE)
         block = dot3(own, own, contract)
@@ -250,11 +260,13 @@
         flat[HALF : HALF + HALF // 2, HALF:] = block[HALF + HALF // 2 :, HALF:]
         left = take(core * HALF, HALF)
         flat[NEAR - HALF :, :] = dot3(left, take(PIECE, PIECE), contract)
-        put_slots(at, flat, out)
-
-
-def cross_kernel(count, at, *refs):
-    slabs, outs, (high, low, flat) = refs[: 2 * count], refs[-5:-3], refs[-3:]
+        put_out(at, side, bases, flat, outs, early)
+
+
+def cross_kernel(count, based, early, at, *refs):
+    slabs, bases = refs[: 2 * count], refs[2 * count : 2 * count + based]
+    high, low, flat = refs[-3:]
+    outs = refs[-4:-3] if early else refs[-5:-3]
     share = slabs[0].shape[1]
     put_rows(slabs[:count], high, low, 0)
     put_rows(slabs[count:], high, low, share)
@@ -265,7 +277,7 @@
 
     contract = ((0,), (0,))
     half = at[3]
-    for side, out in enumerate(outs):
+    for side in range(2):
         core = lax.bitwise_xor(at[2], side)
         for k in range(2):
             mine = core * PIECE
@@ -275,21 +287,26 @@
             flat[k * HALF : (k + 1) * HALF, :] = dot3(
                 take(left, HALF), take(right, PIECE), contract
             )
-        put_slots(at, flat, out)
-
-
-def gram_part(kernel, at, slabs, count, packed, name, after):
+        put_out(at, side, bases, flat, outs, early)
+
+
+def gram_part(kernel, at, slabs, count, packed, name, base=None, early=False, after=()):
     rows = sum(slab.shape[0] for slab in slabs[:count])
     width = slabs[0].shape[1] * (len(slabs) // count)
+    bases = [] if base is None else [base]
+    if early:
+        shapes = [jax.ShapeDtypeStruct((2, packed, PIECE), F32)]
+    else:
+        shapes = [jax.ShapeDtypeStruct((8, packed // 8, PIECE), F32)] * 2
     return pl.pallas_call(
-        functools.partial(kernel, count),
-        in_specs=[SCALARS] + [WHOLE] * len(slabs) + [ANYWHERE] * len(after),
-        out_specs=[WHOLE] * 2,
-        out_shape=[jax.ShapeDtypeStruct((8, packed // 8, PIECE), F32)] * 2,
+        functools.partial(kernel, count, len(bases), early),
+        in_specs=[SCALARS] + [WHOLE] * len(slabs + bases) + [ANYWHERE] * len(after),
+        out_specs=[WHOLE] * len(shapes),
+        out_shape=shapes,
         scratch_shapes=[pltpu.VMEM((rows, width), BF16)] * 2 + [pltpu.VMEM((packed, PIECE), F32)],
         compiler_params=params(),
         name=name,
-    )(at, *slabs, *after)
+    )(at, *slabs, *bases, *after)
 
 
 def unpack(at, pieces, places, packed, length):
@@ -479,18 +496,27 @@
             made["across", n] = across
             owns.append(group)
             acrosses.append(across)
+            if len(owns) == 1:
+                (made["base", n],) = gram_part(
+                    near_kernel, at, owns, 1, NEAR, "gram_near_early", early=True
+                )
             held.clear()
 
     for step, n in STEPS:
         {"sum": add_partials, "halve": halve, "finish": finish}[step](n)
 
-    count = len(owns)
-    own, far = gram_part(near_kernel, at, owns, count, NEAR, "gram_near", [])
+    (cross_base,) = gram_part(
+        cross_kernel, at, owns[:1] + acrosses[:1], 1, CROSS, "gram_cross_early", early=True
+    )
+    own, far = gram_part(
+        near_kernel, at, owns[1:], 1, NEAR, "gram_near", made["base", 1]
+    )
     core = [flip(far[4:], "c"), flip(far[:4], "c")]
     near_sent = add([own[4:], core[0]], [])
     near_x = flip(near_sent, "x")
     cross_own, far = gram_part(
-        cross_kernel, at, owns + acrosses, count, CROSS, "gram_cross", [near_sent]
+        cross_kernel, at, owns[1:] + acrosses[1:], 1, CROSS, "gram_cross", cross_base,
+        after=[near_sent],
     )
     cross_core = [flip(far[4:], "c"), flip(far[:4], "c")]
     cross_x = flip(add([cross_own[4:], cross_core[0]], [near_x]), "x")

time: 121 us -> 121 us (level)
  starting transfers between devices: 55.4 us -> 53.4 us
  Pallas kernels: 13.6 us -> 15.4 us
    ppermute x43, starting transfers between devices: 55.4 us -> 53.4 us  [flip(): lax.ppermute(value, ('dp', 'fsdp'), [(i, i ^ mask) for i in range(count)])]
    pallas_call x2 -> x4, Pallas kernels: 2.44 us -> 4.29 us  [gram_part(): pl.pallas_call(functools.partial(kernel, count, len(bases), early), in_sp...]
  transfers between devices with their start and end apart: 43 -> 43, of which waited for: 21 -> 20; matrix products, arithmetic and copies ran while one was open for 0% -> 0% of each run, Pallas kernels for 5% -> 8%
where the time goes in v6:
time: 121 us
  starting transfers between devices  53.4 us (44%)
  waiting for transfers between devices  50.8 us (42%)
  Pallas kernels  15.4 us (13%)
    ppermute x43, starting transfers between devices, flip(): lax.ppermute(value, ('dp', 'fsdp'), [(i, i ^ mask) for i in range(count)])  53.4 us
    ppermute x43, waiting for transfers between devices, flip(): lax.ppermute(value, ('dp', 'fsdp'), [(i, i ^ mask) for i in range(count)])  50.8 us
    pallas_call x4, Pallas kernels, gram_part(): pl.pallas_call(functools.partial(kernel, count, len(bases), early), in_sp...  4.29 us
    pallas_call x1, Pallas kernels, update(): pl.pallas_call(functools.partial(finish_kernel, scale, places, count), in...  3.43 us
    pallas_call x4, Pallas kernels, dequant(): pl.pallas_call(kernel, in_specs=[SCALARS] + [WHOLE] * 7 + [ANYWHERE] * (l...  2.98 us
    pallas_call x1, Pallas kernels, pack(): pl.pallas_call(functools.partial(pack_kernel, own_rows, spans), in_specs=...  2.51 us
  transfers between devices with their start and end apart: 43, of which 20 were waited for; matrix products, arithmetic and copies ran while one was open for 0% of the time, Pallas kernels for 8%

profile of v6, /device:TPU:1, one launch (start us, length us, event | category | flops | bytes accessed | tf_op | source)
XLA Modules:
  0.0 121.2 jit_solution(17636902432122362499)
XLA Ops:
  0.9 2.5 %pack_rows.1 = (bf16[960,512]{1,0:T(8,128)(2,1)S(1)}, f32[16,512]{1,0:T(8,128)S(1)}, bf16[1008,512]{1,0:T(8,128)(2,1)S(1)}, bf16[240,512]{1,0:T(8,128)(2,1)S(1)}...) custom-call(s32[4]{0:T(128)S(1)} %pad_add_fusion.at.refs_0_, ...), custom_call_target="tpu_custom_call" | custom-call | tf_op jit(solution)/shard_map/pack_rows/pallas_call | solution.py:126
  3.5 2.7 %collective-permute-start.1 = (bf16[240,512]{1,0:T(8,128)(2,1)S(1)}, bf16[240,512]{1,0:T(8,128)(2,1)S(1)}, u32[]{:S(2)}, u32[]{:S(2)}) collective-permute-start(bf16[240,512]{1,0:T(8,128)(2,1)S(1)} %get-tuple-element.44), channel_id=1, source_target_pairs={{0,4},{1,5},{2,6},{3,7},{4,0},{5,1},{6,2},{7,3},{8,12},{9,13},{10,... | collective-permute-start | bytes 737288 | tf_op jit(solution)/shard_map/ppermute | solution.py:429
  8.3 4.2 %collective-permute-done.1.refs_4_.refs_6_ = bf16[240,512]{1,0:T(8,128)(2,1)S(1)} collective-permute-done((bf16[240,512]{1,0:T(8,128)(2,1)S(1)}, bf16[240,512]{1,0:T(8,128)(2,1)S(1)}, u32[]{:S(2)}, u32[]{:S(2)}) %collective-permute-start.1) | collective-permute-done | bytes 245792 | tf_op jit(solution)/shard_map/ppermute | solution.py:429
  12.5 5.5 %collective-permute-done.2.refs_5_.refs_7_ = bf16[240,512]{1,0:T(8,128)(2,1)S(1)} collective-permute-done((bf16[240,512]{1,0:T(8,128)(2,1)S(1)}, bf16[240,512]{1,0:T(8,128)(2,1)S(1)}, u32[]{:S(2)}, u32[]{:S(2)}) %collective-permute-start.2) | collective-permute-done | bytes 245792 | tf_op jit(solution)/shard_map/ppermute | solution.py:429
  21.9 3.7 %collective-permute-done.7.refs_1_ = f32[48,512]{1,0:T(8,128)S(1)} collective-permute-done((f32[48,512]{1,0:T(8,128)S(1)}, f32[48,512]{1,0:T(8,128)S(1)}, u32[]{:S(2)}, u32[]{:S(2)}) %collective-permute-start.7) | collective-permute-done | bytes 98336 | tf_op jit(solution)/shard_map/ppermute | solution.py:429
  25.6 2.0 %collective-permute-start.4 = (bf16[256,512]{1,0:T(8,128)(2,1)S(1)}, bf16[256,512]{1,0:T(8,128)(2,1)S(1)}, u32[]{:S(2)}, u32[]{:S(2)}) collective-permute-start(bf16[256,512]{1,0:T(8,128)(2,1)S(1)} %get-tuple-element.49), channel_id=1, source_target_pairs={{0,6},{1,7},{2,4},{3,5},{4,2},{5,3},{6,0},{7,1},{8,14},{9,15},{10,... | collective-permute-start | bytes 786440 | tf_op jit(solution)/shard_map/ppermute | solution.py:429
  27.6 2.4 %collective-permute-start.15 = (f32[48,512]{1,0:T(8,128)S(1)}, f32[48,512]{1,0:T(8,128)S(1)}, u32[]{:S(2)}, u32[]{:S(2)}) collective-permute-start(f32[48,512]{1,0:T(8,128)S(1)} %add_rows.14.refs_8_), channel_id=1, source_target_pairs={{0,16},{1,17},{2,18},{3,19},{4,20},{5,21},{6,22},{7,23},{8,24},{9,... | collective-permute-start | bytes 294920 | tf_op jit(solution)/shard_map/ppermute | solution.py:429
  30.0 2.2 %collective-permute-done.6.refs_7_ = bf16[320,512]{1,0:T(8,128)(2,1)S(1)} collective-permute-done((bf16[320,512]{1,0:T(8,128)(2,1)S(1)}, bf16[320,512]{1,0:T(8,128)(2,1)S(1)}, u32[]{:S(2)}, u32[]{:S(2)}) %collective-permute-start.6) | collective-permute-done | bytes 327712 | tf_op jit(solution)/shard_map/ppermute | solution.py:429
  35.0 4.6 %collective-permute-done.10.refs_9_.refs_1_ = f32[80,512]{1,0:T(8,128)S(1)} collective-permute-done((f32[80,512]{1,0:T(8,128)S(1)}, f32[80,512]{1,0:T(8,128)S(1)}, u32[]{:S(2)}, u32[]{:S(2)}) %collective-permute-start.10) | collective-permute-done | bytes 163872 | tf_op jit(solution)/shard_map/ppermute | solution.py:429
  41.0 2.1 %collective-permute-done.9.refs_8_ = f32[80,512]{1,0:T(8,128)S(1)} collective-permute-done((f32[80,512]{1,0:T(8,128)S(1)}, f32[80,512]{1,0:T(8,128)S(1)}, u32[]{:S(2)}, u32[]{:S(2)}) %collective-permute-start.9) | collective-permute-done | bytes 163872 | tf_op jit(solution)/shard_map/ppermute | solution.py:429
  47.1 2.3 %collective-permute-start.20 = (f32[80,512]{1,0:T(8,128)S(1)}, f32[80,512]{1,0:T(8,128)S(1)}, u32[]{:S(2)}, u32[]{:S(2)}) collective-permute-start(f32[80,512]{1,0:T(8,128)S(1)} %add_rows.15.refs_8_), channel_id=1, source_target_pairs={{0,16},{1,17},{2,18},{3,19},{4,20},{5,21},{6,22},{7,23},{8,24},{9,... | collective-permute-start | bytes 491528 | tf_op jit(solution)/shard_map/ppermute | solution.py:429
  49.5 2.2 %collective-permute-done.14.refs_7_ = bf16[192,512]{1,0:T(8,128)(2,1)S(1)} collective-permute-done((bf16[192,512]{1,0:T(8,128)(2,1)S(1)}, bf16[192,512]{1,0:T(8,128)(2,1)S(1)}, u32[]{:S(2)}, u32[]{:S(2)}) %collective-permute-start.14) | collective-permute-done | bytes 196640 | tf_op jit(solution)/shard_map/ppermute | solution.py:429
  54.1 2.8 %collective-permute-done.12.refs_1_ = f32[64,512]{1,0:T(8,128)S(1)} collective-permute-done((f32[64,512]{1,0:T(8,128)S(1)}, f32[64,512]{1,0:T(8,128)S(1)}, u32[]{:S(2)}, u32[]{:S(2)}) %collective-permute-start.12) | collective-permute-done | bytes 131104 | tf_op jit(solution)/shard_map/ppermute | solution.py:429
  60.5 2.4 %collective-permute-start.19 = (f32[48,512]{1,0:T(8,128)S(1)}, f32[48,512]{1,0:T(8,128)S(1)}, u32[]{:S(2)}, u32[]{:S(2)}) collective-permute-start(f32[48,512]{1,0:T(8,128)S(1)} %add_rows.19.refs_3_), channel_id=1, source_target_pairs={{0,16},{1,17},{2,18},{3,19},{4,20},{5,21},{6,22},{7,23},{8,24},{9,... | collective-permute-start | bytes 294920 | tf_op jit(solution)/shard_map/ppermute | solution.py:429
  64.6 6.2 %collective-permute-done.19.refs_1_ = f32[48,512]{1,0:T(8,128)S(1)} collective-permute-done((f32[48,512]{1,0:T(8,128)S(1)}, f32[48,512]{1,0:T(8,128)S(1)}, u32[]{:S(2)}, u32[]{:S(2)}) %collective-permute-start.19) | collective-permute-done | bytes 98336 | tf_op jit(solution)/shard_map/ppermute | solution.py:429
  75.6 1.9 %collective-permute-done.22.refs_1_.refs_7_ = f32[112,512]{1,0:T(8,128)S(1)} collective-permute-done((f32[112,512]{1,0:T(8,128)S(1)}, f32[112,512]{1,0:T(8,128)S(1)}, u32[]{:S(2)}, u32[]{:S(2)}) %collective-permute-start.22) | collective-permute-done | bytes 229408 | tf_op jit(solution)/shard_map/ppermute | solution.py:429
  91.3 2.2 %collective-permute-start.32 = (f32[2,32,256]{2,1,0:T(8,128)S(1)}, f32[2,32,256]{2,1,0:T(8,128)S(1)}, u32[]{:S(2)}, u32[]{:S(2)}) collective-permute-start(f32[2,32,256]{2,1,0:T(8,128)S(1)} %add_rows.25.refs_0_), channel_id=1, source_target_pairs={{0,16},{1,17},{2,18},{3,19},{4,20},{5,21},{6,22},{7,23},{8,24},{9,... | collective-permute-start | bytes 196616 | tf_op jit(solution)/shard_map/ppermute | solution.py:429
  97.3 2.0 %collective-permute-done.34 = f32[2,32,256]{2,1,0:T(8,128)S(1)} collective-permute-done((f32[2,32,256]{2,1,0:T(8,128)S(1)}, f32[2,32,256]{2,1,0:T(8,128)S(1)}, u32[]{:S(2)}, u32[]{:S(2)}) %collective-permute-start.34) | collective-permute-done | bytes 65568 | tf_op jit(solution)/shard_map/ppermute | solution.py:429
  101.5 2.0 %collective-permute-done.35 = f32[4,32,256]{2,1,0:T(8,128)S(1)} collective-permute-done((f32[4,32,256]{2,1,0:T(8,128)S(1)}, f32[4,32,256]{2,1,0:T(8,128)S(1)}, u32[]{:S(2)}, u32[]{:S(2)}) %collective-permute-start.35) | collective-permute-done | bytes 131104 | tf_op jit(solution)/shard_map/ppermute | solution.py:429
  103.8 6.1 %collective-permute-start.41 = (f32[8,40,256]{2,1,0:T(8,128)S(1)}, f32[8,40,256]{2,1,0:T(8,128)S(1)}, u32[]{:S(2)}, u32[]{:S(2)}) collective-permute-start(f32[8,40,256]{2,1,0:T(8,128)S(1)} %pad_maximum_fusion.refs_0_), channel_id=1, source_target_pairs={{0,2},{1,3},{2,0},{3,1},{4,6},{5,7},{6,4},{7,5},{8,10},{9,11},{10,... | collective-permute-start | bytes 983048 | tf_op jit(solution)/shard_map/ppermute | solution.py:429
  109.9 3.0 %collective-permute-start.42 = (f32[8,40,256]{2,1,0:T(8,128)S(1)}, f32[8,40,256]{2,1,0:T(8,128)S(1)}, u32[]{:S(2)}, u32[]{:S(2)}) collective-permute-start(f32[8,40,256]{2,1,0:T(8,128)S(1)} %collective-permute-done.40.refs_1_), channel_id=1, source_target_pairs={{0,2},{1,3},{2,0},{3,1},{4,6},{5,7},{6,4},{7,5},{8,10},{9,11},{10,... | collective-permute-start | bytes 983048 | tf_op jit(solution)/shard_map/ppermute | solution.py:429
  112.9 2.9 %collective-permute-start.38 = (f32[8,32,256]{2,1,0:T(8,128)S(1)}, f32[8,32,256]{2,1,0:T(8,128)S(1)}, u32[]{:S(2)}, u32[]{:S(2)}) collective-permute-start(f32[8,32,256]{2,1,0:T(8,128)S(1)} %collective-permute-done.36.refs_1_), channel_id=1, source_target_pairs={{0,2},{1,3},{2,0},{3,1},{4,6},{5,7},{6,4},{7,5},{8,10},{9,11},{10,... | collective-permute-start | bytes 786440 | tf_op jit(solution)/shard_map/ppermute | solution.py:429
  115.8 2.0 %update_start.1 = (bf16[2,512,512]{2,1,0:T(8,128)(2,1)S(1)}, bf16[2,512,512]{2,1,0:T(8,128)(2,1)S(1)}, f32[8,128]{1,0:T(8,128)S(1)}, f32[240,512]{1,0:T(8,128)S(1)}, f32[240,512]{1,0:T(8,128)S(1)}) custom-call(s32[4]{0:T(128)S(1)} %pad_add_fusion.at.refs_0_, f32[8,40,256]{2,1,0:T(8,128)S(1)} %pad_maximum_fusion.refs_0_, ...), custom_call_target="tpu_custom_call" | custom-call | tf_op jit(solution)/shard_map/update_start/pallas_call | solution.py:401
  117.8 3.4 %update_finish.1 = bf16[240,512]{1,0:T(8,128)(2,1)} custom-call(s32[4]{0:T(128)S(1)} %pad_add_fusion.at.refs_0_, f32[8,32,256]{2,1,0:T(8,128)S(1)} %pad_maximum_fusion.2.refs_0_, f32[8,32,256]{2,1,0:T(8,128)S(1)} %collective-permute-done.36.refs_1_, f32[8,32,256]{2,1,0:T(8,128)S(1)} %collective-permute-done.37.refs_2_, ...), custom_call_target="tpu_custom_call" | custom-call | tf_op jit(solution)/shard_map/update_finish/pallas_call | solution.py:411
  (112 shorter events, 47.7 us)
Async XLA Ops:
  3.4 14.5 %collective-permute-start = (bf16[1008,512]{1,0:T(8,128)(2,1)S(1)}, bf16[1008,512]{1,0:T(8,128)(2,1)S(1)}, u32[]{:S(2)}, u32[]{:S(2)}) collective-permute-start(bf16[1008,512]{1,0:T(8,128)(2,1)S(1)} %get-tuple-element.43), channel_id=1, source_target_pairs={{0,2},{1,3},{2,0},{3,1},{4,6},{5,7},{6,4},{7,5},{8,10},{9,11},{10,... | collective-permute-start | bytes 3096584 | tf_op jit(solution)/shard_map/ppermute | solution.py:429
  3.5 8.9 %collective-permute-start.1 = (bf16[240,512]{1,0:T(8,128)(2,1)S(1)}, bf16[240,512]{1,0:T(8,128)(2,1)S(1)}, u32[]{:S(2)}, u32[]{:S(2)}) collective-permute-start(bf16[240,512]{1,0:T(8,128)(2,1)S(1)} %get-tuple-element.44), channel_id=1, source_target_pairs={{0,4},{1,5},{2,6},{3,7},{4,0},{5,1},{6,2},{7,3},{8,12},{9,13},{10,... | collective-permute-start | bytes 737288 | tf_op jit(solution)/shard_map/ppermute | solution.py:429
  6.2 11.7 %collective-permute-start.2 = (bf16[240,512]{1,0:T(8,128)(2,1)S(1)}, bf16[240,512]{1,0:T(8,128)(2,1)S(1)}, u32[]{:S(2)}, u32[]{:S(2)}) collective-permute-start(bf16[240,512]{1,0:T(8,128)(2,1)S(1)} %get-tuple-element.45), channel_id=1, source_target_pairs={{0,6},{1,7},{2,4},{3,5},{4,2},{5,3},{6,0},{7,1},{8,14},{9,15},{10,... | collective-permute-start | bytes 737288 | tf_op jit(solution)/shard_map/ppermute | solution.py:429
  6.3 23.8 %collective-permute-start.5 = (bf16[320,512]{1,0:T(8,128)(2,1)S(1)}, bf16[320,512]{1,0:T(8,128)(2,1)S(1)}, u32[]{:S(2)}, u32[]{:S(2)}) collective-permute-start(bf16[320,512]{1,0:T(8,128)(2,1)S(1)} %get-tuple-element.50), channel_id=1, source_target_pairs={{0,4},{1,5},{2,6},{3,7},{4,0},{5,1},{6,2},{7,3},{8,12},{9,13},{10,... | collective-permute-start | bytes 983048 | tf_op jit(solution)/shard_map/ppermute | solution.py:429
  7.9 24.4 %collective-permute-start.6 = (bf16[320,512]{1,0:T(8,128)(2,1)S(1)}, bf16[320,512]{1,0:T(8,128)(2,1)S(1)}, u32[]{:S(2)}, u32[]{:S(2)}) collective-permute-start(bf16[320,512]{1,0:T(8,128)(2,1)S(1)} %get-tuple-element.51), channel_id=1, source_target_pairs={{0,6},{1,7},{2,4},{3,5},{4,2},{5,3},{6,0},{7,1},{8,14},{9,15},{10,... | collective-permute-start | bytes 983048 | tf_op jit(solution)/shard_map/ppermute | solution.py:429
  18.7 9.0 %collective-permute-start.8 = (f32[48,512]{1,0:T(8,128)S(1)}, f32[48,512]{1,0:T(8,128)S(1)}, u32[]{:S(2)}, u32[]{:S(2)}) collective-permute-start(f32[48,512]{1,0:T(8,128)S(1)} %get-tuple-element.54), channel_id=1, source_target_pairs={{0,8},{1,9},{2,10},{3,11},{4,12},{5,13},{6,14},{7,15},{8,0},{9,1},... | collective-permute-start | bytes 294920 | tf_op jit(solution)/shard_map/ppermute | solution.py:429
  20.6 24.1 %collective-permute-start.3 = (bf16[256,512]{1,0:T(8,128)(2,1)S(1)}, bf16[256,512]{1,0:T(8,128)(2,1)S(1)}, u32[]{:S(2)}, u32[]{:S(2)}) collective-permute-start(bf16[256,512]{1,0:T(8,128)(2,1)S(1)} %get-tuple-element.48), channel_id=1, source_target_pairs={{0,4},{1,5},{2,6},{3,7},{4,0},{5,1},{6,2},{7,3},{8,12},{9,13},{10,... | collective-permute-start | bytes 786440 | tf_op jit(solution)/shard_map/ppermute | solution.py:429
  25.6 19.1 %collective-permute-start.4 = (bf16[256,512]{1,0:T(8,128)(2,1)S(1)}, bf16[256,512]{1,0:T(8,128)(2,1)S(1)}, u32[]{:S(2)}, u32[]{:S(2)}) collective-permute-start(bf16[256,512]{1,0:T(8,128)(2,1)S(1)} %get-tuple-element.49), channel_id=1, source_target_pairs={{0,6},{1,7},{2,4},{3,5},{4,2},{5,3},{6,0},{7,1},{8,14},{9,15},{10,... | collective-permute-start | bytes 786440 | tf_op jit(solution)/shard_map/ppermute | solution.py:429
  27.6 19.5 %collective-permute-start.15 = (f32[48,512]{1,0:T(8,128)S(1)}, f32[48,512]{1,0:T(8,128)S(1)}, u32[]{:S(2)}, u32[]{:S(2)}) collective-permute-start(f32[48,512]{1,0:T(8,128)S(1)} %add_rows.14.refs_8_), channel_id=1, source_target_pairs={{0,16},{1,17},{2,18},{3,19},{4,20},{5,21},{6,22},{7,23},{8,24},{9,... | collective-permute-start | bytes 294920 | tf_op jit(solution)/shard_map/ppermute | solution.py:429
  34.9 8.2 %collective-permute-start.9 = (f32[80,512]{1,0:T(8,128)S(1)}, f32[80,512]{1,0:T(8,128)S(1)}, u32[]{:S(2)}, u32[]{:S(2)}) collective-permute-start(f32[80,512]{1,0:T(8,128)S(1)} %get-tuple-element.57), channel_id=1, source_target_pairs={{0,8},{1,9},{2,10},{3,11},{4,12},{5,13},{6,14},{7,15},{8,0},{9,1},... | collective-permute-start | bytes 491528 | tf_op jit(solution)/shard_map/ppermute | solution.py:429
  39.6 9.8 %collective-permute-start.13 = (bf16[192,512]{1,0:T(8,128)(2,1)S(1)}, bf16[192,512]{1,0:T(8,128)(2,1)S(1)}, u32[]{:S(2)}, u32[]{:S(2)}) collective-permute-start(bf16[192,512]{1,0:T(8,128)(2,1)S(1)} %get-tuple-element.62), channel_id=1, source_target_pairs={{0,4},{1,5},{2,6},{3,7},{4,0},{5,1},{6,2},{7,3},{8,12},{9,13},{10,... | collective-permute-start | bytes 589832 | tf_op jit(solution)/shard_map/ppermute | solution.py:429
  43.1 8.5 %collective-permute-start.14 = (bf16[192,512]{1,0:T(8,128)(2,1)S(1)}, bf16[192,512]{1,0:T(8,128)(2,1)S(1)}, u32[]{:S(2)}, u32[]{:S(2)}) collective-permute-start(bf16[192,512]{1,0:T(8,128)(2,1)S(1)} %get-tuple-element.63), channel_id=1, source_target_pairs={{0,6},{1,7},{2,4},{3,5},{4,2},{5,3},{6,0},{7,1},{8,14},{9,15},{10,... | collective-permute-start | bytes 589832 | tf_op jit(solution)/shard_map/ppermute | solution.py:429
  45.5 15.0 %collective-permute-start.11 = (f32[64,512]{1,0:T(8,128)S(1)}, f32[64,512]{1,0:T(8,128)S(1)}, u32[]{:S(2)}, u32[]{:S(2)}) collective-permute-start(f32[64,512]{1,0:T(8,128)S(1)} %get-tuple-element.60), channel_id=1, source_target_pairs={{0,8},{1,9},{2,10},{3,11},{4,12},{5,13},{6,14},{7,15},{8,0},{9,1},... | collective-permute-start | bytes 393224 | tf_op jit(solution)/shard_map/ppermute | solution.py:429
  46.7 10.2 %collective-permute-start.12 = (f32[64,512]{1,0:T(8,128)S(1)}, f32[64,512]{1,0:T(8,128)S(1)}, u32[]{:S(2)}, u32[]{:S(2)}) collective-permute-start(f32[64,512]{1,0:T(8,128)S(1)} %get-tuple-element.61), channel_id=1, source_target_pairs={{0,8},{1,9},{2,10},{3,11},{4,12},{5,13},{6,14},{7,15},{8,0},{9,1},... | collective-permute-start | bytes 393224 | tf_op jit(solution)/shard_map/ppermute | solution.py:429
  47.1 12.0 %collective-permute-start.20 = (f32[80,512]{1,0:T(8,128)S(1)}, f32[80,512]{1,0:T(8,128)S(1)}, u32[]{:S(2)}, u32[]{:S(2)}) collective-permute-start(f32[80,512]{1,0:T(8,128)S(1)} %add_rows.15.refs_8_), channel_id=1, source_target_pairs={{0,16},{1,17},{2,18},{3,19},{4,20},{5,21},{6,22},{7,23},{8,24},{9,... | collective-permute-start | bytes 491528 | tf_op jit(solution)/shard_map/ppermute | solution.py:429
  52.4 6.7 %collective-permute-start.18 = (f32[48,512]{1,0:T(8,128)S(1)}, f32[48,512]{1,0:T(8,128)S(1)}, u32[]{:S(2)}, u32[]{:S(2)}) collective-permute-start(f32[48,512]{1,0:T(8,128)S(1)} %get-tuple-element.67), channel_id=1, source_target_pairs={{0,8},{1,9},{2,10},{3,11},{4,12},{5,13},{6,14},{7,15},{8,0},{9,1},... | collective-permute-start | bytes 294920 | tf_op jit(solution)/shard_map/ppermute | solution.py:429
  54.0 9.4 %collective-permute-start.17 = (f32[48,512]{1,0:T(8,128)S(1)}, f32[48,512]{1,0:T(8,128)S(1)}, u32[]{:S(2)}, u32[]{:S(2)}) collective-permute-start(f32[48,512]{1,0:T(8,128)S(1)} %get-tuple-element.66), channel_id=1, source_target_pairs={{0,8},{1,9},{2,10},{3,11},{4,12},{5,13},{6,14},{7,15},{8,0},{9,1},... | collective-permute-start | bytes 294920 | tf_op jit(solution)/shard_map/ppermute | solution.py:429
  57.0 7.6 %collective-permute-start.16 = (f32[64,512]{1,0:T(8,128)S(1)}, f32[64,512]{1,0:T(8,128)S(1)}, u32[]{:S(2)}, u32[]{:S(2)}) collective-permute-start(f32[64,512]{1,0:T(8,128)S(1)} %add_rows.17.refs_2_), channel_id=1, source_target_pairs={{0,16},{1,17},{2,18},{3,19},{4,20},{5,21},{6,22},{7,23},{8,24},{9,... | collective-permute-start | bytes 393224 | tf_op jit(solution)/shard_map/ppermute | solution.py:429
  59.1 11.6 %collective-permute-start.21 = (f32[128,512]{1,0:T(8,128)S(1)}, f32[128,512]{1,0:T(8,128)S(1)}, u32[]{:S(2)}, u32[]{:S(2)}) collective-permute-start(f32[128,512]{1,0:T(8,128)S(1)} %pad_maximum_fusion.1.refs_0_.refs_4_), channel_id=1, source_target_pairs={{0,1},{1,0},{2,3},{3,2},{4,5},{5,4},{6,7},{7,6},{8,9},{9,8},{10,11... | collective-permute-start | bytes 786440 | tf_op jit(solution)/shard_map/ppermute | solution.py:429
  60.5 10.3 %collective-permute-start.19 = (f32[48,512]{1,0:T(8,128)S(1)}, f32[48,512]{1,0:T(8,128)S(1)}, u32[]{:S(2)}, u32[]{:S(2)}) collective-permute-start(f32[48,512]{1,0:T(8,128)S(1)} %add_rows.19.refs_3_), channel_id=1, source_target_pairs={{0,16},{1,17},{2,18},{3,19},{4,20},{5,21},{6,22},{7,23},{8,24},{9,... | collective-permute-start | bytes 294920 | tf_op jit(solution)/shard_map/ppermute | solution.py:429
  70.8 6.7 %collective-permute-start.22 = (f32[112,512]{1,0:T(8,128)S(1)}, f32[112,512]{1,0:T(8,128)S(1)}, u32[]{:S(2)}, u32[]{:S(2)}) collective-permute-start(f32[112,512]{1,0:T(8,128)S(1)} %pad_maximum_fusion.3.refs_0_.refs_5_), channel_id=1, source_target_pairs={{0,1},{1,0},{2,3},{3,2},{4,5},{5,4},{6,7},{7,6},{8,9},{9,8},{10,11... | collective-permute-start | bytes 688136 | tf_op jit(solution)/shard_map/ppermute | solution.py:429
  101.2 8.7 %collective-permute-start.40 = (f32[8,40,256]{2,1,0:T(8,128)S(1)}, f32[8,40,256]{2,1,0:T(8,128)S(1)}, u32[]{:S(2)}, u32[]{:S(2)}) collective-permute-start(f32[8,40,256]{2,1,0:T(8,128)S(1)} %pad_maximum_fusion.refs_0_), channel_id=1, source_target_pairs={{0,1},{1,0},{2,3},{3,2},{4,5},{5,4},{6,7},{7,6},{8,9},{9,8},{10,11... | collective-permute-start | bytes 983048 | tf_op jit(solution)/shard_map/ppermute | solution.py:429
  103.5 9.4 %collective-permute-start.36 = (f32[8,32,256]{2,1,0:T(8,128)S(1)}, f32[8,32,256]{2,1,0:T(8,128)S(1)}, u32[]{:S(2)}, u32[]{:S(2)}) collective-permute-start(f32[8,32,256]{2,1,0:T(8,128)S(1)} %pad_maximum_fusion.2.refs_0_), channel_id=1, source_target_pairs={{0,4},{1,5},{2,6},{3,7},{4,0},{5,1},{6,2},{7,3},{8,12},{9,13},{10,... | collective-permute-start | bytes 786440 | tf_op jit(solution)/shard_map/ppermute | solution.py:429
  103.8 12.0 %collective-permute-start.41 = (f32[8,40,256]{2,1,0:T(8,128)S(1)}, f32[8,40,256]{2,1,0:T(8,128)S(1)}, u32[]{:S(2)}, u32[]{:S(2)}) collective-permute-start(f32[8,40,256]{2,1,0:T(8,128)S(1)} %pad_maximum_fusion.refs_0_), channel_id=1, source_target_pairs={{0,2},{1,3},{2,0},{3,1},{4,6},{5,7},{6,4},{7,5},{8,10},{9,11},{10,... | collective-permute-start | bytes 983048 | tf_op jit(solution)/shard_map/ppermute | solution.py:429
  (20 other events, 88.5 us)

commit v7 on v6

--- a/solution.py
+++ b/solution.py
@@ -505,21 +505,22 @@
     for step, n in STEPS:
         {"sum": add_partials, "halve": halve, "finish": finish}[step](n)
 
-    (cross_base,) = gram_part(
-        cross_kernel, at, owns[:1] + acrosses[:1], 1, CROSS, "gram_cross_early", early=True
-    )
     own, far = gram_part(
         near_kernel, at, owns[1:], 1, NEAR, "gram_near", made["base", 1]
     )
     core = [flip(far[4:], "c"), flip(far[:4], "c")]
     near_sent = add([own[4:], core[0]], [])
     near_x = flip(near_sent, "x")
+    (cross_base,) = gram_part(
+        cross_kernel, at, owns[:1] + acrosses[:1], 1, CROSS, "gram_cross_early", early=True,
+        after=[near_sent],
+    )
     cross_own, far = gram_part(
         cross_kernel, at, owns[1:] + acrosses[1:], 1, CROSS, "gram_cross", cross_base,
         after=[near_sent],
     )
     cross_core = [flip(far[4:], "c"), flip(far[:4], "c")]
-    cross_x = flip(add([cross_own[4:], cross_core[0]], [near_x]), "x")
+    cross_x = flip(add([cross_own[4:], cross_core[0]], []), "x")
 
     near = own[:4] + core[1] + near_x
     near_z1 = flip(near[2:], "z1")

time: 121 us -> 121 us (level)
  transfers between devices with their start and end apart: 43 -> 43, of which waited for: 20 -> 21; matrix products, arithmetic and copies ran while one was open for 0% -> 0% of each run, Pallas kernels for 8% -> 8%
where the time goes in v7:
time: 121 us
  starting transfers between devices  53.1 us (44%)
  waiting for transfers between devices  51 us (42%)
  Pallas kernels  15.4 us (13%)
    ppermute x43, starting transfers between devices, flip(): lax.ppermute(value, ('dp', 'fsdp'), [(i, i ^ mask) for i in range(count)])  53.1 us
    ppermute x43, waiting for transfers between devices, flip(): lax.ppermute(value, ('dp', 'fsdp'), [(i, i ^ mask) for i in range(count)])  51 us
    pallas_call x4, Pallas kernels, gram_part(): pl.pallas_call(functools.partial(kernel, count, len(bases), early), in_sp...  4.29 us
    pallas_call x1, Pallas kernels, update(): pl.pallas_call(functools.partial(finish_kernel, scale, places, count), in...  3.43 us
    pallas_call x4, Pallas kernels, dequant(): pl.pallas_call(kernel, in_specs=[SCALARS] + [WHOLE] * 7 + [ANYWHERE] * (l...  2.98 us
    pallas_call x1, Pallas kernels, pack(): pl.pallas_call(functools.partial(pack_kernel, own_rows, spans), in_specs=...  2.51 us
  transfers between devices with their start and end apart: 43, of which 21 were waited for; matrix products, arithmetic and copies ran while one was open for 0% of the time, Pallas kernels for 8%

profile of v7, /device:TPU:1, one launch (start us, length us, event | category | flops | bytes accessed | tf_op | source)
XLA Modules:
  0.0 121.1 jit_solution(6013335595847001968)
XLA Ops:
  0.9 2.5 %pack_rows.1 = (bf16[960,512]{1,0:T(8,128)(2,1)S(1)}, f32[16,512]{1,0:T(8,128)S(1)}, bf16[1008,512]{1,0:T(8,128)(2,1)S(1)}, bf16[240,512]{1,0:T(8,128)(2,1)S(1)}...) custom-call(s32[4]{0:T(128)S(1)} %pad_add_fusion.at.refs_0_, ...), custom_call_target="tpu_custom_call" | custom-call | tf_op jit(solution)/shard_map/pack_rows/pallas_call | solution.py:126
  3.5 2.7 %collective-permute-start.1 = (bf16[240,512]{1,0:T(8,128)(2,1)S(1)}, bf16[240,512]{1,0:T(8,128)(2,1)S(1)}, u32[]{:S(2)}, u32[]{:S(2)}) collective-permute-start(bf16[240,512]{1,0:T(8,128)(2,1)S(1)} %get-tuple-element.44), channel_id=1, source_target_pairs={{0,4},{1,5},{2,6},{3,7},{4,0},{5,1},{6,2},{7,3},{8,12},{9,13},{10,... | collective-permute-start | bytes 737288 | tf_op jit(solution)/shard_map/ppermute | solution.py:429
  8.3 4.2 %collective-permute-done.1.refs_4_.refs_6_ = bf16[240,512]{1,0:T(8,128)(2,1)S(1)} collective-permute-done((bf16[240,512]{1,0:T(8,128)(2,1)S(1)}, bf16[240,512]{1,0:T(8,128)(2,1)S(1)}, u32[]{:S(2)}, u32[]{:S(2)}) %collective-permute-start.1) | collective-permute-done | bytes 245792 | tf_op jit(solution)/shard_map/ppermute | solution.py:429
  12.5 5.5 %collective-permute-done.2.refs_5_.refs_7_ = bf16[240,512]{1,0:T(8,128)(2,1)S(1)} collective-permute-done((bf16[240,512]{1,0:T(8,128)(2,1)S(1)}, bf16[240,512]{1,0:T(8,128)(2,1)S(1)}, u32[]{:S(2)}, u32[]{:S(2)}) %collective-permute-start.2) | collective-permute-done | bytes 245792 | tf_op jit(solution)/shard_map/ppermute | solution.py:429
  21.9 3.7 %collective-permute-done.7.refs_1_ = f32[48,512]{1,0:T(8,128)S(1)} collective-permute-done((f32[48,512]{1,0:T(8,128)S(1)}, f32[48,512]{1,0:T(8,128)S(1)}, u32[]{:S(2)}, u32[]{:S(2)}) %collective-permute-start.7) | collective-permute-done | bytes 98336 | tf_op jit(solution)/shard_map/ppermute | solution.py:429
  25.6 2.0 %collective-permute-start.4 = (bf16[256,512]{1,0:T(8,128)(2,1)S(1)}, bf16[256,512]{1,0:T(8,128)(2,1)S(1)}, u32[]{:S(2)}, u32[]{:S(2)}) collective-permute-start(bf16[256,512]{1,0:T(8,128)(2,1)S(1)} %get-tuple-element.49), channel_id=1, source_target_pairs={{0,6},{1,7},{2,4},{3,5},{4,2},{5,3},{6,0},{7,1},{8,14},{9,15},{10,... | collective-permute-start | bytes 786440 | tf_op jit(solution)/shard_map/ppermute | solution.py:429
  27.6 2.4 %collective-permute-start.15 = (f32[48,512]{1,0:T(8,128)S(1)}, f32[48,512]{1,0:T(8,128)S(1)}, u32[]{:S(2)}, u32[]{:S(2)}) collective-permute-start(f32[48,512]{1,0:T(8,128)S(1)} %add_rows.14.refs_8_), channel_id=1, source_target_pairs={{0,16},{1,17},{2,18},{3,19},{4,20},{5,21},{6,22},{7,23},{8,24},{9,... | collective-permute-start | bytes 294920 | tf_op jit(solution)/shard_map/ppermute | solution.py:429
  30.0 2.2 %collective-permute-done.6.refs_7_ = bf16[320,512]{1,0:T(8,128)(2,1)S(1)} collective-permute-done((bf16[320,512]{1,0:T(8,128)(2,1)S(1)}, bf16[320,512]{1,0:T(8,128)(2,1)S(1)}, u32[]{:S(2)}, u32[]{:S(2)}) %collective-permute-start.6) | collective-permute-done | bytes 327712 | tf_op jit(solution)/shard_map/ppermute | solution.py:429
  35.0 4.6 %collective-permute-done.10.refs_9_.refs_1_ = f32[80,512]{1,0:T(8,128)S(1)} collective-permute-done((f32[80,512]{1,0:T(8,128)S(1)}, f32[80,512]{1,0:T(8,128)S(1)}, u32[]{:S(2)}, u32[]{:S(2)}) %collective-permute-start.10) | collective-permute-done | bytes 163872 | tf_op jit(solution)/shard_map/ppermute | solution.py:429
  41.0 2.1 %collective-permute-done.9.refs_8_ = f32[80,512]{1,0:T(8,128)S(1)} collective-permute-done((f32[80,512]{1,0:T(8,128)S(1)}, f32[80,512]{1,0:T(8,128)S(1)}, u32[]{:S(2)}, u32[]{:S(2)}) %collective-permute-start.9) | collective-permute-done | bytes 163872 | tf_op jit(solution)/shard_map/ppermute | solution.py:429
  47.1 2.3 %collective-permute-start.20 = (f32[80,512]{1,0:T(8,128)S(1)}, f32[80,512]{1,0:T(8,128)S(1)}, u32[]{:S(2)}, u32[]{:S(2)}) collective-permute-start(f32[80,512]{1,0:T(8,128)S(1)} %add_rows.15.refs_8_), channel_id=1, source_target_pairs={{0,16},{1,17},{2,18},{3,19},{4,20},{5,21},{6,22},{7,23},{8,24},{9,... | collective-permute-start | bytes 491528 | tf_op jit(solution)/shard_map/ppermute | solution.py:429
  49.5 2.2 %collective-permute-done.14.refs_7_ = bf16[192,512]{1,0:T(8,128)(2,1)S(1)} collective-permute-done((bf16[192,512]{1,0:T(8,128)(2,1)S(1)}, bf16[192,512]{1,0:T(8,128)(2,1)S(1)}, u32[]{:S(2)}, u32[]{:S(2)}) %collective-permute-start.14) | collective-permute-done | bytes 196640 | tf_op jit(solution)/shard_map/ppermute | solution.py:429
  54.1 2.8 %collective-permute-done.12.refs_1_ = f32[64,512]{1,0:T(8,128)S(1)} collective-permute-done((f32[64,512]{1,0:T(8,128)S(1)}, f32[64,512]{1,0:T(8,128)S(1)}, u32[]{:S(2)}, u32[]{:S(2)}) %collective-permute-start.12) | collective-permute-done | bytes 131104 | tf_op jit(solution)/shard_map/ppermute | solution.py:429
  60.5 2.4 %collective-permute-start.19 = (f32[48,512]{1,0:T(8,128)S(1)}, f32[48,512]{1,0:T(8,128)S(1)}, u32[]{:S(2)}, u32[]{:S(2)}) collective-permute-start(f32[48,512]{1,0:T(8,128)S(1)} %add_rows.19.refs_3_), channel_id=1, source_target_pairs={{0,16},{1,17},{2,18},{3,19},{4,20},{5,21},{6,22},{7,23},{8,24},{9,... | collective-permute-start | bytes 294920 | tf_op jit(solution)/shard_map/ppermute | solution.py:429
  64.6 6.2 %collective-permute-done.19.refs_1_ = f32[48,512]{1,0:T(8,128)S(1)} collective-permute-done((f32[48,512]{1,0:T(8,128)S(1)}, f32[48,512]{1,0:T(8,128)S(1)}, u32[]{:S(2)}, u32[]{:S(2)}) %collective-permute-start.19) | collective-permute-done | bytes 98336 | tf_op jit(solution)/shard_map/ppermute | solution.py:429
  89.2 1.9 %collective-permute-done.30.refs_1_ = f32[2,32,256]{2,1,0:T(8,128)S(1)} collective-permute-done((f32[2,32,256]{2,1,0:T(8,128)S(1)}, f32[2,32,256]{2,1,0:T(8,128)S(1)}, u32[]{:S(2)}, u32[]{:S(2)}) %collective-permute-start.30) | collective-permute-done | bytes 65568 | tf_op jit(solution)/shard_map/ppermute | solution.py:429
  91.1 2.2 %collective-permute-start.32 = (f32[2,32,256]{2,1,0:T(8,128)S(1)}, f32[2,32,256]{2,1,0:T(8,128)S(1)}, u32[]{:S(2)}, u32[]{:S(2)}) collective-permute-start(f32[2,32,256]{2,1,0:T(8,128)S(1)} %add_rows.25.refs_0_), channel_id=1, source_target_pairs={{0,16},{1,17},{2,18},{3,19},{4,20},{5,21},{6,22},{7,23},{8,24},{9,... | collective-permute-start | bytes 196616 | tf_op jit(solution)/shard_map/ppermute | solution.py:429
  97.2 2.0 %collective-permute-done.34 = f32[2,32,256]{2,1,0:T(8,128)S(1)} collective-permute-done((f32[2,32,256]{2,1,0:T(8,128)S(1)}, f32[2,32,256]{2,1,0:T(8,128)S(1)}, u32[]{:S(2)}, u32[]{:S(2)}) %collective-permute-start.34) | collective-permute-done | bytes 65568 | tf_op jit(solution)/shard_map/ppermute | solution.py:429
  101.4 2.0 %collective-permute-done.35 = f32[4,32,256]{2,1,0:T(8,128)S(1)} collective-permute-done((f32[4,32,256]{2,1,0:T(8,128)S(1)}, f32[4,32,256]{2,1,0:T(8,128)S(1)}, u32[]{:S(2)}, u32[]{:S(2)}) %collective-permute-start.35) | collective-permute-done | bytes 131104 | tf_op jit(solution)/shard_map/ppermute | solution.py:429
  103.7 6.1 %collective-permute-start.41 = (f32[8,40,256]{2,1,0:T(8,128)S(1)}, f32[8,40,256]{2,1,0:T(8,128)S(1)}, u32[]{:S(2)}, u32[]{:S(2)}) collective-permute-start(f32[8,40,256]{2,1,0:T(8,128)S(1)} %pad_maximum_fusion.refs_0_), channel_id=1, source_target_pairs={{0,2},{1,3},{2,0},{3,1},{4,6},{5,7},{6,4},{7,5},{8,10},{9,11},{10,... | collective-permute-start | bytes 983048 | tf_op jit(solution)/shard_map/ppermute | solution.py:429
  109.8 3.0 %collective-permute-start.42 = (f32[8,40,256]{2,1,0:T(8,128)S(1)}, f32[8,40,256]{2,1,0:T(8,128)S(1)}, u32[]{:S(2)}, u32[]{:S(2)}) collective-permute-start(f32[8,40,256]{2,1,0:T(8,128)S(1)} %collective-permute-done.40.refs_1_), channel_id=1, source_target_pairs={{0,2},{1,3},{2,0},{3,1},{4,6},{5,7},{6,4},{7,5},{8,10},{9,11},{10,... | collective-permute-start | bytes 983048 | tf_op jit(solution)/shard_map/ppermute | solution.py:429
  112.8 2.9 %collective-permute-start.38 = (f32[8,32,256]{2,1,0:T(8,128)S(1)}, f32[8,32,256]{2,1,0:T(8,128)S(1)}, u32[]{:S(2)}, u32[]{:S(2)}) collective-permute-start(f32[8,32,256]{2,1,0:T(8,128)S(1)} %collective-permute-done.36.refs_1_), channel_id=1, source_target_pairs={{0,2},{1,3},{2,0},{3,1},{4,6},{5,7},{6,4},{7,5},{8,10},{9,11},{10,... | collective-permute-start | bytes 786440 | tf_op jit(solution)/shard_map/ppermute | solution.py:429
  115.7 2.0 %update_start.1 = (bf16[2,512,512]{2,1,0:T(8,128)(2,1)S(1)}, bf16[2,512,512]{2,1,0:T(8,128)(2,1)S(1)}, f32[8,128]{1,0:T(8,128)S(1)}, f32[240,512]{1,0:T(8,128)S(1)}, f32[240,512]{1,0:T(8,128)S(1)}) custom-call(s32[4]{0:T(128)S(1)} %pad_add_fusion.at.refs_0_, f32[8,40,256]{2,1,0:T(8,128)S(1)} %pad_maximum_fusion.refs_0_, ...), custom_call_target="tpu_custom_call" | custom-call | tf_op jit(solution)/shard_map/update_start/pallas_call | solution.py:401
  117.7 3.4 %update_finish.1 = bf16[240,512]{1,0:T(8,128)(2,1)} custom-call(s32[4]{0:T(128)S(1)} %pad_add_fusion.at.refs_0_, f32[8,32,256]{2,1,0:T(8,128)S(1)} %pad_maximum_fusion.2.refs_0_, f32[8,32,256]{2,1,0:T(8,128)S(1)} %collective-permute-done.36.refs_1_, f32[8,32,256]{2,1,0:T(8,128)S(1)} %collective-permute-done.37.refs_2_, ...), custom_call_target="tpu_custom_call" | custom-call | tf_op jit(solution)/shard_map/update_finish/pallas_call | solution.py:411
  (112 shorter events, 47.6 us)
Async XLA Ops:
  3.4 14.5 %collective-permute-start = (bf16[1008,512]{1,0:T(8,128)(2,1)S(1)}, bf16[1008,512]{1,0:T(8,128)(2,1)S(1)}, u32[]{:S(2)}, u32[]{:S(2)}) collective-permute-start(bf16[1008,512]{1,0:T(8,128)(2,1)S(1)} %get-tuple-element.43), channel_id=1, source_target_pairs={{0,2},{1,3},{2,0},{3,1},{4,6},{5,7},{6,4},{7,5},{8,10},{9,11},{10,... | collective-permute-start | bytes 3096584 | tf_op jit(solution)/shard_map/ppermute | solution.py:429
  3.5 8.9 %collective-permute-start.1 = (bf16[240,512]{1,0:T(8,128)(2,1)S(1)}, bf16[240,512]{1,0:T(8,128)(2,1)S(1)}, u32[]{:S(2)}, u32[]{:S(2)}) collective-permute-start(bf16[240,512]{1,0:T(8,128)(2,1)S(1)} %get-tuple-element.44), channel_id=1, source_target_pairs={{0,4},{1,5},{2,6},{3,7},{4,0},{5,1},{6,2},{7,3},{8,12},{9,13},{10,... | collective-permute-start | bytes 737288 | tf_op jit(solution)/shard_map/ppermute | solution.py:429
  6.2 11.7 %collective-permute-start.2 = (bf16[240,512]{1,0:T(8,128)(2,1)S(1)}, bf16[240,512]{1,0:T(8,128)(2,1)S(1)}, u32[]{:S(2)}, u32[]{:S(2)}) collective-permute-start(bf16[240,512]{1,0:T(8,128)(2,1)S(1)} %get-tuple-element.45), channel_id=1, source_target_pairs={{0,6},{1,7},{2,4},{3,5},{4,2},{5,3},{6,0},{7,1},{8,14},{9,15},{10,... | collective-permute-start | bytes 737288 | tf_op jit(solution)/shard_map/ppermute | solution.py:429
  6.3 23.8 %collective-permute-start.5 = (bf16[320,512]{1,0:T(8,128)(2,1)S(1)}, bf16[320,512]{1,0:T(8,128)(2,1)S(1)}, u32[]{:S(2)}, u32[]{:S(2)}) collective-permute-start(bf16[320,512]{1,0:T(8,128)(2,1)S(1)} %get-tuple-element.50), channel_id=1, source_target_pairs={{0,4},{1,5},{2,6},{3,7},{4,0},{5,1},{6,2},{7,3},{8,12},{9,13},{10,... | collective-permute-start | bytes 983048 | tf_op jit(solution)/shard_map/ppermute | solution.py:429
  7.9 24.4 %collective-permute-start.6 = (bf16[320,512]{1,0:T(8,128)(2,1)S(1)}, bf16[320,512]{1,0:T(8,128)(2,1)S(1)}, u32[]{:S(2)}, u32[]{:S(2)}) collective-permute-start(bf16[320,512]{1,0:T(8,128)(2,1)S(1)} %get-tuple-element.51), channel_id=1, source_target_pairs={{0,6},{1,7},{2,4},{3,5},{4,2},{5,3},{6,0},{7,1},{8,14},{9,15},{10,... | collective-permute-start | bytes 983048 | tf_op jit(solution)/shard_map/ppermute | solution.py:429
  18.7 9.0 %collective-permute-start.8 = (f32[48,512]{1,0:T(8,128)S(1)}, f32[48,512]{1,0:T(8,128)S(1)}, u32[]{:S(2)}, u32[]{:S(2)}) collective-permute-start(f32[48,512]{1,0:T(8,128)S(1)} %get-tuple-element.54), channel_id=1, source_target_pairs={{0,8},{1,9},{2,10},{3,11},{4,12},{5,13},{6,14},{7,15},{8,0},{9,1},... | collective-permute-start | bytes 294920 | tf_op jit(solution)/shard_map/ppermute | solution.py:429
  20.6 24.1 %collective-permute-start.3 = (bf16[256,512]{1,0:T(8,128)(2,1)S(1)}, bf16[256,512]{1,0:T(8,128)(2,1)S(1)}, u32[]{:S(2)}, u32[]{:S(2)}) collective-permute-start(bf16[256,512]{1,0:T(8,128)(2,1)S(1)} %get-tuple-element.48), channel_id=1, source_target_pairs={{0,4},{1,5},{2,6},{3,7},{4,0},{5,1},{6,2},{7,3},{8,12},{9,13},{10,... | collective-permute-start | bytes 786440 | tf_op jit(solution)/shard_map/ppermute | solution.py:429
  25.6 19.1 %collective-permute-start.4 = (bf16[256,512]{1,0:T(8,128)(2,1)S(1)}, bf16[256,512]{1,0:T(8,128)(2,1)S(1)}, u32[]{:S(2)}, u32[]{:S(2)}) collective-permute-start(bf16[256,512]{1,0:T(8,128)(2,1)S(1)} %get-tuple-element.49), channel_id=1, source_target_pairs={{0,6},{1,7},{2,4},{3,5},{4,2},{5,3},{6,0},{7,1},{8,14},{9,15},{10,... | collective-permute-start | bytes 786440 | tf_op jit(solution)/shard_map/ppermute | solution.py:429
  27.6 19.5 %collective-permute-start.15 = (f32[48,512]{1,0:T(8,128)S(1)}, f32[48,512]{1,0:T(8,128)S(1)}, u32[]{:S(2)}, u32[]{:S(2)}) collective-permute-start(f32[48,512]{1,0:T(8,128)S(1)} %add_rows.14.refs_8_), channel_id=1, source_target_pairs={{0,16},{1,17},{2,18},{3,19},{4,20},{5,21},{6,22},{7,23},{8,24},{9,... | collective-permute-start | bytes 294920 | tf_op jit(solution)/shard_map/ppermute | solution.py:429
  34.9 8.2 %collective-permute-start.9 = (f32[80,512]{1,0:T(8,128)S(1)}, f32[80,512]{1,0:T(8,128)S(1)}, u32[]{:S(2)}, u32[]{:S(2)}) collective-permute-start(f32[80,512]{1,0:T(8,128)S(1)} %get-tuple-element.57), channel_id=1, source_target_pairs={{0,8},{1,9},{2,10},{3,11},{4,12},{5,13},{6,14},{7,15},{8,0},{9,1},... | collective-permute-start | bytes 491528 | tf_op jit(solution)/shard_map/ppermute | solution.py:429
  39.6 9.8 %collective-permute-start.13 = (bf16[192,512]{1,0:T(8,128)(2,1)S(1)}, bf16[192,512]{1,0:T(8,128)(2,1)S(1)}, u32[]{:S(2)}, u32[]{:S(2)}) collective-permute-start(bf16[192,512]{1,0:T(8,128)(2,1)S(1)} %get-tuple-element.62), channel_id=1, source_target_pairs={{0,4},{1,5},{2,6},{3,7},{4,0},{5,1},{6,2},{7,3},{8,12},{9,13},{10,... | collective-permute-start | bytes 589832 | tf_op jit(solution)/shard_map/ppermute | solution.py:429
  43.1 8.5 %collective-permute-start.14 = (bf16[192,512]{1,0:T(8,128)(2,1)S(1)}, bf16[192,512]{1,0:T(8,128)(2,1)S(1)}, u32[]{:S(2)}, u32[]{:S(2)}) collective-permute-start(bf16[192,512]{1,0:T(8,128)(2,1)S(1)} %get-tuple-element.63), channel_id=1, source_target_pairs={{0,6},{1,7},{2,4},{3,5},{4,2},{5,3},{6,0},{7,1},{8,14},{9,15},{10,... | collective-permute-start | bytes 589832 | tf_op jit(solution)/shard_map/ppermute | solution.py:429
  45.5 15.0 %collective-permute-start.11 = (f32[64,512]{1,0:T(8,128)S(1)}, f32[64,512]{1,0:T(8,128)S(1)}, u32[]{:S(2)}, u32[]{:S(2)}) collective-permute-start(f32[64,512]{1,0:T(8,128)S(1)} %get-tuple-element.60), channel_id=1, source_target_pairs={{0,8},{1,9},{2,10},{3,11},{4,12},{5,13},{6,14},{7,15},{8,0},{9,1},... | collective-permute-start | bytes 393224 | tf_op jit(solution)/shard_map/ppermute | solution.py:429
  46.7 10.2 %collective-permute-start.12 = (f32[64,512]{1,0:T(8,128)S(1)}, f32[64,512]{1,0:T(8,128)S(1)}, u32[]{:S(2)}, u32[]{:S(2)}) collective-permute-start(f32[64,512]{1,0:T(8,128)S(1)} %get-tuple-element.61), channel_id=1, source_target_pairs={{0,8},{1,9},{2,10},{3,11},{4,12},{5,13},{6,14},{7,15},{8,0},{9,1},... | collective-permute-start | bytes 393224 | tf_op jit(solution)/shard_map/ppermute | solution.py:429
  47.1 12.0 %collective-permute-start.20 = (f32[80,512]{1,0:T(8,128)S(1)}, f32[80,512]{1,0:T(8,128)S(1)}, u32[]{:S(2)}, u32[]{:S(2)}) collective-permute-start(f32[80,512]{1,0:T(8,128)S(1)} %add_rows.15.refs_8_), channel_id=1, source_target_pairs={{0,16},{1,17},{2,18},{3,19},{4,20},{5,21},{6,22},{7,23},{8,24},{9,... | collective-permute-start | bytes 491528 | tf_op jit(solution)/shard_map/ppermute | solution.py:429
  52.4 6.7 %collective-permute-start.18 = (f32[48,512]{1,0:T(8,128)S(1)}, f32[48,512]{1,0:T(8,128)S(1)}, u32[]{:S(2)}, u32[]{:S(2)}) collective-permute-start(f32[48,512]{1,0:T(8,128)S(1)} %get-tuple-element.67), channel_id=1, source_target_pairs={{0,8},{1,9},{2,10},{3,11},{4,12},{5,13},{6,14},{7,15},{8,0},{9,1},... | collective-permute-start | bytes 294920 | tf_op jit(solution)/shard_map/ppermute | solution.py:429
  54.0 9.4 %collective-permute-start.17 = (f32[48,512]{1,0:T(8,128)S(1)}, f32[48,512]{1,0:T(8,128)S(1)}, u32[]{:S(2)}, u32[]{:S(2)}) collective-permute-start(f32[48,512]{1,0:T(8,128)S(1)} %get-tuple-element.66), channel_id=1, source_target_pairs={{0,8},{1,9},{2,10},{3,11},{4,12},{5,13},{6,14},{7,15},{8,0},{9,1},... | collective-permute-start | bytes 294920 | tf_op jit(solution)/shard_map/ppermute | solution.py:429
  57.0 7.6 %collective-permute-start.16 = (f32[64,512]{1,0:T(8,128)S(1)}, f32[64,512]{1,0:T(8,128)S(1)}, u32[]{:S(2)}, u32[]{:S(2)}) collective-permute-start(f32[64,512]{1,0:T(8,128)S(1)} %add_rows.17.refs_2_), channel_id=1, source_target_pairs={{0,16},{1,17},{2,18},{3,19},{4,20},{5,21},{6,22},{7,23},{8,24},{9,... | collective-permute-start | bytes 393224 | tf_op jit(solution)/shard_map/ppermute | solution.py:429
  59.1 11.6 %collective-permute-start.21 = (f32[128,512]{1,0:T(8,128)S(1)}, f32[128,512]{1,0:T(8,128)S(1)}, u32[]{:S(2)}, u32[]{:S(2)}) collective-permute-start(f32[128,512]{1,0:T(8,128)S(1)} %pad_maximum_fusion.1.refs_0_.refs_4_), channel_id=1, source_target_pairs={{0,1},{1,0},{2,3},{3,2},{4,5},{5,4},{6,7},{7,6},{8,9},{9,8},{10,11... | collective-permute-start | bytes 786440 | tf_op jit(solution)/shard_map/ppermute | solution.py:429
  60.5 10.3 %collective-permute-start.19 = (f32[48,512]{1,0:T(8,128)S(1)}, f32[48,512]{1,0:T(8,128)S(1)}, u32[]{:S(2)}, u32[]{:S(2)}) collective-permute-start(f32[48,512]{1,0:T(8,128)S(1)} %add_rows.19.refs_3_), channel_id=1, source_target_pairs={{0,16},{1,17},{2,18},{3,19},{4,20},{5,21},{6,22},{7,23},{8,24},{9,... | collective-permute-start | bytes 294920 | tf_op jit(solution)/shard_map/ppermute | solution.py:429
  70.8 6.7 %collective-permute-start.22 = (f32[112,512]{1,0:T(8,128)S(1)}, f32[112,512]{1,0:T(8,128)S(1)}, u32[]{:S(2)}, u32[]{:S(2)}) collective-permute-start(f32[112,512]{1,0:T(8,128)S(1)} %pad_maximum_fusion.3.refs_0_.refs_5_), channel_id=1, source_target_pairs={{0,1},{1,0},{2,3},{3,2},{4,5},{5,4},{6,7},{7,6},{8,9},{9,8},{10,11... | collective-permute-start | bytes 688136 | tf_op jit(solution)/shard_map/ppermute | solution.py:429
  101.1 8.7 %collective-permute-start.40 = (f32[8,40,256]{2,1,0:T(8,128)S(1)}, f32[8,40,256]{2,1,0:T(8,128)S(1)}, u32[]{:S(2)}, u32[]{:S(2)}) collective-permute-start(f32[8,40,256]{2,1,0:T(8,128)S(1)} %pad_maximum_fusion.refs_0_), channel_id=1, source_target_pairs={{0,1},{1,0},{2,3},{3,2},{4,5},{5,4},{6,7},{7,6},{8,9},{9,8},{10,11... | collective-permute-start | bytes 983048 | tf_op jit(solution)/shard_map/ppermute | solution.py:429
  103.4 9.4 %collective-permute-start.36 = (f32[8,32,256]{2,1,0:T(8,128)S(1)}, f32[8,32,256]{2,1,0:T(8,128)S(1)}, u32[]{:S(2)}, u32[]{:S(2)}) collective-permute-start(f32[8,32,256]{2,1,0:T(8,128)S(1)} %pad_maximum_fusion.2.refs_0_), channel_id=1, source_target_pairs={{0,4},{1,5},{2,6},{3,7},{4,0},{5,1},{6,2},{7,3},{8,12},{9,13},{10,... | collective-permute-start | bytes 786440 | tf_op jit(solution)/shard_map/ppermute | solution.py:429
  103.7 12.0 %collective-permute-start.41 = (f32[8,40,256]{2,1,0:T(8,128)S(1)}, f32[8,40,256]{2,1,0:T(8,128)S(1)}, u32[]{:S(2)}, u32[]{:S(2)}) collective-permute-start(f32[8,40,256]{2,1,0:T(8,128)S(1)} %pad_maximum_fusion.refs_0_), channel_id=1, source_target_pairs={{0,2},{1,3},{2,0},{3,1},{4,6},{5,7},{6,4},{7,5},{8,10},{9,11},{10,... | collective-permute-start | bytes 983048 | tf_op jit(solution)/shard_map/ppermute | solution.py:429
  (20 other events, 88.1 us)

commit v8 on v7

--- a/solution.py
+++ b/solution.py
@@ -10,7 +10,7 @@
 
 BLOCK = 128
 GRAIN = 16
-CHUNKS = (3, 5, 4, 3)
+CHUNKS = (4, 4, 4, 3)
 LEAVE = (1, 3)
 STEPS = (
     ("sum", 0), ("halve", 0), ("sum", 1), ("sum", 2), ("halve", 1), ("finish", 0), ("sum", 3),

time: 121 us -> 124 us (1.025)
  waiting for transfers between devices: 51 us -> 57.9 us
  starting transfers between devices: 53.1 us -> 48.4 us
    ppermute x43, waiting for transfers between devices: 51 us -> 57.9 us  [flip(): lax.ppermute(value, ('dp', 'fsdp'), [(i, i ^ mask) for i in range(count)])]
    ppermute x43, starting transfers between devices: 53.1 us -> 48.4 us  [flip(): lax.ppermute(value, ('dp', 'fsdp'), [(i, i ^ mask) for i in range(count)])]
where the time goes in v8:
time: 124 us; the launch traced here: 123 us
  waiting for transfers between devices  57.9 us (47%)
  starting transfers between devices  48.4 us (39%)
  Pallas kernels  15.4 us (12%)
    ppermute x43, waiting for transfers between devices, flip(): lax.ppermute(value, ('dp', 'fsdp'), [(i, i ^ mask) for i in range(count)])  57.9 us
    ppermute x43, starting transfers between devices, flip(): lax.ppermute(value, ('dp', 'fsdp'), [(i, i ^ mask) for i in range(count)])  48.4 us
    pallas_call x4, Pallas kernels, gram_part(): pl.pallas_call(functools.partial(kernel, count, len(bases), early), in_sp...  4.29 us
    pallas_call x1, Pallas kernels, update(): pl.pallas_call(functools.partial(finish_kernel, scale, places, count), in...  3.43 us
    pallas_call x4, Pallas kernels, dequant(): pl.pallas_call(kernel, in_specs=[SCALARS] + [WHOLE] * 7 + [ANYWHERE] * (l...  2.99 us
    pallas_call x1, Pallas kernels, pack(): pl.pallas_call(functools.partial(pack_kernel, own_rows, spans), in_specs=...  2.5 us
  transfers between devices with their start and end apart: 43, of which 21 were waited for; matrix products, arithmetic and copies ran while one was open for 0% of the time, Pallas kernels for 8%

profile of v8, /device:TPU:1, one launch (start us, length us, event | category | flops | bytes accessed | tf_op | source)
XLA Modules:
  0.0 123.3 jit_solution(9896023806125512255)
XLA Ops:
  0.9 2.5 %pack_rows.1 = (bf16[960,512]{1,0:T(8,128)(2,1)S(1)}, f32[16,512]{1,0:T(8,128)S(1)}, bf16[1008,512]{1,0:T(8,128)(2,1)S(1)}, bf16[304,512]{1,0:T(8,128)(2,1)S(1)}...) custom-call(s32[4]{0:T(128)S(1)} %pad_add_fusion.at.refs_0_, ...), custom_call_target="tpu_custom_call" | custom-call | tf_op jit(solution)/shard_map/pack_rows/pallas_call | solution.py:126
  3.5 2.7 %collective-permute-start.1 = (bf16[304,512]{1,0:T(8,128)(2,1)S(1)}, bf16[304,512]{1,0:T(8,128)(2,1)S(1)}, u32[]{:S(2)}, u32[]{:S(2)}) collective-permute-start(bf16[304,512]{1,0:T(8,128)(2,1)S(1)} %get-tuple-element.44), channel_id=1, source_target_pairs={{0,4},{1,5},{2,6},{3,7},{4,0},{5,1},{6,2},{7,3},{8,12},{9,13},{10,... | collective-permute-start | bytes 933896 | tf_op jit(solution)/shard_map/ppermute | solution.py:429
  6.3 1.7 %collective-permute-start.5 = (bf16[256,512]{1,0:T(8,128)(2,1)S(1)}, bf16[256,512]{1,0:T(8,128)(2,1)S(1)}, u32[]{:S(2)}, u32[]{:S(2)}) collective-permute-start(bf16[256,512]{1,0:T(8,128)(2,1)S(1)} %get-tuple-element.50), channel_id=1, source_target_pairs={{0,4},{1,5},{2,6},{3,7},{4,0},{5,1},{6,2},{7,3},{8,12},{9,13},{10,... | collective-permute-start | bytes 786440 | tf_op jit(solution)/shard_map/ppermute | solution.py:429
  8.3 5.6 %collective-permute-done.1.refs_4_.refs_6_ = bf16[304,512]{1,0:T(8,128)(2,1)S(1)} collective-permute-done((bf16[304,512]{1,0:T(8,128)(2,1)S(1)}, bf16[304,512]{1,0:T(8,128)(2,1)S(1)}, u32[]{:S(2)}, u32[]{:S(2)}) %collective-permute-start.1) | collective-permute-done | bytes 311328 | tf_op jit(solution)/shard_map/ppermute | solution.py:429
  13.9 6.9 %collective-permute-done.2.refs_5_.refs_7_ = bf16[304,512]{1,0:T(8,128)(2,1)S(1)} collective-permute-done((bf16[304,512]{1,0:T(8,128)(2,1)S(1)}, bf16[304,512]{1,0:T(8,128)(2,1)S(1)}, u32[]{:S(2)}, u32[]{:S(2)}) %collective-permute-start.2) | collective-permute-done | bytes 311328 | tf_op jit(solution)/shard_map/ppermute | solution.py:429
  21.5 1.8 %collective-permute-start.8 = (f32[64,512]{1,0:T(8,128)S(1)}, f32[64,512]{1,0:T(8,128)S(1)}, u32[]{:S(2)}, u32[]{:S(2)}) collective-permute-start(f32[64,512]{1,0:T(8,128)S(1)} %get-tuple-element.54), channel_id=1, source_target_pairs={{0,8},{1,9},{2,10},{3,11},{4,12},{5,13},{6,14},{7,15},{8,0},{9,1},... | collective-permute-start | bytes 393224 | tf_op jit(solution)/shard_map/ppermute | solution.py:429
  24.8 5.1 %collective-permute-done.7.refs_1_ = f32[64,512]{1,0:T(8,128)S(1)} collective-permute-done((f32[64,512]{1,0:T(8,128)S(1)}, f32[64,512]{1,0:T(8,128)S(1)}, u32[]{:S(2)}, u32[]{:S(2)}) %collective-permute-start.7) | collective-permute-done | bytes 131104 | tf_op jit(solution)/shard_map/ppermute | solution.py:429
  29.9 2.0 %collective-permute-start.4 = (bf16[256,512]{1,0:T(8,128)(2,1)S(1)}, bf16[256,512]{1,0:T(8,128)(2,1)S(1)}, u32[]{:S(2)}, u32[]{:S(2)}) collective-permute-start(bf16[256,512]{1,0:T(8,128)(2,1)S(1)} %get-tuple-element.49), channel_id=1, source_target_pairs={{0,6},{1,7},{2,4},{3,5},{4,2},{5,3},{6,0},{7,1},{8,14},{9,15},{10,... | collective-permute-start | bytes 786440 | tf_op jit(solution)/shard_map/ppermute | solution.py:429
  31.9 2.4 %collective-permute-start.15 = (f32[64,512]{1,0:T(8,128)S(1)}, f32[64,512]{1,0:T(8,128)S(1)}, u32[]{:S(2)}, u32[]{:S(2)}) collective-permute-start(f32[64,512]{1,0:T(8,128)S(1)} %add_rows.14.refs_8_), channel_id=1, source_target_pairs={{0,16},{1,17},{2,18},{3,19},{4,20},{5,21},{6,22},{7,23},{8,24},{9,... | collective-permute-start | bytes 393224 | tf_op jit(solution)/shard_map/ppermute | solution.py:429
  36.6 8.0 %collective-permute-done.9.refs_8_ = f32[64,512]{1,0:T(8,128)S(1)} collective-permute-done((f32[64,512]{1,0:T(8,128)S(1)}, f32[64,512]{1,0:T(8,128)S(1)}, u32[]{:S(2)}, u32[]{:S(2)}) %collective-permute-start.9) | collective-permute-done | bytes 131104 | tf_op jit(solution)/shard_map/ppermute | solution.py:429
  44.8 2.5 %collective-permute-start.14 = (bf16[192,512]{1,0:T(8,128)(2,1)S(1)}, bf16[192,512]{1,0:T(8,128)(2,1)S(1)}, u32[]{:S(2)}, u32[]{:S(2)}) collective-permute-start(bf16[192,512]{1,0:T(8,128)(2,1)S(1)} %get-tuple-element.63), channel_id=1, source_target_pairs={{0,6},{1,7},{2,4},{3,5},{4,2},{5,3},{6,0},{7,1},{8,14},{9,15},{10,... | collective-permute-start | bytes 589832 | tf_op jit(solution)/shard_map/ppermute | solution.py:429
  51.2 4.5 %collective-permute-done.14.refs_7_ = bf16[192,512]{1,0:T(8,128)(2,1)S(1)} collective-permute-done((bf16[192,512]{1,0:T(8,128)(2,1)S(1)}, bf16[192,512]{1,0:T(8,128)(2,1)S(1)}, u32[]{:S(2)}, u32[]{:S(2)}) %collective-permute-start.14) | collective-permute-done | bytes 196640 | tf_op jit(solution)/shard_map/ppermute | solution.py:429
  65.9 4.5 %collective-permute-done.16.refs_1_ = f32[64,512]{1,0:T(8,128)S(1)} collective-permute-done((f32[64,512]{1,0:T(8,128)S(1)}, f32[64,512]{1,0:T(8,128)S(1)}, u32[]{:S(2)}, u32[]{:S(2)}) %collective-permute-start.16) | collective-permute-done | bytes 131104 | tf_op jit(solution)/shard_map/ppermute | solution.py:429
  70.4 2.1 %collective-permute-done.19.refs_1_ = f32[48,512]{1,0:T(8,128)S(1)} collective-permute-done((f32[48,512]{1,0:T(8,128)S(1)}, f32[48,512]{1,0:T(8,128)S(1)}, u32[]{:S(2)}, u32[]{:S(2)}) %collective-permute-start.19) | collective-permute-done | bytes 98336 | tf_op jit(solution)/shard_map/ppermute | solution.py:429
  89.3 1.8 %collective-permute-start.30 = (f32[2,32,256]{2,1,0:T(8,128)S(1)}, f32[2,32,256]{2,1,0:T(8,128)S(1)}, u32[]{:S(2)}, u32[]{:S(2)}) collective-permute-start(f32[2,32,256]{2,1,0:T(8,128)S(1)} %get-tuple-element.83), channel_id=1, source_target_pairs={{0,8},{1,9},{2,10},{3,11},{4,12},{5,13},{6,14},{7,15},{8,0},{9,1},... | collective-permute-start | bytes 196616 | tf_op jit(solution)/shard_map/ppermute | solution.py:429
  91.2 2.8 %collective-permute-done.30.refs_1_ = f32[2,32,256]{2,1,0:T(8,128)S(1)} collective-permute-done((f32[2,32,256]{2,1,0:T(8,128)S(1)}, f32[2,32,256]{2,1,0:T(8,128)S(1)}, u32[]{:S(2)}, u32[]{:S(2)}) %collective-permute-start.30) | collective-permute-done | bytes 65568 | tf_op jit(solution)/shard_map/ppermute | solution.py:429
  95.2 3.5 %collective-permute-done.32.refs_1_ = f32[2,32,256]{2,1,0:T(8,128)S(1)} collective-permute-done((f32[2,32,256]{2,1,0:T(8,128)S(1)}, f32[2,32,256]{2,1,0:T(8,128)S(1)}, u32[]{:S(2)}, u32[]{:S(2)}) %collective-permute-start.32) | collective-permute-done | bytes 65568 | tf_op jit(solution)/shard_map/ppermute | solution.py:429
  99.5 2.5 %collective-permute-done.34 = f32[2,32,256]{2,1,0:T(8,128)S(1)} collective-permute-done((f32[2,32,256]{2,1,0:T(8,128)S(1)}, f32[2,32,256]{2,1,0:T(8,128)S(1)}, u32[]{:S(2)}, u32[]{:S(2)}) %collective-permute-start.34) | collective-permute-done | bytes 65568 | tf_op jit(solution)/shard_map/ppermute | solution.py:429
  103.6 2.6 %collective-permute-done.35 = f32[4,32,256]{2,1,0:T(8,128)S(1)} collective-permute-done((f32[4,32,256]{2,1,0:T(8,128)S(1)}, f32[4,32,256]{2,1,0:T(8,128)S(1)}, u32[]{:S(2)}, u32[]{:S(2)}) %collective-permute-start.35) | collective-permute-done | bytes 131104 | tf_op jit(solution)/shard_map/ppermute | solution.py:429
  106.2 5.9 %collective-permute-start.41 = (f32[8,40,256]{2,1,0:T(8,128)S(1)}, f32[8,40,256]{2,1,0:T(8,128)S(1)}, u32[]{:S(2)}, u32[]{:S(2)}) collective-permute-start(f32[8,40,256]{2,1,0:T(8,128)S(1)} %pad_maximum_fusion.refs_0_), channel_id=1, source_target_pairs={{0,2},{1,3},{2,0},{3,1},{4,6},{5,7},{6,4},{7,5},{8,10},{9,11},{10,... | collective-permute-start | bytes 983048 | tf_op jit(solution)/shard_map/ppermute | solution.py:429
  112.1 2.8 %collective-permute-start.42 = (f32[8,40,256]{2,1,0:T(8,128)S(1)}, f32[8,40,256]{2,1,0:T(8,128)S(1)}, u32[]{:S(2)}, u32[]{:S(2)}) collective-permute-start(f32[8,40,256]{2,1,0:T(8,128)S(1)} %collective-permute-done.40.refs_1_), channel_id=1, source_target_pairs={{0,2},{1,3},{2,0},{3,1},{4,6},{5,7},{6,4},{7,5},{8,10},{9,11},{10,... | collective-permute-start | bytes 983048 | tf_op jit(solution)/shard_map/ppermute | solution.py:429
  115.0 2.9 %collective-permute-start.38 = (f32[8,32,256]{2,1,0:T(8,128)S(1)}, f32[8,32,256]{2,1,0:T(8,128)S(1)}, u32[]{:S(2)}, u32[]{:S(2)}) collective-permute-start(f32[8,32,256]{2,1,0:T(8,128)S(1)} %collective-permute-done.36.refs_1_), channel_id=1, source_target_pairs={{0,2},{1,3},{2,0},{3,1},{4,6},{5,7},{6,4},{7,5},{8,10},{9,11},{10,... | collective-permute-start | bytes 786440 | tf_op jit(solution)/shard_map/ppermute | solution.py:429
  117.9 2.0 %update_start.1 = (bf16[2,512,512]{2,1,0:T(8,128)(2,1)S(1)}, bf16[2,512,512]{2,1,0:T(8,128)(2,1)S(1)}, f32[8,128]{1,0:T(8,128)S(1)}, f32[240,512]{1,0:T(8,128)S(1)}, f32[240,512]{1,0:T(8,128)S(1)}) custom-call(s32[4]{0:T(128)S(1)} %pad_add_fusion.at.refs_0_, f32[8,40,256]{2,1,0:T(8,128)S(1)} %pad_maximum_fusion.refs_0_, ...), custom_call_target="tpu_custom_call" | custom-call | tf_op jit(solution)/shard_map/update_start/pallas_call | solution.py:401
  119.9 3.4 %update_finish.1 = bf16[240,512]{1,0:T(8,128)(2,1)} custom-call(s32[4]{0:T(128)S(1)} %pad_add_fusion.at.refs_0_, f32[8,32,256]{2,1,0:T(8,128)S(1)} %pad_maximum_fusion.2.refs_0_, f32[8,32,256]{2,1,0:T(8,128)S(1)} %collective-permute-done.36.refs_1_, f32[8,32,256]{2,1,0:T(8,128)S(1)} %collective-permute-done.37.refs_2_, ...), custom_call_target="tpu_custom_call" | custom-call | tf_op jit(solution)/shard_map/update_finish/pallas_call | solution.py:411
  (112 shorter events, 40.7 us)
Async XLA Ops:
  3.4 17.3 %collective-permute-start = (bf16[1008,512]{1,0:T(8,128)(2,1)S(1)}, bf16[1008,512]{1,0:T(8,128)(2,1)S(1)}, u32[]{:S(2)}, u32[]{:S(2)}) collective-permute-start(bf16[1008,512]{1,0:T(8,128)(2,1)S(1)} %get-tuple-element.43), channel_id=1, source_target_pairs={{0,2},{1,3},{2,0},{3,1},{4,6},{5,7},{6,4},{7,5},{8,10},{9,11},{10,... | collective-permute-start | bytes 3096584 | tf_op jit(solution)/shard_map/ppermute | solution.py:429
  3.5 10.3 %collective-permute-start.1 = (bf16[304,512]{1,0:T(8,128)(2,1)S(1)}, bf16[304,512]{1,0:T(8,128)(2,1)S(1)}, u32[]{:S(2)}, u32[]{:S(2)}) collective-permute-start(bf16[304,512]{1,0:T(8,128)(2,1)S(1)} %get-tuple-element.44), channel_id=1, source_target_pairs={{0,4},{1,5},{2,6},{3,7},{4,0},{5,1},{6,2},{7,3},{8,12},{9,13},{10,... | collective-permute-start | bytes 933896 | tf_op jit(solution)/shard_map/ppermute | solution.py:429
  6.2 14.5 %collective-permute-start.2 = (bf16[304,512]{1,0:T(8,128)(2,1)S(1)}, bf16[304,512]{1,0:T(8,128)(2,1)S(1)}, u32[]{:S(2)}, u32[]{:S(2)}) collective-permute-start(bf16[304,512]{1,0:T(8,128)(2,1)S(1)} %get-tuple-element.45), channel_id=1, source_target_pairs={{0,6},{1,7},{2,4},{3,5},{4,2},{5,3},{6,0},{7,1},{8,14},{9,15},{10,... | collective-permute-start | bytes 933896 | tf_op jit(solution)/shard_map/ppermute | solution.py:429
  6.3 28.0 %collective-permute-start.5 = (bf16[256,512]{1,0:T(8,128)(2,1)S(1)}, bf16[256,512]{1,0:T(8,128)(2,1)S(1)}, u32[]{:S(2)}, u32[]{:S(2)}) collective-permute-start(bf16[256,512]{1,0:T(8,128)(2,1)S(1)} %get-tuple-element.50), channel_id=1, source_target_pairs={{0,4},{1,5},{2,6},{3,7},{4,0},{5,1},{6,2},{7,3},{8,12},{9,13},{10,... | collective-permute-start | bytes 786440 | tf_op jit(solution)/shard_map/ppermute | solution.py:429
  7.9 26.4 %collective-permute-start.6 = (bf16[256,512]{1,0:T(8,128)(2,1)S(1)}, bf16[256,512]{1,0:T(8,128)(2,1)S(1)}, u32[]{:S(2)}, u32[]{:S(2)}) collective-permute-start(bf16[256,512]{1,0:T(8,128)(2,1)S(1)} %get-tuple-element.51), channel_id=1, source_target_pairs={{0,6},{1,7},{2,4},{3,5},{4,2},{5,3},{6,0},{7,1},{8,14},{9,15},{10,... | collective-permute-start | bytes 786440 | tf_op jit(solution)/shard_map/ppermute | solution.py:429
  21.5 10.4 %collective-permute-start.8 = (f32[64,512]{1,0:T(8,128)S(1)}, f32[64,512]{1,0:T(8,128)S(1)}, u32[]{:S(2)}, u32[]{:S(2)}) collective-permute-start(f32[64,512]{1,0:T(8,128)S(1)} %get-tuple-element.54), channel_id=1, source_target_pairs={{0,8},{1,9},{2,10},{3,11},{4,12},{5,13},{6,14},{7,15},{8,0},{9,1},... | collective-permute-start | bytes 393224 | tf_op jit(solution)/shard_map/ppermute | solution.py:429
  23.3 6.5 %collective-permute-start.7 = (f32[64,512]{1,0:T(8,128)S(1)}, f32[64,512]{1,0:T(8,128)S(1)}, u32[]{:S(2)}, u32[]{:S(2)}) collective-permute-start(f32[64,512]{1,0:T(8,128)S(1)} %get-tuple-element.53), channel_id=1, source_target_pairs={{0,8},{1,9},{2,10},{3,11},{4,12},{5,13},{6,14},{7,15},{8,0},{9,1},... | collective-permute-start | bytes 393224 | tf_op jit(solution)/shard_map/ppermute | solution.py:429
  23.4 23.8 %collective-permute-start.3 = (bf16[256,512]{1,0:T(8,128)(2,1)S(1)}, bf16[256,512]{1,0:T(8,128)(2,1)S(1)}, u32[]{:S(2)}, u32[]{:S(2)}) collective-permute-start(bf16[256,512]{1,0:T(8,128)(2,1)S(1)} %get-tuple-element.48), channel_id=1, source_target_pairs={{0,4},{1,5},{2,6},{3,7},{4,0},{5,1},{6,2},{7,3},{8,12},{9,13},{10,... | collective-permute-start | bytes 786440 | tf_op jit(solution)/shard_map/ppermute | solution.py:429
  29.9 17.4 %collective-permute-start.4 = (bf16[256,512]{1,0:T(8,128)(2,1)S(1)}, bf16[256,512]{1,0:T(8,128)(2,1)S(1)}, u32[]{:S(2)}, u32[]{:S(2)}) collective-permute-start(bf16[256,512]{1,0:T(8,128)(2,1)S(1)} %get-tuple-element.49), channel_id=1, source_target_pairs={{0,6},{1,7},{2,4},{3,5},{4,2},{5,3},{6,0},{7,1},{8,14},{9,15},{10,... | collective-permute-start | bytes 786440 | tf_op jit(solution)/shard_map/ppermute | solution.py:429
  31.9 17.7 %collective-permute-start.15 = (f32[64,512]{1,0:T(8,128)S(1)}, f32[64,512]{1,0:T(8,128)S(1)}, u32[]{:S(2)}, u32[]{:S(2)}) collective-permute-start(f32[64,512]{1,0:T(8,128)S(1)} %add_rows.14.refs_8_), channel_id=1, source_target_pairs={{0,16},{1,17},{2,18},{3,19},{4,20},{5,21},{6,22},{7,23},{8,24},{9,... | collective-permute-start | bytes 393224 | tf_op jit(solution)/shard_map/ppermute | solution.py:429
  35.1 9.7 %collective-permute-start.10 = (f32[64,512]{1,0:T(8,128)S(1)}, f32[64,512]{1,0:T(8,128)S(1)}, u32[]{:S(2)}, u32[]{:S(2)}) collective-permute-start(f32[64,512]{1,0:T(8,128)S(1)} %get-tuple-element.58), channel_id=1, source_target_pairs={{0,8},{1,9},{2,10},{3,11},{4,12},{5,13},{6,14},{7,15},{8,0},{9,1},... | collective-permute-start | bytes 393224 | tf_op jit(solution)/shard_map/ppermute | solution.py:429
  36.4 8.2 %collective-permute-start.9 = (f32[64,512]{1,0:T(8,128)S(1)}, f32[64,512]{1,0:T(8,128)S(1)}, u32[]{:S(2)}, u32[]{:S(2)}) collective-permute-start(f32[64,512]{1,0:T(8,128)S(1)} %get-tuple-element.57), channel_id=1, source_target_pairs={{0,8},{1,9},{2,10},{3,11},{4,12},{5,13},{6,14},{7,15},{8,0},{9,1},... | collective-permute-start | bytes 393224 | tf_op jit(solution)/shard_map/ppermute | solution.py:429
  44.6 6.6 %collective-permute-start.13 = (bf16[192,512]{1,0:T(8,128)(2,1)S(1)}, bf16[192,512]{1,0:T(8,128)(2,1)S(1)}, u32[]{:S(2)}, u32[]{:S(2)}) collective-permute-start(bf16[192,512]{1,0:T(8,128)(2,1)S(1)} %get-tuple-element.62), channel_id=1, source_target_pairs={{0,4},{1,5},{2,6},{3,7},{4,0},{5,1},{6,2},{7,3},{8,12},{9,13},{10,... | collective-permute-start | bytes 589832 | tf_op jit(solution)/shard_map/ppermute | solution.py:429
  44.8 10.9 %collective-permute-start.14 = (bf16[192,512]{1,0:T(8,128)(2,1)S(1)}, bf16[192,512]{1,0:T(8,128)(2,1)S(1)}, u32[]{:S(2)}, u32[]{:S(2)}) collective-permute-start(bf16[192,512]{1,0:T(8,128)(2,1)S(1)} %get-tuple-element.63), channel_id=1, source_target_pairs={{0,6},{1,7},{2,4},{3,5},{4,2},{5,3},{6,0},{7,1},{8,14},{9,15},{10,... | collective-permute-start | bytes 589832 | tf_op jit(solution)/shard_map/ppermute | solution.py:429
  48.0 14.7 %collective-permute-start.11 = (f32[64,512]{1,0:T(8,128)S(1)}, f32[64,512]{1,0:T(8,128)S(1)}, u32[]{:S(2)}, u32[]{:S(2)}) collective-permute-start(f32[64,512]{1,0:T(8,128)S(1)} %get-tuple-element.60), channel_id=1, source_target_pairs={{0,8},{1,9},{2,10},{3,11},{4,12},{5,13},{6,14},{7,15},{8,0},{9,1},... | collective-permute-start | bytes 393224 | tf_op jit(solution)/shard_map/ppermute | solution.py:429
  48.4 10.9 %collective-permute-start.12 = (f32[64,512]{1,0:T(8,128)S(1)}, f32[64,512]{1,0:T(8,128)S(1)}, u32[]{:S(2)}, u32[]{:S(2)}) collective-permute-start(f32[64,512]{1,0:T(8,128)S(1)} %get-tuple-element.61), channel_id=1, source_target_pairs={{0,8},{1,9},{2,10},{3,11},{4,12},{5,13},{6,14},{7,15},{8,0},{9,1},... | collective-permute-start | bytes 393224 | tf_op jit(solution)/shard_map/ppermute | solution.py:429
  49.6 11.8 %collective-permute-start.20 = (f32[64,512]{1,0:T(8,128)S(1)}, f32[64,512]{1,0:T(8,128)S(1)}, u32[]{:S(2)}, u32[]{:S(2)}) collective-permute-start(f32[64,512]{1,0:T(8,128)S(1)} %add_rows.15.refs_8_), channel_id=1, source_target_pairs={{0,16},{1,17},{2,18},{3,19},{4,20},{5,21},{6,22},{7,23},{8,24},{9,... | collective-permute-start | bytes 393224 | tf_op jit(solution)/shard_map/ppermute | solution.py:429
  57.0 7.8 %collective-permute-start.17 = (f32[48,512]{1,0:T(8,128)S(1)}, f32[48,512]{1,0:T(8,128)S(1)}, u32[]{:S(2)}, u32[]{:S(2)}) collective-permute-start(f32[48,512]{1,0:T(8,128)S(1)} %get-tuple-element.66), channel_id=1, source_target_pairs={{0,8},{1,9},{2,10},{3,11},{4,12},{5,13},{6,14},{7,15},{8,0},{9,1},... | collective-permute-start | bytes 294920 | tf_op jit(solution)/shard_map/ppermute | solution.py:429
  59.3 11.1 %collective-permute-start.16 = (f32[64,512]{1,0:T(8,128)S(1)}, f32[64,512]{1,0:T(8,128)S(1)}, u32[]{:S(2)}, u32[]{:S(2)}) collective-permute-start(f32[64,512]{1,0:T(8,128)S(1)} %add_rows.17.refs_2_), channel_id=1, source_target_pairs={{0,16},{1,17},{2,18},{3,19},{4,20},{5,21},{6,22},{7,23},{8,24},{9,... | collective-permute-start | bytes 393224 | tf_op jit(solution)/shard_map/ppermute | solution.py:429
  61.4 11.1 %collective-permute-start.21 = (f32[128,512]{1,0:T(8,128)S(1)}, f32[128,512]{1,0:T(8,128)S(1)}, u32[]{:S(2)}, u32[]{:S(2)}) collective-permute-start(f32[128,512]{1,0:T(8,128)S(1)} %pad_maximum_fusion.1.refs_0_.refs_4_), channel_id=1, source_target_pairs={{0,1},{1,0},{2,3},{3,2},{4,5},{5,4},{6,7},{7,6},{8,9},{9,8},{10,11... | collective-permute-start | bytes 786440 | tf_op jit(solution)/shard_map/ppermute | solution.py:429
  62.8 9.8 %collective-permute-start.19 = (f32[48,512]{1,0:T(8,128)S(1)}, f32[48,512]{1,0:T(8,128)S(1)}, u32[]{:S(2)}, u32[]{:S(2)}) collective-permute-start(f32[48,512]{1,0:T(8,128)S(1)} %add_rows.19.refs_3_), channel_id=1, source_target_pairs={{0,16},{1,17},{2,18},{3,19},{4,20},{5,21},{6,22},{7,23},{8,24},{9,... | collective-permute-start | bytes 294920 | tf_op jit(solution)/shard_map/ppermute | solution.py:429
  103.1 9.0 %collective-permute-start.40 = (f32[8,40,256]{2,1,0:T(8,128)S(1)}, f32[8,40,256]{2,1,0:T(8,128)S(1)}, u32[]{:S(2)}, u32[]{:S(2)}) collective-permute-start(f32[8,40,256]{2,1,0:T(8,128)S(1)} %pad_maximum_fusion.refs_0_), channel_id=1, source_target_pairs={{0,1},{1,0},{2,3},{3,2},{4,5},{5,4},{6,7},{7,6},{8,9},{9,8},{10,11... | collective-permute-start | bytes 983048 | tf_op jit(solution)/shard_map/ppermute | solution.py:429
  106.2 8.8 %collective-permute-start.36 = (f32[8,32,256]{2,1,0:T(8,128)S(1)}, f32[8,32,256]{2,1,0:T(8,128)S(1)}, u32[]{:S(2)}, u32[]{:S(2)}) collective-permute-start(f32[8,32,256]{2,1,0:T(8,128)S(1)} %pad_maximum_fusion.2.refs_0_), channel_id=1, source_target_pairs={{0,4},{1,5},{2,6},{3,7},{4,0},{5,1},{6,2},{7,3},{8,12},{9,13},{10,... | collective-permute-start | bytes 786440 | tf_op jit(solution)/shard_map/ppermute | solution.py:429
  106.2 11.7 %collective-permute-start.41 = (f32[8,40,256]{2,1,0:T(8,128)S(1)}, f32[8,40,256]{2,1,0:T(8,128)S(1)}, u32[]{:S(2)}, u32[]{:S(2)}) collective-permute-start(f32[8,40,256]{2,1,0:T(8,128)S(1)} %pad_maximum_fusion.refs_0_), channel_id=1, source_target_pairs={{0,2},{1,3},{2,0},{3,1},{4,6},{5,7},{6,4},{7,5},{8,10},{9,11},{10,... | collective-permute-start | bytes 983048 | tf_op jit(solution)/shard_map/ppermute | solution.py:429
  (20 other events, 88.7 us)

commit v9 on v8

--- a/solution.py
+++ b/solution.py
@@ -10,7 +10,7 @@
 
 BLOCK = 128
 GRAIN = 16
-CHUNKS = (4, 4, 4, 3)
+CHUNKS = (2, 5, 4, 4)
 LEAVE = (1, 3)
 STEPS = (
     ("sum", 0), ("halve", 0), ("sum", 1), ("sum", 2), ("halve", 1), ("finish", 0), ("sum", 3),

time: 124 us -> 122 us (0.984)
  waiting for transfers between devices: 57.9 us -> 40.2 us
  starting transfers between devices: 48.4 us -> 64.5 us
    ppermute x43, waiting for transfers between devices: 57.9 us -> 40.2 us  [flip(): lax.ppermute(value, ('dp', 'fsdp'), [(i, i ^ mask) for i in range(count)])]
    ppermute x43, starting transfers between devices: 48.4 us -> 64.5 us  [flip(): lax.ppermute(value, ('dp', 'fsdp'), [(i, i ^ mask) for i in range(count)])]
  transfers between devices with their start and end apart: 43 -> 43, of which waited for: 21 -> 22; matrix products, arithmetic and copies ran while one was open for 0% -> 0% of each run, Pallas kernels for 8% -> 8%
where the time goes in v9:
time: 122 us
  starting transfers between devices  64.5 us (53%)
  waiting for transfers between devices  40.2 us (33%)
  Pallas kernels  15.4 us (13%)
    ppermute x43, starting transfers between devices, flip(): lax.ppermute(value, ('dp', 'fsdp'), [(i, i ^ mask) for i in range(count)])  64.5 us
    ppermute x43, waiting for transfers between devices, flip(): lax.ppermute(value, ('dp', 'fsdp'), [(i, i ^ mask) for i in range(count)])  40.2 us
    pallas_call x4, Pallas kernels, gram_part(): pl.pallas_call(functools.partial(kernel, count, len(bases), early), in_sp...  4.29 us
    pallas_call x1, Pallas kernels, update(): pl.pallas_call(functools.partial(finish_kernel, scale, places, count), in...  3.43 us
    pallas_call x4, Pallas kernels, dequant(): pl.pallas_call(kernel, in_specs=[SCALARS] + [WHOLE] * 7 + [ANYWHERE] * (l...  2.97 us
    pallas_call x1, Pallas kernels, pack(): pl.pallas_call(functools.partial(pack_kernel, own_rows, spans), in_specs=...  2.51 us
  transfers between devices with their start and end apart: 43, of which 22 were waited for; matrix products, arithmetic and copies ran while one was open for 0% of the time, Pallas kernels for 8%

profile of v9, /device:TPU:1, one launch (start us, length us, event | category | flops | bytes accessed | tf_op | source)
XLA Modules:
  0.0 121.7 jit_solution(6621916896501097968)
XLA Ops:
  0.9 2.5 %pack_rows.1 = (bf16[960,512]{1,0:T(8,128)(2,1)S(1)}, f32[16,512]{1,0:T(8,128)S(1)}, bf16[1008,512]{1,0:T(8,128)(2,1)S(1)}, bf16[176,512]{1,0:T(8,128)(2,1)S(1)}...) custom-call(s32[4]{0:T(128)S(1)} %pad_add_fusion.at.refs_0_, ...), custom_call_target="tpu_custom_call" | custom-call | tf_op jit(solution)/shard_map/pack_rows/pallas_call | solution.py:126
  3.5 2.7 %collective-permute-start.1 = (bf16[176,512]{1,0:T(8,128)(2,1)S(1)}, bf16[176,512]{1,0:T(8,128)(2,1)S(1)}, u32[]{:S(2)}, u32[]{:S(2)}) collective-permute-start(bf16[176,512]{1,0:T(8,128)(2,1)S(1)} %get-tuple-element.44), channel_id=1, source_target_pairs={{0,4},{1,5},{2,6},{3,7},{4,0},{5,1},{6,2},{7,3},{8,12},{9,13},{10,... | collective-permute-start | bytes 540680 | tf_op jit(solution)/shard_map/ppermute | solution.py:429
  8.3 2.8 %collective-permute-done.1.refs_4_.refs_6_ = bf16[176,512]{1,0:T(8,128)(2,1)S(1)} collective-permute-done((bf16[176,512]{1,0:T(8,128)(2,1)S(1)}, bf16[176,512]{1,0:T(8,128)(2,1)S(1)}, u32[]{:S(2)}, u32[]{:S(2)}) %collective-permute-start.1) | collective-permute-done | bytes 180256 | tf_op jit(solution)/shard_map/ppermute | solution.py:429
  11.1 4.1 %collective-permute-done.2.refs_5_.refs_7_ = bf16[176,512]{1,0:T(8,128)(2,1)S(1)} collective-permute-done((bf16[176,512]{1,0:T(8,128)(2,1)S(1)}, bf16[176,512]{1,0:T(8,128)(2,1)S(1)}, u32[]{:S(2)}, u32[]{:S(2)}) %collective-permute-start.2) | collective-permute-done | bytes 180256 | tf_op jit(solution)/shard_map/ppermute | solution.py:429
  19.0 2.3 %collective-permute-done.7.refs_1_ = f32[32,512]{1,0:T(8,128)S(1)} collective-permute-done((f32[32,512]{1,0:T(8,128)S(1)}, f32[32,512]{1,0:T(8,128)S(1)}, u32[]{:S(2)}, u32[]{:S(2)}) %collective-permute-start.7) | collective-permute-done | bytes 65568 | tf_op jit(solution)/shard_map/ppermute | solution.py:429
  21.3 2.1 %collective-permute-start.4 = (bf16[256,512]{1,0:T(8,128)(2,1)S(1)}, bf16[256,512]{1,0:T(8,128)(2,1)S(1)}, u32[]{:S(2)}, u32[]{:S(2)}) collective-permute-start(bf16[256,512]{1,0:T(8,128)(2,1)S(1)} %get-tuple-element.49), channel_id=1, source_target_pairs={{0,6},{1,7},{2,4},{3,5},{4,2},{5,3},{6,0},{7,1},{8,14},{9,15},{10,... | collective-permute-start | bytes 786440 | tf_op jit(solution)/shard_map/ppermute | solution.py:429
  23.4 2.4 %collective-permute-start.15 = (f32[32,512]{1,0:T(8,128)S(1)}, f32[32,512]{1,0:T(8,128)S(1)}, u32[]{:S(2)}, u32[]{:S(2)}) collective-permute-start(f32[32,512]{1,0:T(8,128)S(1)} %add_rows.14.refs_8_), channel_id=1, source_target_pairs={{0,16},{1,17},{2,18},{3,19},{4,20},{5,21},{6,22},{7,23},{8,24},{9,... | collective-permute-start | bytes 196616 | tf_op jit(solution)/shard_map/ppermute | solution.py:429
  25.8 3.7 %collective-permute-done.6.refs_7_ = bf16[320,512]{1,0:T(8,128)(2,1)S(1)} collective-permute-done((bf16[320,512]{1,0:T(8,128)(2,1)S(1)}, bf16[320,512]{1,0:T(8,128)(2,1)S(1)}, u32[]{:S(2)}, u32[]{:S(2)}) %collective-permute-start.6) | collective-permute-done | bytes 327712 | tf_op jit(solution)/shard_map/ppermute | solution.py:429
  31.9 4.3 %collective-permute-done.10.refs_9_.refs_1_ = f32[80,512]{1,0:T(8,128)S(1)} collective-permute-done((f32[80,512]{1,0:T(8,128)S(1)}, f32[80,512]{1,0:T(8,128)S(1)}, u32[]{:S(2)}, u32[]{:S(2)}) %collective-permute-start.10) | collective-permute-done | bytes 163872 | tf_op jit(solution)/shard_map/ppermute | solution.py:429
  37.7 2.0 %collective-permute-done.9.refs_8_ = f32[80,512]{1,0:T(8,128)S(1)} collective-permute-done((f32[80,512]{1,0:T(8,128)S(1)}, f32[80,512]{1,0:T(8,128)S(1)}, u32[]{:S(2)}, u32[]{:S(2)}) %collective-permute-start.9) | collective-permute-done | bytes 163872 | tf_op jit(solution)/shard_map/ppermute | solution.py:429
  39.7 2.0 %collective-permute-start.14 = (bf16[256,512]{1,0:T(8,128)(2,1)S(1)}, bf16[256,512]{1,0:T(8,128)(2,1)S(1)}, u32[]{:S(2)}, u32[]{:S(2)}) collective-permute-start(bf16[256,512]{1,0:T(8,128)(2,1)S(1)} %get-tuple-element.63), channel_id=1, source_target_pairs={{0,6},{1,7},{2,4},{3,5},{4,2},{5,3},{6,0},{7,1},{8,14},{9,15},{10,... | collective-permute-start | bytes 786440 | tf_op jit(solution)/shard_map/ppermute | solution.py:429
  44.1 2.4 %collective-permute-start.20 = (f32[80,512]{1,0:T(8,128)S(1)}, f32[80,512]{1,0:T(8,128)S(1)}, u32[]{:S(2)}, u32[]{:S(2)}) collective-permute-start(f32[80,512]{1,0:T(8,128)S(1)} %add_rows.15.refs_8_), channel_id=1, source_target_pairs={{0,16},{1,17},{2,18},{3,19},{4,20},{5,21},{6,22},{7,23},{8,24},{9,... | collective-permute-start | bytes 491528 | tf_op jit(solution)/shard_map/ppermute | solution.py:429
  46.5 5.2 %collective-permute-done.14.refs_7_ = bf16[256,512]{1,0:T(8,128)(2,1)S(1)} collective-permute-done((bf16[256,512]{1,0:T(8,128)(2,1)S(1)}, bf16[256,512]{1,0:T(8,128)(2,1)S(1)}, u32[]{:S(2)}, u32[]{:S(2)}) %collective-permute-start.14) | collective-permute-done | bytes 262176 | tf_op jit(solution)/shard_map/ppermute | solution.py:429
  54.1 2.5 %collective-permute-start.16 = (f32[64,512]{1,0:T(8,128)S(1)}, f32[64,512]{1,0:T(8,128)S(1)}, u32[]{:S(2)}, u32[]{:S(2)}) collective-permute-start(f32[64,512]{1,0:T(8,128)S(1)} %add_rows.17.refs_2_), channel_id=1, source_target_pairs={{0,16},{1,17},{2,18},{3,19},{4,20},{5,21},{6,22},{7,23},{8,24},{9,... | collective-permute-start | bytes 393224 | tf_op jit(solution)/shard_map/ppermute | solution.py:429
  57.5 2.9 %collective-permute-start.19 = (f32[64,512]{1,0:T(8,128)S(1)}, f32[64,512]{1,0:T(8,128)S(1)}, u32[]{:S(2)}, u32[]{:S(2)}) collective-permute-start(f32[64,512]{1,0:T(8,128)S(1)} %add_rows.19.refs_3_), channel_id=1, source_target_pairs={{0,16},{1,17},{2,18},{3,19},{4,20},{5,21},{6,22},{7,23},{8,24},{9,... | collective-permute-start | bytes 393224 | tf_op jit(solution)/shard_map/ppermute | solution.py:429
  67.9 5.5 %collective-permute-start.23 = (f32[4,40,256]{2,1,0:T(8,128)S(1)}, f32[4,40,256]{2,1,0:T(8,128)S(1)}, u32[]{:S(2)}, u32[]{:S(2)}) collective-permute-start(f32[4,40,256]{2,1,0:T(8,128)S(1)} %get-tuple-element.78), channel_id=1, source_target_pairs={{0,2},{1,3},{2,0},{3,1},{4,6},{5,7},{6,4},{7,5},{8,10},{9,11},{10,... | collective-permute-start | bytes 491528 | tf_op jit(solution)/shard_map/ppermute | solution.py:429
  85.8 2.2 %collective-permute-done.26.refs_2_ = f32[4,32,256]{2,1,0:T(8,128)S(1)} collective-permute-done((f32[4,32,256]{2,1,0:T(8,128)S(1)}, f32[4,32,256]{2,1,0:T(8,128)S(1)}, u32[]{:S(2)}, u32[]{:S(2)}) %collective-permute-start.26) | collective-permute-done | bytes 131104 | tf_op jit(solution)/shard_map/ppermute | solution.py:429
  93.3 2.5 %collective-permute-done.32.refs_1_ = f32[2,32,256]{2,1,0:T(8,128)S(1)} collective-permute-done((f32[2,32,256]{2,1,0:T(8,128)S(1)}, f32[2,32,256]{2,1,0:T(8,128)S(1)}, u32[]{:S(2)}, u32[]{:S(2)}) %collective-permute-start.32) | collective-permute-done | bytes 65568 | tf_op jit(solution)/shard_map/ppermute | solution.py:429
  100.7 2.5 %collective-permute-start.40 = (f32[8,40,256]{2,1,0:T(8,128)S(1)}, f32[8,40,256]{2,1,0:T(8,128)S(1)}, u32[]{:S(2)}, u32[]{:S(2)}) collective-permute-start(f32[8,40,256]{2,1,0:T(8,128)S(1)} %pad_maximum_fusion.refs_0_), channel_id=1, source_target_pairs={{0,1},{1,0},{2,3},{3,2},{4,5},{5,4},{6,7},{7,6},{8,9},{9,8},{10,11... | collective-permute-start | bytes 983048 | tf_op jit(solution)/shard_map/ppermute | solution.py:429
  105.1 6.0 %collective-permute-start.41 = (f32[8,40,256]{2,1,0:T(8,128)S(1)}, f32[8,40,256]{2,1,0:T(8,128)S(1)}, u32[]{:S(2)}, u32[]{:S(2)}) collective-permute-start(f32[8,40,256]{2,1,0:T(8,128)S(1)} %pad_maximum_fusion.refs_0_), channel_id=1, source_target_pairs={{0,2},{1,3},{2,0},{3,1},{4,6},{5,7},{6,4},{7,5},{8,10},{9,11},{10,... | collective-permute-start | bytes 983048 | tf_op jit(solution)/shard_map/ppermute | solution.py:429
  111.1 2.2 %collective-permute-start.42 = (f32[8,40,256]{2,1,0:T(8,128)S(1)}, f32[8,40,256]{2,1,0:T(8,128)S(1)}, u32[]{:S(2)}, u32[]{:S(2)}) collective-permute-start(f32[8,40,256]{2,1,0:T(8,128)S(1)} %collective-permute-done.40.refs_1_), channel_id=1, source_target_pairs={{0,2},{1,3},{2,0},{3,1},{4,6},{5,7},{6,4},{7,5},{8,10},{9,11},{10,... | collective-permute-start | bytes 983048 | tf_op jit(solution)/shard_map/ppermute | solution.py:429
  113.3 2.9 %collective-permute-start.38 = (f32[8,32,256]{2,1,0:T(8,128)S(1)}, f32[8,32,256]{2,1,0:T(8,128)S(1)}, u32[]{:S(2)}, u32[]{:S(2)}) collective-permute-start(f32[8,32,256]{2,1,0:T(8,128)S(1)} %collective-permute-done.36.refs_1_), channel_id=1, source_target_pairs={{0,2},{1,3},{2,0},{3,1},{4,6},{5,7},{6,4},{7,5},{8,10},{9,11},{10,... | collective-permute-start | bytes 786440 | tf_op jit(solution)/shard_map/ppermute | solution.py:429
  116.3 2.0 %update_start.1 = (bf16[2,512,512]{2,1,0:T(8,128)(2,1)S(1)}, bf16[2,512,512]{2,1,0:T(8,128)(2,1)S(1)}, f32[8,128]{1,0:T(8,128)S(1)}, f32[240,512]{1,0:T(8,128)S(1)}, f32[240,512]{1,0:T(8,128)S(1)}) custom-call(s32[4]{0:T(128)S(1)} %pad_add_fusion.at.refs_0_, f32[8,40,256]{2,1,0:T(8,128)S(1)} %pad_maximum_fusion.refs_0_, ...), custom_call_target="tpu_custom_call" | custom-call | tf_op jit(solution)/shard_map/update_start/pallas_call | solution.py:401
  118.3 3.4 %update_finish.1 = bf16[240,512]{1,0:T(8,128)(2,1)} custom-call(s32[4]{0:T(128)S(1)} %pad_add_fusion.at.refs_0_, f32[8,32,256]{2,1,0:T(8,128)S(1)} %pad_maximum_fusion.2.refs_0_, f32[8,32,256]{2,1,0:T(8,128)S(1)} %collective-permute-done.36.refs_1_, f32[8,32,256]{2,1,0:T(8,128)S(1)} %collective-permute-done.37.refs_2_, ...), custom_call_target="tpu_custom_call" | custom-call | tf_op jit(solution)/shard_map/update_finish/pallas_call | solution.py:411
  (112 shorter events, 48.3 us)
Async XLA Ops:
  3.4 11.7 %collective-permute-start = (bf16[1008,512]{1,0:T(8,128)(2,1)S(1)}, bf16[1008,512]{1,0:T(8,128)(2,1)S(1)}, u32[]{:S(2)}, u32[]{:S(2)}) collective-permute-start(bf16[1008,512]{1,0:T(8,128)(2,1)S(1)} %get-tuple-element.43), channel_id=1, source_target_pairs={{0,2},{1,3},{2,0},{3,1},{4,6},{5,7},{6,4},{7,5},{8,10},{9,11},{10,... | collective-permute-start | bytes 3096584 | tf_op jit(solution)/shard_map/ppermute | solution.py:429
  3.5 7.5 %collective-permute-start.1 = (bf16[176,512]{1,0:T(8,128)(2,1)S(1)}, bf16[176,512]{1,0:T(8,128)(2,1)S(1)}, u32[]{:S(2)}, u32[]{:S(2)}) collective-permute-start(bf16[176,512]{1,0:T(8,128)(2,1)S(1)} %get-tuple-element.44), channel_id=1, source_target_pairs={{0,4},{1,5},{2,6},{3,7},{4,0},{5,1},{6,2},{7,3},{8,12},{9,13},{10,... | collective-permute-start | bytes 540680 | tf_op jit(solution)/shard_map/ppermute | solution.py:429
  6.2 8.9 %collective-permute-start.2 = (bf16[176,512]{1,0:T(8,128)(2,1)S(1)}, bf16[176,512]{1,0:T(8,128)(2,1)S(1)}, u32[]{:S(2)}, u32[]{:S(2)}) collective-permute-start(bf16[176,512]{1,0:T(8,128)(2,1)S(1)} %get-tuple-element.45), channel_id=1, source_target_pairs={{0,6},{1,7},{2,4},{3,5},{4,2},{5,3},{6,0},{7,1},{8,14},{9,15},{10,... | collective-permute-start | bytes 540680 | tf_op jit(solution)/shard_map/ppermute | solution.py:429
  6.3 19.5 %collective-permute-start.5 = (bf16[320,512]{1,0:T(8,128)(2,1)S(1)}, bf16[320,512]{1,0:T(8,128)(2,1)S(1)}, u32[]{:S(2)}, u32[]{:S(2)}) collective-permute-start(bf16[320,512]{1,0:T(8,128)(2,1)S(1)} %get-tuple-element.50), channel_id=1, source_target_pairs={{0,4},{1,5},{2,6},{3,7},{4,0},{5,1},{6,2},{7,3},{8,12},{9,13},{10,... | collective-permute-start | bytes 983048 | tf_op jit(solution)/shard_map/ppermute | solution.py:429
  7.9 21.6 %collective-permute-start.6 = (bf16[320,512]{1,0:T(8,128)(2,1)S(1)}, bf16[320,512]{1,0:T(8,128)(2,1)S(1)}, u32[]{:S(2)}, u32[]{:S(2)}) collective-permute-start(bf16[320,512]{1,0:T(8,128)(2,1)S(1)} %get-tuple-element.51), channel_id=1, source_target_pairs={{0,6},{1,7},{2,4},{3,5},{4,2},{5,3},{6,0},{7,1},{8,14},{9,15},{10,... | collective-permute-start | bytes 983048 | tf_op jit(solution)/shard_map/ppermute | solution.py:429
  15.8 7.5 %collective-permute-start.8 = (f32[32,512]{1,0:T(8,128)S(1)}, f32[32,512]{1,0:T(8,128)S(1)}, u32[]{:S(2)}, u32[]{:S(2)}) collective-permute-start(f32[32,512]{1,0:T(8,128)S(1)} %get-tuple-element.54), channel_id=1, source_target_pairs={{0,8},{1,9},{2,10},{3,11},{4,12},{5,13},{6,14},{7,15},{8,0},{9,1},... | collective-permute-start | bytes 196616 | tf_op jit(solution)/shard_map/ppermute | solution.py:429
  17.7 24.0 %collective-permute-start.3 = (bf16[256,512]{1,0:T(8,128)(2,1)S(1)}, bf16[256,512]{1,0:T(8,128)(2,1)S(1)}, u32[]{:S(2)}, u32[]{:S(2)}) collective-permute-start(bf16[256,512]{1,0:T(8,128)(2,1)S(1)} %get-tuple-element.48), channel_id=1, source_target_pairs={{0,4},{1,5},{2,6},{3,7},{4,0},{5,1},{6,2},{7,3},{8,12},{9,13},{10,... | collective-permute-start | bytes 786440 | tf_op jit(solution)/shard_map/ppermute | solution.py:429
  21.3 20.5 %collective-permute-start.4 = (bf16[256,512]{1,0:T(8,128)(2,1)S(1)}, bf16[256,512]{1,0:T(8,128)(2,1)S(1)}, u32[]{:S(2)}, u32[]{:S(2)}) collective-permute-start(bf16[256,512]{1,0:T(8,128)(2,1)S(1)} %get-tuple-element.49), channel_id=1, source_target_pairs={{0,6},{1,7},{2,4},{3,5},{4,2},{5,3},{6,0},{7,1},{8,14},{9,15},{10,... | collective-permute-start | bytes 786440 | tf_op jit(solution)/shard_map/ppermute | solution.py:429
  23.4 20.7 %collective-permute-start.15 = (f32[32,512]{1,0:T(8,128)S(1)}, f32[32,512]{1,0:T(8,128)S(1)}, u32[]{:S(2)}, u32[]{:S(2)}) collective-permute-start(f32[32,512]{1,0:T(8,128)S(1)} %add_rows.14.refs_8_), channel_id=1, source_target_pairs={{0,16},{1,17},{2,18},{3,19},{4,20},{5,21},{6,22},{7,23},{8,24},{9,... | collective-permute-start | bytes 196616 | tf_op jit(solution)/shard_map/ppermute | solution.py:429
  30.3 6.0 %collective-permute-start.10 = (f32[80,512]{1,0:T(8,128)S(1)}, f32[80,512]{1,0:T(8,128)S(1)}, u32[]{:S(2)}, u32[]{:S(2)}) collective-permute-start(f32[80,512]{1,0:T(8,128)S(1)} %get-tuple-element.58), channel_id=1, source_target_pairs={{0,8},{1,9},{2,10},{3,11},{4,12},{5,13},{6,14},{7,15},{8,0},{9,1},... | collective-permute-start | bytes 491528 | tf_op jit(solution)/shard_map/ppermute | solution.py:429
  31.8 7.9 %collective-permute-start.9 = (f32[80,512]{1,0:T(8,128)S(1)}, f32[80,512]{1,0:T(8,128)S(1)}, u32[]{:S(2)}, u32[]{:S(2)}) collective-permute-start(f32[80,512]{1,0:T(8,128)S(1)} %get-tuple-element.57), channel_id=1, source_target_pairs={{0,8},{1,9},{2,10},{3,11},{4,12},{5,13},{6,14},{7,15},{8,0},{9,1},... | collective-permute-start | bytes 491528 | tf_op jit(solution)/shard_map/ppermute | solution.py:429
  36.2 10.3 %collective-permute-start.13 = (bf16[256,512]{1,0:T(8,128)(2,1)S(1)}, bf16[256,512]{1,0:T(8,128)(2,1)S(1)}, u32[]{:S(2)}, u32[]{:S(2)}) collective-permute-start(bf16[256,512]{1,0:T(8,128)(2,1)S(1)} %get-tuple-element.62), channel_id=1, source_target_pairs={{0,4},{1,5},{2,6},{3,7},{4,0},{5,1},{6,2},{7,3},{8,12},{9,13},{10,... | collective-permute-start | bytes 786440 | tf_op jit(solution)/shard_map/ppermute | solution.py:429
  39.7 11.9 %collective-permute-start.14 = (bf16[256,512]{1,0:T(8,128)(2,1)S(1)}, bf16[256,512]{1,0:T(8,128)(2,1)S(1)}, u32[]{:S(2)}, u32[]{:S(2)}) collective-permute-start(bf16[256,512]{1,0:T(8,128)(2,1)S(1)} %get-tuple-element.63), channel_id=1, source_target_pairs={{0,6},{1,7},{2,4},{3,5},{4,2},{5,3},{6,0},{7,1},{8,14},{9,15},{10,... | collective-permute-start | bytes 786440 | tf_op jit(solution)/shard_map/ppermute | solution.py:429
  42.5 14.1 %collective-permute-start.11 = (f32[64,512]{1,0:T(8,128)S(1)}, f32[64,512]{1,0:T(8,128)S(1)}, u32[]{:S(2)}, u32[]{:S(2)}) collective-permute-start(f32[64,512]{1,0:T(8,128)S(1)} %get-tuple-element.60), channel_id=1, source_target_pairs={{0,8},{1,9},{2,10},{3,11},{4,12},{5,13},{6,14},{7,15},{8,0},{9,1},... | collective-permute-start | bytes 393224 | tf_op jit(solution)/shard_map/ppermute | solution.py:429
  43.9 10.2 %collective-permute-start.12 = (f32[64,512]{1,0:T(8,128)S(1)}, f32[64,512]{1,0:T(8,128)S(1)}, u32[]{:S(2)}, u32[]{:S(2)}) collective-permute-start(f32[64,512]{1,0:T(8,128)S(1)} %get-tuple-element.61), channel_id=1, source_target_pairs={{0,8},{1,9},{2,10},{3,11},{4,12},{5,13},{6,14},{7,15},{8,0},{9,1},... | collective-permute-start | bytes 393224 | tf_op jit(solution)/shard_map/ppermute | solution.py:429
  44.1 16.3 %collective-permute-start.20 = (f32[80,512]{1,0:T(8,128)S(1)}, f32[80,512]{1,0:T(8,128)S(1)}, u32[]{:S(2)}, u32[]{:S(2)}) collective-permute-start(f32[80,512]{1,0:T(8,128)S(1)} %add_rows.15.refs_8_), channel_id=1, source_target_pairs={{0,16},{1,17},{2,18},{3,19},{4,20},{5,21},{6,22},{7,23},{8,24},{9,... | collective-permute-start | bytes 491528 | tf_op jit(solution)/shard_map/ppermute | solution.py:429
  53.8 10.7 %collective-permute-start.17 = (f32[64,512]{1,0:T(8,128)S(1)}, f32[64,512]{1,0:T(8,128)S(1)}, u32[]{:S(2)}, u32[]{:S(2)}) collective-permute-start(f32[64,512]{1,0:T(8,128)S(1)} %get-tuple-element.66), channel_id=1, source_target_pairs={{0,8},{1,9},{2,10},{3,11},{4,12},{5,13},{6,14},{7,15},{8,0},{9,1},... | collective-permute-start | bytes 393224 | tf_op jit(solution)/shard_map/ppermute | solution.py:429
  54.1 10.4 %collective-permute-start.16 = (f32[64,512]{1,0:T(8,128)S(1)}, f32[64,512]{1,0:T(8,128)S(1)}, u32[]{:S(2)}, u32[]{:S(2)}) collective-permute-start(f32[64,512]{1,0:T(8,128)S(1)} %add_rows.17.refs_2_), channel_id=1, source_target_pairs={{0,16},{1,17},{2,18},{3,19},{4,20},{5,21},{6,22},{7,23},{8,24},{9,... | collective-permute-start | bytes 393224 | tf_op jit(solution)/shard_map/ppermute | solution.py:429
  57.5 7.3 %collective-permute-start.19 = (f32[64,512]{1,0:T(8,128)S(1)}, f32[64,512]{1,0:T(8,128)S(1)}, u32[]{:S(2)}, u32[]{:S(2)}) collective-permute-start(f32[64,512]{1,0:T(8,128)S(1)} %add_rows.19.refs_3_), channel_id=1, source_target_pairs={{0,16},{1,17},{2,18},{3,19},{4,20},{5,21},{6,22},{7,23},{8,24},{9,... | collective-permute-start | bytes 393224 | tf_op jit(solution)/shard_map/ppermute | solution.py:429
  65.4 11.4 %collective-permute-start.22 = (f32[128,512]{1,0:T(8,128)S(1)}, f32[128,512]{1,0:T(8,128)S(1)}, u32[]{:S(2)}, u32[]{:S(2)}) collective-permute-start(f32[128,512]{1,0:T(8,128)S(1)} %pad_maximum_fusion.1.refs_0_.refs_5_), channel_id=1, source_target_pairs={{0,1},{1,0},{2,3},{3,2},{4,5},{5,4},{6,7},{7,6},{8,9},{9,8},{10,11... | collective-permute-start | bytes 786440 | tf_op jit(solution)/shard_map/ppermute | solution.py:429
  67.9 6.6 %collective-permute-start.23 = (f32[4,40,256]{2,1,0:T(8,128)S(1)}, f32[4,40,256]{2,1,0:T(8,128)S(1)}, u32[]{:S(2)}, u32[]{:S(2)}) collective-permute-start(f32[4,40,256]{2,1,0:T(8,128)S(1)} %get-tuple-element.78), channel_id=1, source_target_pairs={{0,2},{1,3},{2,0},{3,1},{4,6},{5,7},{6,4},{7,5},{8,10},{9,11},{10,... | collective-permute-start | bytes 491528 | tf_op jit(solution)/shard_map/ppermute | solution.py:429
  100.7 10.4 %collective-permute-start.40 = (f32[8,40,256]{2,1,0:T(8,128)S(1)}, f32[8,40,256]{2,1,0:T(8,128)S(1)}, u32[]{:S(2)}, u32[]{:S(2)}) collective-permute-start(f32[8,40,256]{2,1,0:T(8,128)S(1)} %pad_maximum_fusion.refs_0_), channel_id=1, source_target_pairs={{0,1},{1,0},{2,3},{3,2},{4,5},{5,4},{6,7},{7,6},{8,9},{9,8},{10,11... | collective-permute-start | bytes 983048 | tf_op jit(solution)/shard_map/ppermute | solution.py:429
  103.6 9.7 %collective-permute-start.36 = (f32[8,32,256]{2,1,0:T(8,128)S(1)}, f32[8,32,256]{2,1,0:T(8,128)S(1)}, u32[]{:S(2)}, u32[]{:S(2)}) collective-permute-start(f32[8,32,256]{2,1,0:T(8,128)S(1)} %pad_maximum_fusion.2.refs_0_), channel_id=1, source_target_pairs={{0,4},{1,5},{2,6},{3,7},{4,0},{5,1},{6,2},{7,3},{8,12},{9,13},{10,... | collective-permute-start | bytes 786440 | tf_op jit(solution)/shard_map/ppermute | solution.py:429
  105.1 11.1 %collective-permute-start.41 = (f32[8,40,256]{2,1,0:T(8,128)S(1)}, f32[8,40,256]{2,1,0:T(8,128)S(1)}, u32[]{:S(2)}, u32[]{:S(2)}) collective-permute-start(f32[8,40,256]{2,1,0:T(8,128)S(1)} %pad_maximum_fusion.refs_0_), channel_id=1, source_target_pairs={{0,2},{1,3},{2,0},{3,1},{4,6},{5,7},{6,4},{7,5},{8,10},{9,11},{10,... | collective-permute-start | bytes 983048 | tf_op jit(solution)/shard_map/ppermute | solution.py:429
  (20 other events, 87.8 us)

commit v10 on v9

--- a/solution.py
+++ b/solution.py
@@ -10,7 +10,7 @@
 
 BLOCK = 128
 GRAIN = 16
-CHUNKS = (2, 5, 4, 4)
+CHUNKS = (2, 5, 5, 3)
 LEAVE = (1, 3)
 STEPS = (
     ("sum", 0), ("halve", 0), ("sum", 1), ("sum", 2), ("halve", 1), ("finish", 0), ("sum", 3),

time: 122 us -> 126 us (1.033)
  waiting for transfers between devices: 40.2 us -> 45.5 us
  starting transfers between devices: 64.5 us -> 63.1 us
    ppermute x43, waiting for transfers between devices: 40.2 us -> 45.5 us  [flip(): lax.ppermute(value, ('dp', 'fsdp'), [(i, i ^ mask) for i in range(count)])]
    ppermute x43, starting transfers between devices: 64.5 us -> 63.1 us  [flip(): lax.ppermute(value, ('dp', 'fsdp'), [(i, i ^ mask) for i in range(count)])]
  transfers between devices with their start and end apart: 43 -> 43, of which waited for: 22 -> 18; matrix products, arithmetic and copies ran while one was open for 0% -> 0% of each run, Pallas kernels for 8% -> 8%
where the time goes in v10:
time: 126 us
  starting transfers between devices  63.1 us (50%)
  waiting for transfers between devices  45.5 us (36%)
  Pallas kernels  15.4 us (12%)
    ppermute x43, starting transfers between devices, flip(): lax.ppermute(value, ('dp', 'fsdp'), [(i, i ^ mask) for i in range(count)])  63.1 us
    ppermute x43, waiting for transfers between devices, flip(): lax.ppermute(value, ('dp', 'fsdp'), [(i, i ^ mask) for i in range(count)])  45.5 us
    pallas_call x4, Pallas kernels, gram_part(): pl.pallas_call(functools.partial(kernel, count, len(bases), early), in_sp...  4.29 us
    pallas_call x1, Pallas kernels, update(): pl.pallas_call(functools.partial(finish_kernel, scale, places, count), in...  3.44 us
    pallas_call x4, Pallas kernels, dequant(): pl.pallas_call(kernel, in_specs=[SCALARS] + [WHOLE] * 7 + [ANYWHERE] * (l...  2.98 us
  transfers between devices with their start and end apart: 43, of which 18 were waited for; matrix products, arithmetic and copies ran while one was open for 0% of the time, Pallas kernels for 8%

profile of v10, /device:TPU:1, one launch (start us, length us, event | category | flops | bytes accessed | tf_op | source)
XLA Modules:
  0.0 125.6 jit_solution(15156133241366822321)
XLA Ops:
  0.9 2.5 %pack_rows.1 = (bf16[960,512]{1,0:T(8,128)(2,1)S(1)}, f32[16,512]{1,0:T(8,128)S(1)}, bf16[1008,512]{1,0:T(8,128)(2,1)S(1)}, bf16[176,512]{1,0:T(8,128)(2,1)S(1)}...) custom-call(s32[4]{0:T(128)S(1)} %pad_add_fusion.at.refs_0_, ...), custom_call_target="tpu_custom_call" | custom-call | tf_op jit(solution)/shard_map/pack_rows/pallas_call | solution.py:126
  3.5 2.7 %collective-permute-start.1 = (bf16[176,512]{1,0:T(8,128)(2,1)S(1)}, bf16[176,512]{1,0:T(8,128)(2,1)S(1)}, u32[]{:S(2)}, u32[]{:S(2)}) collective-permute-start(bf16[176,512]{1,0:T(8,128)(2,1)S(1)} %get-tuple-element.44), channel_id=1, source_target_pairs={{0,4},{1,5},{2,6},{3,7},{4,0},{5,1},{6,2},{7,3},{8,12},{9,13},{10,... | collective-permute-start | bytes 540680 | tf_op jit(solution)/shard_map/ppermute | solution.py:429
  8.3 2.8 %collective-permute-done.1.refs_4_.refs_6_ = bf16[176,512]{1,0:T(8,128)(2,1)S(1)} collective-permute-done((bf16[176,512]{1,0:T(8,128)(2,1)S(1)}, bf16[176,512]{1,0:T(8,128)(2,1)S(1)}, u32[]{:S(2)}, u32[]{:S(2)}) %collective-permute-start.1) | collective-permute-done | bytes 180256 | tf_op jit(solution)/shard_map/ppermute | solution.py:429
  11.1 4.1 %collective-permute-done.2.refs_5_.refs_7_ = bf16[176,512]{1,0:T(8,128)(2,1)S(1)} collective-permute-done((bf16[176,512]{1,0:T(8,128)(2,1)S(1)}, bf16[176,512]{1,0:T(8,128)(2,1)S(1)}, u32[]{:S(2)}, u32[]{:S(2)}) %collective-permute-start.2) | collective-permute-done | bytes 180256 | tf_op jit(solution)/shard_map/ppermute | solution.py:429
  19.0 2.3 %collective-permute-done.7.refs_1_ = f32[32,512]{1,0:T(8,128)S(1)} collective-permute-done((f32[32,512]{1,0:T(8,128)S(1)}, f32[32,512]{1,0:T(8,128)S(1)}, u32[]{:S(2)}, u32[]{:S(2)}) %collective-permute-start.7) | collective-permute-done | bytes 65568 | tf_op jit(solution)/shard_map/ppermute | solution.py:429
  21.3 2.1 %collective-permute-start.4 = (bf16[320,512]{1,0:T(8,128)(2,1)S(1)}, bf16[320,512]{1,0:T(8,128)(2,1)S(1)}, u32[]{:S(2)}, u32[]{:S(2)}) collective-permute-start(bf16[320,512]{1,0:T(8,128)(2,1)S(1)} %get-tuple-element.49), channel_id=1, source_target_pairs={{0,6},{1,7},{2,4},{3,5},{4,2},{5,3},{6,0},{7,1},{8,14},{9,15},{10,... | collective-permute-start | bytes 983048 | tf_op jit(solution)/shard_map/ppermute | solution.py:429
  23.4 2.4 %collective-permute-start.15 = (f32[32,512]{1,0:T(8,128)S(1)}, f32[32,512]{1,0:T(8,128)S(1)}, u32[]{:S(2)}, u32[]{:S(2)}) collective-permute-start(f32[32,512]{1,0:T(8,128)S(1)} %add_rows.14.refs_8_), channel_id=1, source_target_pairs={{0,16},{1,17},{2,18},{3,19},{4,20},{5,21},{6,22},{7,23},{8,24},{9,... | collective-permute-start | bytes 196616 | tf_op jit(solution)/shard_map/ppermute | solution.py:429
  25.8 3.7 %collective-permute-done.6.refs_7_ = bf16[320,512]{1,0:T(8,128)(2,1)S(1)} collective-permute-done((bf16[320,512]{1,0:T(8,128)(2,1)S(1)}, bf16[320,512]{1,0:T(8,128)(2,1)S(1)}, u32[]{:S(2)}, u32[]{:S(2)}) %collective-permute-start.6) | collective-permute-done | bytes 327712 | tf_op jit(solution)/shard_map/ppermute | solution.py:429
  31.9 7.8 %collective-permute-done.9.refs_8_ = f32[80,512]{1,0:T(8,128)S(1)} collective-permute-done((f32[80,512]{1,0:T(8,128)S(1)}, f32[80,512]{1,0:T(8,128)S(1)}, u32[]{:S(2)}, u32[]{:S(2)}) %collective-permute-start.9) | collective-permute-done | bytes 163872 | tf_op jit(solution)/shard_map/ppermute | solution.py:429
  46.0 2.5 %collective-permute-start.20 = (f32[80,512]{1,0:T(8,128)S(1)}, f32[80,512]{1,0:T(8,128)S(1)}, u32[]{:S(2)}, u32[]{:S(2)}) collective-permute-start(f32[80,512]{1,0:T(8,128)S(1)} %add_rows.15.refs_8_), channel_id=1, source_target_pairs={{0,16},{1,17},{2,18},{3,19},{4,20},{5,21},{6,22},{7,23},{8,24},{9,... | collective-permute-start | bytes 491528 | tf_op jit(solution)/shard_map/ppermute | solution.py:429
  48.5 3.2 %collective-permute-done.14.refs_7_ = bf16[192,512]{1,0:T(8,128)(2,1)S(1)} collective-permute-done((bf16[192,512]{1,0:T(8,128)(2,1)S(1)}, bf16[192,512]{1,0:T(8,128)(2,1)S(1)}, u32[]{:S(2)}, u32[]{:S(2)}) %collective-permute-start.14) | collective-permute-done | bytes 196640 | tf_op jit(solution)/shard_map/ppermute | solution.py:429
  54.1 5.3 %collective-permute-done.18.refs_1_ = f32[48,512]{1,0:T(8,128)S(1)} collective-permute-done((f32[48,512]{1,0:T(8,128)S(1)}, f32[48,512]{1,0:T(8,128)S(1)}, u32[]{:S(2)}, u32[]{:S(2)}) %collective-permute-start.18) | collective-permute-done | bytes 98336 | tf_op jit(solution)/shard_map/ppermute | solution.py:429
  59.4 2.6 %collective-permute-start.19 = (f32[48,512]{1,0:T(8,128)S(1)}, f32[48,512]{1,0:T(8,128)S(1)}, u32[]{:S(2)}, u32[]{:S(2)}) collective-permute-start(f32[48,512]{1,0:T(8,128)S(1)} %add_rows.19.refs_3_), channel_id=1, source_target_pairs={{0,16},{1,17},{2,18},{3,19},{4,20},{5,21},{6,22},{7,23},{8,24},{9,... | collective-permute-start | bytes 294920 | tf_op jit(solution)/shard_map/ppermute | solution.py:429
  62.1 2.1 %collective-permute-start.16 = (f32[80,512]{1,0:T(8,128)S(1)}, f32[80,512]{1,0:T(8,128)S(1)}, u32[]{:S(2)}, u32[]{:S(2)}) collective-permute-start(f32[80,512]{1,0:T(8,128)S(1)} %add_rows.17.refs_2_), channel_id=1, source_target_pairs={{0,16},{1,17},{2,18},{3,19},{4,20},{5,21},{6,22},{7,23},{8,24},{9,... | collective-permute-start | bytes 491528 | tf_op jit(solution)/shard_map/ppermute | solution.py:429
  66.7 7.1 %collective-permute-done.16.refs_1_ = f32[80,512]{1,0:T(8,128)S(1)} collective-permute-done((f32[80,512]{1,0:T(8,128)S(1)}, f32[80,512]{1,0:T(8,128)S(1)}, u32[]{:S(2)}, u32[]{:S(2)}) %collective-permute-start.16) | collective-permute-done | bytes 163872 | tf_op jit(solution)/shard_map/ppermute | solution.py:429
  87.8 3.2 %collective-permute-start.31 = (f32[2,40,256]{2,1,0:T(8,128)S(1)}, f32[2,40,256]{2,1,0:T(8,128)S(1)}, u32[]{:S(2)}, u32[]{:S(2)}) collective-permute-start(f32[2,40,256]{2,1,0:T(8,128)S(1)} %slice_add_fusion.refs_0_), channel_id=1, source_target_pairs={{0,16},{1,17},{2,18},{3,19},{4,20},{5,21},{6,22},{7,23},{8,24},{9,... | collective-permute-start | bytes 245768 | tf_op jit(solution)/shard_map/ppermute | solution.py:429
  93.8 1.9 %collective-permute-done.30.refs_1_ = f32[2,32,256]{2,1,0:T(8,128)S(1)} collective-permute-done((f32[2,32,256]{2,1,0:T(8,128)S(1)}, f32[2,32,256]{2,1,0:T(8,128)S(1)}, u32[]{:S(2)}, u32[]{:S(2)}) %collective-permute-start.30) | collective-permute-done | bytes 65568 | tf_op jit(solution)/shard_map/ppermute | solution.py:429
  95.7 2.4 %collective-permute-start.32 = (f32[2,32,256]{2,1,0:T(8,128)S(1)}, f32[2,32,256]{2,1,0:T(8,128)S(1)}, u32[]{:S(2)}, u32[]{:S(2)}) collective-permute-start(f32[2,32,256]{2,1,0:T(8,128)S(1)} %add_rows.25.refs_0_), channel_id=1, source_target_pairs={{0,16},{1,17},{2,18},{3,19},{4,20},{5,21},{6,22},{7,23},{8,24},{9,... | collective-permute-start | bytes 196616 | tf_op jit(solution)/shard_map/ppermute | solution.py:429
  103.0 2.2 %collective-permute-start.35 = (f32[4,32,256]{2,1,0:T(8,128)S(1)}, f32[4,32,256]{2,1,0:T(8,128)S(1)}, u32[]{:S(2)}, u32[]{:S(2)}) collective-permute-start(f32[4,32,256]{2,1,0:T(8,128)S(1)} %pad_maximum_fusion.5), channel_id=1, source_target_pairs={{0,1},{1,0},{2,3},{3,2},{4,5},{5,4},{6,7},{7,6},{8,9},{9,8},{10,11... | collective-permute-start | bytes 393224 | tf_op jit(solution)/shard_map/ppermute | solution.py:429
  109.2 6.0 %collective-permute-start.41 = (f32[8,40,256]{2,1,0:T(8,128)S(1)}, f32[8,40,256]{2,1,0:T(8,128)S(1)}, u32[]{:S(2)}, u32[]{:S(2)}) collective-permute-start(f32[8,40,256]{2,1,0:T(8,128)S(1)} %pad_maximum_fusion.refs_0_), channel_id=1, source_target_pairs={{0,2},{1,3},{2,0},{3,1},{4,6},{5,7},{6,4},{7,5},{8,10},{9,11},{10,... | collective-permute-start | bytes 983048 | tf_op jit(solution)/shard_map/ppermute | solution.py:429
  115.3 1.9 %collective-permute-start.42 = (f32[8,40,256]{2,1,0:T(8,128)S(1)}, f32[8,40,256]{2,1,0:T(8,128)S(1)}, u32[]{:S(2)}, u32[]{:S(2)}) collective-permute-start(f32[8,40,256]{2,1,0:T(8,128)S(1)} %collective-permute-done.40.refs_1_), channel_id=1, source_target_pairs={{0,2},{1,3},{2,0},{3,1},{4,6},{5,7},{6,4},{7,5},{8,10},{9,11},{10,... | collective-permute-start | bytes 983048 | tf_op jit(solution)/shard_map/ppermute | solution.py:429
  117.2 2.9 %collective-permute-start.38 = (f32[8,32,256]{2,1,0:T(8,128)S(1)}, f32[8,32,256]{2,1,0:T(8,128)S(1)}, u32[]{:S(2)}, u32[]{:S(2)}) collective-permute-start(f32[8,32,256]{2,1,0:T(8,128)S(1)} %collective-permute-done.36.refs_1_), channel_id=1, source_target_pairs={{0,2},{1,3},{2,0},{3,1},{4,6},{5,7},{6,4},{7,5},{8,10},{9,11},{10,... | collective-permute-start | bytes 786440 | tf_op jit(solution)/shard_map/ppermute | solution.py:429
  120.1 2.0 %update_start.1 = (bf16[2,512,512]{2,1,0:T(8,128)(2,1)S(1)}, bf16[2,512,512]{2,1,0:T(8,128)(2,1)S(1)}, f32[8,128]{1,0:T(8,128)S(1)}, f32[240,512]{1,0:T(8,128)S(1)}, f32[240,512]{1,0:T(8,128)S(1)}) custom-call(s32[4]{0:T(128)S(1)} %pad_add_fusion.at.refs_0_, f32[8,40,256]{2,1,0:T(8,128)S(1)} %pad_maximum_fusion.refs_0_, ...), custom_call_target="tpu_custom_call" | custom-call | tf_op jit(solution)/shard_map/update_start/pallas_call | solution.py:401
  122.1 3.4 %update_finish.1 = bf16[240,512]{1,0:T(8,128)(2,1)} custom-call(s32[4]{0:T(128)S(1)} %pad_add_fusion.at.refs_0_, f32[8,32,256]{2,1,0:T(8,128)S(1)} %pad_maximum_fusion.2.refs_0_, f32[8,32,256]{2,1,0:T(8,128)S(1)} %collective-permute-done.36.refs_1_, f32[8,32,256]{2,1,0:T(8,128)S(1)} %collective-permute-done.37.refs_2_, ...), custom_call_target="tpu_custom_call" | custom-call | tf_op jit(solution)/shard_map/update_finish/pallas_call | solution.py:411
  (112 shorter events, 46.1 us)
Async XLA Ops:
  3.4 11.7 %collective-permute-start = (bf16[1008,512]{1,0:T(8,128)(2,1)S(1)}, bf16[1008,512]{1,0:T(8,128)(2,1)S(1)}, u32[]{:S(2)}, u32[]{:S(2)}) collective-permute-start(bf16[1008,512]{1,0:T(8,128)(2,1)S(1)} %get-tuple-element.43), channel_id=1, source_target_pairs={{0,2},{1,3},{2,0},{3,1},{4,6},{5,7},{6,4},{7,5},{8,10},{9,11},{10,... | collective-permute-start | bytes 3096584 | tf_op jit(solution)/shard_map/ppermute | solution.py:429
  3.5 7.5 %collective-permute-start.1 = (bf16[176,512]{1,0:T(8,128)(2,1)S(1)}, bf16[176,512]{1,0:T(8,128)(2,1)S(1)}, u32[]{:S(2)}, u32[]{:S(2)}) collective-permute-start(bf16[176,512]{1,0:T(8,128)(2,1)S(1)} %get-tuple-element.44), channel_id=1, source_target_pairs={{0,4},{1,5},{2,6},{3,7},{4,0},{5,1},{6,2},{7,3},{8,12},{9,13},{10,... | collective-permute-start | bytes 540680 | tf_op jit(solution)/shard_map/ppermute | solution.py:429
  6.2 8.9 %collective-permute-start.2 = (bf16[176,512]{1,0:T(8,128)(2,1)S(1)}, bf16[176,512]{1,0:T(8,128)(2,1)S(1)}, u32[]{:S(2)}, u32[]{:S(2)}) collective-permute-start(bf16[176,512]{1,0:T(8,128)(2,1)S(1)} %get-tuple-element.45), channel_id=1, source_target_pairs={{0,6},{1,7},{2,4},{3,5},{4,2},{5,3},{6,0},{7,1},{8,14},{9,15},{10,... | collective-permute-start | bytes 540680 | tf_op jit(solution)/shard_map/ppermute | solution.py:429
  6.3 19.5 %collective-permute-start.5 = (bf16[320,512]{1,0:T(8,128)(2,1)S(1)}, bf16[320,512]{1,0:T(8,128)(2,1)S(1)}, u32[]{:S(2)}, u32[]{:S(2)}) collective-permute-start(bf16[320,512]{1,0:T(8,128)(2,1)S(1)} %get-tuple-element.50), channel_id=1, source_target_pairs={{0,4},{1,5},{2,6},{3,7},{4,0},{5,1},{6,2},{7,3},{8,12},{9,13},{10,... | collective-permute-start | bytes 983048 | tf_op jit(solution)/shard_map/ppermute | solution.py:429
  7.9 21.6 %collective-permute-start.6 = (bf16[320,512]{1,0:T(8,128)(2,1)S(1)}, bf16[320,512]{1,0:T(8,128)(2,1)S(1)}, u32[]{:S(2)}, u32[]{:S(2)}) collective-permute-start(bf16[320,512]{1,0:T(8,128)(2,1)S(1)} %get-tuple-element.51), channel_id=1, source_target_pairs={{0,6},{1,7},{2,4},{3,5},{4,2},{5,3},{6,0},{7,1},{8,14},{9,15},{10,... | collective-permute-start | bytes 983048 | tf_op jit(solution)/shard_map/ppermute | solution.py:429
  15.8 7.5 %collective-permute-start.8 = (f32[32,512]{1,0:T(8,128)S(1)}, f32[32,512]{1,0:T(8,128)S(1)}, u32[]{:S(2)}, u32[]{:S(2)}) collective-permute-start(f32[32,512]{1,0:T(8,128)S(1)} %get-tuple-element.54), channel_id=1, source_target_pairs={{0,8},{1,9},{2,10},{3,11},{4,12},{5,13},{6,14},{7,15},{8,0},{9,1},... | collective-permute-start | bytes 196616 | tf_op jit(solution)/shard_map/ppermute | solution.py:429
  17.7 24.5 %collective-permute-start.3 = (bf16[320,512]{1,0:T(8,128)(2,1)S(1)}, bf16[320,512]{1,0:T(8,128)(2,1)S(1)}, u32[]{:S(2)}, u32[]{:S(2)}) collective-permute-start(bf16[320,512]{1,0:T(8,128)(2,1)S(1)} %get-tuple-element.48), channel_id=1, source_target_pairs={{0,4},{1,5},{2,6},{3,7},{4,0},{5,1},{6,2},{7,3},{8,12},{9,13},{10,... | collective-permute-start | bytes 983048 | tf_op jit(solution)/shard_map/ppermute | solution.py:429
  21.3 21.9 %collective-permute-start.4 = (bf16[320,512]{1,0:T(8,128)(2,1)S(1)}, bf16[320,512]{1,0:T(8,128)(2,1)S(1)}, u32[]{:S(2)}, u32[]{:S(2)}) collective-permute-start(bf16[320,512]{1,0:T(8,128)(2,1)S(1)} %get-tuple-element.49), channel_id=1, source_target_pairs={{0,6},{1,7},{2,4},{3,5},{4,2},{5,3},{6,0},{7,1},{8,14},{9,15},{10,... | collective-permute-start | bytes 983048 | tf_op jit(solution)/shard_map/ppermute | solution.py:429
  23.4 22.6 %collective-permute-start.15 = (f32[32,512]{1,0:T(8,128)S(1)}, f32[32,512]{1,0:T(8,128)S(1)}, u32[]{:S(2)}, u32[]{:S(2)}) collective-permute-start(f32[32,512]{1,0:T(8,128)S(1)} %add_rows.14.refs_8_), channel_id=1, source_target_pairs={{0,16},{1,17},{2,18},{3,19},{4,20},{5,21},{6,22},{7,23},{8,24},{9,... | collective-permute-start | bytes 196616 | tf_op jit(solution)/shard_map/ppermute | solution.py:429
  30.3 11.0 %collective-permute-start.10 = (f32[80,512]{1,0:T(8,128)S(1)}, f32[80,512]{1,0:T(8,128)S(1)}, u32[]{:S(2)}, u32[]{:S(2)}) collective-permute-start(f32[80,512]{1,0:T(8,128)S(1)} %get-tuple-element.58), channel_id=1, source_target_pairs={{0,8},{1,9},{2,10},{3,11},{4,12},{5,13},{6,14},{7,15},{8,0},{9,1},... | collective-permute-start | bytes 491528 | tf_op jit(solution)/shard_map/ppermute | solution.py:429
  31.8 7.9 %collective-permute-start.9 = (f32[80,512]{1,0:T(8,128)S(1)}, f32[80,512]{1,0:T(8,128)S(1)}, u32[]{:S(2)}, u32[]{:S(2)}) collective-permute-start(f32[80,512]{1,0:T(8,128)S(1)} %get-tuple-element.57), channel_id=1, source_target_pairs={{0,8},{1,9},{2,10},{3,11},{4,12},{5,13},{6,14},{7,15},{8,0},{9,1},... | collective-permute-start | bytes 491528 | tf_op jit(solution)/shard_map/ppermute | solution.py:429
  39.7 8.7 %collective-permute-start.13 = (bf16[192,512]{1,0:T(8,128)(2,1)S(1)}, bf16[192,512]{1,0:T(8,128)(2,1)S(1)}, u32[]{:S(2)}, u32[]{:S(2)}) collective-permute-start(bf16[192,512]{1,0:T(8,128)(2,1)S(1)} %get-tuple-element.62), channel_id=1, source_target_pairs={{0,4},{1,5},{2,6},{3,7},{4,0},{5,1},{6,2},{7,3},{8,12},{9,13},{10,... | collective-permute-start | bytes 589832 | tf_op jit(solution)/shard_map/ppermute | solution.py:429
  41.2 10.4 %collective-permute-start.14 = (bf16[192,512]{1,0:T(8,128)(2,1)S(1)}, bf16[192,512]{1,0:T(8,128)(2,1)S(1)}, u32[]{:S(2)}, u32[]{:S(2)}) collective-permute-start(bf16[192,512]{1,0:T(8,128)(2,1)S(1)} %get-tuple-element.63), channel_id=1, source_target_pairs={{0,6},{1,7},{2,4},{3,5},{4,2},{5,3},{6,0},{7,1},{8,14},{9,15},{10,... | collective-permute-start | bytes 589832 | tf_op jit(solution)/shard_map/ppermute | solution.py:429
  44.0 21.5 %collective-permute-start.11 = (f32[80,512]{1,0:T(8,128)S(1)}, f32[80,512]{1,0:T(8,128)S(1)}, u32[]{:S(2)}, u32[]{:S(2)}) collective-permute-start(f32[80,512]{1,0:T(8,128)S(1)} %get-tuple-element.60), channel_id=1, source_target_pairs={{0,8},{1,9},{2,10},{3,11},{4,12},{5,13},{6,14},{7,15},{8,0},{9,1},... | collective-permute-start | bytes 491528 | tf_op jit(solution)/shard_map/ppermute | solution.py:429
  45.9 16.2 %collective-permute-start.12 = (f32[80,512]{1,0:T(8,128)S(1)}, f32[80,512]{1,0:T(8,128)S(1)}, u32[]{:S(2)}, u32[]{:S(2)}) collective-permute-start(f32[80,512]{1,0:T(8,128)S(1)} %get-tuple-element.61), channel_id=1, source_target_pairs={{0,8},{1,9},{2,10},{3,11},{4,12},{5,13},{6,14},{7,15},{8,0},{9,1},... | collective-permute-start | bytes 491528 | tf_op jit(solution)/shard_map/ppermute | solution.py:429
  46.0 18.2 %collective-permute-start.20 = (f32[80,512]{1,0:T(8,128)S(1)}, f32[80,512]{1,0:T(8,128)S(1)}, u32[]{:S(2)}, u32[]{:S(2)}) collective-permute-start(f32[80,512]{1,0:T(8,128)S(1)} %add_rows.15.refs_8_), channel_id=1, source_target_pairs={{0,16},{1,17},{2,18},{3,19},{4,20},{5,21},{6,22},{7,23},{8,24},{9,... | collective-permute-start | bytes 491528 | tf_op jit(solution)/shard_map/ppermute | solution.py:429
  54.0 8.0 %collective-permute-start.17 = (f32[48,512]{1,0:T(8,128)S(1)}, f32[48,512]{1,0:T(8,128)S(1)}, u32[]{:S(2)}, u32[]{:S(2)}) collective-permute-start(f32[48,512]{1,0:T(8,128)S(1)} %get-tuple-element.66), channel_id=1, source_target_pairs={{0,8},{1,9},{2,10},{3,11},{4,12},{5,13},{6,14},{7,15},{8,0},{9,1},... | collective-permute-start | bytes 294920 | tf_op jit(solution)/shard_map/ppermute | solution.py:429
  59.4 14.4 %collective-permute-start.19 = (f32[48,512]{1,0:T(8,128)S(1)}, f32[48,512]{1,0:T(8,128)S(1)}, u32[]{:S(2)}, u32[]{:S(2)}) collective-permute-start(f32[48,512]{1,0:T(8,128)S(1)} %add_rows.19.refs_3_), channel_id=1, source_target_pairs={{0,16},{1,17},{2,18},{3,19},{4,20},{5,21},{6,22},{7,23},{8,24},{9,... | collective-permute-start | bytes 294920 | tf_op jit(solution)/shard_map/ppermute | solution.py:429
  62.1 11.7 %collective-permute-start.16 = (f32[80,512]{1,0:T(8,128)S(1)}, f32[80,512]{1,0:T(8,128)S(1)}, u32[]{:S(2)}, u32[]{:S(2)}) collective-permute-start(f32[80,512]{1,0:T(8,128)S(1)} %add_rows.17.refs_2_), channel_id=1, source_target_pairs={{0,16},{1,17},{2,18},{3,19},{4,20},{5,21},{6,22},{7,23},{8,24},{9,... | collective-permute-start | bytes 491528 | tf_op jit(solution)/shard_map/ppermute | solution.py:429
  64.2 9.6 %collective-permute-start.21 = (f32[112,512]{1,0:T(8,128)S(1)}, f32[112,512]{1,0:T(8,128)S(1)}, u32[]{:S(2)}, u32[]{:S(2)}) collective-permute-start(f32[112,512]{1,0:T(8,128)S(1)} %pad_maximum_fusion.3.refs_0_.refs_4_), channel_id=1, source_target_pairs={{0,1},{1,0},{2,3},{3,2},{4,5},{5,4},{6,7},{7,6},{8,9},{9,8},{10,11... | collective-permute-start | bytes 688136 | tf_op jit(solution)/shard_map/ppermute | solution.py:429
  73.9 7.4 %collective-permute-start.22 = (f32[128,512]{1,0:T(8,128)S(1)}, f32[128,512]{1,0:T(8,128)S(1)}, u32[]{:S(2)}, u32[]{:S(2)}) collective-permute-start(f32[128,512]{1,0:T(8,128)S(1)} %pad_maximum_fusion.1.refs_0_.refs_5_), channel_id=1, source_target_pairs={{0,1},{1,0},{2,3},{3,2},{4,5},{5,4},{6,7},{7,6},{8,9},{9,8},{10,11... | collective-permute-start | bytes 786440 | tf_op jit(solution)/shard_map/ppermute | solution.py:429
  105.5 9.7 %collective-permute-start.40 = (f32[8,40,256]{2,1,0:T(8,128)S(1)}, f32[8,40,256]{2,1,0:T(8,128)S(1)}, u32[]{:S(2)}, u32[]{:S(2)}) collective-permute-start(f32[8,40,256]{2,1,0:T(8,128)S(1)} %pad_maximum_fusion.refs_0_), channel_id=1, source_target_pairs={{0,1},{1,0},{2,3},{3,2},{4,5},{5,4},{6,7},{7,6},{8,9},{9,8},{10,11... | collective-permute-start | bytes 983048 | tf_op jit(solution)/shard_map/ppermute | solution.py:429
  107.9 9.2 %collective-permute-start.36 = (f32[8,32,256]{2,1,0:T(8,128)S(1)}, f32[8,32,256]{2,1,0:T(8,128)S(1)}, u32[]{:S(2)}, u32[]{:S(2)}) collective-permute-start(f32[8,32,256]{2,1,0:T(8,128)S(1)} %pad_maximum_fusion.2.refs_0_), channel_id=1, source_target_pairs={{0,4},{1,5},{2,6},{3,7},{4,0},{5,1},{6,2},{7,3},{8,12},{9,13},{10,... | collective-permute-start | bytes 786440 | tf_op jit(solution)/shard_map/ppermute | solution.py:429
  109.2 10.9 %collective-permute-start.41 = (f32[8,40,256]{2,1,0:T(8,128)S(1)}, f32[8,40,256]{2,1,0:T(8,128)S(1)}, u32[]{:S(2)}, u32[]{:S(2)}) collective-permute-start(f32[8,40,256]{2,1,0:T(8,128)S(1)} %pad_maximum_fusion.refs_0_), channel_id=1, source_target_pairs={{0,2},{1,3},{2,0},{3,1},{4,6},{5,7},{6,4},{7,5},{8,10},{9,11},{10,... | collective-permute-start | bytes 983048 | tf_op jit(solution)/shard_map/ppermute | solution.py:429
  (20 other events, 89.6 us)

commit v11 on v9

--- a/solution.py
+++ b/solution.py
@@ -11,7 +11,7 @@
 BLOCK = 128
 GRAIN = 16
 CHUNKS = (2, 5, 4, 4)
-LEAVE = (1, 3)
+LEAVE = (1, 2, 3)
 STEPS = (
     ("sum", 0), ("halve", 0), ("sum", 1), ("sum", 2), ("halve", 1), ("finish", 0), ("sum", 3),
     ("halve", 2), ("halve", 3), ("finish", 1), ("finish", 2), ("finish", 3),
@@ -24,7 +24,7 @@
     ("sum", 3): (("sent", 1), ("grad", 0)),
     ("halve", 2): (("keep", 3),),
     ("finish", 1): (("sent", 2), ("sent", 3)),
-    ("finish", 3): (("across", 1),),
+    ("finish", 3): (("across", 1), ("across", 2)),
 }
 ORDER = (0, 2, 1, 3)
 PIECE = 256
@@ -496,17 +496,17 @@
             made["across", n] = across
             owns.append(group)
             acrosses.append(across)
-            if len(owns) == 1:
-                (made["base", n],) = gram_part(
-                    near_kernel, at, owns, 1, NEAR, "gram_near_early", early=True
-                )
             held.clear()
 
     for step, n in STEPS:
         {"sum": add_partials, "halve": halve, "finish": finish}[step](n)
 
+    count = len(owns)
+    (near_base,) = gram_part(
+        near_kernel, at, owns[:1], 1, NEAR, "gram_near_early", early=True, after=[made["grad", 2]]
+    )
     own, far = gram_part(
-        near_kernel, at, owns[1:], 1, NEAR, "gram_near", made["base", 1]
+        near_kernel, at, owns[1:], count - 1, NEAR, "gram_near", near_base
     )
     core = [flip(far[4:], "c"), flip(far[:4], "c")]
     near_sent = add([own[4:], core[0]], [])
@@ -516,7 +516,7 @@
         after=[near_sent],
     )
     cross_own, far = gram_part(
-        cross_kernel, at, owns[1:] + acrosses[1:], 1, CROSS, "gram_cross", cross_base,
+        cross_kernel, at, owns[1:] + acrosses[1:], count - 1, CROSS, "gram_cross", cross_base,
         after=[near_sent],
     )
     cross_core = [flip(far[4:], "c"), flip(far[:4], "c")]

time: 122 us -> 122 us (level)
  waiting for transfers between devices: 40.2 us -> 45.6 us
  starting transfers between devices: 64.5 us -> 59.6 us
    ppermute x43 -> x44, waiting for transfers between devices: 40.2 us -> 45.6 us  [flip(): lax.ppermute(value, ('dp', 'fsdp'), [(i, i ^ mask) for i in range(count)])]
    ppermute x43 -> x44, starting transfers between devices: 64.5 us -> 59.6 us  [flip(): lax.ppermute(value, ('dp', 'fsdp'), [(i, i ^ mask) for i in range(count)])]
  transfers between devices with their start and end apart: 43 -> 44, of which waited for: 22 -> 20; matrix products, arithmetic and copies ran while one was open for 0% -> 0% of each run, Pallas kernels for 8% -> 7%
where the time goes in v11:
time: 122 us
  starting transfers between devices  59.6 us (49%)
  waiting for transfers between devices  45.6 us (37%)
  Pallas kernels  15.4 us (13%)
    ppermute x44, starting transfers between devices, flip(): lax.ppermute(value, ('dp', 'fsdp'), [(i, i ^ mask) for i in range(count)])  59.6 us
    ppermute x44, waiting for transfers between devices, flip(): lax.ppermute(value, ('dp', 'fsdp'), [(i, i ^ mask) for i in range(count)])  45.6 us
    pallas_call x4, Pallas kernels, gram_part(): pl.pallas_call(functools.partial(kernel, count, len(bases), early), in_sp...  4.26 us
    pallas_call x1, Pallas kernels, update(): pl.pallas_call(functools.partial(finish_kernel, scale, places, count), in...  3.44 us
    pallas_call x4, Pallas kernels, dequant(): pl.pallas_call(kernel, in_specs=[SCALARS] + [WHOLE] * 7 + [ANYWHERE] * (l...  2.97 us
    pallas_call x1, Pallas kernels, pack(): pl.pallas_call(functools.partial(pack_kernel, own_rows, spans), in_specs=...  2.51 us
  transfers between devices with their start and end apart: 44, of which 20 were waited for; matrix products, arithmetic and copies ran while one was open for 0% of the time, Pallas kernels for 7%

profile of v11, /device:TPU:1, one launch (start us, length us, event | category | flops | bytes accessed | tf_op | source)
XLA Modules:
  0.0 122.2 jit_solution(11701027300686888473)
XLA Ops:
  0.9 2.5 %pack_rows.1 = (bf16[960,512]{1,0:T(8,128)(2,1)S(1)}, f32[16,512]{1,0:T(8,128)S(1)}, bf16[1008,512]{1,0:T(8,128)(2,1)S(1)}, bf16[176,512]{1,0:T(8,128)(2,1)S(1)}...) custom-call(s32[4]{0:T(128)S(1)} %pad_add_fusion.at.refs_0_, ...), custom_call_target="tpu_custom_call" | custom-call | tf_op jit(solution)/shard_map/pack_rows/pallas_call | solution.py:126
  3.5 2.7 %collective-permute-start.1 = (bf16[176,512]{1,0:T(8,128)(2,1)S(1)}, bf16[176,512]{1,0:T(8,128)(2,1)S(1)}, u32[]{:S(2)}, u32[]{:S(2)}) collective-permute-start(bf16[176,512]{1,0:T(8,128)(2,1)S(1)} %get-tuple-element.44), channel_id=1, source_target_pairs={{0,4},{1,5},{2,6},{3,7},{4,0},{5,1},{6,2},{7,3},{8,12},{9,13},{10,... | collective-permute-start | bytes 540680 | tf_op jit(solution)/shard_map/ppermute | solution.py:429
  8.3 2.8 %collective-permute-done.1.refs_4_.refs_6_ = bf16[176,512]{1,0:T(8,128)(2,1)S(1)} collective-permute-done((bf16[176,512]{1,0:T(8,128)(2,1)S(1)}, bf16[176,512]{1,0:T(8,128)(2,1)S(1)}, u32[]{:S(2)}, u32[]{:S(2)}) %collective-permute-start.1) | collective-permute-done | bytes 180256 | tf_op jit(solution)/shard_map/ppermute | solution.py:429
  11.1 4.1 %collective-permute-done.2.refs_5_.refs_7_ = bf16[176,512]{1,0:T(8,128)(2,1)S(1)} collective-permute-done((bf16[176,512]{1,0:T(8,128)(2,1)S(1)}, bf16[176,512]{1,0:T(8,128)(2,1)S(1)}, u32[]{:S(2)}, u32[]{:S(2)}) %collective-permute-start.2) | collective-permute-done | bytes 180256 | tf_op jit(solution)/shard_map/ppermute | solution.py:429
  19.0 2.3 %collective-permute-done.7.refs_1_ = f32[32,512]{1,0:T(8,128)S(1)} collective-permute-done((f32[32,512]{1,0:T(8,128)S(1)}, f32[32,512]{1,0:T(8,128)S(1)}, u32[]{:S(2)}, u32[]{:S(2)}) %collective-permute-start.7) | collective-permute-done | bytes 65568 | tf_op jit(solution)/shard_map/ppermute | solution.py:429
  21.3 2.1 %collective-permute-start.4 = (bf16[256,512]{1,0:T(8,128)(2,1)S(1)}, bf16[256,512]{1,0:T(8,128)(2,1)S(1)}, u32[]{:S(2)}, u32[]{:S(2)}) collective-permute-start(bf16[256,512]{1,0:T(8,128)(2,1)S(1)} %get-tuple-element.49), channel_id=1, source_target_pairs={{0,6},{1,7},{2,4},{3,5},{4,2},{5,3},{6,0},{7,1},{8,14},{9,15},{10,... | collective-permute-start | bytes 786440 | tf_op jit(solution)/shard_map/ppermute | solution.py:429
  23.4 2.4 %collective-permute-start.15 = (f32[32,512]{1,0:T(8,128)S(1)}, f32[32,512]{1,0:T(8,128)S(1)}, u32[]{:S(2)}, u32[]{:S(2)}) collective-permute-start(f32[32,512]{1,0:T(8,128)S(1)} %add_rows.14.refs_8_), channel_id=1, source_target_pairs={{0,16},{1,17},{2,18},{3,19},{4,20},{5,21},{6,22},{7,23},{8,24},{9,... | collective-permute-start | bytes 196616 | tf_op jit(solution)/shard_map/ppermute | solution.py:429
  25.8 3.7 %collective-permute-done.6.refs_7_ = bf16[320,512]{1,0:T(8,128)(2,1)S(1)} collective-permute-done((bf16[320,512]{1,0:T(8,128)(2,1)S(1)}, bf16[320,512]{1,0:T(8,128)(2,1)S(1)}, u32[]{:S(2)}, u32[]{:S(2)}) %collective-permute-start.6) | collective-permute-done | bytes 327712 | tf_op jit(solution)/shard_map/ppermute | solution.py:429
  31.9 4.3 %collective-permute-done.9.refs_8_ = f32[80,512]{1,0:T(8,128)S(1)} collective-permute-done((f32[80,512]{1,0:T(8,128)S(1)}, f32[80,512]{1,0:T(8,128)S(1)}, u32[]{:S(2)}, u32[]{:S(2)}) %collective-permute-start.9) | collective-permute-done | bytes 163872 | tf_op jit(solution)/shard_map/ppermute | solution.py:429
  37.7 2.0 %collective-permute-done.10.refs_9_.refs_1_ = f32[80,512]{1,0:T(8,128)S(1)} collective-permute-done((f32[80,512]{1,0:T(8,128)S(1)}, f32[80,512]{1,0:T(8,128)S(1)}, u32[]{:S(2)}, u32[]{:S(2)}) %collective-permute-start.10) | collective-permute-done | bytes 163872 | tf_op jit(solution)/shard_map/ppermute | solution.py:429
  39.7 2.0 %collective-permute-start.14 = (bf16[256,512]{1,0:T(8,128)(2,1)S(1)}, bf16[256,512]{1,0:T(8,128)(2,1)S(1)}, u32[]{:S(2)}, u32[]{:S(2)}) collective-permute-start(bf16[256,512]{1,0:T(8,128)(2,1)S(1)} %get-tuple-element.63), channel_id=1, source_target_pairs={{0,6},{1,7},{2,4},{3,5},{4,2},{5,3},{6,0},{7,1},{8,14},{9,15},{10,... | collective-permute-start | bytes 786440 | tf_op jit(solution)/shard_map/ppermute | solution.py:429
  43.9 2.4 %collective-permute-start.20 = (f32[80,512]{1,0:T(8,128)S(1)}, f32[80,512]{1,0:T(8,128)S(1)}, u32[]{:S(2)}, u32[]{:S(2)}) collective-permute-start(f32[80,512]{1,0:T(8,128)S(1)} %add_rows.15.refs_8_), channel_id=1, source_target_pairs={{0,16},{1,17},{2,18},{3,19},{4,20},{5,21},{6,22},{7,23},{8,24},{9,... | collective-permute-start | bytes 491528 | tf_op jit(solution)/shard_map/ppermute | solution.py:429
  46.5 5.2 %collective-permute-done.14.refs_7_ = bf16[256,512]{1,0:T(8,128)(2,1)S(1)} collective-permute-done((bf16[256,512]{1,0:T(8,128)(2,1)S(1)}, bf16[256,512]{1,0:T(8,128)(2,1)S(1)}, u32[]{:S(2)}, u32[]{:S(2)}) %collective-permute-start.14) | collective-permute-done | bytes 262176 | tf_op jit(solution)/shard_map/ppermute | solution.py:429
  54.2 2.4 %collective-permute-start.16 = (f32[64,512]{1,0:T(8,128)S(1)}, f32[64,512]{1,0:T(8,128)S(1)}, u32[]{:S(2)}, u32[]{:S(2)}) collective-permute-start(f32[64,512]{1,0:T(8,128)S(1)} %add_rows.17.refs_2_), channel_id=1, source_target_pairs={{0,16},{1,17},{2,18},{3,19},{4,20},{5,21},{6,22},{7,23},{8,24},{9,... | collective-permute-start | bytes 393224 | tf_op jit(solution)/shard_map/ppermute | solution.py:429
  57.7 2.5 %collective-permute-start.19 = (f32[64,512]{1,0:T(8,128)S(1)}, f32[64,512]{1,0:T(8,128)S(1)}, u32[]{:S(2)}, u32[]{:S(2)}) collective-permute-start(f32[64,512]{1,0:T(8,128)S(1)} %add_rows.19.refs_3_), channel_id=1, source_target_pairs={{0,16},{1,17},{2,18},{3,19},{4,20},{5,21},{6,22},{7,23},{8,24},{9,... | collective-permute-start | bytes 393224 | tf_op jit(solution)/shard_map/ppermute | solution.py:429
  68.3 4.2 %collective-permute-start.24 = (f32[4,40,256]{2,1,0:T(8,128)S(1)}, f32[4,40,256]{2,1,0:T(8,128)S(1)}, u32[]{:S(2)}, u32[]{:S(2)}) collective-permute-start(f32[4,40,256]{2,1,0:T(8,128)S(1)} %get-tuple-element.78), channel_id=1, source_target_pairs={{0,2},{1,3},{2,0},{3,1},{4,6},{5,7},{6,4},{7,5},{8,10},{9,11},{10,... | collective-permute-start | bytes 491528 | tf_op jit(solution)/shard_map/ppermute | solution.py:429
  79.9 3.1 %collective-permute-start.30 = (f32[2,40,256]{2,1,0:T(8,128)S(1)}, f32[2,40,256]{2,1,0:T(8,128)S(1)}, u32[]{:S(2)}, u32[]{:S(2)}) collective-permute-start(f32[2,40,256]{2,1,0:T(8,128)S(1)} %slice.80), channel_id=1, source_target_pairs={{0,8},{1,9},{2,10},{3,11},{4,12},{5,13},{6,14},{7,15},{8,0},{9,1},... | collective-permute-start | bytes 245768 | tf_op jit(solution)/shard_map/ppermute | solution.py:429
  85.9 3.7 %collective-permute-done.27.refs_2_ = f32[4,32,256]{2,1,0:T(8,128)S(1)} collective-permute-done((f32[4,32,256]{2,1,0:T(8,128)S(1)}, f32[4,32,256]{2,1,0:T(8,128)S(1)}, u32[]{:S(2)}, u32[]{:S(2)}) %collective-permute-start.27) | collective-permute-done | bytes 131104 | tf_op jit(solution)/shard_map/ppermute | solution.py:429
  92.8 4.7 %collective-permute-done.33.refs_1_ = f32[2,32,256]{2,1,0:T(8,128)S(1)} collective-permute-done((f32[2,32,256]{2,1,0:T(8,128)S(1)}, f32[2,32,256]{2,1,0:T(8,128)S(1)}, u32[]{:S(2)}, u32[]{:S(2)}) %collective-permute-start.33) | collective-permute-done | bytes 65568 | tf_op jit(solution)/shard_map/ppermute | solution.py:429
  102.8 2.1 %collective-permute-done.36 = f32[4,32,256]{2,1,0:T(8,128)S(1)} collective-permute-done((f32[4,32,256]{2,1,0:T(8,128)S(1)}, f32[4,32,256]{2,1,0:T(8,128)S(1)}, u32[]{:S(2)}, u32[]{:S(2)}) %collective-permute-start.36) | collective-permute-done | bytes 131104 | tf_op jit(solution)/shard_map/ppermute | solution.py:429
  106.4 5.6 %collective-permute-start.42 = (f32[8,40,256]{2,1,0:T(8,128)S(1)}, f32[8,40,256]{2,1,0:T(8,128)S(1)}, u32[]{:S(2)}, u32[]{:S(2)}) collective-permute-start(f32[8,40,256]{2,1,0:T(8,128)S(1)} %pad_maximum_fusion.refs_0_), channel_id=1, source_target_pairs={{0,2},{1,3},{2,0},{3,1},{4,6},{5,7},{6,4},{7,5},{8,10},{9,11},{10,... | collective-permute-start | bytes 983048 | tf_op jit(solution)/shard_map/ppermute | solution.py:429
  113.8 2.9 %collective-permute-start.39 = (f32[8,32,256]{2,1,0:T(8,128)S(1)}, f32[8,32,256]{2,1,0:T(8,128)S(1)}, u32[]{:S(2)}, u32[]{:S(2)}) collective-permute-start(f32[8,32,256]{2,1,0:T(8,128)S(1)} %collective-permute-done.37.refs_1_), channel_id=1, source_target_pairs={{0,2},{1,3},{2,0},{3,1},{4,6},{5,7},{6,4},{7,5},{8,10},{9,11},{10,... | collective-permute-start | bytes 786440 | tf_op jit(solution)/shard_map/ppermute | solution.py:429
  116.7 2.0 %update_start.1 = (bf16[2,512,512]{2,1,0:T(8,128)(2,1)S(1)}, bf16[2,512,512]{2,1,0:T(8,128)(2,1)S(1)}, f32[8,128]{1,0:T(8,128)S(1)}, f32[240,512]{1,0:T(8,128)S(1)}, f32[240,512]{1,0:T(8,128)S(1)}) custom-call(s32[4]{0:T(128)S(1)} %pad_add_fusion.at.refs_0_, f32[8,40,256]{2,1,0:T(8,128)S(1)} %pad_maximum_fusion.refs_0_, ...), custom_call_target="tpu_custom_call" | custom-call | tf_op jit(solution)/shard_map/update_start/pallas_call | solution.py:401
  118.7 3.4 %update_finish.1 = bf16[240,512]{1,0:T(8,128)(2,1)} custom-call(s32[4]{0:T(128)S(1)} %pad_add_fusion.at.refs_0_, f32[8,32,256]{2,1,0:T(8,128)S(1)} %pad_maximum_fusion.1.refs_0_, f32[8,32,256]{2,1,0:T(8,128)S(1)} %collective-permute-done.37.refs_1_, f32[8,32,256]{2,1,0:T(8,128)S(1)} %collective-permute-done.38.refs_2_, ...), custom_call_target="tpu_custom_call" | custom-call | tf_op jit(solution)/shard_map/update_finish/pallas_call | solution.py:411
  (113 shorter events, 46.8 us)
Async XLA Ops:
  3.4 11.7 %collective-permute-start = (bf16[1008,512]{1,0:T(8,128)(2,1)S(1)}, bf16[1008,512]{1,0:T(8,128)(2,1)S(1)}, u32[]{:S(2)}, u32[]{:S(2)}) collective-permute-start(bf16[1008,512]{1,0:T(8,128)(2,1)S(1)} %get-tuple-element.43), channel_id=1, source_target_pairs={{0,2},{1,3},{2,0},{3,1},{4,6},{5,7},{6,4},{7,5},{8,10},{9,11},{10,... | collective-permute-start | bytes 3096584 | tf_op jit(solution)/shard_map/ppermute | solution.py:429
  3.5 7.5 %collective-permute-start.1 = (bf16[176,512]{1,0:T(8,128)(2,1)S(1)}, bf16[176,512]{1,0:T(8,128)(2,1)S(1)}, u32[]{:S(2)}, u32[]{:S(2)}) collective-permute-start(bf16[176,512]{1,0:T(8,128)(2,1)S(1)} %get-tuple-element.44), channel_id=1, source_target_pairs={{0,4},{1,5},{2,6},{3,7},{4,0},{5,1},{6,2},{7,3},{8,12},{9,13},{10,... | collective-permute-start | bytes 540680 | tf_op jit(solution)/shard_map/ppermute | solution.py:429
  6.2 8.9 %collective-permute-start.2 = (bf16[176,512]{1,0:T(8,128)(2,1)S(1)}, bf16[176,512]{1,0:T(8,128)(2,1)S(1)}, u32[]{:S(2)}, u32[]{:S(2)}) collective-permute-start(bf16[176,512]{1,0:T(8,128)(2,1)S(1)} %get-tuple-element.45), channel_id=1, source_target_pairs={{0,6},{1,7},{2,4},{3,5},{4,2},{5,3},{6,0},{7,1},{8,14},{9,15},{10,... | collective-permute-start | bytes 540680 | tf_op jit(solution)/shard_map/ppermute | solution.py:429
  6.3 19.5 %collective-permute-start.5 = (bf16[320,512]{1,0:T(8,128)(2,1)S(1)}, bf16[320,512]{1,0:T(8,128)(2,1)S(1)}, u32[]{:S(2)}, u32[]{:S(2)}) collective-permute-start(bf16[320,512]{1,0:T(8,128)(2,1)S(1)} %get-tuple-element.50), channel_id=1, source_target_pairs={{0,4},{1,5},{2,6},{3,7},{4,0},{5,1},{6,2},{7,3},{8,12},{9,13},{10,... | collective-permute-start | bytes 983048 | tf_op jit(solution)/shard_map/ppermute | solution.py:429
  7.9 21.6 %collective-permute-start.6 = (bf16[320,512]{1,0:T(8,128)(2,1)S(1)}, bf16[320,512]{1,0:T(8,128)(2,1)S(1)}, u32[]{:S(2)}, u32[]{:S(2)}) collective-permute-start(bf16[320,512]{1,0:T(8,128)(2,1)S(1)} %get-tuple-element.51), channel_id=1, source_target_pairs={{0,6},{1,7},{2,4},{3,5},{4,2},{5,3},{6,0},{7,1},{8,14},{9,15},{10,... | collective-permute-start | bytes 983048 | tf_op jit(solution)/shard_map/ppermute | solution.py:429
  15.8 7.5 %collective-permute-start.8 = (f32[32,512]{1,0:T(8,128)S(1)}, f32[32,512]{1,0:T(8,128)S(1)}, u32[]{:S(2)}, u32[]{:S(2)}) collective-permute-start(f32[32,512]{1,0:T(8,128)S(1)} %get-tuple-element.54), channel_id=1, source_target_pairs={{0,8},{1,9},{2,10},{3,11},{4,12},{5,13},{6,14},{7,15},{8,0},{9,1},... | collective-permute-start | bytes 196616 | tf_op jit(solution)/shard_map/ppermute | solution.py:429
  17.7 24.0 %collective-permute-start.3 = (bf16[256,512]{1,0:T(8,128)(2,1)S(1)}, bf16[256,512]{1,0:T(8,128)(2,1)S(1)}, u32[]{:S(2)}, u32[]{:S(2)}) collective-permute-start(bf16[256,512]{1,0:T(8,128)(2,1)S(1)} %get-tuple-element.48), channel_id=1, source_target_pairs={{0,4},{1,5},{2,6},{3,7},{4,0},{5,1},{6,2},{7,3},{8,12},{9,13},{10,... | collective-permute-start | bytes 786440 | tf_op jit(solution)/shard_map/ppermute | solution.py:429
  21.3 20.5 %collective-permute-start.4 = (bf16[256,512]{1,0:T(8,128)(2,1)S(1)}, bf16[256,512]{1,0:T(8,128)(2,1)S(1)}, u32[]{:S(2)}, u32[]{:S(2)}) collective-permute-start(bf16[256,512]{1,0:T(8,128)(2,1)S(1)} %get-tuple-element.49), channel_id=1, source_target_pairs={{0,6},{1,7},{2,4},{3,5},{4,2},{5,3},{6,0},{7,1},{8,14},{9,15},{10,... | collective-permute-start | bytes 786440 | tf_op jit(solution)/shard_map/ppermute | solution.py:429
  23.4 22.9 %collective-permute-start.15 = (f32[32,512]{1,0:T(8,128)S(1)}, f32[32,512]{1,0:T(8,128)S(1)}, u32[]{:S(2)}, u32[]{:S(2)}) collective-permute-start(f32[32,512]{1,0:T(8,128)S(1)} %add_rows.14.refs_8_), channel_id=1, source_target_pairs={{0,16},{1,17},{2,18},{3,19},{4,20},{5,21},{6,22},{7,23},{8,24},{9,... | collective-permute-start | bytes 196616 | tf_op jit(solution)/shard_map/ppermute | solution.py:429
  30.3 6.0 %collective-permute-start.9 = (f32[80,512]{1,0:T(8,128)S(1)}, f32[80,512]{1,0:T(8,128)S(1)}, u32[]{:S(2)}, u32[]{:S(2)}) collective-permute-start(f32[80,512]{1,0:T(8,128)S(1)} %get-tuple-element.57), channel_id=1, source_target_pairs={{0,8},{1,9},{2,10},{3,11},{4,12},{5,13},{6,14},{7,15},{8,0},{9,1},... | collective-permute-start | bytes 491528 | tf_op jit(solution)/shard_map/ppermute | solution.py:429
  31.8 7.9 %collective-permute-start.10 = (f32[80,512]{1,0:T(8,128)S(1)}, f32[80,512]{1,0:T(8,128)S(1)}, u32[]{:S(2)}, u32[]{:S(2)}) collective-permute-start(f32[80,512]{1,0:T(8,128)S(1)} %get-tuple-element.58), channel_id=1, source_target_pairs={{0,8},{1,9},{2,10},{3,11},{4,12},{5,13},{6,14},{7,15},{8,0},{9,1},... | collective-permute-start | bytes 491528 | tf_op jit(solution)/shard_map/ppermute | solution.py:429
  36.2 10.3 %collective-permute-start.13 = (bf16[256,512]{1,0:T(8,128)(2,1)S(1)}, bf16[256,512]{1,0:T(8,128)(2,1)S(1)}, u32[]{:S(2)}, u32[]{:S(2)}) collective-permute-start(bf16[256,512]{1,0:T(8,128)(2,1)S(1)} %get-tuple-element.62), channel_id=1, source_target_pairs={{0,4},{1,5},{2,6},{3,7},{4,0},{5,1},{6,2},{7,3},{8,12},{9,13},{10,... | collective-permute-start | bytes 786440 | tf_op jit(solution)/shard_map/ppermute | solution.py:429
  39.7 11.9 %collective-permute-start.14 = (bf16[256,512]{1,0:T(8,128)(2,1)S(1)}, bf16[256,512]{1,0:T(8,128)(2,1)S(1)}, u32[]{:S(2)}, u32[]{:S(2)}) collective-permute-start(bf16[256,512]{1,0:T(8,128)(2,1)S(1)} %get-tuple-element.63), channel_id=1, source_target_pairs={{0,6},{1,7},{2,4},{3,5},{4,2},{5,3},{6,0},{7,1},{8,14},{9,15},{10,... | collective-permute-start | bytes 786440 | tf_op jit(solution)/shard_map/ppermute | solution.py:429
  42.5 11.6 %collective-permute-start.12 = (f32[64,512]{1,0:T(8,128)S(1)}, f32[64,512]{1,0:T(8,128)S(1)}, u32[]{:S(2)}, u32[]{:S(2)}) collective-permute-start(f32[64,512]{1,0:T(8,128)S(1)} %get-tuple-element.61), channel_id=1, source_target_pairs={{0,8},{1,9},{2,10},{3,11},{4,12},{5,13},{6,14},{7,15},{8,0},{9,1},... | collective-permute-start | bytes 393224 | tf_op jit(solution)/shard_map/ppermute | solution.py:429
  43.9 16.3 %collective-permute-start.20 = (f32[80,512]{1,0:T(8,128)S(1)}, f32[80,512]{1,0:T(8,128)S(1)}, u32[]{:S(2)}, u32[]{:S(2)}) collective-permute-start(f32[80,512]{1,0:T(8,128)S(1)} %add_rows.15.refs_8_), channel_id=1, source_target_pairs={{0,16},{1,17},{2,18},{3,19},{4,20},{5,21},{6,22},{7,23},{8,24},{9,... | collective-permute-start | bytes 491528 | tf_op jit(solution)/shard_map/ppermute | solution.py:429
  46.3 10.3 %collective-permute-start.11 = (f32[64,512]{1,0:T(8,128)S(1)}, f32[64,512]{1,0:T(8,128)S(1)}, u32[]{:S(2)}, u32[]{:S(2)}) collective-permute-start(f32[64,512]{1,0:T(8,128)S(1)} %get-tuple-element.60), channel_id=1, source_target_pairs={{0,8},{1,9},{2,10},{3,11},{4,12},{5,13},{6,14},{7,15},{8,0},{9,1},... | collective-permute-start | bytes 393224 | tf_op jit(solution)/shard_map/ppermute | solution.py:429
  54.1 10.6 %collective-permute-start.17 = (f32[64,512]{1,0:T(8,128)S(1)}, f32[64,512]{1,0:T(8,128)S(1)}, u32[]{:S(2)}, u32[]{:S(2)}) collective-permute-start(f32[64,512]{1,0:T(8,128)S(1)} %get-tuple-element.66), channel_id=1, source_target_pairs={{0,8},{1,9},{2,10},{3,11},{4,12},{5,13},{6,14},{7,15},{8,0},{9,1},... | collective-permute-start | bytes 393224 | tf_op jit(solution)/shard_map/ppermute | solution.py:429
  54.2 8.5 %collective-permute-start.16 = (f32[64,512]{1,0:T(8,128)S(1)}, f32[64,512]{1,0:T(8,128)S(1)}, u32[]{:S(2)}, u32[]{:S(2)}) collective-permute-start(f32[64,512]{1,0:T(8,128)S(1)} %add_rows.17.refs_2_), channel_id=1, source_target_pairs={{0,16},{1,17},{2,18},{3,19},{4,20},{5,21},{6,22},{7,23},{8,24},{9,... | collective-permute-start | bytes 393224 | tf_op jit(solution)/shard_map/ppermute | solution.py:429
  57.7 8.1 %collective-permute-start.19 = (f32[64,512]{1,0:T(8,128)S(1)}, f32[64,512]{1,0:T(8,128)S(1)}, u32[]{:S(2)}, u32[]{:S(2)}) collective-permute-start(f32[64,512]{1,0:T(8,128)S(1)} %add_rows.19.refs_3_), channel_id=1, source_target_pairs={{0,16},{1,17},{2,18},{3,19},{4,20},{5,21},{6,22},{7,23},{8,24},{9,... | collective-permute-start | bytes 393224 | tf_op jit(solution)/shard_map/ppermute | solution.py:429
  60.3 6.8 %collective-permute-start.21 = (f32[112,512]{1,0:T(8,128)S(1)}, f32[112,512]{1,0:T(8,128)S(1)}, u32[]{:S(2)}, u32[]{:S(2)}) collective-permute-start(f32[112,512]{1,0:T(8,128)S(1)} %pad_maximum_fusion.2.refs_0_.refs_4_), channel_id=1, source_target_pairs={{0,1},{1,0},{2,3},{3,2},{4,5},{5,4},{6,7},{7,6},{8,9},{9,8},{10,11... | collective-permute-start | bytes 688136 | tf_op jit(solution)/shard_map/ppermute | solution.py:429
  91.6 6.0 %collective-permute-start.34 = (f32[2,40,256]{2,1,0:T(8,128)S(1)}, f32[2,40,256]{2,1,0:T(8,128)S(1)}, u32[]{:S(2)}, u32[]{:S(2)}) collective-permute-start(f32[2,40,256]{2,1,0:T(8,128)S(1)} %add_rows.26), channel_id=1, source_target_pairs={{0,8},{1,9},{2,10},{3,11},{4,12},{5,13},{6,14},{7,15},{8,0},{9,1},... | collective-permute-start | bytes 245768 | tf_op jit(solution)/shard_map/ppermute | solution.py:429
  102.1 9.9 %collective-permute-start.41 = (f32[8,40,256]{2,1,0:T(8,128)S(1)}, f32[8,40,256]{2,1,0:T(8,128)S(1)}, u32[]{:S(2)}, u32[]{:S(2)}) collective-permute-start(f32[8,40,256]{2,1,0:T(8,128)S(1)} %pad_maximum_fusion.refs_0_), channel_id=1, source_target_pairs={{0,1},{1,0},{2,3},{3,2},{4,5},{5,4},{6,7},{7,6},{8,9},{9,8},{10,11... | collective-permute-start | bytes 983048 | tf_op jit(solution)/shard_map/ppermute | solution.py:429
  105.0 8.8 %collective-permute-start.37 = (f32[8,32,256]{2,1,0:T(8,128)S(1)}, f32[8,32,256]{2,1,0:T(8,128)S(1)}, u32[]{:S(2)}, u32[]{:S(2)}) collective-permute-start(f32[8,32,256]{2,1,0:T(8,128)S(1)} %pad_maximum_fusion.1.refs_0_), channel_id=1, source_target_pairs={{0,4},{1,5},{2,6},{3,7},{4,0},{5,1},{6,2},{7,3},{8,12},{9,13},{10,... | collective-permute-start | bytes 786440 | tf_op jit(solution)/shard_map/ppermute | solution.py:429
  106.4 10.3 %collective-permute-start.42 = (f32[8,40,256]{2,1,0:T(8,128)S(1)}, f32[8,40,256]{2,1,0:T(8,128)S(1)}, u32[]{:S(2)}, u32[]{:S(2)}) collective-permute-start(f32[8,40,256]{2,1,0:T(8,128)S(1)} %pad_maximum_fusion.refs_0_), channel_id=1, source_target_pairs={{0,2},{1,3},{2,0},{3,1},{4,6},{5,7},{6,4},{7,5},{8,10},{9,11},{10,... | collective-permute-start | bytes 983048 | tf_op jit(solution)/shard_map/ppermute | solution.py:429
  (21 other events, 96.2 us)

commit v12 on v7

--- a/solution.py
+++ b/solution.py
@@ -520,9 +520,10 @@
         after=[near_sent],
     )
     cross_core = [flip(far[4:], "c"), flip(far[:4], "c")]
-    cross_x = flip(add([cross_own[4:], cross_core[0]], []), "x")
-
-    near = own[:4] + core[1] + near_x
+    cross_sent = add([cross_own[4:], cross_core[0]], [])
+    cross_x = flip(cross_sent, "x")
+
+    near = add([own[:4], core[1], near_x], [cross_sent])
     near_z1 = flip(near[2:], "z1")
     near = near[:2] + near_z1
     near_z2 = flip(near, "z2")

time: 121 us -> 121 us (level)
  transfers between devices with their start and end apart: 43 -> 43, of which waited for: 21 -> 22; matrix products, arithmetic and copies ran while one was open for 0% -> 0% of each run, Pallas kernels for 8% -> 8%
where the time goes in v12:
time: 121 us
  starting transfers between devices  52.4 us (43%)
  waiting for transfers between devices  51.4 us (42%)
  Pallas kernels  15.4 us (13%)
    ppermute x43, starting transfers between devices, flip(): lax.ppermute(value, ('dp', 'fsdp'), [(i, i ^ mask) for i in range(count)])  52.4 us
    ppermute x43, waiting for transfers between devices, flip(): lax.ppermute(value, ('dp', 'fsdp'), [(i, i ^ mask) for i in range(count)])  51.4 us
    pallas_call x4, Pallas kernels, gram_part(): pl.pallas_call(functools.partial(kernel, count, len(bases), early), in_sp...  4.29 us
    pallas_call x1, Pallas kernels, update(): pl.pallas_call(functools.partial(finish_kernel, scale, places, count), in...  3.43 us
    pallas_call x4, Pallas kernels, dequant(): pl.pallas_call(kernel, in_specs=[SCALARS] + [WHOLE] * 7 + [ANYWHERE] * (l...  2.98 us
    pallas_call x1, Pallas kernels, pack(): pl.pallas_call(functools.partial(pack_kernel, own_rows, spans), in_specs=...  2.51 us
  transfers between devices with their start and end apart: 43, of which 22 were waited for; matrix products, arithmetic and copies ran while one was open for 0% of the time, Pallas kernels for 8%

profile of v12, /device:TPU:1, one launch (start us, length us, event | category | flops | bytes accessed | tf_op | source)
XLA Modules:
  0.0 120.8 jit_solution(11664500650139682285)
XLA Ops:
  0.9 2.5 %pack_rows.1 = (bf16[960,512]{1,0:T(8,128)(2,1)S(1)}, f32[16,512]{1,0:T(8,128)S(1)}, bf16[1008,512]{1,0:T(8,128)(2,1)S(1)}, bf16[240,512]{1,0:T(8,128)(2,1)S(1)}...) custom-call(s32[4]{0:T(128)S(1)} %pad_add_fusion.at.refs_0_, ...), custom_call_target="tpu_custom_call" | custom-call | tf_op jit(solution)/shard_map/pack_rows/pallas_call | solution.py:126
  3.5 2.7 %collective-permute-start.1 = (bf16[240,512]{1,0:T(8,128)(2,1)S(1)}, bf16[240,512]{1,0:T(8,128)(2,1)S(1)}, u32[]{:S(2)}, u32[]{:S(2)}) collective-permute-start(bf16[240,512]{1,0:T(8,128)(2,1)S(1)} %get-tuple-element.44), channel_id=1, source_target_pairs={{0,4},{1,5},{2,6},{3,7},{4,0},{5,1},{6,2},{7,3},{8,12},{9,13},{10,... | collective-permute-start | bytes 737288 | tf_op jit(solution)/shard_map/ppermute | solution.py:429
  8.3 4.2 %collective-permute-done.1.refs_4_.refs_6_ = bf16[240,512]{1,0:T(8,128)(2,1)S(1)} collective-permute-done((bf16[240,512]{1,0:T(8,128)(2,1)S(1)}, bf16[240,512]{1,0:T(8,128)(2,1)S(1)}, u32[]{:S(2)}, u32[]{:S(2)}) %collective-permute-start.1) | collective-permute-done | bytes 245792 | tf_op jit(solution)/shard_map/ppermute | solution.py:429
  12.5 5.5 %collective-permute-done.2.refs_5_.refs_7_ = bf16[240,512]{1,0:T(8,128)(2,1)S(1)} collective-permute-done((bf16[240,512]{1,0:T(8,128)(2,1)S(1)}, bf16[240,512]{1,0:T(8,128)(2,1)S(1)}, u32[]{:S(2)}, u32[]{:S(2)}) %collective-permute-start.2) | collective-permute-done | bytes 245792 | tf_op jit(solution)/shard_map/ppermute | solution.py:429
  21.9 3.7 %collective-permute-done.7.refs_1_ = f32[48,512]{1,0:T(8,128)S(1)} collective-permute-done((f32[48,512]{1,0:T(8,128)S(1)}, f32[48,512]{1,0:T(8,128)S(1)}, u32[]{:S(2)}, u32[]{:S(2)}) %collective-permute-start.7) | collective-permute-done | bytes 98336 | tf_op jit(solution)/shard_map/ppermute | solution.py:429
  25.6 2.0 %collective-permute-start.4 = (bf16[256,512]{1,0:T(8,128)(2,1)S(1)}, bf16[256,512]{1,0:T(8,128)(2,1)S(1)}, u32[]{:S(2)}, u32[]{:S(2)}) collective-permute-start(bf16[256,512]{1,0:T(8,128)(2,1)S(1)} %get-tuple-element.49), channel_id=1, source_target_pairs={{0,6},{1,7},{2,4},{3,5},{4,2},{5,3},{6,0},{7,1},{8,14},{9,15},{10,... | collective-permute-start | bytes 786440 | tf_op jit(solution)/shard_map/ppermute | solution.py:429
  27.6 2.4 %collective-permute-start.15 = (f32[48,512]{1,0:T(8,128)S(1)}, f32[48,512]{1,0:T(8,128)S(1)}, u32[]{:S(2)}, u32[]{:S(2)}) collective-permute-start(f32[48,512]{1,0:T(8,128)S(1)} %add_rows.15.refs_8_), channel_id=1, source_target_pairs={{0,16},{1,17},{2,18},{3,19},{4,20},{5,21},{6,22},{7,23},{8,24},{9,... | collective-permute-start | bytes 294920 | tf_op jit(solution)/shard_map/ppermute | solution.py:429
  30.0 2.2 %collective-permute-done.6.refs_7_ = bf16[320,512]{1,0:T(8,128)(2,1)S(1)} collective-permute-done((bf16[320,512]{1,0:T(8,128)(2,1)S(1)}, bf16[320,512]{1,0:T(8,128)(2,1)S(1)}, u32[]{:S(2)}, u32[]{:S(2)}) %collective-permute-start.6) | collective-permute-done | bytes 327712 | tf_op jit(solution)/shard_map/ppermute | solution.py:429
  35.0 4.6 %collective-permute-done.10.refs_9_.refs_1_ = f32[80,512]{1,0:T(8,128)S(1)} collective-permute-done((f32[80,512]{1,0:T(8,128)S(1)}, f32[80,512]{1,0:T(8,128)S(1)}, u32[]{:S(2)}, u32[]{:S(2)}) %collective-permute-start.10) | collective-permute-done | bytes 163872 | tf_op jit(solution)/shard_map/ppermute | solution.py:429
  41.0 2.1 %collective-permute-done.9.refs_8_ = f32[80,512]{1,0:T(8,128)S(1)} collective-permute-done((f32[80,512]{1,0:T(8,128)S(1)}, f32[80,512]{1,0:T(8,128)S(1)}, u32[]{:S(2)}, u32[]{:S(2)}) %collective-permute-start.9) | collective-permute-done | bytes 163872 | tf_op jit(solution)/shard_map/ppermute | solution.py:429
  47.1 2.3 %collective-permute-start.20 = (f32[80,512]{1,0:T(8,128)S(1)}, f32[80,512]{1,0:T(8,128)S(1)}, u32[]{:S(2)}, u32[]{:S(2)}) collective-permute-start(f32[80,512]{1,0:T(8,128)S(1)} %add_rows.16.refs_8_), channel_id=1, source_target_pairs={{0,16},{1,17},{2,18},{3,19},{4,20},{5,21},{6,22},{7,23},{8,24},{9,... | collective-permute-start | bytes 491528 | tf_op jit(solution)/shard_map/ppermute | solution.py:429
  49.5 2.2 %collective-permute-done.14.refs_7_ = bf16[192,512]{1,0:T(8,128)(2,1)S(1)} collective-permute-done((bf16[192,512]{1,0:T(8,128)(2,1)S(1)}, bf16[192,512]{1,0:T(8,128)(2,1)S(1)}, u32[]{:S(2)}, u32[]{:S(2)}) %collective-permute-start.14) | collective-permute-done | bytes 196640 | tf_op jit(solution)/shard_map/ppermute | solution.py:429
  54.1 2.8 %collective-permute-done.12.refs_1_ = f32[64,512]{1,0:T(8,128)S(1)} collective-permute-done((f32[64,512]{1,0:T(8,128)S(1)}, f32[64,512]{1,0:T(8,128)S(1)}, u32[]{:S(2)}, u32[]{:S(2)}) %collective-permute-start.12) | collective-permute-done | bytes 131104 | tf_op jit(solution)/shard_map/ppermute | solution.py:429
  60.5 2.4 %collective-permute-start.19 = (f32[48,512]{1,0:T(8,128)S(1)}, f32[48,512]{1,0:T(8,128)S(1)}, u32[]{:S(2)}, u32[]{:S(2)}) collective-permute-start(f32[48,512]{1,0:T(8,128)S(1)} %add_rows.20.refs_3_), channel_id=1, source_target_pairs={{0,16},{1,17},{2,18},{3,19},{4,20},{5,21},{6,22},{7,23},{8,24},{9,... | collective-permute-start | bytes 294920 | tf_op jit(solution)/shard_map/ppermute | solution.py:429
  64.6 6.2 %collective-permute-done.19.refs_1_ = f32[48,512]{1,0:T(8,128)S(1)} collective-permute-done((f32[48,512]{1,0:T(8,128)S(1)}, f32[48,512]{1,0:T(8,128)S(1)}, u32[]{:S(2)}, u32[]{:S(2)}) %collective-permute-start.19) | collective-permute-done | bytes 98336 | tf_op jit(solution)/shard_map/ppermute | solution.py:429
  82.3 2.2 %collective-permute-done.29.refs_3_ = f32[2,40,256]{2,1,0:T(8,128)S(1)} collective-permute-done((f32[2,40,256]{2,1,0:T(8,128)S(1)}, f32[2,40,256]{2,1,0:T(8,128)S(1)}, u32[]{:S(2)}, u32[]{:S(2)}) %collective-permute-start.29) | collective-permute-done | bytes 81952 | tf_op jit(solution)/shard_map/ppermute | solution.py:429
  85.2 1.9 %collective-permute-done.26.refs_2_ = f32[4,32,256]{2,1,0:T(8,128)S(1)} collective-permute-done((f32[4,32,256]{2,1,0:T(8,128)S(1)}, f32[4,32,256]{2,1,0:T(8,128)S(1)}, u32[]{:S(2)}, u32[]{:S(2)}) %collective-permute-start.26) | collective-permute-done | bytes 131104 | tf_op jit(solution)/shard_map/ppermute | solution.py:429
  91.0 2.2 %collective-permute-start.32 = (f32[2,32,256]{2,1,0:T(8,128)S(1)}, f32[2,32,256]{2,1,0:T(8,128)S(1)}, u32[]{:S(2)}, u32[]{:S(2)}) collective-permute-start(f32[2,32,256]{2,1,0:T(8,128)S(1)} %add_rows.27.refs_0_), channel_id=1, source_target_pairs={{0,16},{1,17},{2,18},{3,19},{4,20},{5,21},{6,22},{7,23},{8,24},{9,... | collective-permute-start | bytes 196616 | tf_op jit(solution)/shard_map/ppermute | solution.py:429
  96.7 2.3 %collective-permute-done.34 = f32[2,32,256]{2,1,0:T(8,128)S(1)} collective-permute-done((f32[2,32,256]{2,1,0:T(8,128)S(1)}, f32[2,32,256]{2,1,0:T(8,128)S(1)}, u32[]{:S(2)}, u32[]{:S(2)}) %collective-permute-start.34) | collective-permute-done | bytes 65568 | tf_op jit(solution)/shard_map/ppermute | solution.py:429
  103.3 6.5 %collective-permute-start.41 = (f32[8,40,256]{2,1,0:T(8,128)S(1)}, f32[8,40,256]{2,1,0:T(8,128)S(1)}, u32[]{:S(2)}, u32[]{:S(2)}) collective-permute-start(f32[8,40,256]{2,1,0:T(8,128)S(1)} %pad_maximum_fusion.refs_0_), channel_id=1, source_target_pairs={{0,2},{1,3},{2,0},{3,1},{4,6},{5,7},{6,4},{7,5},{8,10},{9,11},{10,... | collective-permute-start | bytes 983048 | tf_op jit(solution)/shard_map/ppermute | solution.py:429
  109.8 2.8 %collective-permute-start.42 = (f32[8,40,256]{2,1,0:T(8,128)S(1)}, f32[8,40,256]{2,1,0:T(8,128)S(1)}, u32[]{:S(2)}, u32[]{:S(2)}) collective-permute-start(f32[8,40,256]{2,1,0:T(8,128)S(1)} %collective-permute-done.40.refs_1_), channel_id=1, source_target_pairs={{0,2},{1,3},{2,0},{3,1},{4,6},{5,7},{6,4},{7,5},{8,10},{9,11},{10,... | collective-permute-start | bytes 983048 | tf_op jit(solution)/shard_map/ppermute | solution.py:429
  112.6 2.7 %collective-permute-start.38 = (f32[8,32,256]{2,1,0:T(8,128)S(1)}, f32[8,32,256]{2,1,0:T(8,128)S(1)}, u32[]{:S(2)}, u32[]{:S(2)}) collective-permute-start(f32[8,32,256]{2,1,0:T(8,128)S(1)} %collective-permute-done.36.refs_1_), channel_id=1, source_target_pairs={{0,2},{1,3},{2,0},{3,1},{4,6},{5,7},{6,4},{7,5},{8,10},{9,11},{10,... | collective-permute-start | bytes 786440 | tf_op jit(solution)/shard_map/ppermute | solution.py:429
  115.3 2.0 %update_start.1 = (bf16[2,512,512]{2,1,0:T(8,128)(2,1)S(1)}, bf16[2,512,512]{2,1,0:T(8,128)(2,1)S(1)}, f32[8,128]{1,0:T(8,128)S(1)}, f32[240,512]{1,0:T(8,128)S(1)}, f32[240,512]{1,0:T(8,128)S(1)}) custom-call(s32[4]{0:T(128)S(1)} %pad_add_fusion.at.refs_0_, f32[8,40,256]{2,1,0:T(8,128)S(1)} %pad_maximum_fusion.refs_0_, ...), custom_call_target="tpu_custom_call" | custom-call | tf_op jit(solution)/shard_map/update_start/pallas_call | solution.py:401
  117.3 3.4 %update_finish.1 = bf16[240,512]{1,0:T(8,128)(2,1)} custom-call(s32[4]{0:T(128)S(1)} %pad_add_fusion.at.refs_0_, f32[8,32,256]{2,1,0:T(8,128)S(1)} %pad_maximum_fusion.2.refs_0_, f32[8,32,256]{2,1,0:T(8,128)S(1)} %collective-permute-done.36.refs_1_, f32[8,32,256]{2,1,0:T(8,128)S(1)} %collective-permute-done.37.refs_2_, ...), custom_call_target="tpu_custom_call" | custom-call | tf_op jit(solution)/shard_map/update_finish/pallas_call | solution.py:411
  (112 shorter events, 46.6 us)
Async XLA Ops:
  3.4 14.5 %collective-permute-start = (bf16[1008,512]{1,0:T(8,128)(2,1)S(1)}, bf16[1008,512]{1,0:T(8,128)(2,1)S(1)}, u32[]{:S(2)}, u32[]{:S(2)}) collective-permute-start(bf16[1008,512]{1,0:T(8,128)(2,1)S(1)} %get-tuple-element.43), channel_id=1, source_target_pairs={{0,2},{1,3},{2,0},{3,1},{4,6},{5,7},{6,4},{7,5},{8,10},{9,11},{10,... | collective-permute-start | bytes 3096584 | tf_op jit(solution)/shard_map/ppermute | solution.py:429
  3.5 8.9 %collective-permute-start.1 = (bf16[240,512]{1,0:T(8,128)(2,1)S(1)}, bf16[240,512]{1,0:T(8,128)(2,1)S(1)}, u32[]{:S(2)}, u32[]{:S(2)}) collective-permute-start(bf16[240,512]{1,0:T(8,128)(2,1)S(1)} %get-tuple-element.44), channel_id=1, source_target_pairs={{0,4},{1,5},{2,6},{3,7},{4,0},{5,1},{6,2},{7,3},{8,12},{9,13},{10,... | collective-permute-start | bytes 737288 | tf_op jit(solution)/shard_map/ppermute | solution.py:429
  6.2 11.7 %collective-permute-start.2 = (bf16[240,512]{1,0:T(8,128)(2,1)S(1)}, bf16[240,512]{1,0:T(8,128)(2,1)S(1)}, u32[]{:S(2)}, u32[]{:S(2)}) collective-permute-start(bf16[240,512]{1,0:T(8,128)(2,1)S(1)} %get-tuple-element.45), channel_id=1, source_target_pairs={{0,6},{1,7},{2,4},{3,5},{4,2},{5,3},{6,0},{7,1},{8,14},{9,15},{10,... | collective-permute-start | bytes 737288 | tf_op jit(solution)/shard_map/ppermute | solution.py:429
  6.3 23.8 %collective-permute-start.5 = (bf16[320,512]{1,0:T(8,128)(2,1)S(1)}, bf16[320,512]{1,0:T(8,128)(2,1)S(1)}, u32[]{:S(2)}, u32[]{:S(2)}) collective-permute-start(bf16[320,512]{1,0:T(8,128)(2,1)S(1)} %get-tuple-element.50), channel_id=1, source_target_pairs={{0,4},{1,5},{2,6},{3,7},{4,0},{5,1},{6,2},{7,3},{8,12},{9,13},{10,... | collective-permute-start | bytes 983048 | tf_op jit(solution)/shard_map/ppermute | solution.py:429
  7.9 24.4 %collective-permute-start.6 = (bf16[320,512]{1,0:T(8,128)(2,1)S(1)}, bf16[320,512]{1,0:T(8,128)(2,1)S(1)}, u32[]{:S(2)}, u32[]{:S(2)}) collective-permute-start(bf16[320,512]{1,0:T(8,128)(2,1)S(1)} %get-tuple-element.51), channel_id=1, source_target_pairs={{0,6},{1,7},{2,4},{3,5},{4,2},{5,3},{6,0},{7,1},{8,14},{9,15},{10,... | collective-permute-start | bytes 983048 | tf_op jit(solution)/shard_map/ppermute | solution.py:429
  18.7 9.0 %collective-permute-start.8 = (f32[48,512]{1,0:T(8,128)S(1)}, f32[48,512]{1,0:T(8,128)S(1)}, u32[]{:S(2)}, u32[]{:S(2)}) collective-permute-start(f32[48,512]{1,0:T(8,128)S(1)} %get-tuple-element.54), channel_id=1, source_target_pairs={{0,8},{1,9},{2,10},{3,11},{4,12},{5,13},{6,14},{7,15},{8,0},{9,1},... | collective-permute-start | bytes 294920 | tf_op jit(solution)/shard_map/ppermute | solution.py:429
  20.6 24.1 %collective-permute-start.3 = (bf16[256,512]{1,0:T(8,128)(2,1)S(1)}, bf16[256,512]{1,0:T(8,128)(2,1)S(1)}, u32[]{:S(2)}, u32[]{:S(2)}) collective-permute-start(bf16[256,512]{1,0:T(8,128)(2,1)S(1)} %get-tuple-element.48), channel_id=1, source_target_pairs={{0,4},{1,5},{2,6},{3,7},{4,0},{5,1},{6,2},{7,3},{8,12},{9,13},{10,... | collective-permute-start | bytes 786440 | tf_op jit(solution)/shard_map/ppermute | solution.py:429
  25.6 19.1 %collective-permute-start.4 = (bf16[256,512]{1,0:T(8,128)(2,1)S(1)}, bf16[256,512]{1,0:T(8,128)(2,1)S(1)}, u32[]{:S(2)}, u32[]{:S(2)}) collective-permute-start(bf16[256,512]{1,0:T(8,128)(2,1)S(1)} %get-tuple-element.49), channel_id=1, source_target_pairs={{0,6},{1,7},{2,4},{3,5},{4,2},{5,3},{6,0},{7,1},{8,14},{9,15},{10,... | collective-permute-start | bytes 786440 | tf_op jit(solution)/shard_map/ppermute | solution.py:429
  27.6 19.5 %collective-permute-start.15 = (f32[48,512]{1,0:T(8,128)S(1)}, f32[48,512]{1,0:T(8,128)S(1)}, u32[]{:S(2)}, u32[]{:S(2)}) collective-permute-start(f32[48,512]{1,0:T(8,128)S(1)} %add_rows.15.refs_8_), channel_id=1, source_target_pairs={{0,16},{1,17},{2,18},{3,19},{4,20},{5,21},{6,22},{7,23},{8,24},{9,... | collective-permute-start | bytes 294920 | tf_op jit(solution)/shard_map/ppermute | solution.py:429
  34.9 8.2 %collective-permute-start.9 = (f32[80,512]{1,0:T(8,128)S(1)}, f32[80,512]{1,0:T(8,128)S(1)}, u32[]{:S(2)}, u32[]{:S(2)}) collective-permute-start(f32[80,512]{1,0:T(8,128)S(1)} %get-tuple-element.57), channel_id=1, source_target_pairs={{0,8},{1,9},{2,10},{3,11},{4,12},{5,13},{6,14},{7,15},{8,0},{9,1},... | collective-permute-start | bytes 491528 | tf_op jit(solution)/shard_map/ppermute | solution.py:429
  39.6 9.8 %collective-permute-start.13 = (bf16[192,512]{1,0:T(8,128)(2,1)S(1)}, bf16[192,512]{1,0:T(8,128)(2,1)S(1)}, u32[]{:S(2)}, u32[]{:S(2)}) collective-permute-start(bf16[192,512]{1,0:T(8,128)(2,1)S(1)} %get-tuple-element.62), channel_id=1, source_target_pairs={{0,4},{1,5},{2,6},{3,7},{4,0},{5,1},{6,2},{7,3},{8,12},{9,13},{10,... | collective-permute-start | bytes 589832 | tf_op jit(solution)/shard_map/ppermute | solution.py:429
  43.1 8.5 %collective-permute-start.14 = (bf16[192,512]{1,0:T(8,128)(2,1)S(1)}, bf16[192,512]{1,0:T(8,128)(2,1)S(1)}, u32[]{:S(2)}, u32[]{:S(2)}) collective-permute-start(bf16[192,512]{1,0:T(8,128)(2,1)S(1)} %get-tuple-element.63), channel_id=1, source_target_pairs={{0,6},{1,7},{2,4},{3,5},{4,2},{5,3},{6,0},{7,1},{8,14},{9,15},{10,... | collective-permute-start | bytes 589832 | tf_op jit(solution)/shard_map/ppermute | solution.py:429
  45.5 15.0 %collective-permute-start.11 = (f32[64,512]{1,0:T(8,128)S(1)}, f32[64,512]{1,0:T(8,128)S(1)}, u32[]{:S(2)}, u32[]{:S(2)}) collective-permute-start(f32[64,512]{1,0:T(8,128)S(1)} %get-tuple-element.60), channel_id=1, source_target_pairs={{0,8},{1,9},{2,10},{3,11},{4,12},{5,13},{6,14},{7,15},{8,0},{9,1},... | collective-permute-start | bytes 393224 | tf_op jit(solution)/shard_map/ppermute | solution.py:429
  46.7 10.2 %collective-permute-start.12 = (f32[64,512]{1,0:T(8,128)S(1)}, f32[64,512]{1,0:T(8,128)S(1)}, u32[]{:S(2)}, u32[]{:S(2)}) collective-permute-start(f32[64,512]{1,0:T(8,128)S(1)} %get-tuple-element.61), channel_id=1, source_target_pairs={{0,8},{1,9},{2,10},{3,11},{4,12},{5,13},{6,14},{7,15},{8,0},{9,1},... | collective-permute-start | bytes 393224 | tf_op jit(solution)/shard_map/ppermute | solution.py:429
  47.1 12.0 %collective-permute-start.20 = (f32[80,512]{1,0:T(8,128)S(1)}, f32[80,512]{1,0:T(8,128)S(1)}, u32[]{:S(2)}, u32[]{:S(2)}) collective-permute-start(f32[80,512]{1,0:T(8,128)S(1)} %add_rows.16.refs_8_), channel_id=1, source_target_pairs={{0,16},{1,17},{2,18},{3,19},{4,20},{5,21},{6,22},{7,23},{8,24},{9,... | collective-permute-start | bytes 491528 | tf_op jit(solution)/shard_map/ppermute | solution.py:429
  54.0 9.4 %collective-permute-start.17 = (f32[48,512]{1,0:T(8,128)S(1)}, f32[48,512]{1,0:T(8,128)S(1)}, u32[]{:S(2)}, u32[]{:S(2)}) collective-permute-start(f32[48,512]{1,0:T(8,128)S(1)} %get-tuple-element.66), channel_id=1, source_target_pairs={{0,8},{1,9},{2,10},{3,11},{4,12},{5,13},{6,14},{7,15},{8,0},{9,1},... | collective-permute-start | bytes 294920 | tf_op jit(solution)/shard_map/ppermute | solution.py:429
  57.0 7.6 %collective-permute-start.16 = (f32[64,512]{1,0:T(8,128)S(1)}, f32[64,512]{1,0:T(8,128)S(1)}, u32[]{:S(2)}, u32[]{:S(2)}) collective-permute-start(f32[64,512]{1,0:T(8,128)S(1)} %add_rows.18.refs_2_), channel_id=1, source_target_pairs={{0,16},{1,17},{2,18},{3,19},{4,20},{5,21},{6,22},{7,23},{8,24},{9,... | collective-permute-start | bytes 393224 | tf_op jit(solution)/shard_map/ppermute | solution.py:429
  59.1 11.6 %collective-permute-start.21 = (f32[128,512]{1,0:T(8,128)S(1)}, f32[128,512]{1,0:T(8,128)S(1)}, u32[]{:S(2)}, u32[]{:S(2)}) collective-permute-start(f32[128,512]{1,0:T(8,128)S(1)} %pad_maximum_fusion.1.refs_0_.refs_4_), channel_id=1, source_target_pairs={{0,1},{1,0},{2,3},{3,2},{4,5},{5,4},{6,7},{7,6},{8,9},{9,8},{10,11... | collective-permute-start | bytes 786440 | tf_op jit(solution)/shard_map/ppermute | solution.py:429
  60.5 10.3 %collective-permute-start.19 = (f32[48,512]{1,0:T(8,128)S(1)}, f32[48,512]{1,0:T(8,128)S(1)}, u32[]{:S(2)}, u32[]{:S(2)}) collective-permute-start(f32[48,512]{1,0:T(8,128)S(1)} %add_rows.20.refs_3_), channel_id=1, source_target_pairs={{0,16},{1,17},{2,18},{3,19},{4,20},{5,21},{6,22},{7,23},{8,24},{9,... | collective-permute-start | bytes 294920 | tf_op jit(solution)/shard_map/ppermute | solution.py:429
  70.8 6.7 %collective-permute-start.22 = (f32[112,512]{1,0:T(8,128)S(1)}, f32[112,512]{1,0:T(8,128)S(1)}, u32[]{:S(2)}, u32[]{:S(2)}) collective-permute-start(f32[112,512]{1,0:T(8,128)S(1)} %pad_maximum_fusion.3.refs_0_.refs_5_), channel_id=1, source_target_pairs={{0,1},{1,0},{2,3},{3,2},{4,5},{5,4},{6,7},{7,6},{8,9},{9,8},{10,11... | collective-permute-start | bytes 688136 | tf_op jit(solution)/shard_map/ppermute | solution.py:429
  74.1 6.9 %collective-permute-start.27 = (f32[4,40,256]{2,1,0:T(8,128)S(1)}, f32[4,40,256]{2,1,0:T(8,128)S(1)}, u32[]{:S(2)}, u32[]{:S(2)}) collective-permute-start(f32[4,40,256]{2,1,0:T(8,128)S(1)} %get-tuple-element.77), channel_id=1, source_target_pairs={{0,2},{1,3},{2,0},{3,1},{4,6},{5,7},{6,4},{7,5},{8,10},{9,11},{10,... | collective-permute-start | bytes 491528 | tf_op jit(solution)/shard_map/ppermute | solution.py:429
  100.8 9.0 %collective-permute-start.40 = (f32[8,40,256]{2,1,0:T(8,128)S(1)}, f32[8,40,256]{2,1,0:T(8,128)S(1)}, u32[]{:S(2)}, u32[]{:S(2)}) collective-permute-start(f32[8,40,256]{2,1,0:T(8,128)S(1)} %pad_maximum_fusion.refs_0_), channel_id=1, source_target_pairs={{0,1},{1,0},{2,3},{3,2},{4,5},{5,4},{6,7},{7,6},{8,9},{9,8},{10,11... | collective-permute-start | bytes 983048 | tf_op jit(solution)/shard_map/ppermute | solution.py:429
  103.2 9.4 %collective-permute-start.36 = (f32[8,32,256]{2,1,0:T(8,128)S(1)}, f32[8,32,256]{2,1,0:T(8,128)S(1)}, u32[]{:S(2)}, u32[]{:S(2)}) collective-permute-start(f32[8,32,256]{2,1,0:T(8,128)S(1)} %pad_maximum_fusion.2.refs_0_), channel_id=1, source_target_pairs={{0,4},{1,5},{2,6},{3,7},{4,0},{5,1},{6,2},{7,3},{8,12},{9,13},{10,... | collective-permute-start | bytes 786440 | tf_op jit(solution)/shard_map/ppermute | solution.py:429
  103.3 12.0 %collective-permute-start.41 = (f32[8,40,256]{2,1,0:T(8,128)S(1)}, f32[8,40,256]{2,1,0:T(8,128)S(1)}, u32[]{:S(2)}, u32[]{:S(2)}) collective-permute-start(f32[8,40,256]{2,1,0:T(8,128)S(1)} %pad_maximum_fusion.refs_0_), channel_id=1, source_target_pairs={{0,2},{1,3},{2,0},{3,1},{4,6},{5,7},{6,4},{7,5},{8,10},{9,11},{10,... | collective-permute-start | bytes 983048 | tf_op jit(solution)/shard_map/ppermute | solution.py:429
  (20 other events, 86.3 us)
